TPU v7x, 32 devices: a whole 2x2x4 slice. The times are simulated.
32 devices in a mesh: groups: 2 (over y), tm: 4 (over z), band: 2 (over x), pol: 2 (over core).
Axes of the slice: x: 2, y: 2, z: 4, core: 2. Of those that a mesh axis runs over, the one named last changes fastest.
Arguments:
- signal: float32 [16, 2, 2, 16384], P(('groups', 'band'), 'pol', None, 'tm'), parts along dimension 0, may hold values from -3 to 3
- cotangent: float32 [16, 2, 2, 16384], P(('groups', 'band'), 'pol', None, 'tm'), parts along dimension 0, may hold values from -6 to 6
- taps: float32 [2, 8, 2, 128], P(None, 'band'), may hold values from -0.375 to 0.375
- gains: float32 [2, 8], P(None, 'band'), may hold values from 0.005 to 0.02
- walk_off: int32 [2, 8], P(None, 'band'), may hold values from 0 to 2048, as said below
- tap_shift: int32 [2, 8], P(None, 'band'), may hold values from -64 to 64, as said below
Outputs:
- grad_signal: float32 [16, 2, 2, 16384], P(('groups', 'band'), 'pol', None, 'tm'), parts along dimension 0
- grad_taps: float32 [4, 8, 2, 128], P('groups', 'band'), parts along dimension 0
There are 2 independent parts, one for each index of `groups`. A program takes and returns all parts, laid end to end along the dimension named above; an argument that names none is the same for every part. Nothing has to cross between parts.
Inputs may be any that keep to these rules, and one draw needn't show every extreme that they name: `walk_off`: in every step the delay is 0 at one end subband and 2048 at the other, and rises or falls roughly evenly with the subband index. `tap_shift`: in every step some subband has 64 and another has minus 64.
All inputs are finite; a program needn't handle non-finite values.
Results may differ from a plain program's by a relative error of at most 0.00011.
Values sent between devices are 32-bit elements; how exact they have to be, the bound alone decides.
No kernel may reach another device: no remote copies, remote signals or barrier semaphores. Data moves between devices by JAX's collectives and lax.ppermute only.
A program may use at most 64 MiB of HBM per device.

v0:
```python
import functools
import math

import jax
import jax.numpy as jnp
from jax import lax
from jax.experimental import pallas as pl
from jax.experimental.pallas import tpu as pltpu
from jax.sharding import PartitionSpec as P

LANES = 128
REACH = 2048 // LANES
EDGE = 4
PAD = 8
F32 = jnp.float32
BF16 = jnp.bfloat16

TWO_OVER_PI = 2.0 / math.pi
HALF_PI_1 = 1.5625
HALF_PI_2 = 67.0 / 8192.0
HALF_PI_3 = 123.0 / 1048576.0
HALF_PI_4 = math.pi / 2.0 - HALF_PI_1 - HALF_PI_2 - HALF_PI_3


def split(x):
    high = x.astype(BF16)
    return high, (x - high.astype(F32)).astype(BF16)


def sine_cosine(x):
    turns = jnp.floor(x * TWO_OVER_PI + 0.5)
    quadrant = turns.astype(jnp.int32)
    r = x - turns * HALF_PI_1
    r = r - turns * HALF_PI_2
    r = r - turns * HALF_PI_3
    r = r - turns * HALF_PI_4
    r2 = r * r
    s = r + r * r2 * (-1.6666654611e-1 + r2 * (8.3321608736e-3 + r2 * -1.9515295891e-4))
    c = 1.0 - 0.5 * r2 + r2 * r2 * (
        4.166664568298827e-2 + r2 * (-1.388731625493765e-3 + r2 * 2.443315711809948e-5)
    )
    odd = (quadrant & 1) == 1
    sine = jnp.where(odd, c, s)
    cosine = jnp.where(odd, s, c)
    sine = jnp.where((quadrant & 2) == 2, -sine, sine)
    cosine = jnp.where(((quadrant + 1) & 2) == 2, -cosine, cosine)
    return sine, cosine


def lanes_of(shape):
    return lax.broadcasted_iota(jnp.int32, shape, len(shape) - 1)


def later(x, amount):
    rolled = pltpu.roll(x, amount & (LANES - 1), 1)
    return jnp.where(lanes_of(x.shape) >= amount, rolled, pltpu.roll(rolled, 1, 0))


def earlier(x, amount):
    rows = x.shape[0]
    rolled = pltpu.roll(x, (LANES - amount) & (LANES - 1), 1)
    follow = pltpu.roll(rolled, rows - 1, 0)
    return jnp.where(lanes_of(x.shape) + amount < LANES, rolled, follow)


def is_even():
    return lax.rem(lax.axis_index("tm"), 2) == 0


def keep_inside(values, rows):
    z = lax.axis_index("tm")
    row = lax.broadcasted_iota(jnp.int32, values.shape, 0)
    low = jnp.where(z == 0, PAD, 0)
    high = jnp.where(z == lax.axis_size("tm") - 1, PAD + rows, 2 * PAD + rows)
    return jnp.where((row >= low) & (row < high), values, 0.0)


def extend(out, own, even_in, odd_in, first):
    bands, _, rows, _ = own.shape
    even = is_even()
    for b in range(bands):
        for c in range(2):
            e = even_in[b, c, first : first + EDGE, :]
            o = odd_in[b, c, first : first + EDGE, :]
            out[b, c, 0:PAD, :] = jnp.zeros((PAD, LANES), F32)
            out[b, c, PAD - EDGE : PAD, :] = jnp.where(even, o, e)
            out[b, c, PAD : PAD + rows, :] = own[b, c]
            out[b, c, PAD + rows :, :] = jnp.zeros((PAD, LANES), F32)
            out[b, c, PAD + rows : PAD + rows + EDGE, :] = jnp.where(even, e, o)


def fir(real, imag, high, low):
    rows = real.shape[0]
    x = jnp.concatenate(
        [real, pltpu.roll(real, rows - 1, 0), imag, pltpu.roll(imag, rows - 1, 0)], 1
    )
    xh, xl = split(x)
    contract = (((1,), (1,)), ((), ()))
    both = lax.dot_general(jnp.concatenate([xh, xl], 0), high, contract, preferred_element_type=F32)
    rest = lax.dot_general(xh, low, contract, preferred_element_type=F32)
    y = both[:rows] + both[rows:] + rest
    return y[:, :LANES], y[:, LANES:]


def fir_adjoint(real, imag, high, low):
    rows = real.shape[0]
    xh, xl = split(jnp.concatenate([real, imag], 1))
    both = jnp.dot(jnp.concatenate([xh, xl], 0), high, preferred_element_type=F32)
    rest = jnp.dot(xh, low, preferred_element_type=F32)
    g = both[:rows] + both[rows:] + rest
    out_real = g[:, :LANES] + pltpu.roll(g[:, LANES : 2 * LANES], 1, 0)
    out_imag = g[:, 2 * LANES : 3 * LANES] + pltpu.roll(g[:, 3 * LANES :], 1, 0)
    return out_real, out_imag


def scatter_delayed(values, delays, step, held, out):
    bands = len(values)
    rows = values[0].shape[0]
    total = rows + REACH
    base = REACH + 8
    lane = lanes_of((total, LANES))
    acc = None
    for b in range(bands):
        delay = delays[step, b]
        q = lax.shift_right_logical(delay, 7)
        s = delay & (LANES - 1)
        held[b, 0:base, :] = jnp.zeros((base, LANES), F32)
        held[b, base : base + rows, :] = pltpu.roll(values[b], s, 1)
        held[b, base + rows :, :] = jnp.zeros((held.shape[1] - base - rows, LANES), F32)
        near = held[b, pl.ds(base - q, total), :]
        far = held[b, pl.ds(base - q - 1, total), :]
        part = jnp.where(lane >= s, near, far)
        acc = part if acc is None else acc + part
    out[...] = acc


def gather_spread(own, even_in, odd_in, spread, rows):
    even = is_even()
    e, o = even_in[...], odd_in[...]
    before = jnp.where(even, o, e)
    after = jnp.where(even, e, o)
    width = REACH + PAD
    total = rows + REACH + 2 * PAD
    spread[0:PAD, :] = before[rows - PAD : rows]
    spread[PAD:total - PAD, :] = own[...]
    spread[total - PAD : total, :] = after[REACH : REACH + PAD]
    spread[PAD : PAD + REACH, :] += before[rows : rows + REACH]
    spread[PAD + rows : PAD + rows + REACH, :] += after[0:REACH]
    values = spread[...]
    row = lax.broadcasted_iota(jnp.int32, values.shape, 0)
    last = lax.axis_index("tm") == lax.axis_size("tm") - 1
    return jnp.where(row < jnp.where(last, PAD + rows, total), values, 0.0)


def read_spread(values, delay, held, b, rows):
    total = values.shape[0]
    q = lax.shift_right_logical(delay, 7)
    s = delay & (LANES - 1)
    held[b, 0:total, :] = pltpu.roll(values, (LANES - s) & (LANES - 1), 1)
    held[b, total:, :] = jnp.zeros((held.shape[1] - total, LANES), F32)
    count = rows + 2 * PAD
    near = held[b, pl.ds(q, count), :]
    far = held[b, pl.ds(q + 1, count), :]
    return jnp.where(lanes_of((count, LANES)) + s < LANES, near, far)


def k_rows(signal, cotangent, sig_rows, cot_rows, even_out, odd_out):
    bands = signal.shape[0]
    rows = sig_rows.shape[2]
    even = is_even()
    for source, target, first in ((signal, sig_rows, 0), (cotangent, cot_rows, EDGE)):
        for b in range(bands):
            for r in range(rows):
                pair = source[b, 0, :, r * LANES : (r + 1) * LANES]
                target[b, 0, r : r + 1, :] = pair[0:1]
                target[b, 1, r : r + 1, :] = pair[1:2]
            for c in range(2):
                left = target[b, c, 0:EDGE, :]
                right = target[b, c, rows - EDGE : rows, :]
                even_out[b, c, first : first + EDGE, :] = jnp.where(even, right, left)
                odd_out[b, c, first : first + EDGE, :] = jnp.where(even, left, right)


def k_tables(taps, *tables):
    steps, bands = taps.shape[:2]
    shape = (LANES, LANES)
    diagonal = lanes_of(shape) >= lax.broadcasted_iota(jnp.int32, shape, 0)
    for step in range(steps):
        high, low = tables[2 * step : 2 * step + 2]
        for b in range(bands):
            for c in range(2):
                row = jnp.broadcast_to(taps[step, b, c : c + 1, :], shape)
                ring = pltpu.roll(row, 0, 1, stride=1, stride_axis=0)
                first = jnp.where(diagonal, ring, 0.0)
                for place, half in ((0, first), (1, ring - first)):
                    for target, value in zip((high, low), split(half)):
                        a = place * LANES
                        d = (2 + place) * LANES
                        if c == 0:
                            target[b, 0:LANES, a : a + LANES] = value
                            target[b, LANES:, d : d + LANES] = value
                        else:
                            target[b, LANES:, a : a + LANES] = value
                            target[b, 0:LANES, d : d + LANES] = -value


def k_first(delays, shifts, sig_rows, even_in, odd_in, high, low, shifted, linear, out, ext, held):
    bands, _, rows, _ = sig_rows.shape
    extend(ext, sig_rows, even_in, odd_in, 0)
    powers = []
    for b in range(bands):
        amount = LANES // 2 - shifts[0, b]
        real = later(ext[b, 0], amount)
        imag = later(ext[b, 1], amount)
        shifted[b, 0] = real
        shifted[b, 1] = imag
        lr, li = fir(real, imag, high[b], low[b])
        linear[b, 0] = lr
        linear[b, 1] = li
        lr, li = lr[PAD : PAD + rows], li[PAD : PAD + rows]
        powers.append(lr * lr + li * li)
    scatter_delayed(powers, delays, 0, held, out)


def k_second(
    delays, shifts, gains, linear0, own, even_in, odd_in, high, low,
    cosine0, sine0, field1, shifted, linear1, out, spread, held, held_out,
):
    bands = linear0.shape[0]
    rows = linear0.shape[2] - 2 * PAD
    values = gather_spread(own, even_in, odd_in, spread, rows)
    powers = []
    for b in range(bands):
        phase = gains[0, b] * read_spread(values, delays[0, b], held, b, rows)
        sine, cosine = sine_cosine(phase)
        cosine0[b] = cosine
        sine0[b] = sine
        lr, li = linear0[b, 0], linear0[b, 1]
        fr = keep_inside(lr * cosine - li * sine, rows)
        fi = keep_inside(lr * sine + li * cosine, rows)
        field1[b, 0] = fr
        field1[b, 1] = fi
        amount = LANES // 2 - shifts[1, b]
        real = later(fr, amount)
        imag = later(fi, amount)
        shifted[b, 0] = real
        shifted[b, 1] = imag
        lr, li = fir(real, imag, high[b], low[b])
        linear1[b, 0] = lr
        linear1[b, 1] = li
        lr, li = lr[PAD : PAD + rows], li[PAD : PAD + rows]
        powers.append(lr * lr + li * li)
    scatter_delayed(powers, delays, 1, held_out, out)


def k_third(
    delays, gains, linear1, own, even_in, odd_in, cot_rows, even_edge, odd_edge,
    turned1, out, ext, spread, held, held_out,
):
    bands = linear1.shape[0]
    rows = linear1.shape[2] - 2 * PAD
    extend(ext, cot_rows, even_edge, odd_edge, EDGE)
    values = gather_spread(own, even_in, odd_in, spread, rows)
    terms = []
    for b in range(bands):
        phase = gains[1, b] * read_spread(values, delays[1, b], held, b, rows)
        sine, cosine = sine_cosine(phase)
        gr, gi = ext[b, 0], ext[b, 1]
        er = gr * cosine + gi * sine
        ei = gi * cosine - gr * sine
        turned1[b, 0] = er
        turned1[b, 1] = ei
        term = ei * linear1[b, 0] - er * linear1[b, 1]
        terms.append(gains[1, b] * term[PAD : PAD + rows])
    scatter_delayed(terms, delays, 1, held_out, out)


def k_fourth(
    delays, shifts, gains, turned1, linear1, own, even_in, odd_in, high, low, cosine0, sine0, field1,
    grad1, turned0, out, spread, held, held_out,
):
    bands = linear1.shape[0]
    rows = linear1.shape[2] - 2 * PAD
    values = gather_spread(own, even_in, odd_in, spread, rows)
    terms = []
    for b in range(bands):
        twice = 2.0 * read_spread(values, delays[1, b], held, b, rows)
        gr = keep_inside(turned1[b, 0] + linear1[b, 0] * twice, rows)
        gi = keep_inside(turned1[b, 1] + linear1[b, 1] * twice, rows)
        grad1[b, 0] = gr
        grad1[b, 1] = gi
        gr, gi = fir_adjoint(gr, gi, high[b], low[b])
        amount = LANES // 2 - shifts[1, b]
        gr = earlier(gr, amount)
        gi = earlier(gi, amount)
        cosine, sine = cosine0[b], sine0[b]
        turned0[b, 0] = gr * cosine + gi * sine
        turned0[b, 1] = gi * cosine - gr * sine
        term = gi * field1[b, 0] - gr * field1[b, 1]
        terms.append(gains[0, b] * term[PAD : PAD + rows])
    scatter_delayed(terms, delays, 0, held_out, out)


def correlate(real, imag, grad_real, grad_imag, rows):
    inside = slice(PAD, PAD + rows)
    following = slice(PAD + 1, PAD + rows + 1)
    a = jnp.concatenate(
        [
            jnp.concatenate([real[inside], real[following]], 1),
            jnp.concatenate([imag[inside], imag[following]], 1),
        ],
        0,
    )
    gr, gi = grad_real[inside], grad_imag[inside]
    d = jnp.concatenate([jnp.concatenate([gr, gi], 1), jnp.concatenate([gi, -gr], 1)], 0)
    ah, al = split(a)
    dh, dl = split(d)
    table = lax.dot_general(
        jnp.concatenate([dh, dh, dl], 0),
        jnp.concatenate([ah, al, ah], 0),
        (((0,), (0,)), ((), ())),
        preferred_element_type=F32,
    )
    width = 2 * LANES
    results = []
    for c in range(2):
        acc = table[c * LANES : c * LANES + 8]
        for g in range(1, LANES // 8):
            first = c * LANES + 8 * g
            acc = acc + pltpu.roll(table[first : first + 8], width - 8 * g, 1)
        total = acc[0:1]
        for s in range(1, 8):
            total = total + pltpu.roll(acc, width - s, 1)[s : s + 1]
        results.append(total[:, :LANES])
    return results


def k_taps(shifted, grad, out):
    bands = grad.shape[0]
    rows = grad.shape[2] - 2 * PAD
    for b in range(bands):
        parts = correlate(shifted[b, 0], shifted[b, 1], grad[b, 0], grad[b, 1], rows)
        for c in range(2):
            out[2 * b + c : 2 * b + c + 1, :] = parts[c]


def k_fifth(
    scale, delays, turned0, linear0, own, even_in, odd_in, shifted, taps1,
    grad0, out, spread, held,
):
    bands = linear0.shape[0]
    rows = linear0.shape[2] - 2 * PAD
    values = gather_spread(own, even_in, odd_in, spread, rows)
    for b in range(bands):
        twice = 2.0 * read_spread(values, delays[0, b], held, b, rows)
        gr = keep_inside(turned0[b, 0] + linear0[b, 0] * twice, rows)
        gi = keep_inside(turned0[b, 1] + linear0[b, 1] * twice, rows)
        grad0[b, 0] = gr
        grad0[b, 1] = gi
        parts = correlate(shifted[b, 0], shifted[b, 1], gr, gi, rows)
        for c in range(2):
            out[2 * b + c : 2 * b + c + 1, :] = parts[c] * scale
    out[2 * bands :, :] = taps1[...] * scale


def k_last(shifts, grad0, high, low, result):
    bands = grad0.shape[0]
    rows = grad0.shape[2] - 2 * PAD
    for b in range(bands):
        gr, gi = fir_adjoint(grad0[b, 0], grad0[b, 1], high[b], low[b])
        amount = LANES // 2 - shifts[0, b]
        gr = earlier(gr, amount)[PAD : PAD + rows]
        gi = earlier(gi, amount)[PAD : PAD + rows]
        for r in range(rows):
            result[b, 0, 0:1, r * LANES : (r + 1) * LANES] = gr[r : r + 1]
            result[b, 0, 1:2, r * LANES : (r + 1) * LANES] = gi[r : r + 1]


def call(kernel, scalars, arrays, shapes, scratch=(), micros=2.0):
    smem = pl.BlockSpec(memory_space=pltpu.SMEM)
    vmem = pl.BlockSpec(memory_space=pltpu.VMEM)
    return pl.pallas_call(
        kernel,
        out_shape=shapes,
        in_specs=[smem] * len(scalars) + [vmem] * len(arrays),
        out_specs=[vmem] * len(shapes),
        scratch_shapes=[pltpu.VMEM(s, F32) for s in scratch],
        compiler_params=pltpu.CompilerParams(vmem_limit_bytes=24 * 1024 * 1024),
        cost_estimate=pl.CostEstimate(
            flops=int(micros * 1e8), bytes_accessed=int(micros * 3e6), transcendentals=0
        ),
    )(*scalars, *arrays)


def swapped(x, axis, distance):
    size = lax.axis_size(axis)
    return lax.ppermute(x, axis, [(i, i ^ distance) for i in range(size)])


def summed(x, axis):
    size = lax.axis_size(axis)
    if size & (size - 1):
        return lax.psum(x, axis)
    distance = 1
    while distance < size:
        x = x + swapped(x, axis, distance)
        distance *= 2
    return x


def neighbours(even_out, odd_out):
    size = lax.axis_size("tm")
    evens = [(i, i ^ 1) for i in range(size) if (i ^ 1) < size]
    odds = [(i, ((i + 1) ^ 1) - 1) for i in range(size)]
    odds = [(i, j) for i, j in odds if 0 <= j < size]
    return lax.ppermute(even_out, "tm", evens), lax.ppermute(odd_out, "tm", odds)


def exchanged(part):
    part = summed(part, "pol")
    part = summed(part, "band")
    return (part,) + neighbours(part, part)


def on_device(signal, cotangent, taps, gains, walk_off, tap_shift):
    bands, _, _, length = signal.shape
    steps = taps.shape[0]
    rows = length // LANES
    held_rows = rows + 2 * PAD

    def shape(*dims, dtype=F32):
        return jax.ShapeDtypeStruct(dims, dtype)

    own = shape(bands, 2, rows, LANES)
    field = shape(bands, 2, held_rows, LANES)
    angle = shape(bands, held_rows, LANES)
    edge = shape(bands, 2, 2 * EDGE, LANES)
    part = shape(rows + REACH, LANES)
    table = shape(bands, 2 * LANES, 4 * LANES, dtype=BF16)
    ext = (bands, 2, held_rows, LANES)
    spread = (rows + REACH + 2 * PAD, LANES)
    held_in = (bands, rows + REACH + 3 * PAD, LANES)
    held_out = (bands, rows + 3 * REACH, LANES)

    sig_rows, cot_rows, even_out, odd_out = call(
        k_rows, (), (signal, cotangent), [own, own, edge, edge]
    )
    even_edge, odd_edge = neighbours(even_out, odd_out)
    taps, even_out = lax.optimization_barrier((taps, even_out))
    high0, low0, high1, low1 = call(k_tables, (), (taps,), [table] * (2 * steps))
    shifted0, linear0, sent = call(
        k_first, (walk_off, tap_shift), (sig_rows, even_edge, odd_edge, high0, low0),
        [field, field, part], (ext, held_out),
    )
    cosine0, sine0, field1, shifted1, linear1, sent = call(
        k_second, (walk_off, tap_shift, gains), (linear0, *exchanged(sent), high1, low1),
        [angle, angle, field, field, field, part], (spread, held_in, held_out),
    )
    turned1, sent = call(
        k_third, (walk_off, gains),
        (linear1, *exchanged(sent), cot_rows, even_edge, odd_edge),
        [field, part], (ext, spread, held_in, held_out),
    )
    grad1, turned0, sent = call(
        k_fourth, (walk_off, tap_shift, gains),
        (turned1, linear1, *exchanged(sent), high1, low1, cosine0, sine0, field1),
        [field, field, part], (spread, held_in, held_out),
    )
    (taps1,) = call(k_taps, (), (shifted1, grad1), [shape(2 * bands, LANES)])
    scale = 1.0 / math.sqrt(2.0 * length * lax.axis_size("tm"))
    grad0, grad_taps = call(
        functools.partial(k_fifth, scale),
        (walk_off,), (turned0, linear0, *exchanged(sent), shifted0, taps1),
        [field, shape(steps * 2 * bands, LANES)], (spread, held_in),
    )
    (grad_signal,) = call(
        k_last, (tap_shift,), (grad0, high0, low0), [shape(bands, 1, 2, length)]
    )
    grad_taps = summed(summed(grad_taps, "pol"), "tm")
    return grad_signal, grad_taps.reshape(steps, bands, 2, LANES)


def solution(mesh):
    return jax.shard_map(
        on_device,
        mesh=mesh,
        in_specs=(
            P(("groups", "band"), "pol", None, "tm"),
            P(("groups", "band"), "pol", None, "tm"),
            P(None, "band", None, None),
            P(None, "band"),
            P(None, "band"),
            P(None, "band"),
        ),
        out_specs=(P(("groups", "band"), "pol", None, "tm"), P("groups", "band", None, None)),
        check_vma=False,
    )
```

profile of v0, /device:TPU:0, one launch (start us, length us, event | category | flops | bytes accessed | tf_op | source)
XLA Modules:
  0.0 76.9 jit_solution(6037784237884711198)
XLA Ops:
  0.6 0.0 copy-start.3
  0.6 0.9 %copy-done.3 = f32[4,1,2,4096]{3,2,1,0:T(2,128)S(1)} copy-done((f32[4,1,2,4096]{3,2,1,0:T(2,128)S(1)}, f32[4,1,2,4096]{3,2,1,0:T(2,128)}, u32[]{:S(2)}) %copy-start.3) | copy-done | bytes 131096
  1.5 0.0 copy-start.4
  1.5 0.9 %copy-done.4 = f32[4,1,2,4096]{3,2,1,0:T(2,128)S(1)} copy-done((f32[4,1,2,4096]{3,2,1,0:T(2,128)S(1)}, f32[4,1,2,4096]{3,2,1,0:T(2,128)}, u32[]{:S(2)}) %copy-start.4) | copy-done | bytes 131096
  2.4 0.0 copy-start.5
  2.4 0.2 shard_map.77
  2.6 0.7 collective-permute-start.1
  3.3 5.9 %collective-permute-start = (f32[4,2,8,128]{3,2,1,0:T(8,128)S(1)}, f32[4,2,8,128]{3,2,1,0:T(8,128)S(1)}, u32[]{:S(2)}, u32[]{:S(2)}) collective-permute-start(f32[4,2,8,128]{3,2,1,0:T(8,128)S(1)} %get-tuple-element.28), channel_id=1, source_target_pairs={{0,4},{4,0},{8,12},{12,8},{1,5},{5,1},{9,13},{13,9},{2,6},{6,2},{1... | collective-permute-start | bytes 98312 | tf_op jit(solution)/shard_map/ppermute | solution.py:416
  9.2 0.0 copy-done.5
  9.2 0.0 copy-start.1
  9.2 0.6 shard_map.78
  9.8 0.0 collective-permute-done.1.odd_in.odd_edge
  9.8 1.3 %collective-permute-done.even_in.even_edge = f32[4,2,8,128]{3,2,1,0:T(8,128)S(1)} collective-permute-done((f32[4,2,8,128]{3,2,1,0:T(8,128)S(1)}, f32[4,2,8,128]{3,2,1,0:T(8,128)S(1)}, u32[]{:S(2)}, u32[]{:S(2)}) %collective-permute-start) | collective-permute-done | bytes 32800 | tf_op jit(solution)/shard_map/ppermute | solution.py:416
  11.1 0.0 copy-start
  11.1 0.0 copy-done.1
  11.1 0.7 copy-done
  11.8 1.4 %shard_map.79 = (f32[4,2,48,128]{3,2,1,0:T(8,128)S(1)}, f32[4,2,48,128]{3,2,1,0:T(8,128)S(1)}, f32[48,128]{1,0:T(8,128)S(1)}) custom-call(s32[2,4]{1,0:T(2,128)S(1)} %copy-done.1, s32[2,4]{1,0:T(2,128)S(1)} %copy-done, f32[4,2,32,128]{3,2,1,0:T(8,128)S(1)} %get-tuple-element.27.sig_rows, f32[4,2,8,128]{3,2,1,0:T(8,128)S(1)} %collective-permute-done.even_in.even_edge, ...), custom_call_target="tpu_custom_call" | custom-call | flops 200000000 | bytes 6000000 | tf_op jit(solution)/shard_map/pallas_call | solution.py:382
  13.2 0.1 collective-permute-start.2
  13.2 1.2 %collective-permute-done.2 = f32[48,128]{1,0:T(8,128)S(1)} collective-permute-done((f32[48,128]{1,0:T(8,128)S(1)}, f32[48,128]{1,0:T(8,128)S(1)}, u32[]{:S(2)}, u32[]{:S(2)}) %collective-permute-start.2) | collective-permute-done | bytes 24608 | tf_op jit(solution)/shard_map/ppermute | solution.py:397
  14.4 1.5 %collective-permute-start.3 = (f32[48,128]{1,0:T(8,128)S(1)}, f32[48,128]{1,0:T(8,128)S(1)}, u32[]{:S(2)}, u32[]{:S(2)}) collective-permute-start(f32[48,128]{1,0:T(8,128)S(1)} %add.33), channel_id=1, source_target_pairs={{0,2},{2,0},{1,3},{3,1},{4,6},{6,4},{5,7},{7,5},{8,10},{10,8},{9,1... | collective-permute-start | bytes 73736 | tf_op jit(solution)/shard_map/ppermute | solution.py:397
  15.9 2.3 %collective-permute-done.3 = f32[48,128]{1,0:T(8,128)S(1)} collective-permute-done((f32[48,128]{1,0:T(8,128)S(1)}, f32[48,128]{1,0:T(8,128)S(1)}, u32[]{:S(2)}, u32[]{:S(2)}) %collective-permute-start.3) | collective-permute-done | bytes 24608 | tf_op jit(solution)/shard_map/ppermute | solution.py:397
  18.3 0.7 collective-permute-start.5
  18.9 3.8 %collective-permute-start.4 = (f32[48,128]{1,0:T(8,128)S(1)}, f32[48,128]{1,0:T(8,128)S(1)}, u32[]{:S(2)}, u32[]{:S(2)}) collective-permute-start(f32[48,128]{1,0:T(8,128)S(1)} %add.34.own), channel_id=1, source_target_pairs={{0,4},{4,0},{8,12},{12,8},{1,5},{5,1},{9,13},{13,9},{2,6},{6,2},{1... | collective-permute-start | bytes 73736 | tf_op jit(solution)/shard_map/ppermute | solution.py:416
  22.7 0.0 collective-permute-done.5.odd_in
  22.7 1.8 %collective-permute-done.4.even_in = f32[48,128]{1,0:T(8,128)S(1)} collective-permute-done((f32[48,128]{1,0:T(8,128)S(1)}, f32[48,128]{1,0:T(8,128)S(1)}, u32[]{:S(2)}, u32[]{:S(2)}) %collective-permute-start.4) | collective-permute-done | bytes 24608 | tf_op jit(solution)/shard_map/ppermute | solution.py:416
  24.5 0.0 copy-start.2
  24.5 0.7 copy-done.2
  25.2 1.6 %shard_map.80 = (f32[4,48,128]{2,1,0:T(8,128)S(1)}, f32[4,48,128]{2,1,0:T(8,128)S(1)}, f32[4,2,48,128]{3,2,1,0:T(8,128)S(1)}, f32[4,2,48,128]{3,2,1,0:T(8,128)S(...) custom-call(s32[2,4]{1,0:T(2,128)S(1)} %copy-done.1, s32[2,4]{1,0:T(2,128)S(1)} %copy-done, ...), custom_call_target="tpu_custom_call" | custom-call | flops 200000000 | bytes 6000000 | tf_op jit(solution)/shard_map/pallas_call | solution.py:382
  26.8 0.1 collective-permute-start.6
  26.8 1.2 %collective-permute-done.6 = f32[48,128]{1,0:T(8,128)S(1)} collective-permute-done((f32[48,128]{1,0:T(8,128)S(1)}, f32[48,128]{1,0:T(8,128)S(1)}, u32[]{:S(2)}, u32[]{:S(2)}) %collective-permute-start.6) | collective-permute-done | bytes 24608 | tf_op jit(solution)/shard_map/ppermute | solution.py:397
  28.0 1.5 %collective-permute-start.7 = (f32[48,128]{1,0:T(8,128)S(1)}, f32[48,128]{1,0:T(8,128)S(1)}, u32[]{:S(2)}, u32[]{:S(2)}) collective-permute-start(f32[48,128]{1,0:T(8,128)S(1)} %add.35), channel_id=1, source_target_pairs={{0,2},{2,0},{1,3},{3,1},{4,6},{6,4},{5,7},{7,5},{8,10},{10,8},{9,1... | collective-permute-start | bytes 73736 | tf_op jit(solution)/shard_map/ppermute | solution.py:397
  29.5 2.3 %collective-permute-done.7 = f32[48,128]{1,0:T(8,128)S(1)} collective-permute-done((f32[48,128]{1,0:T(8,128)S(1)}, f32[48,128]{1,0:T(8,128)S(1)}, u32[]{:S(2)}, u32[]{:S(2)}) %collective-permute-start.7) | collective-permute-done | bytes 24608 | tf_op jit(solution)/shard_map/ppermute | solution.py:397
  31.9 0.7 collective-permute-start.9
  32.5 4.9 %collective-permute-start.8 = (f32[48,128]{1,0:T(8,128)S(1)}, f32[48,128]{1,0:T(8,128)S(1)}, u32[]{:S(2)}, u32[]{:S(2)}) collective-permute-start(f32[48,128]{1,0:T(8,128)S(1)} %add.36.own), channel_id=1, source_target_pairs={{0,4},{4,0},{8,12},{12,8},{1,5},{5,1},{9,13},{13,9},{2,6},{6,2},{1... | collective-permute-start | bytes 73736 | tf_op jit(solution)/shard_map/ppermute | solution.py:416
  37.4 0.0 collective-permute-done.9.odd_in
  37.4 1.8 %collective-permute-done.8.even_in = f32[48,128]{1,0:T(8,128)S(1)} collective-permute-done((f32[48,128]{1,0:T(8,128)S(1)}, f32[48,128]{1,0:T(8,128)S(1)}, u32[]{:S(2)}, u32[]{:S(2)}) %collective-permute-start.8) | collective-permute-done | bytes 24608 | tf_op jit(solution)/shard_map/ppermute | solution.py:416
  39.2 0.9 %shard_map.81 = (f32[4,2,48,128]{3,2,1,0:T(8,128)S(1)}, f32[48,128]{1,0:T(8,128)S(1)}) custom-call(s32[2,4]{1,0:T(2,128)S(1)} %copy-done.1, f32[2,4]{1,0:T(2,128)S(1)} %copy-done.2, f32[4,2,48,128]{3,2,1,0:T(8,128)S(1)} %get-tuple-element.37.linear1, f32[48,128]{1,0:T(8,128)S(1)} %add.36.own, f32[48,128]{1,0:T(8,128)S(1)} %collective-permute-done.8.even_in, ...), custom_call_target="tpu_custom_call" | custom-call | flops 200000000 | bytes 6000000 | tf_op jit(solution)/shard_map/pallas_call | solution.py:382
  40.2 0.1 collective-permute-start.10
  40.2 1.2 %collective-permute-done.10 = f32[48,128]{1,0:T(8,128)S(1)} collective-permute-done((f32[48,128]{1,0:T(8,128)S(1)}, f32[48,128]{1,0:T(8,128)S(1)}, u32[]{:S(2)}, u32[]{:S(2)}) %collective-permute-start.10) | collective-permute-done | bytes 24608 | tf_op jit(solution)/shard_map/ppermute | solution.py:397
  41.4 1.5 %collective-permute-start.11 = (f32[48,128]{1,0:T(8,128)S(1)}, f32[48,128]{1,0:T(8,128)S(1)}, u32[]{:S(2)}, u32[]{:S(2)}) collective-permute-start(f32[48,128]{1,0:T(8,128)S(1)} %add.37), channel_id=1, source_target_pairs={{0,2},{2,0},{1,3},{3,1},{4,6},{6,4},{5,7},{7,5},{8,10},{10,8},{9,1... | collective-permute-start | bytes 73736 | tf_op jit(solution)/shard_map/ppermute | solution.py:397
  42.9 2.3 %collective-permute-done.11 = f32[48,128]{1,0:T(8,128)S(1)} collective-permute-done((f32[48,128]{1,0:T(8,128)S(1)}, f32[48,128]{1,0:T(8,128)S(1)}, u32[]{:S(2)}, u32[]{:S(2)}) %collective-permute-start.11) | collective-permute-done | bytes 24608 | tf_op jit(solution)/shard_map/ppermute | solution.py:397
  45.3 0.7 collective-permute-start.13
  45.9 3.8 %collective-permute-start.12 = (f32[48,128]{1,0:T(8,128)S(1)}, f32[48,128]{1,0:T(8,128)S(1)}, u32[]{:S(2)}, u32[]{:S(2)}) collective-permute-start(f32[48,128]{1,0:T(8,128)S(1)} %add.38.own), channel_id=1, source_target_pairs={{0,4},{4,0},{8,12},{12,8},{1,5},{5,1},{9,13},{13,9},{2,6},{6,2},{1... | collective-permute-start | bytes 73736 | tf_op jit(solution)/shard_map/ppermute | solution.py:416
  49.7 0.0 collective-permute-done.13.odd_in
  49.7 1.8 %collective-permute-done.12.even_in = f32[48,128]{1,0:T(8,128)S(1)} collective-permute-done((f32[48,128]{1,0:T(8,128)S(1)}, f32[48,128]{1,0:T(8,128)S(1)}, u32[]{:S(2)}, u32[]{:S(2)}) %collective-permute-start.12) | collective-permute-done | bytes 24608 | tf_op jit(solution)/shard_map/ppermute | solution.py:416
  51.5 1.3 %shard_map.82 = (f32[4,2,48,128]{3,2,1,0:T(8,128)S(1)}, f32[4,2,48,128]{3,2,1,0:T(8,128)S(1)}, f32[48,128]{1,0:T(8,128)S(1)}) custom-call(s32[2,4]{1,0:T(2,128)S(1)} %copy-done.1, s32[2,4]{1,0:T(2,128)S(1)} %copy-done, f32[2,4]{1,0:T(2,128)S(1)} %copy-done.2, f32[4,2,48,128]{3,2,1,0:T(8,128)S(1)} %get-tuple-element.40.turned1, ...), custom_call_target="tpu_custom_call" | custom-call | flops 200000000 | bytes 6000000 | tf_op jit(solution)/shard_map/pallas_call | solution.py:382
  52.8 0.1 collective-permute-start.14
  52.9 1.2 %collective-permute-done.14 = f32[48,128]{1,0:T(8,128)S(1)} collective-permute-done((f32[48,128]{1,0:T(8,128)S(1)}, f32[48,128]{1,0:T(8,128)S(1)}, u32[]{:S(2)}, u32[]{:S(2)}) %collective-permute-start.14) | collective-permute-done | bytes 24608 | tf_op jit(solution)/shard_map/ppermute | solution.py:397
  54.0 1.5 %collective-permute-start.15 = (f32[48,128]{1,0:T(8,128)S(1)}, f32[48,128]{1,0:T(8,128)S(1)}, u32[]{:S(2)}, u32[]{:S(2)}) collective-permute-start(f32[48,128]{1,0:T(8,128)S(1)} %add.39), channel_id=1, source_target_pairs={{0,2},{2,0},{1,3},{3,1},{4,6},{6,4},{5,7},{7,5},{8,10},{10,8},{9,1... | collective-permute-start | bytes 73736 | tf_op jit(solution)/shard_map/ppermute | solution.py:397
  55.5 2.4 %collective-permute-done.15 = f32[48,128]{1,0:T(8,128)S(1)} collective-permute-done((f32[48,128]{1,0:T(8,128)S(1)}, f32[48,128]{1,0:T(8,128)S(1)}, u32[]{:S(2)}, u32[]{:S(2)}) %collective-permute-start.15) | collective-permute-done | bytes 24608 | tf_op jit(solution)/shard_map/ppermute | solution.py:397
  57.9 0.7 collective-permute-start.17
  58.5 4.9 %collective-permute-start.16 = (f32[48,128]{1,0:T(8,128)S(1)}, f32[48,128]{1,0:T(8,128)S(1)}, u32[]{:S(2)}, u32[]{:S(2)}) collective-permute-start(f32[48,128]{1,0:T(8,128)S(1)} %add.40.own), channel_id=1, source_target_pairs={{0,4},{4,0},{8,12},{12,8},{1,5},{5,1},{9,13},{13,9},{2,6},{6,2},{1... | collective-permute-start | bytes 73736 | tf_op jit(solution)/shard_map/ppermute | solution.py:416
  63.4 1.1 %shard_map.83.taps1 = f32[8,128]{1,0:T(8,128)S(1)} custom-call(f32[4,2,48,128]{3,2,1,0:T(8,128)S(1)} %get-tuple-element.48.shifted, f32[4,2,48,128]{3,2,1,0:T(8,128)S(1)} %get-tuple-element.49.grad), custom_call_target="tpu_custom_call" | custom-call | flops 200000000 | bytes 6000000 | tf_op jit(solution)/shard_map/pallas_call | solution.py:382
  64.5 0.0 collective-permute-done.17.odd_in
  64.5 0.7 collective-permute-done.16.even_in
  65.2 1.6 %shard_map.84 = (f32[4,2,48,128]{3,2,1,0:T(8,128)S(1)}, f32[16,128]{1,0:T(8,128)S(1)}) custom-call(s32[2,4]{1,0:T(2,128)S(1)} %copy-done.1, f32[4,2,48,128]{3,2,1,0:T(8,128)S(1)} %get-tuple-element.45.turned0, f32[4,2,48,128]{3,2,1,0:T(8,128)S(1)} %get-tuple-element.33.linear0, f32[48,128]{1,0:T(8,128)S(1)} %add.40.own, ...), custom_call_target="tpu_custom_call" | custom-call | flops 200000000 | bytes 6000000 | tf_op jit(solution)/shard_map/pallas_call | solution.py:382
  66.9 0.1 collective-permute-start.18
  67.0 1.2 %collective-permute-done.18 = f32[16,128]{1,0:T(8,128)S(1)} collective-permute-done((f32[16,128]{1,0:T(8,128)S(1)}, f32[16,128]{1,0:T(8,128)S(1)}, u32[]{:S(2)}, u32[]{:S(2)}) %collective-permute-start.18) | collective-permute-done | bytes 8224 | tf_op jit(solution)/shard_map/ppermute | solution.py:397
  68.1 2.0 %collective-permute-start.19 = (f32[16,128]{1,0:T(8,128)S(1)}, f32[16,128]{1,0:T(8,128)S(1)}, u32[]{:S(2)}, u32[]{:S(2)}) collective-permute-start(f32[16,128]{1,0:T(8,128)S(1)} %add.41), channel_id=1, source_target_pairs={{0,4},{4,0},{8,12},{12,8},{1,5},{5,1},{9,13},{13,9},{2,6},{6,2},{1... | collective-permute-start | bytes 24584 | tf_op jit(solution)/shard_map/ppermute | solution.py:397
  70.1 1.6 %collective-permute-done.19 = f32[16,128]{1,0:T(8,128)S(1)} collective-permute-done((f32[16,128]{1,0:T(8,128)S(1)}, f32[16,128]{1,0:T(8,128)S(1)}, u32[]{:S(2)}, u32[]{:S(2)}) %collective-permute-start.19) | collective-permute-done | bytes 8224 | tf_op jit(solution)/shard_map/ppermute | solution.py:397
  71.8 1.9 %collective-permute-start.20 = (f32[16,128]{1,0:T(8,128)S(1)}, f32[16,128]{1,0:T(8,128)S(1)}, u32[]{:S(2)}, u32[]{:S(2)}) collective-permute-start(f32[16,128]{1,0:T(8,128)S(1)} %add.42), channel_id=1, source_target_pairs={{0,8},{4,12},{8,0},{12,4},{1,9},{5,13},{9,1},{13,5},{2,10},{6,14},... | collective-permute-start | bytes 24584 | tf_op jit(solution)/shard_map/ppermute | solution.py:397
  73.7 1.7 %shard_map.85 = f32[4,1,2,4096]{3,2,1,0:T(2,128)} custom-call(s32[2,4]{1,0:T(2,128)S(1)} %copy-done, f32[4,2,48,128]{3,2,1,0:T(8,128)S(1)} %get-tuple-element.50.grad0, bf16[4,256,512]{2,1,0:T(8,128)(2,1)S(1)} %get-tuple-element.31.high, bf16[4,256,512]{2,1,0:T(8,128)(2,1)S(1)} %get-tuple-element.32.low), custom_call_target="tpu_custom_call" | custom-call | flops 200000000 | bytes 6000000 | tf_op jit(solution)/shard_map/pallas_call | solution.py:382
  75.4 0.9 %collective-permute-done.20 = f32[16,128]{1,0:T(8,128)S(1)} collective-permute-done((f32[16,128]{1,0:T(8,128)S(1)}, f32[16,128]{1,0:T(8,128)S(1)}, u32[]{:S(2)}, u32[]{:S(2)}) %collective-permute-start.20) | collective-permute-done | bytes 8224 | tf_op jit(solution)/shard_map/ppermute | solution.py:397
  76.3 0.6 add.43
  (10 shorter events, 0.0 us)
Async XLA Ops:
  0.6 0.9 %copy-start.3 = (f32[4,1,2,4096]{3,2,1,0:T(2,128)S(1)}, f32[4,1,2,4096]{3,2,1,0:T(2,128)}, u32[]{:S(2)}) copy-start(f32[4,1,2,4096]{3,2,1,0:T(2,128)} %signal.1) | copy-start | bytes 393220
  1.5 0.9 %copy-start.4 = (f32[4,1,2,4096]{3,2,1,0:T(2,128)S(1)}, f32[4,1,2,4096]{3,2,1,0:T(2,128)}, u32[]{:S(2)}) copy-start(f32[4,1,2,4096]{3,2,1,0:T(2,128)} %cotangent.1) | copy-start | bytes 393220
  2.4 6.7 %copy-start.5 = (f32[2,4,2,128]{3,2,1,0:T(2,128)S(1)}, f32[2,4,2,128]{3,2,1,0:T(2,128)}, u32[]{:S(2)}) copy-start(f32[2,4,2,128]{3,2,1,0:T(2,128)} %taps) | copy-start | bytes 24580
  2.6 7.2 %collective-permute-start.1 = (f32[4,2,8,128]{3,2,1,0:T(8,128)S(1)}, f32[4,2,8,128]{3,2,1,0:T(8,128)S(1)}, u32[]{:S(2)}, u32[]{:S(2)}) collective-permute-start(f32[4,2,8,128]{3,2,1,0:T(8,128)S(1)} %get-tuple-element.29), channel_id=1, source_target_pairs={{4,8},{8,4},{5,9},{9,5},{6,10},{10,6},{7,11},{11,7},{20,24},{24,20... | collective-permute-start | bytes 98312 | tf_op jit(solution)/shard_map/ppermute | solution.py:416
  3.3 7.8 %collective-permute-start = (f32[4,2,8,128]{3,2,1,0:T(8,128)S(1)}, f32[4,2,8,128]{3,2,1,0:T(8,128)S(1)}, u32[]{:S(2)}, u32[]{:S(2)}) collective-permute-start(f32[4,2,8,128]{3,2,1,0:T(8,128)S(1)} %get-tuple-element.28), channel_id=1, source_target_pairs={{0,4},{4,0},{8,12},{12,8},{1,5},{5,1},{9,13},{13,9},{2,6},{6,2},{1... | collective-permute-start | bytes 98312 | tf_op jit(solution)/shard_map/ppermute | solution.py:416
  9.2 1.9 %copy-start.1 = (s32[2,4]{1,0:T(2,128)S(1)}, s32[2,4]{1,0:T(2,128)}, u32[]{:S(2)}) copy-start(s32[2,4]{1,0:T(2,128)} %delays.9) | copy-start | bytes 100
  11.1 0.7 copy-start
  13.2 1.3 %collective-permute-start.2 = (f32[48,128]{1,0:T(8,128)S(1)}, f32[48,128]{1,0:T(8,128)S(1)}, u32[]{:S(2)}, u32[]{:S(2)}) collective-permute-start(f32[48,128]{1,0:T(8,128)S(1)} %get-tuple-element.34), channel_id=1, source_target_pairs={{0,1},{1,0},{2,3},{3,2},{4,5},{5,4},{6,7},{7,6},{8,9},{9,8},{10,11... | collective-permute-start | bytes 73736 | tf_op jit(solution)/shard_map/ppermute | solution.py:397
  14.4 3.8 %collective-permute-start.3 = (f32[48,128]{1,0:T(8,128)S(1)}, f32[48,128]{1,0:T(8,128)S(1)}, u32[]{:S(2)}, u32[]{:S(2)}) collective-permute-start(f32[48,128]{1,0:T(8,128)S(1)} %add.33), channel_id=1, source_target_pairs={{0,2},{2,0},{1,3},{3,1},{4,6},{6,4},{5,7},{7,5},{8,10},{10,8},{9,1... | collective-permute-start | bytes 73736 | tf_op jit(solution)/shard_map/ppermute | solution.py:397
  18.3 4.4 %collective-permute-start.5 = (f32[48,128]{1,0:T(8,128)S(1)}, f32[48,128]{1,0:T(8,128)S(1)}, u32[]{:S(2)}, u32[]{:S(2)}) collective-permute-start(f32[48,128]{1,0:T(8,128)S(1)} %add.34.own), channel_id=1, source_target_pairs={{4,8},{8,4},{5,9},{9,5},{6,10},{10,6},{7,11},{11,7},{20,24},{24,20... | collective-permute-start | bytes 73736 | tf_op jit(solution)/shard_map/ppermute | solution.py:416
  18.9 5.6 %collective-permute-start.4 = (f32[48,128]{1,0:T(8,128)S(1)}, f32[48,128]{1,0:T(8,128)S(1)}, u32[]{:S(2)}, u32[]{:S(2)}) collective-permute-start(f32[48,128]{1,0:T(8,128)S(1)} %add.34.own), channel_id=1, source_target_pairs={{0,4},{4,0},{8,12},{12,8},{1,5},{5,1},{9,13},{13,9},{2,6},{6,2},{1... | collective-permute-start | bytes 73736 | tf_op jit(solution)/shard_map/ppermute | solution.py:416
  24.5 0.7 copy-start.2
  26.8 1.3 %collective-permute-start.6 = (f32[48,128]{1,0:T(8,128)S(1)}, f32[48,128]{1,0:T(8,128)S(1)}, u32[]{:S(2)}, u32[]{:S(2)}) collective-permute-start(f32[48,128]{1,0:T(8,128)S(1)} %get-tuple-element.38), channel_id=1, source_target_pairs={{0,1},{1,0},{2,3},{3,2},{4,5},{5,4},{6,7},{7,6},{8,9},{9,8},{10,11... | collective-permute-start | bytes 73736 | tf_op jit(solution)/shard_map/ppermute | solution.py:397
  28.0 3.8 %collective-permute-start.7 = (f32[48,128]{1,0:T(8,128)S(1)}, f32[48,128]{1,0:T(8,128)S(1)}, u32[]{:S(2)}, u32[]{:S(2)}) collective-permute-start(f32[48,128]{1,0:T(8,128)S(1)} %add.35), channel_id=1, source_target_pairs={{0,2},{2,0},{1,3},{3,1},{4,6},{6,4},{5,7},{7,5},{8,10},{10,8},{9,1... | collective-permute-start | bytes 73736 | tf_op jit(solution)/shard_map/ppermute | solution.py:397
  31.9 5.6 %collective-permute-start.9 = (f32[48,128]{1,0:T(8,128)S(1)}, f32[48,128]{1,0:T(8,128)S(1)}, u32[]{:S(2)}, u32[]{:S(2)}) collective-permute-start(f32[48,128]{1,0:T(8,128)S(1)} %add.36.own), channel_id=1, source_target_pairs={{4,8},{8,4},{5,9},{9,5},{6,10},{10,6},{7,11},{11,7},{20,24},{24,20... | collective-permute-start | bytes 73736 | tf_op jit(solution)/shard_map/ppermute | solution.py:416
  32.5 6.7 %collective-permute-start.8 = (f32[48,128]{1,0:T(8,128)S(1)}, f32[48,128]{1,0:T(8,128)S(1)}, u32[]{:S(2)}, u32[]{:S(2)}) collective-permute-start(f32[48,128]{1,0:T(8,128)S(1)} %add.36.own), channel_id=1, source_target_pairs={{0,4},{4,0},{8,12},{12,8},{1,5},{5,1},{9,13},{13,9},{2,6},{6,2},{1... | collective-permute-start | bytes 73736 | tf_op jit(solution)/shard_map/ppermute | solution.py:416
  40.2 1.2 %collective-permute-start.10 = (f32[48,128]{1,0:T(8,128)S(1)}, f32[48,128]{1,0:T(8,128)S(1)}, u32[]{:S(2)}, u32[]{:S(2)}) collective-permute-start(f32[48,128]{1,0:T(8,128)S(1)} %get-tuple-element.41), channel_id=1, source_target_pairs={{0,1},{1,0},{2,3},{3,2},{4,5},{5,4},{6,7},{7,6},{8,9},{9,8},{10,11... | collective-permute-start | bytes 73736 | tf_op jit(solution)/shard_map/ppermute | solution.py:397
  41.4 3.8 %collective-permute-start.11 = (f32[48,128]{1,0:T(8,128)S(1)}, f32[48,128]{1,0:T(8,128)S(1)}, u32[]{:S(2)}, u32[]{:S(2)}) collective-permute-start(f32[48,128]{1,0:T(8,128)S(1)} %add.37), channel_id=1, source_target_pairs={{0,2},{2,0},{1,3},{3,1},{4,6},{6,4},{5,7},{7,5},{8,10},{10,8},{9,1... | collective-permute-start | bytes 73736 | tf_op jit(solution)/shard_map/ppermute | solution.py:397
  45.3 4.4 %collective-permute-start.13 = (f32[48,128]{1,0:T(8,128)S(1)}, f32[48,128]{1,0:T(8,128)S(1)}, u32[]{:S(2)}, u32[]{:S(2)}) collective-permute-start(f32[48,128]{1,0:T(8,128)S(1)} %add.38.own), channel_id=1, source_target_pairs={{4,8},{8,4},{5,9},{9,5},{6,10},{10,6},{7,11},{11,7},{20,24},{24,20... | collective-permute-start | bytes 73736 | tf_op jit(solution)/shard_map/ppermute | solution.py:416
  45.9 5.6 %collective-permute-start.12 = (f32[48,128]{1,0:T(8,128)S(1)}, f32[48,128]{1,0:T(8,128)S(1)}, u32[]{:S(2)}, u32[]{:S(2)}) collective-permute-start(f32[48,128]{1,0:T(8,128)S(1)} %add.38.own), channel_id=1, source_target_pairs={{0,4},{4,0},{8,12},{12,8},{1,5},{5,1},{9,13},{13,9},{2,6},{6,2},{1... | collective-permute-start | bytes 73736 | tf_op jit(solution)/shard_map/ppermute | solution.py:416
  52.8 1.3 %collective-permute-start.14 = (f32[48,128]{1,0:T(8,128)S(1)}, f32[48,128]{1,0:T(8,128)S(1)}, u32[]{:S(2)}, u32[]{:S(2)}) collective-permute-start(f32[48,128]{1,0:T(8,128)S(1)} %get-tuple-element.46), channel_id=1, source_target_pairs={{0,1},{1,0},{2,3},{3,2},{4,5},{5,4},{6,7},{7,6},{8,9},{9,8},{10,11... | collective-permute-start | bytes 73736 | tf_op jit(solution)/shard_map/ppermute | solution.py:397
  54.0 3.8 %collective-permute-start.15 = (f32[48,128]{1,0:T(8,128)S(1)}, f32[48,128]{1,0:T(8,128)S(1)}, u32[]{:S(2)}, u32[]{:S(2)}) collective-permute-start(f32[48,128]{1,0:T(8,128)S(1)} %add.39), channel_id=1, source_target_pairs={{0,2},{2,0},{1,3},{3,1},{4,6},{6,4},{5,7},{7,5},{8,10},{10,8},{9,1... | collective-permute-start | bytes 73736 | tf_op jit(solution)/shard_map/ppermute | solution.py:397
  57.9 6.6 %collective-permute-start.17 = (f32[48,128]{1,0:T(8,128)S(1)}, f32[48,128]{1,0:T(8,128)S(1)}, u32[]{:S(2)}, u32[]{:S(2)}) collective-permute-start(f32[48,128]{1,0:T(8,128)S(1)} %add.40.own), channel_id=1, source_target_pairs={{4,8},{8,4},{5,9},{9,5},{6,10},{10,6},{7,11},{11,7},{20,24},{24,20... | collective-permute-start | bytes 73736 | tf_op jit(solution)/shard_map/ppermute | solution.py:416
  58.5 6.7 %collective-permute-start.16 = (f32[48,128]{1,0:T(8,128)S(1)}, f32[48,128]{1,0:T(8,128)S(1)}, u32[]{:S(2)}, u32[]{:S(2)}) collective-permute-start(f32[48,128]{1,0:T(8,128)S(1)} %add.40.own), channel_id=1, source_target_pairs={{0,4},{4,0},{8,12},{12,8},{1,5},{5,1},{9,13},{13,9},{2,6},{6,2},{1... | collective-permute-start | bytes 73736 | tf_op jit(solution)/shard_map/ppermute | solution.py:416
  66.9 1.2 %collective-permute-start.18 = (f32[16,128]{1,0:T(8,128)S(1)}, f32[16,128]{1,0:T(8,128)S(1)}, u32[]{:S(2)}, u32[]{:S(2)}) collective-permute-start(f32[16,128]{1,0:T(8,128)S(1)} %get-tuple-element.51), channel_id=1, source_target_pairs={{0,1},{1,0},{2,3},{3,2},{4,5},{5,4},{6,7},{7,6},{8,9},{9,8},{10,11... | collective-permute-start | bytes 24584 | tf_op jit(solution)/shard_map/ppermute | solution.py:397
  68.1 3.7 %collective-permute-start.19 = (f32[16,128]{1,0:T(8,128)S(1)}, f32[16,128]{1,0:T(8,128)S(1)}, u32[]{:S(2)}, u32[]{:S(2)}) collective-permute-start(f32[16,128]{1,0:T(8,128)S(1)} %add.41), channel_id=1, source_target_pairs={{0,4},{4,0},{8,12},{12,8},{1,5},{5,1},{9,13},{13,9},{2,6},{6,2},{1... | collective-permute-start | bytes 24584 | tf_op jit(solution)/shard_map/ppermute | solution.py:397
  71.8 4.5 %collective-permute-start.20 = (f32[16,128]{1,0:T(8,128)S(1)}, f32[16,128]{1,0:T(8,128)S(1)}, u32[]{:S(2)}, u32[]{:S(2)}) collective-permute-start(f32[16,128]{1,0:T(8,128)S(1)} %add.42), channel_id=1, source_target_pairs={{0,8},{4,12},{8,0},{12,4},{1,9},{5,13},{9,1},{13,5},{2,10},{6,14},... | collective-permute-start | bytes 24584 | tf_op jit(solution)/shard_map/ppermute | solution.py:397
where the time goes:
time: 77.2 us; the launch traced here: 76.9 us
  starting transfers between devices  36.8 us (48%)
  waiting for transfers between devices  25.2 us (33%)
  Pallas kernels  10.4 us (13%)
  local copies, waits for them, and re-layouts  3.16 us (4%)
  between operations  0.8 us (1%)
    ppermute x5, starting transfers between devices, neighbours(): lax.ppermute(even_out, 'tm', evens)  23.3 us
    ppermute x11, waiting for transfers between devices, swapped(): return lax.ppermute(x, axis, [(i, i ^ distance) for i in range(size)])  17.8 us
    pallas_call x9, Pallas kernels, call(): pl.pallas_call(kernel, out_shape=shapes, in_specs=[smem] * len(scalars) +...  10.4 us
    ppermute x11, starting transfers between devices, swapped(): return lax.ppermute(x, axis, [(i, i ^ distance) for i in range(size)])  10.2 us
    ppermute x5, waiting for transfers between devices, neighbours(): lax.ppermute(even_out, 'tm', evens)  7.37 us
    ppermute x5, starting transfers between devices, neighbours(): lax.ppermute(odd_out, 'tm', odds)  3.27 us
    unnamed x12, local copies, waits for them, and re-layouts  3.16 us
  transfers between devices with their start and end apart: 21, of which 16 were waited for; matrix products, arithmetic and copies ran while one was open for 0% of the time, Pallas kernels for 4%

commit v1 on v0

--- a/solution.py
+++ b/solution.py
@@ -75,18 +75,28 @@
     return jnp.where((row >= low) & (row < high), values, 0.0)
 
 
+def from_sides(even_value, odd_value):
+    z = lax.axis_index("tm")
+    even = is_even()
+    before = jnp.where(even, odd_value, even_value)
+    after = jnp.where(even, even_value, odd_value)
+    before = jnp.where(z == 0, 0.0, before)
+    after = jnp.where(z == lax.axis_size("tm") - 1, 0.0, after)
+    return before, after
+
+
 def extend(out, own, even_in, odd_in, first):
     bands, _, rows, _ = own.shape
-    even = is_even()
     for b in range(bands):
         for c in range(2):
-            e = even_in[b, c, first : first + EDGE, :]
-            o = odd_in[b, c, first : first + EDGE, :]
+            before, after = from_sides(
+                even_in[b, c, first : first + EDGE, :], odd_in[b, c, first : first + EDGE, :]
+            )
             out[b, c, 0:PAD, :] = jnp.zeros((PAD, LANES), F32)
-            out[b, c, PAD - EDGE : PAD, :] = jnp.where(even, o, e)
+            out[b, c, PAD - EDGE : PAD, :] = before
             out[b, c, PAD : PAD + rows, :] = own[b, c]
             out[b, c, PAD + rows :, :] = jnp.zeros((PAD, LANES), F32)
-            out[b, c, PAD + rows : PAD + rows + EDGE, :] = jnp.where(even, e, o)
+            out[b, c, PAD + rows : PAD + rows + EDGE, :] = after
 
 
 def fir(real, imag, high, low):
@@ -135,11 +145,7 @@
 
 
 def gather_spread(own, even_in, odd_in, spread, rows):
-    even = is_even()
-    e, o = even_in[...], odd_in[...]
-    before = jnp.where(even, o, e)
-    after = jnp.where(even, e, o)
-    width = REACH + PAD
+    before, after = from_sides(even_in[...], odd_in[...])
     total = rows + REACH + 2 * PAD
     spread[0:PAD, :] = before[rows - PAD : rows]
     spread[PAD:total - PAD, :] = own[...]
@@ -164,11 +170,21 @@
     return jnp.where(lanes_of((count, LANES)) + s < LANES, near, far)
 
 
-def k_rows(signal, cotangent, sig_rows, cot_rows, even_out, odd_out):
+def k_rows(signal, cotangent, sig_rows, cot_rows, even_out, odd_out, sig_held, cot_held, done):
     bands = signal.shape[0]
     rows = sig_rows.shape[2]
     even = is_even()
-    for source, target, first in ((signal, sig_rows, 0), (cotangent, cot_rows, EDGE)):
+    copies = (
+        pltpu.make_async_copy(signal, sig_held, done.at[0]),
+        pltpu.make_async_copy(cotangent, cot_held, done.at[1]),
+    )
+    for copy in copies:
+        copy.start()
+    for copy, source, target, first in (
+        (copies[0], sig_held, sig_rows, 0),
+        (copies[1], cot_held, cot_rows, EDGE),
+    ):
+        copy.wait()
         for b in range(bands):
             for r in range(rows):
                 pair = source[b, 0, :, r * LANES : (r + 1) * LANES]
@@ -181,8 +197,11 @@
                 odd_out[b, c, first : first + EDGE, :] = jnp.where(even, left, right)
 
 
-def k_tables(taps, *tables):
+def k_tables(taps, delays, shifts, gains, delays_out, shifts_out, gains_out, *tables):
     steps, bands = taps.shape[:2]
+    delays_out[...] = delays[...]
+    shifts_out[...] = shifts[...]
+    gains_out[...] = gains[...]
     shape = (LANES, LANES)
     diagonal = lanes_of(shape) >= lax.broadcasted_iota(jnp.int32, shape, 0)
     for step in range(steps):
@@ -392,34 +411,44 @@
     )(*scalars, *arrays)
 
 
-def swapped(x, axis, distance):
-    size = lax.axis_size(axis)
-    return lax.ppermute(x, axis, [(i, i ^ distance) for i in range(size)])
-
-
-def summed(x, axis):
+def swapped(x, axis, partner, cross):
+    size, cores = lax.axis_size(axis), lax.axis_size("pol")
+    pairs = []
+    for i in range(size):
+        for p in range(cores):
+            j, q = partner(i), cores - 1 - p
+            if 0 <= j < size:
+                pairs.append((i * cores + p, j * cores + (q if cross else p)))
+            else:
+                pairs.append((i * cores + p, i * cores + q))
+    return lax.ppermute(x, (axis, "pol"), pairs)
+
+
+def summed(x, axis, cross=True):
     size = lax.axis_size(axis)
     if size & (size - 1):
         return lax.psum(x, axis)
     distance = 1
     while distance < size:
-        x = x + swapped(x, axis, distance)
+        x = x + swapped(x, axis, lambda i, d=distance: i ^ d, cross)
         distance *= 2
     return x
 
 
-def neighbours(even_out, odd_out):
-    size = lax.axis_size("tm")
-    evens = [(i, i ^ 1) for i in range(size) if (i ^ 1) < size]
-    odds = [(i, ((i + 1) ^ 1) - 1) for i in range(size)]
-    odds = [(i, j) for i, j in odds if 0 <= j < size]
-    return lax.ppermute(even_out, "tm", evens), lax.ppermute(odd_out, "tm", odds)
+def over_cores(x):
+    cores = lax.axis_size("pol")
+    return x + lax.ppermute(x, "pol", [(p, cores - 1 - p) for p in range(cores)])
+
+
+def neighbours(even_out, odd_out, cross):
+    odd_in = swapped(odd_out, "tm", lambda i: ((i + 1) ^ 1) - 1, cross)
+    even_in = swapped(even_out, "tm", lambda i: i ^ 1, cross)
+    return even_in, odd_in
 
 
 def exchanged(part):
-    part = summed(part, "pol")
-    part = summed(part, "band")
-    return (part,) + neighbours(part, part)
+    part = summed(over_cores(part), "band")
+    return (part,) + neighbours(part, part, True)
 
 
 def on_device(signal, cotangent, taps, gains, walk_off, tap_shift):
@@ -442,12 +471,22 @@
     held_in = (bands, rows + REACH + 3 * PAD, LANES)
     held_out = (bands, rows + 3 * REACH, LANES)
 
-    sig_rows, cot_rows, even_out, odd_out = call(
-        k_rows, (), (signal, cotangent), [own, own, edge, edge]
-    )
-    even_edge, odd_edge = neighbours(even_out, odd_out)
+    whole = pltpu.VMEM((bands, 1, 2, length), F32)
+    vmem = pl.BlockSpec(memory_space=pltpu.VMEM)
+    sig_rows, cot_rows, even_out, odd_out = pl.pallas_call(
+        k_rows,
+        out_shape=[own, own, edge, edge],
+        in_specs=[pl.BlockSpec(memory_space=pltpu.HBM)] * 2,
+        out_specs=[vmem] * 4,
+        scratch_shapes=[whole, whole, pltpu.SemaphoreType.DMA((2,))],
+        compiler_params=pltpu.CompilerParams(vmem_limit_bytes=24 * 1024 * 1024),
+    )(signal, cotangent)
+    even_edge, odd_edge = neighbours(even_out, odd_out, False)
     taps, even_out = lax.optimization_barrier((taps, even_out))
-    high0, low0, high1, low1 = call(k_tables, (), (taps,), [table] * (2 * steps))
+    small = [shape(*a.shape, dtype=a.dtype) for a in (walk_off, tap_shift, gains)]
+    walk_off, tap_shift, gains, high0, low0, high1, low1 = call(
+        k_tables, (), (taps, walk_off, tap_shift, gains), small + [table] * (2 * steps)
+    )
     shifted0, linear0, sent = call(
         k_first, (walk_off, tap_shift), (sig_rows, even_edge, odd_edge, high0, low0),
         [field, field, part], (ext, held_out),
@@ -476,7 +515,7 @@
     (grad_signal,) = call(
         k_last, (tap_shift,), (grad0, high0, low0), [shape(bands, 1, 2, length)]
     )
-    grad_taps = summed(summed(grad_taps, "pol"), "tm")
+    grad_taps = summed(over_cores(grad_taps), "tm")
     return grad_signal, grad_taps.reshape(steps, bands, 2, LANES)
 
 

time: 77.2 us -> 60.1 us (0.78)
  starting transfers between devices: 36.8 us -> 24.9 us
  waiting for transfers between devices: 25.2 us -> 21 us
  local copies, waits for them, and re-layouts: 3.16 us -> 1.82 us
    ppermute x21, starting transfers between devices: 36.8 us -> 24.9 us  [the longest x16 23.7 us: swapped(): return lax.ppermute(x, (axis, 'pol'), pairs)]
    ppermute x21, waiting for transfers between devices: 25.2 us -> 21 us  [the longest x16 16 us: swapped(): return lax.ppermute(x, (axis, 'pol'), pairs)]
    unnamed x12, local copies, waits for them, and re-layouts: 3.16 us -> 1.82 us
    pallas_call x9 -> x8, Pallas kernels: 10.4 us -> 10.3 us  [call(): pl.pallas_call(kernel, out_shape=shapes, in_specs=[smem] * len(scalars) +...]
  transfers between devices with their start and end apart: 21 -> 21, of which waited for: 16 -> 16; matrix products, arithmetic and copies ran while one was open for 0% -> 0% of each run, Pallas kernels for 4% -> 6%
where the time goes in v1:
time: 60.1 us; the launch traced here: 59.9 us
  starting transfers between devices  24.9 us (41%)
  waiting for transfers between devices  21 us (35%)
  Pallas kernels  10.7 us (18%)
  local copies, waits for them, and re-layouts  1.82 us (3%)
  between operations  0.77 us (1%)
  other arithmetic  0.65 us (1%)
    ppermute x16, starting transfers between devices, swapped(): return lax.ppermute(x, (axis, 'pol'), pairs)  23.7 us
    ppermute x16, waiting for transfers between devices, swapped(): return lax.ppermute(x, (axis, 'pol'), pairs)  16 us
    pallas_call x8, Pallas kernels, call(): pl.pallas_call(kernel, out_shape=shapes, in_specs=[smem] * len(scalars) +...  10.3 us
    ppermute x5, waiting for transfers between devices, over_cores(): lax.ppermute(x, 'pol', [(p, cores - 1 - p) for p in range(cores)])  4.98 us
    unnamed x12, local copies, waits for them, and re-layouts  1.82 us
    ppermute x5, starting transfers between devices, over_cores(): lax.ppermute(x, 'pol', [(p, cores - 1 - p) for p in range(cores)])  1.28 us
  transfers between devices with their start and end apart: 21, of which 16 were waited for; matrix products, arithmetic and copies ran while one was open for 0% of the time, Pallas kernels for 6%

profile of v1, /device:TPU:0, one launch (start us, length us, event | category | flops | bytes accessed | tf_op | source)
XLA Modules:
  0.0 59.9 jit_solution(5524709831403212540)
XLA Ops:
  0.6 0.0 copy-start
  0.6 0.9 %copy-done = f32[4,1,2,4096]{3,2,1,0:T(2,128)S(1)} copy-done((f32[4,1,2,4096]{3,2,1,0:T(2,128)S(1)}, f32[4,1,2,4096]{3,2,1,0:T(2,128)}, u32[]{:S(2)}) %copy-start) | copy-done | bytes 131096
  1.5 0.0 copy-start.1
  1.5 0.9 %copy-done.1 = f32[4,1,2,4096]{3,2,1,0:T(2,128)S(1)} copy-done((f32[4,1,2,4096]{3,2,1,0:T(2,128)S(1)}, f32[4,1,2,4096]{3,2,1,0:T(2,128)}, u32[]{:S(2)}) %copy-start.1) | copy-done | bytes 131096
  2.4 0.0 copy-start.2
  2.4 0.5 shard_map.77
  2.9 0.0 copy-start.4
  3.0 0.0 copy-start.5
  3.0 0.0 copy-start.3
  3.0 0.5 collective-permute-start.1
  3.5 4.1 %collective-permute-start = (f32[4,2,8,128]{3,2,1,0:T(8,128)S(1)}, f32[4,2,8,128]{3,2,1,0:T(8,128)S(1)}, u32[]{:S(2)}, u32[]{:S(2)}) collective-permute-start(f32[4,2,8,128]{3,2,1,0:T(8,128)S(1)} %get-tuple-element.30), channel_id=1, source_target_pairs={{0,4},{1,5},{4,0},{5,1},{8,12},{9,13},{12,8},{13,9},{2,6},{3,7},{6... | collective-permute-start | bytes 98312 | tf_op jit(solution)/shard_map/ppermute | solution.py:424
  7.6 0.0 copy-done.2
  7.6 0.0 copy-done.4
  7.6 0.0 copy-done.5
  7.7 0.0 copy-done.3
  7.7 0.6 %shard_map.78 = (s32[2,4]{1,0:T(2,128)S(1)}, s32[2,4]{1,0:T(2,128)S(1)}, f32[2,4]{1,0:T(2,128)S(1)}, bf16[4,256,512]{2,1,0:T(8,128)(2,1)S(1)}, bf16[4,256,512]{2...) custom-call(f32[2,4,2,128]{3,2,1,0:T(2,128)S(1)} %copy-done.2, ...), custom_call_target="tpu_custom_call" | custom-call | flops 200000000 | bytes 6000000 | tf_op jit(solution)/shard_map/pallas_call | solution.py:401
  8.3 0.0 collective-permute-done.1.odd_in.odd_edge
  8.3 1.2 %collective-permute-done.even_in.even_edge = f32[4,2,8,128]{3,2,1,0:T(8,128)S(1)} collective-permute-done((f32[4,2,8,128]{3,2,1,0:T(8,128)S(1)}, f32[4,2,8,128]{3,2,1,0:T(8,128)S(1)}, u32[]{:S(2)}, u32[]{:S(2)}) %collective-permute-start) | collective-permute-done | bytes 32800 | tf_op jit(solution)/shard_map/ppermute | solution.py:424
  9.5 1.4 %shard_map.79 = (f32[4,2,48,128]{3,2,1,0:T(8,128)S(1)}, f32[4,2,48,128]{3,2,1,0:T(8,128)S(1)}, f32[48,128]{1,0:T(8,128)S(1)}) custom-call(s32[2,4]{1,0:T(2,128)S(1)} %get-tuple-element.33.delays, s32[2,4]{1,0:T(2,128)S(1)} %get-tuple-element.32.shifts, f32[4,2,32,128]{3,2,1,0:T(8,128)S(1)} %get-tuple-element.35.sig_rows, ...), custom_call_target="tpu_custom_call" | custom-call | flops 200000000 | bytes 6000000 | tf_op jit(solution)/shard_map/pallas_call | solution.py:401
  11.0 0.1 collective-permute-start.2
  11.0 1.2 %collective-permute-done.2 = f32[48,128]{1,0:T(8,128)S(1)} collective-permute-done((f32[48,128]{1,0:T(8,128)S(1)}, f32[48,128]{1,0:T(8,128)S(1)}, u32[]{:S(2)}, u32[]{:S(2)}) %collective-permute-start.2) | collective-permute-done | bytes 24608 | tf_op jit(solution)/shard_map/ppermute | solution.py:440
  12.2 1.3 %collective-permute-start.3 = (f32[48,128]{1,0:T(8,128)S(1)}, f32[48,128]{1,0:T(8,128)S(1)}, u32[]{:S(2)}, u32[]{:S(2)}) collective-permute-start(f32[48,128]{1,0:T(8,128)S(1)} %add.33), channel_id=1, source_target_pairs={{0,3},{1,2},{2,1},{3,0},{4,7},{5,6},{6,5},{7,4},{8,11},{9,10},{10,... | collective-permute-start | bytes 73736 | tf_op jit(solution)/shard_map/ppermute | solution.py:424
  13.5 2.0 %collective-permute-done.3 = f32[48,128]{1,0:T(8,128)S(1)} collective-permute-done((f32[48,128]{1,0:T(8,128)S(1)}, f32[48,128]{1,0:T(8,128)S(1)}, u32[]{:S(2)}, u32[]{:S(2)}) %collective-permute-start.3) | collective-permute-done | bytes 24608 | tf_op jit(solution)/shard_map/ppermute | solution.py:424
  15.5 0.2 collective-permute-start.5
  15.6 2.0 %collective-permute-start.4 = (f32[48,128]{1,0:T(8,128)S(1)}, f32[48,128]{1,0:T(8,128)S(1)}, u32[]{:S(2)}, u32[]{:S(2)}) collective-permute-start(f32[48,128]{1,0:T(8,128)S(1)} %add.34.own), channel_id=1, source_target_pairs={{0,5},{1,4},{4,1},{5,0},{8,13},{9,12},{12,9},{13,8},{2,7},{3,6},{6... | collective-permute-start | bytes 73736 | tf_op jit(solution)/shard_map/ppermute | solution.py:424
  17.7 0.0 collective-permute-done.5.odd_in
  17.7 1.5 %collective-permute-done.4.even_in = f32[48,128]{1,0:T(8,128)S(1)} collective-permute-done((f32[48,128]{1,0:T(8,128)S(1)}, f32[48,128]{1,0:T(8,128)S(1)}, u32[]{:S(2)}, u32[]{:S(2)}) %collective-permute-start.4) | collective-permute-done | bytes 24608 | tf_op jit(solution)/shard_map/ppermute | solution.py:424
  19.2 1.6 %shard_map.80 = (f32[4,48,128]{2,1,0:T(8,128)S(1)}, f32[4,48,128]{2,1,0:T(8,128)S(1)}, f32[4,2,48,128]{3,2,1,0:T(8,128)S(1)}, f32[4,2,48,128]{3,2,1,0:T(8,128)S(...) custom-call(s32[2,4]{1,0:T(2,128)S(1)} %get-tuple-element.33.delays, s32[2,4]{1,0:T(2,128)S(1)} %get-tuple-element.32.shifts, ...), custom_call_target="tpu_custom_call" | custom-call | flops 200000000 | bytes 6000000 | tf_op jit(solution)/shard_map/pallas_call | solution.py:401
  20.8 0.2 collective-permute-start.6
  21.0 1.0 %collective-permute-done.6 = f32[48,128]{1,0:T(8,128)S(1)} collective-permute-done((f32[48,128]{1,0:T(8,128)S(1)}, f32[48,128]{1,0:T(8,128)S(1)}, u32[]{:S(2)}, u32[]{:S(2)}) %collective-permute-start.6) | collective-permute-done | bytes 24608 | tf_op jit(solution)/shard_map/ppermute | solution.py:440
  22.0 1.3 %collective-permute-start.7 = (f32[48,128]{1,0:T(8,128)S(1)}, f32[48,128]{1,0:T(8,128)S(1)}, u32[]{:S(2)}, u32[]{:S(2)}) collective-permute-start(f32[48,128]{1,0:T(8,128)S(1)} %add.35), channel_id=1, source_target_pairs={{0,3},{1,2},{2,1},{3,0},{4,7},{5,6},{6,5},{7,4},{8,11},{9,10},{10,... | collective-permute-start | bytes 73736 | tf_op jit(solution)/shard_map/ppermute | solution.py:424
  23.3 2.0 %collective-permute-done.7 = f32[48,128]{1,0:T(8,128)S(1)} collective-permute-done((f32[48,128]{1,0:T(8,128)S(1)}, f32[48,128]{1,0:T(8,128)S(1)}, u32[]{:S(2)}, u32[]{:S(2)}) %collective-permute-start.7) | collective-permute-done | bytes 24608 | tf_op jit(solution)/shard_map/ppermute | solution.py:424
  25.3 0.2 collective-permute-start.9
  25.5 2.9 %collective-permute-start.8 = (f32[48,128]{1,0:T(8,128)S(1)}, f32[48,128]{1,0:T(8,128)S(1)}, u32[]{:S(2)}, u32[]{:S(2)}) collective-permute-start(f32[48,128]{1,0:T(8,128)S(1)} %add.36.own), channel_id=1, source_target_pairs={{0,5},{1,4},{4,1},{5,0},{8,13},{9,12},{12,9},{13,8},{2,7},{3,6},{6... | collective-permute-start | bytes 73736 | tf_op jit(solution)/shard_map/ppermute | solution.py:424
  28.4 0.0 collective-permute-done.9.odd_in
  28.4 1.5 %collective-permute-done.8.even_in = f32[48,128]{1,0:T(8,128)S(1)} collective-permute-done((f32[48,128]{1,0:T(8,128)S(1)}, f32[48,128]{1,0:T(8,128)S(1)}, u32[]{:S(2)}, u32[]{:S(2)}) %collective-permute-start.8) | collective-permute-done | bytes 24608 | tf_op jit(solution)/shard_map/ppermute | solution.py:424
  29.9 0.9 %shard_map.81 = (f32[4,2,48,128]{3,2,1,0:T(8,128)S(1)}, f32[48,128]{1,0:T(8,128)S(1)}) custom-call(s32[2,4]{1,0:T(2,128)S(1)} %get-tuple-element.33.delays, f32[2,4]{1,0:T(2,128)S(1)} %get-tuple-element.34.gains, f32[4,2,48,128]{3,2,1,0:T(8,128)S(1)} %get-tuple-element.43.linear1, f32[48,128]{1,0:T(8,128)S(1)} %add.36.own, ...), custom_call_target="tpu_custom_call" | custom-call | flops 200000000 | bytes 6000000 | tf_op jit(solution)/shard_map/pallas_call | solution.py:401
  30.8 0.4 collective-permute-start.10
  31.2 0.9 %collective-permute-done.10 = f32[48,128]{1,0:T(8,128)S(1)} collective-permute-done((f32[48,128]{1,0:T(8,128)S(1)}, f32[48,128]{1,0:T(8,128)S(1)}, u32[]{:S(2)}, u32[]{:S(2)}) %collective-permute-start.10) | collective-permute-done | bytes 24608 | tf_op jit(solution)/shard_map/ppermute | solution.py:440
  32.1 1.4 %collective-permute-start.11 = (f32[48,128]{1,0:T(8,128)S(1)}, f32[48,128]{1,0:T(8,128)S(1)}, u32[]{:S(2)}, u32[]{:S(2)}) collective-permute-start(f32[48,128]{1,0:T(8,128)S(1)} %add.37), channel_id=1, source_target_pairs={{0,3},{1,2},{2,1},{3,0},{4,7},{5,6},{6,5},{7,4},{8,11},{9,10},{10,... | collective-permute-start | bytes 73736 | tf_op jit(solution)/shard_map/ppermute | solution.py:424
  33.5 1.8 %collective-permute-done.11 = f32[48,128]{1,0:T(8,128)S(1)} collective-permute-done((f32[48,128]{1,0:T(8,128)S(1)}, f32[48,128]{1,0:T(8,128)S(1)}, u32[]{:S(2)}, u32[]{:S(2)}) %collective-permute-start.11) | collective-permute-done | bytes 24608 | tf_op jit(solution)/shard_map/ppermute | solution.py:424
  35.3 0.3 collective-permute-start.13
  35.7 1.8 %collective-permute-start.12 = (f32[48,128]{1,0:T(8,128)S(1)}, f32[48,128]{1,0:T(8,128)S(1)}, u32[]{:S(2)}, u32[]{:S(2)}) collective-permute-start(f32[48,128]{1,0:T(8,128)S(1)} %add.38.own), channel_id=1, source_target_pairs={{0,5},{1,4},{4,1},{5,0},{8,13},{9,12},{12,9},{13,8},{2,7},{3,6},{6... | collective-permute-start | bytes 73736 | tf_op jit(solution)/shard_map/ppermute | solution.py:424
  37.4 0.0 collective-permute-done.13.odd_in
  37.5 1.5 %collective-permute-done.12.even_in = f32[48,128]{1,0:T(8,128)S(1)} collective-permute-done((f32[48,128]{1,0:T(8,128)S(1)}, f32[48,128]{1,0:T(8,128)S(1)}, u32[]{:S(2)}, u32[]{:S(2)}) %collective-permute-start.12) | collective-permute-done | bytes 24608 | tf_op jit(solution)/shard_map/ppermute | solution.py:424
  39.0 1.3 %shard_map.82 = (f32[4,2,48,128]{3,2,1,0:T(8,128)S(1)}, f32[4,2,48,128]{3,2,1,0:T(8,128)S(1)}, f32[48,128]{1,0:T(8,128)S(1)}) custom-call(s32[2,4]{1,0:T(2,128)S(1)} %get-tuple-element.33.delays, s32[2,4]{1,0:T(2,128)S(1)} %get-tuple-element.32.shifts, f32[2,4]{1,0:T(2,128)S(1)} %get-tuple-element.34.gains, f32[4,2,48,128]{3,2,1,0:T(8,128)S(1)} %get-tuple-element.46.turned1, ...), custom_call_target="tpu_custom_call" | custom-call | flops 200000000 | bytes 6000000 | tf_op jit(solution)/shard_map/pallas_call | solution.py:401
  40.2 0.2 collective-permute-start.14
  40.5 1.0 %collective-permute-done.14 = f32[48,128]{1,0:T(8,128)S(1)} collective-permute-done((f32[48,128]{1,0:T(8,128)S(1)}, f32[48,128]{1,0:T(8,128)S(1)}, u32[]{:S(2)}, u32[]{:S(2)}) %collective-permute-start.14) | collective-permute-done | bytes 24608 | tf_op jit(solution)/shard_map/ppermute | solution.py:440
  41.5 1.3 %collective-permute-start.15 = (f32[48,128]{1,0:T(8,128)S(1)}, f32[48,128]{1,0:T(8,128)S(1)}, u32[]{:S(2)}, u32[]{:S(2)}) collective-permute-start(f32[48,128]{1,0:T(8,128)S(1)} %add.39), channel_id=1, source_target_pairs={{0,3},{1,2},{2,1},{3,0},{4,7},{5,6},{6,5},{7,4},{8,11},{9,10},{10,... | collective-permute-start | bytes 73736 | tf_op jit(solution)/shard_map/ppermute | solution.py:424
  42.8 2.0 %collective-permute-done.15 = f32[48,128]{1,0:T(8,128)S(1)} collective-permute-done((f32[48,128]{1,0:T(8,128)S(1)}, f32[48,128]{1,0:T(8,128)S(1)}, u32[]{:S(2)}, u32[]{:S(2)}) %collective-permute-start.15) | collective-permute-done | bytes 24608 | tf_op jit(solution)/shard_map/ppermute | solution.py:424
  44.8 0.2 collective-permute-start.17
  44.9 2.9 %collective-permute-start.16 = (f32[48,128]{1,0:T(8,128)S(1)}, f32[48,128]{1,0:T(8,128)S(1)}, u32[]{:S(2)}, u32[]{:S(2)}) collective-permute-start(f32[48,128]{1,0:T(8,128)S(1)} %add.40.own), channel_id=1, source_target_pairs={{0,5},{1,4},{4,1},{5,0},{8,13},{9,12},{12,9},{13,8},{2,7},{3,6},{6... | collective-permute-start | bytes 73736 | tf_op jit(solution)/shard_map/ppermute | solution.py:424
  47.9 1.1 %shard_map.83.taps1 = f32[8,128]{1,0:T(8,128)S(1)} custom-call(f32[4,2,48,128]{3,2,1,0:T(8,128)S(1)} %get-tuple-element.54.shifted, f32[4,2,48,128]{3,2,1,0:T(8,128)S(1)} %get-tuple-element.55.grad), custom_call_target="tpu_custom_call" | custom-call | flops 200000000 | bytes 6000000 | tf_op jit(solution)/shard_map/pallas_call | solution.py:401
  48.9 0.0 collective-permute-done.17.odd_in
  48.9 0.4 collective-permute-done.16.even_in
  49.4 1.6 %shard_map.84 = (f32[4,2,48,128]{3,2,1,0:T(8,128)S(1)}, f32[16,128]{1,0:T(8,128)S(1)}) custom-call(s32[2,4]{1,0:T(2,128)S(1)} %get-tuple-element.33.delays, f32[4,2,48,128]{3,2,1,0:T(8,128)S(1)} %get-tuple-element.51.turned0, f32[4,2,48,128]{3,2,1,0:T(8,128)S(1)} %get-tuple-element.39.linear0, f32[48,128]{1,0:T(8,128)S(1)} %add.40.own, ...), custom_call_target="tpu_custom_call" | custom-call | flops 200000000 | bytes 6000000 | tf_op jit(solution)/shard_map/pallas_call | solution.py:401
  51.0 0.4 collective-permute-start.18
  51.4 0.8 %collective-permute-done.18 = f32[16,128]{1,0:T(8,128)S(1)} collective-permute-done((f32[16,128]{1,0:T(8,128)S(1)}, f32[16,128]{1,0:T(8,128)S(1)}, u32[]{:S(2)}, u32[]{:S(2)}) %collective-permute-start.18) | collective-permute-done | bytes 8224 | tf_op jit(solution)/shard_map/ppermute | solution.py:440
  52.3 1.7 %collective-permute-start.19 = (f32[16,128]{1,0:T(8,128)S(1)}, f32[16,128]{1,0:T(8,128)S(1)}, u32[]{:S(2)}, u32[]{:S(2)}) collective-permute-start(f32[16,128]{1,0:T(8,128)S(1)} %add.41), channel_id=1, source_target_pairs={{0,5},{1,4},{4,1},{5,0},{8,13},{9,12},{12,9},{13,8},{2,7},{3,6},{6... | collective-permute-start | bytes 24584 | tf_op jit(solution)/shard_map/ppermute | solution.py:424
  54.0 1.4 %collective-permute-done.19 = f32[16,128]{1,0:T(8,128)S(1)} collective-permute-done((f32[16,128]{1,0:T(8,128)S(1)}, f32[16,128]{1,0:T(8,128)S(1)}, u32[]{:S(2)}, u32[]{:S(2)}) %collective-permute-start.19) | collective-permute-done | bytes 8224 | tf_op jit(solution)/shard_map/ppermute | solution.py:424
  55.4 1.6 %collective-permute-start.20 = (f32[16,128]{1,0:T(8,128)S(1)}, f32[16,128]{1,0:T(8,128)S(1)}, u32[]{:S(2)}, u32[]{:S(2)}) collective-permute-start(f32[16,128]{1,0:T(8,128)S(1)} %add.42), channel_id=1, source_target_pairs={{0,9},{1,8},{4,13},{5,12},{8,1},{9,0},{12,5},{13,4},{2,11},{3,10},... | collective-permute-start | bytes 24584 | tf_op jit(solution)/shard_map/ppermute | solution.py:424
  57.0 1.7 %shard_map.85 = f32[4,1,2,4096]{3,2,1,0:T(2,128)} custom-call(s32[2,4]{1,0:T(2,128)S(1)} %get-tuple-element.32.shifts, f32[4,2,48,128]{3,2,1,0:T(8,128)S(1)} %get-tuple-element.56.grad0, bf16[4,256,512]{2,1,0:T(8,128)(2,1)S(1)} %get-tuple-element.37.high, bf16[4,256,512]{2,1,0:T(8,128)(2,1)S(1)} %get-tuple-element.38.low), custom_call_target="tpu_custom_call" | custom-call | flops 200000000 | bytes 6000000 | tf_op jit(solution)/shard_map/pallas_call | solution.py:401
  58.7 0.6 %collective-permute-done.20 = f32[16,128]{1,0:T(8,128)S(1)} collective-permute-done((f32[16,128]{1,0:T(8,128)S(1)}, f32[16,128]{1,0:T(8,128)S(1)}, u32[]{:S(2)}, u32[]{:S(2)}) %collective-permute-start.20) | collective-permute-done | bytes 8224 | tf_op jit(solution)/shard_map/ppermute | solution.py:424
  59.3 0.6 %add.43 = f32[16,128]{1,0:T(8,128)} add(f32[16,128]{1,0:T(8,128)S(1)} %add.42, f32[16,128]{1,0:T(8,128)S(1)} %collective-permute-done.20) | non-fusion elementwise | flops 2048 | bytes 24576 | tf_op jit(solution)/shard_map/add | solution.py:433
  (10 shorter events, 0.0 us)
Async XLA Ops:
  0.6 0.9 %copy-start = (f32[4,1,2,4096]{3,2,1,0:T(2,128)S(1)}, f32[4,1,2,4096]{3,2,1,0:T(2,128)}, u32[]{:S(2)}) copy-start(f32[4,1,2,4096]{3,2,1,0:T(2,128)} %signal.1) | copy-start | bytes 393220
  1.5 0.9 %copy-start.1 = (f32[4,1,2,4096]{3,2,1,0:T(2,128)S(1)}, f32[4,1,2,4096]{3,2,1,0:T(2,128)}, u32[]{:S(2)}) copy-start(f32[4,1,2,4096]{3,2,1,0:T(2,128)} %cotangent.1) | copy-start | bytes 393220
  2.4 5.2 %copy-start.2 = (f32[2,4,2,128]{3,2,1,0:T(2,128)S(1)}, f32[2,4,2,128]{3,2,1,0:T(2,128)}, u32[]{:S(2)}) copy-start(f32[2,4,2,128]{3,2,1,0:T(2,128)} %taps) | copy-start | bytes 24580
  2.9 4.7 %copy-start.4 = (s32[2,4]{1,0:T(2,128)S(1)}, s32[2,4]{1,0:T(2,128)}, u32[]{:S(2)}) copy-start(s32[2,4]{1,0:T(2,128)} %shifts.1) | copy-start | bytes 100
  3.0 4.7 %copy-start.5 = (f32[2,4]{1,0:T(2,128)S(1)}, f32[2,4]{1,0:T(2,128)}, u32[]{:S(2)}) copy-start(f32[2,4]{1,0:T(2,128)} %gains.1) | copy-start | bytes 100
  3.0 4.7 %copy-start.3 = (s32[2,4]{1,0:T(2,128)S(1)}, s32[2,4]{1,0:T(2,128)}, u32[]{:S(2)}) copy-start(s32[2,4]{1,0:T(2,128)} %delays.1) | copy-start | bytes 100
  3.0 5.3 %collective-permute-start.1 = (f32[4,2,8,128]{3,2,1,0:T(8,128)S(1)}, f32[4,2,8,128]{3,2,1,0:T(8,128)S(1)}, u32[]{:S(2)}, u32[]{:S(2)}) collective-permute-start(f32[4,2,8,128]{3,2,1,0:T(8,128)S(1)} %get-tuple-element.36), channel_id=1, source_target_pairs={{0,1},{1,0},{4,8},{5,9},{8,4},{9,5},{12,13},{13,12},{2,3},{3,2},{6... | collective-permute-start | bytes 98312 | tf_op jit(solution)/shard_map/ppermute | solution.py:424
  3.5 6.0 %collective-permute-start = (f32[4,2,8,128]{3,2,1,0:T(8,128)S(1)}, f32[4,2,8,128]{3,2,1,0:T(8,128)S(1)}, u32[]{:S(2)}, u32[]{:S(2)}) collective-permute-start(f32[4,2,8,128]{3,2,1,0:T(8,128)S(1)} %get-tuple-element.30), channel_id=1, source_target_pairs={{0,4},{1,5},{4,0},{5,1},{8,12},{9,13},{12,8},{13,9},{2,6},{3,7},{6... | collective-permute-start | bytes 98312 | tf_op jit(solution)/shard_map/ppermute | solution.py:424
  11.0 1.3 %collective-permute-start.2 = (f32[48,128]{1,0:T(8,128)S(1)}, f32[48,128]{1,0:T(8,128)S(1)}, u32[]{:S(2)}, u32[]{:S(2)}) collective-permute-start(f32[48,128]{1,0:T(8,128)S(1)} %get-tuple-element.40), channel_id=1, source_target_pairs={{0,1},{1,0},{2,3},{3,2},{4,5},{5,4},{6,7},{7,6},{8,9},{9,8},{10,11... | collective-permute-start | bytes 73736 | tf_op jit(solution)/shard_map/ppermute | solution.py:440
  12.2 3.3 %collective-permute-start.3 = (f32[48,128]{1,0:T(8,128)S(1)}, f32[48,128]{1,0:T(8,128)S(1)}, u32[]{:S(2)}, u32[]{:S(2)}) collective-permute-start(f32[48,128]{1,0:T(8,128)S(1)} %add.33), channel_id=1, source_target_pairs={{0,3},{1,2},{2,1},{3,0},{4,7},{5,6},{6,5},{7,4},{8,11},{9,10},{10,... | collective-permute-start | bytes 73736 | tf_op jit(solution)/shard_map/ppermute | solution.py:424
  15.5 2.2 %collective-permute-start.5 = (f32[48,128]{1,0:T(8,128)S(1)}, f32[48,128]{1,0:T(8,128)S(1)}, u32[]{:S(2)}, u32[]{:S(2)}) collective-permute-start(f32[48,128]{1,0:T(8,128)S(1)} %add.34.own), channel_id=1, source_target_pairs={{0,1},{1,0},{4,9},{5,8},{8,5},{9,4},{12,13},{13,12},{2,3},{3,2},{6... | collective-permute-start | bytes 73736 | tf_op jit(solution)/shard_map/ppermute | solution.py:424
  15.6 3.5 %collective-permute-start.4 = (f32[48,128]{1,0:T(8,128)S(1)}, f32[48,128]{1,0:T(8,128)S(1)}, u32[]{:S(2)}, u32[]{:S(2)}) collective-permute-start(f32[48,128]{1,0:T(8,128)S(1)} %add.34.own), channel_id=1, source_target_pairs={{0,5},{1,4},{4,1},{5,0},{8,13},{9,12},{12,9},{13,8},{2,7},{3,6},{6... | collective-permute-start | bytes 73736 | tf_op jit(solution)/shard_map/ppermute | solution.py:424
  20.8 1.3 %collective-permute-start.6 = (f32[48,128]{1,0:T(8,128)S(1)}, f32[48,128]{1,0:T(8,128)S(1)}, u32[]{:S(2)}, u32[]{:S(2)}) collective-permute-start(f32[48,128]{1,0:T(8,128)S(1)} %get-tuple-element.44), channel_id=1, source_target_pairs={{0,1},{1,0},{2,3},{3,2},{4,5},{5,4},{6,7},{7,6},{8,9},{9,8},{10,11... | collective-permute-start | bytes 73736 | tf_op jit(solution)/shard_map/ppermute | solution.py:440
  22.0 3.3 %collective-permute-start.7 = (f32[48,128]{1,0:T(8,128)S(1)}, f32[48,128]{1,0:T(8,128)S(1)}, u32[]{:S(2)}, u32[]{:S(2)}) collective-permute-start(f32[48,128]{1,0:T(8,128)S(1)} %add.35), channel_id=1, source_target_pairs={{0,3},{1,2},{2,1},{3,0},{4,7},{5,6},{6,5},{7,4},{8,11},{9,10},{10,... | collective-permute-start | bytes 73736 | tf_op jit(solution)/shard_map/ppermute | solution.py:424
  25.3 3.1 %collective-permute-start.9 = (f32[48,128]{1,0:T(8,128)S(1)}, f32[48,128]{1,0:T(8,128)S(1)}, u32[]{:S(2)}, u32[]{:S(2)}) collective-permute-start(f32[48,128]{1,0:T(8,128)S(1)} %add.36.own), channel_id=1, source_target_pairs={{0,1},{1,0},{4,9},{5,8},{8,5},{9,4},{12,13},{13,12},{2,3},{3,2},{6... | collective-permute-start | bytes 73736 | tf_op jit(solution)/shard_map/ppermute | solution.py:424
  25.5 4.4 %collective-permute-start.8 = (f32[48,128]{1,0:T(8,128)S(1)}, f32[48,128]{1,0:T(8,128)S(1)}, u32[]{:S(2)}, u32[]{:S(2)}) collective-permute-start(f32[48,128]{1,0:T(8,128)S(1)} %add.36.own), channel_id=1, source_target_pairs={{0,5},{1,4},{4,1},{5,0},{8,13},{9,12},{12,9},{13,8},{2,7},{3,6},{6... | collective-permute-start | bytes 73736 | tf_op jit(solution)/shard_map/ppermute | solution.py:424
  30.8 1.2 %collective-permute-start.10 = (f32[48,128]{1,0:T(8,128)S(1)}, f32[48,128]{1,0:T(8,128)S(1)}, u32[]{:S(2)}, u32[]{:S(2)}) collective-permute-start(f32[48,128]{1,0:T(8,128)S(1)} %get-tuple-element.47), channel_id=1, source_target_pairs={{0,1},{1,0},{2,3},{3,2},{4,5},{5,4},{6,7},{7,6},{8,9},{9,8},{10,11... | collective-permute-start | bytes 73736 | tf_op jit(solution)/shard_map/ppermute | solution.py:440
  32.1 3.3 %collective-permute-start.11 = (f32[48,128]{1,0:T(8,128)S(1)}, f32[48,128]{1,0:T(8,128)S(1)}, u32[]{:S(2)}, u32[]{:S(2)}) collective-permute-start(f32[48,128]{1,0:T(8,128)S(1)} %add.37), channel_id=1, source_target_pairs={{0,3},{1,2},{2,1},{3,0},{4,7},{5,6},{6,5},{7,4},{8,11},{9,10},{10,... | collective-permute-start | bytes 73736 | tf_op jit(solution)/shard_map/ppermute | solution.py:424
  35.3 2.1 %collective-permute-start.13 = (f32[48,128]{1,0:T(8,128)S(1)}, f32[48,128]{1,0:T(8,128)S(1)}, u32[]{:S(2)}, u32[]{:S(2)}) collective-permute-start(f32[48,128]{1,0:T(8,128)S(1)} %add.38.own), channel_id=1, source_target_pairs={{0,1},{1,0},{4,9},{5,8},{8,5},{9,4},{12,13},{13,12},{2,3},{3,2},{6... | collective-permute-start | bytes 73736 | tf_op jit(solution)/shard_map/ppermute | solution.py:424
  35.7 3.3 %collective-permute-start.12 = (f32[48,128]{1,0:T(8,128)S(1)}, f32[48,128]{1,0:T(8,128)S(1)}, u32[]{:S(2)}, u32[]{:S(2)}) collective-permute-start(f32[48,128]{1,0:T(8,128)S(1)} %add.38.own), channel_id=1, source_target_pairs={{0,5},{1,4},{4,1},{5,0},{8,13},{9,12},{12,9},{13,8},{2,7},{3,6},{6... | collective-permute-start | bytes 73736 | tf_op jit(solution)/shard_map/ppermute | solution.py:424
  40.2 1.3 %collective-permute-start.14 = (f32[48,128]{1,0:T(8,128)S(1)}, f32[48,128]{1,0:T(8,128)S(1)}, u32[]{:S(2)}, u32[]{:S(2)}) collective-permute-start(f32[48,128]{1,0:T(8,128)S(1)} %get-tuple-element.52), channel_id=1, source_target_pairs={{0,1},{1,0},{2,3},{3,2},{4,5},{5,4},{6,7},{7,6},{8,9},{9,8},{10,11... | collective-permute-start | bytes 73736 | tf_op jit(solution)/shard_map/ppermute | solution.py:440
  41.5 3.3 %collective-permute-start.15 = (f32[48,128]{1,0:T(8,128)S(1)}, f32[48,128]{1,0:T(8,128)S(1)}, u32[]{:S(2)}, u32[]{:S(2)}) collective-permute-start(f32[48,128]{1,0:T(8,128)S(1)} %add.39), channel_id=1, source_target_pairs={{0,3},{1,2},{2,1},{3,0},{4,7},{5,6},{6,5},{7,4},{8,11},{9,10},{10,... | collective-permute-start | bytes 73736 | tf_op jit(solution)/shard_map/ppermute | solution.py:424
  44.8 4.2 %collective-permute-start.17 = (f32[48,128]{1,0:T(8,128)S(1)}, f32[48,128]{1,0:T(8,128)S(1)}, u32[]{:S(2)}, u32[]{:S(2)}) collective-permute-start(f32[48,128]{1,0:T(8,128)S(1)} %add.40.own), channel_id=1, source_target_pairs={{0,1},{1,0},{4,9},{5,8},{8,5},{9,4},{12,13},{13,12},{2,3},{3,2},{6... | collective-permute-start | bytes 73736 | tf_op jit(solution)/shard_map/ppermute | solution.py:424
  44.9 4.4 %collective-permute-start.16 = (f32[48,128]{1,0:T(8,128)S(1)}, f32[48,128]{1,0:T(8,128)S(1)}, u32[]{:S(2)}, u32[]{:S(2)}) collective-permute-start(f32[48,128]{1,0:T(8,128)S(1)} %add.40.own), channel_id=1, source_target_pairs={{0,5},{1,4},{4,1},{5,0},{8,13},{9,12},{12,9},{13,8},{2,7},{3,6},{6... | collective-permute-start | bytes 73736 | tf_op jit(solution)/shard_map/ppermute | solution.py:424
  51.0 1.2 %collective-permute-start.18 = (f32[16,128]{1,0:T(8,128)S(1)}, f32[16,128]{1,0:T(8,128)S(1)}, u32[]{:S(2)}, u32[]{:S(2)}) collective-permute-start(f32[16,128]{1,0:T(8,128)S(1)} %get-tuple-element.57), channel_id=1, source_target_pairs={{0,1},{1,0},{2,3},{3,2},{4,5},{5,4},{6,7},{7,6},{8,9},{9,8},{10,11... | collective-permute-start | bytes 24584 | tf_op jit(solution)/shard_map/ppermute | solution.py:440
  52.3 3.1 %collective-permute-start.19 = (f32[16,128]{1,0:T(8,128)S(1)}, f32[16,128]{1,0:T(8,128)S(1)}, u32[]{:S(2)}, u32[]{:S(2)}) collective-permute-start(f32[16,128]{1,0:T(8,128)S(1)} %add.41), channel_id=1, source_target_pairs={{0,5},{1,4},{4,1},{5,0},{8,13},{9,12},{12,9},{13,8},{2,7},{3,6},{6... | collective-permute-start | bytes 24584 | tf_op jit(solution)/shard_map/ppermute | solution.py:424
  55.4 4.0 %collective-permute-start.20 = (f32[16,128]{1,0:T(8,128)S(1)}, f32[16,128]{1,0:T(8,128)S(1)}, u32[]{:S(2)}, u32[]{:S(2)}) collective-permute-start(f32[16,128]{1,0:T(8,128)S(1)} %add.42), channel_id=1, source_target_pairs={{0,9},{1,8},{4,13},{5,12},{8,1},{9,0},{12,5},{13,4},{2,11},{3,10},... | collective-permute-start | bytes 24584 | tf_op jit(solution)/shard_map/ppermute | solution.py:424

commit v2 on v1

--- a/solution.py
+++ b/solution.py
@@ -11,7 +11,9 @@
 LANES = 128
 REACH = 2048 // LANES
 EDGE = 4
+WIDE = REACH + 4
 PAD = 8
+WIDE_PAD = REACH + PAD
 F32 = jnp.float32
 BF16 = jnp.bfloat16
 
@@ -67,11 +69,11 @@
     return lax.rem(lax.axis_index("tm"), 2) == 0
 
 
-def keep_inside(values, rows):
+def keep_inside(values, rows, pad=PAD):
     z = lax.axis_index("tm")
     row = lax.broadcasted_iota(jnp.int32, values.shape, 0)
-    low = jnp.where(z == 0, PAD, 0)
-    high = jnp.where(z == lax.axis_size("tm") - 1, PAD + rows, 2 * PAD + rows)
+    low = jnp.where(z == 0, pad, 0)
+    high = jnp.where(z == lax.axis_size("tm") - 1, pad + rows, 2 * pad + rows)
     return jnp.where((row >= low) & (row < high), values, 0.0)
 
 
@@ -85,18 +87,22 @@
     return before, after
 
 
-def extend(out, own, even_in, odd_in, first):
+def extend(out, own, even_in, odd_in, first, edge):
     bands, _, rows, _ = own.shape
+    pad = (out.shape[2] - rows) // 2
     for b in range(bands):
         for c in range(2):
-            before, after = from_sides(
-                even_in[b, c, first : first + EDGE, :], odd_in[b, c, first : first + EDGE, :]
-            )
-            out[b, c, 0:PAD, :] = jnp.zeros((PAD, LANES), F32)
-            out[b, c, PAD - EDGE : PAD, :] = before
-            out[b, c, PAD : PAD + rows, :] = own[b, c]
-            out[b, c, PAD + rows :, :] = jnp.zeros((PAD, LANES), F32)
-            out[b, c, PAD + rows : PAD + rows + EDGE, :] = after
+            out[b, c, 0:pad, :] = jnp.zeros((pad, LANES), F32)
+            out[b, c, pad : pad + rows, :] = own[b, c]
+            out[b, c, pad + rows :, :] = jnp.zeros((pad, LANES), F32)
+        for r in range(edge):
+            lanes = slice((first + r) * LANES, (first + r + 1) * LANES)
+            before, after = from_sides(even_in[b, :, lanes], odd_in[b, :, lanes])
+            for c in range(2):
+                above = pad - edge + r
+                below = pad + rows + r
+                out[b, c, above : above + 1, :] = before[c : c + 1]
+                out[b, c, below : below + 1, :] = after[c : c + 1]
 
 
 def fir(real, imag, high, low):
@@ -144,6 +150,30 @@
     out[...] = acc
 
 
+def delayed_sum(values, delays, step, held, out):
+    bands = len(values)
+    count, total = values[0].shape[0], out.shape[0]
+    lane = lanes_of((total, LANES))
+    acc = None
+    for b in range(bands):
+        delay = delays[step, b]
+        q = lax.shift_right_logical(delay, 7)
+        s = delay & (LANES - 1)
+        held[b, 0:8, :] = jnp.zeros((8, LANES), F32)
+        held[b, 8 : 8 + count, :] = pltpu.roll(values[b], s, 1)
+        near = held[b, pl.ds(8 + REACH - q, total), :]
+        far = held[b, pl.ds(8 + REACH - q - 1, total), :]
+        part = jnp.where(lane >= s, near, far)
+        acc = part if acc is None else acc + part
+    out[...] = acc
+
+
+def end_at_last(values, rows):
+    row = lax.broadcasted_iota(jnp.int32, values.shape, 0)
+    last = lax.axis_index("tm") == lax.axis_size("tm") - 1
+    return jnp.where(row < jnp.where(last, PAD + rows, values.shape[0]), values, 0.0)
+
+
 def gather_spread(own, even_in, odd_in, spread, rows):
     before, after = from_sides(even_in[...], odd_in[...])
     total = rows + REACH + 2 * PAD
@@ -152,10 +182,7 @@
     spread[total - PAD : total, :] = after[REACH : REACH + PAD]
     spread[PAD : PAD + REACH, :] += before[rows : rows + REACH]
     spread[PAD + rows : PAD + rows + REACH, :] += after[0:REACH]
-    values = spread[...]
-    row = lax.broadcasted_iota(jnp.int32, values.shape, 0)
-    last = lax.axis_index("tm") == lax.axis_size("tm") - 1
-    return jnp.where(row < jnp.where(last, PAD + rows, total), values, 0.0)
+    return end_at_last(spread[...], rows)
 
 
 def read_spread(values, delay, held, b, rows):
@@ -170,35 +197,18 @@
     return jnp.where(lanes_of((count, LANES)) + s < LANES, near, far)
 
 
-def k_rows(signal, cotangent, sig_rows, cot_rows, even_out, odd_out, sig_held, cot_held, done):
-    bands = signal.shape[0]
+def k_setup(
+    signal, cotangent, taps, delays, shifts, gains,
+    sig_rows, cot_rows, delays_out, shifts_out, gains_out, *tables,
+):
+    steps, bands = taps.shape[:2]
     rows = sig_rows.shape[2]
-    even = is_even()
-    copies = (
-        pltpu.make_async_copy(signal, sig_held, done.at[0]),
-        pltpu.make_async_copy(cotangent, cot_held, done.at[1]),
-    )
-    for copy in copies:
-        copy.start()
-    for copy, source, target, first in (
-        (copies[0], sig_held, sig_rows, 0),
-        (copies[1], cot_held, cot_rows, EDGE),
-    ):
-        copy.wait()
+    for source, target in ((signal, sig_rows), (cotangent, cot_rows)):
         for b in range(bands):
             for r in range(rows):
                 pair = source[b, 0, :, r * LANES : (r + 1) * LANES]
                 target[b, 0, r : r + 1, :] = pair[0:1]
                 target[b, 1, r : r + 1, :] = pair[1:2]
-            for c in range(2):
-                left = target[b, c, 0:EDGE, :]
-                right = target[b, c, rows - EDGE : rows, :]
-                even_out[b, c, first : first + EDGE, :] = jnp.where(even, right, left)
-                odd_out[b, c, first : first + EDGE, :] = jnp.where(even, left, right)
-
-
-def k_tables(taps, delays, shifts, gains, delays_out, shifts_out, gains_out, *tables):
-    steps, bands = taps.shape[:2]
     delays_out[...] = delays[...]
     shifts_out[...] = shifts[...]
     gains_out[...] = gains[...]
@@ -225,29 +235,29 @@
 
 def k_first(delays, shifts, sig_rows, even_in, odd_in, high, low, shifted, linear, out, ext, held):
     bands, _, rows, _ = sig_rows.shape
-    extend(ext, sig_rows, even_in, odd_in, 0)
+    extend(ext, sig_rows, even_in, odd_in, 0, WIDE)
+    middle = slice(WIDE_PAD - PAD, WIDE_PAD + rows + PAD)
     powers = []
     for b in range(bands):
         amount = LANES // 2 - shifts[0, b]
         real = later(ext[b, 0], amount)
         imag = later(ext[b, 1], amount)
-        shifted[b, 0] = real
-        shifted[b, 1] = imag
+        shifted[b, 0] = real[middle]
+        shifted[b, 1] = imag[middle]
         lr, li = fir(real, imag, high[b], low[b])
-        linear[b, 0] = lr
-        linear[b, 1] = li
-        lr, li = lr[PAD : PAD + rows], li[PAD : PAD + rows]
-        powers.append(lr * lr + li * li)
-    scatter_delayed(powers, delays, 0, held, out)
+        linear[b, 0] = lr[middle]
+        linear[b, 1] = li[middle]
+        powers.append(keep_inside(lr * lr + li * li, rows, WIDE_PAD))
+    delayed_sum(powers, delays, 0, held, out)
 
 
 def k_second(
-    delays, shifts, gains, linear0, own, even_in, odd_in, high, low,
-    cosine0, sine0, field1, shifted, linear1, out, spread, held, held_out,
+    delays, shifts, gains, linear0, own, high, low,
+    cosine0, sine0, field1, shifted, linear1, out, held, held_out,
 ):
     bands = linear0.shape[0]
     rows = linear0.shape[2] - 2 * PAD
-    values = gather_spread(own, even_in, odd_in, spread, rows)
+    values = end_at_last(own[...], rows)
     powers = []
     for b in range(bands):
         phase = gains[0, b] * read_spread(values, delays[0, b], held, b, rows)
@@ -278,7 +288,7 @@
 ):
     bands = linear1.shape[0]
     rows = linear1.shape[2] - 2 * PAD
-    extend(ext, cot_rows, even_edge, odd_edge, EDGE)
+    extend(ext, cot_rows, even_edge, odd_edge, WIDE, EDGE)
     values = gather_spread(own, even_in, odd_in, spread, rows)
     terms = []
     for b in range(bands):
@@ -396,12 +406,11 @@
 
 
 def call(kernel, scalars, arrays, shapes, scratch=(), micros=2.0):
-    smem = pl.BlockSpec(memory_space=pltpu.SMEM)
     vmem = pl.BlockSpec(memory_space=pltpu.VMEM)
     return pl.pallas_call(
         kernel,
         out_shape=shapes,
-        in_specs=[smem] * len(scalars) + [vmem] * len(arrays),
+        in_specs=[vmem] * (len(scalars) + len(arrays)),
         out_specs=[vmem] * len(shapes),
         scratch_shapes=[pltpu.VMEM(s, F32) for s in scratch],
         compiler_params=pltpu.CompilerParams(vmem_limit_bytes=24 * 1024 * 1024),
@@ -446,9 +455,28 @@
     return even_in, odd_in
 
 
+def over_tm(x):
+    if lax.axis_size("tm") != 4:
+        return summed(x, "tm")
+    others = [swapped(x, "tm", lambda i, d=d: i ^ d, True) for d in (1, 2, 3)]
+    return (x + others[0]) + (others[1] + others[2])
+
+
+def over_powers(part):
+    return summed(over_cores(part), "band")
+
+
 def exchanged(part):
-    part = summed(over_cores(part), "band")
+    part = over_powers(part)
     return (part,) + neighbours(part, part, True)
+
+
+def edges(signal, cotangent):
+    wide, edge = WIDE * LANES, EDGE * LANES
+    left = jnp.concatenate([signal[..., :wide], cotangent[..., :edge]], -1)
+    right = jnp.concatenate([signal[..., -wide:], cotangent[..., -edge:]], -1)
+    even = is_even()
+    return jnp.where(even, right, left), jnp.where(even, left, right)
 
 
 def on_device(signal, cotangent, taps, gains, walk_off, tap_shift):
@@ -463,37 +491,31 @@
     own = shape(bands, 2, rows, LANES)
     field = shape(bands, 2, held_rows, LANES)
     angle = shape(bands, held_rows, LANES)
-    edge = shape(bands, 2, 2 * EDGE, LANES)
+    wide_part = shape(rows + REACH + 2 * PAD, LANES)
     part = shape(rows + REACH, LANES)
     table = shape(bands, 2 * LANES, 4 * LANES, dtype=BF16)
     ext = (bands, 2, held_rows, LANES)
+    ext_wide = (bands, 2, rows + 2 * WIDE_PAD, LANES)
+    held_wide = (bands, rows + 2 * WIDE_PAD + 8, LANES)
     spread = (rows + REACH + 2 * PAD, LANES)
     held_in = (bands, rows + REACH + 3 * PAD, LANES)
     held_out = (bands, rows + 3 * REACH, LANES)
 
-    whole = pltpu.VMEM((bands, 1, 2, length), F32)
-    vmem = pl.BlockSpec(memory_space=pltpu.VMEM)
-    sig_rows, cot_rows, even_out, odd_out = pl.pallas_call(
-        k_rows,
-        out_shape=[own, own, edge, edge],
-        in_specs=[pl.BlockSpec(memory_space=pltpu.HBM)] * 2,
-        out_specs=[vmem] * 4,
-        scratch_shapes=[whole, whole, pltpu.SemaphoreType.DMA((2,))],
-        compiler_params=pltpu.CompilerParams(vmem_limit_bytes=24 * 1024 * 1024),
-    )(signal, cotangent)
+    even_out, odd_out = edges(signal[:, 0], cotangent[:, 0])
     even_edge, odd_edge = neighbours(even_out, odd_out, False)
     taps, even_out = lax.optimization_barrier((taps, even_out))
     small = [shape(*a.shape, dtype=a.dtype) for a in (walk_off, tap_shift, gains)]
-    walk_off, tap_shift, gains, high0, low0, high1, low1 = call(
-        k_tables, (), (taps, walk_off, tap_shift, gains), small + [table] * (2 * steps)
+    sig_rows, cot_rows, walk_off, tap_shift, gains, high0, low0, high1, low1 = call(
+        k_setup, (), (signal, cotangent, taps, walk_off, tap_shift, gains),
+        [own, own] + small + [table] * (2 * steps),
     )
     shifted0, linear0, sent = call(
         k_first, (walk_off, tap_shift), (sig_rows, even_edge, odd_edge, high0, low0),
-        [field, field, part], (ext, held_out),
+        [field, field, wide_part], (ext_wide, held_wide),
     )
     cosine0, sine0, field1, shifted1, linear1, sent = call(
-        k_second, (walk_off, tap_shift, gains), (linear0, *exchanged(sent), high1, low1),
-        [angle, angle, field, field, field, part], (spread, held_in, held_out),
+        k_second, (walk_off, tap_shift, gains), (linear0, over_powers(sent), high1, low1),
+        [angle, angle, field, field, field, part], (held_in, held_out),
     )
     turned1, sent = call(
         k_third, (walk_off, gains),
@@ -515,7 +537,7 @@
     (grad_signal,) = call(
         k_last, (tap_shift,), (grad0, high0, low0), [shape(bands, 1, 2, length)]
     )
-    grad_taps = summed(over_cores(grad_taps), "tm")
+    grad_taps = over_tm(over_cores(grad_taps))
     return grad_signal, grad_taps.reshape(steps, bands, 2, LANES)
 
 

time: 60.1 us -> 52.4 us (0.87)
  Pallas kernels: 10.7 us -> 7.24 us
  starting transfers between devices: 24.9 us -> 22.3 us
  waiting for transfers between devices: 21 us -> 19.4 us
    pallas_call x9 -> x8, Pallas kernels: 10.7 us -> 7.24 us  [call(): pl.pallas_call(kernel, out_shape=shapes, in_specs=[vmem] * (len(scalars)...]
    ppermute x16 -> x15, starting transfers between devices: 23.7 us -> 21.2 us  [swapped(): return lax.ppermute(x, (axis, 'pol'), pairs)]
    unnamed x12, local copies, waits for them, and re-layouts: 1.82 us -> 0.04 us
    ppermute x16 -> x15, waiting for transfers between devices: 16 us -> 14.3 us  [swapped(): return lax.ppermute(x, (axis, 'pol'), pairs)]
    slice x0 -> x2, local copies, waits for them, and re-layouts: none -> 1.72 us  [edges(): right = jnp.concatenate([signal[..., -wide:], cotangent[..., -edge:]], -1)]
    add x0 -> x1, other arithmetic: none -> 0.6 us  [over_tm(): return x + others[0] + (others[1] + others[2])]
    add x6 -> x4, other arithmetic: 0.62 us -> 0.02 us  [summed(): x = x + swapped(x, axis, lambda i, d=distance: i ^ d, cross)]
  transfers between devices with their start and end apart: 21 -> 20, of which waited for: 16 -> 14; matrix products, arithmetic and copies ran while one was open for 0% -> 0% of each run, Pallas kernels for 6% -> 6%
where the time goes in v2:
time: 52.4 us; the launch traced here: 52.2 us
  starting transfers between devices  22.3 us (43%)
  waiting for transfers between devices  19.4 us (37%)
  Pallas kernels  7.24 us (14%)
  local copies, waits for them, and re-layouts  1.75 us (3%)
  between operations  0.79 us (2%)
  other arithmetic  0.73 us (1%)
    ppermute x15, starting transfers between devices, swapped(): return lax.ppermute(x, (axis, 'pol'), pairs)  21.2 us
    ppermute x15, waiting for transfers between devices, swapped(): return lax.ppermute(x, (axis, 'pol'), pairs)  14.3 us
    pallas_call x8, Pallas kernels, call(): pl.pallas_call(kernel, out_shape=shapes, in_specs=[vmem] * (len(scalars)...  7.24 us
    ppermute x5, waiting for transfers between devices, over_cores(): lax.ppermute(x, 'pol', [(p, cores - 1 - p) for p in range(cores)])  5.15 us
    slice x2, local copies, waits for them, and re-layouts, edges(): right = jnp.concatenate([signal[..., -wide:], cotangent[..., -edge:]], -1)  1.72 us
    ppermute x5, starting transfers between devices, over_cores(): lax.ppermute(x, 'pol', [(p, cores - 1 - p) for p in range(cores)])  1.11 us
  transfers between devices with their start and end apart: 20, of which 14 were waited for; matrix products, arithmetic and copies ran while one was open for 0% of the time, Pallas kernels for 6%

profile of v2, /device:TPU:0, one launch (start us, length us, event | category | flops | bytes accessed | tf_op | source)
XLA Modules:
  0.0 52.2 jit_solution(12835284734951891698)
XLA Ops:
  0.6 0.7 %fusion.1 = (f32[4,2,512]{2,1,0:T(2,128)S(1)}, f32[4,2,512]{2,1,0:T(2,128)S(1)}) fusion(f32[4,2,4096]{2,1,0:T(2,128)} %bitcast.4), kind=kLoop, calls=%fused_computation.6 | loop fusion | bytes 65536 | tf_op jit(solution)/shard_map/slice | solution.py:477
  1.4 1.0 %fusion = (f32[4,2,2560]{2,1,0:T(2,128)S(1)}, f32[4,2,2560]{2,1,0:T(2,128)S(1)}) fusion(f32[4,2,4096]{2,1,0:T(2,128)} %bitcast.3), kind=kLoop, calls=%fused_computation.5 | loop fusion | bytes 327680 | tf_op jit(solution)/shard_map/slice | solution.py:477
  2.4 0.0 copy-start
  2.4 0.0 copy-start.1
  2.4 0.0 copy-start.2
  2.4 0.1 broadcast_select_fusion
  2.5 0.0 copy-start.4
  2.5 0.0 copy-start.5
  2.5 0.0 copy-start.3
  2.5 0.5 collective-permute-start.1
  3.0 4.1 %collective-permute-start = (f32[4,2,3072]{2,1,0:T(2,128)S(1)}, f32[4,2,3072]{2,1,0:T(2,128)S(1)}, u32[]{:S(2)}, u32[]{:S(2)}) collective-permute-start(f32[4,2,3072]{2,1,0:T(2,128)S(1)} %get-tuple-element.55), channel_id=1, source_target_pairs={{0,4},{1,5},{4,0},{5,1},{8,12},{9,13},{12,8},{13,9},{2,6},{3,7},{6... | collective-permute-start | bytes 294920 | tf_op jit(solution)/shard_map/ppermute | solution.py:433
  7.2 0.0 copy-done
  7.2 0.0 copy-done.1
  7.2 0.0 copy-done.2
  7.2 0.0 copy-done.4
  7.2 0.0 copy-done.5
  7.2 0.0 copy-done.3
  7.2 0.8 %shard_map.77 = (f32[4,2,32,128]{3,2,1,0:T(8,128)S(1)}, f32[4,2,32,128]{3,2,1,0:T(8,128)S(1)}, s32[2,4]{1,0:T(2,128)S(1)}, s32[2,4]{1,0:T(2,128)S(1)}, f32[2,4]{...) custom-call(f32[4,1,2,4096]{3,2,1,0:T(2,128)S(1)} %copy-done, ...), custom_call_target="tpu_custom_call" | custom-call | flops 200000000 | bytes 6000000 | tf_op jit(solution)/shard_map/pallas_call | solution.py:410
  8.0 0.0 collective-permute-done.1.odd_in.odd_edge
  8.0 1.8 %collective-permute-done.even_in.even_edge = f32[4,2,3072]{2,1,0:T(2,128)S(1)} collective-permute-done((f32[4,2,3072]{2,1,0:T(2,128)S(1)}, f32[4,2,3072]{2,1,0:T(2,128)S(1)}, u32[]{:S(2)}, u32[]{:S(2)}) %collective-permute-start) | collective-permute-done | bytes 98336 | tf_op jit(solution)/shard_map/ppermute | solution.py:433
  9.8 0.9 %shard_map.78 = (f32[4,2,48,128]{3,2,1,0:T(8,128)S(1)}, f32[4,2,48,128]{3,2,1,0:T(8,128)S(1)}, f32[64,128]{1,0:T(8,128)S(1)}) custom-call(s32[2,4]{1,0:T(2,128)S(1)} %get-tuple-element.30.delays, s32[2,4]{1,0:T(2,128)S(1)} %get-tuple-element.29.shifts, f32[4,2,32,128]{3,2,1,0:T(8,128)S(1)} %get-tuple-element.32.sig_rows, ...), custom_call_target="tpu_custom_call" | custom-call | flops 200000000 | bytes 6000000 | tf_op jit(solution)/shard_map/pallas_call | solution.py:410
  10.7 0.1 collective-permute-start.2
  10.8 1.2 %collective-permute-done.2 = f32[64,128]{1,0:T(8,128)S(1)} collective-permute-done((f32[64,128]{1,0:T(8,128)S(1)}, f32[64,128]{1,0:T(8,128)S(1)}, u32[]{:S(2)}, u32[]{:S(2)}) %collective-permute-start.2) | collective-permute-done | bytes 32800 | tf_op jit(solution)/shard_map/ppermute | solution.py:449
  12.0 1.3 %collective-permute-start.3 = (f32[64,128]{1,0:T(8,128)S(1)}, f32[64,128]{1,0:T(8,128)S(1)}, u32[]{:S(2)}, u32[]{:S(2)}) collective-permute-start(f32[64,128]{1,0:T(8,128)S(1)} %add.36), channel_id=1, source_target_pairs={{0,3},{1,2},{2,1},{3,0},{4,7},{5,6},{6,5},{7,4},{8,11},{9,10},{10,... | collective-permute-start | bytes 98312 | tf_op jit(solution)/shard_map/ppermute | solution.py:433
  13.3 2.1 %collective-permute-done.3 = f32[64,128]{1,0:T(8,128)S(1)} collective-permute-done((f32[64,128]{1,0:T(8,128)S(1)}, f32[64,128]{1,0:T(8,128)S(1)}, u32[]{:S(2)}, u32[]{:S(2)}) %collective-permute-start.3) | collective-permute-done | bytes 32800 | tf_op jit(solution)/shard_map/ppermute | solution.py:433
  15.4 1.0 %shard_map.79 = (f32[4,48,128]{2,1,0:T(8,128)S(1)}, f32[4,48,128]{2,1,0:T(8,128)S(1)}, f32[4,2,48,128]{3,2,1,0:T(8,128)S(1)}, f32[4,2,48,128]{3,2,1,0:T(8,128)S(...) custom-call(s32[2,4]{1,0:T(2,128)S(1)} %get-tuple-element.30.delays, s32[2,4]{1,0:T(2,128)S(1)} %get-tuple-element.29.shifts, ...), custom_call_target="tpu_custom_call" | custom-call | flops 200000000 | bytes 6000000 | tf_op jit(solution)/shard_map/pallas_call | solution.py:410
  16.4 0.2 collective-permute-start.4
  16.6 1.0 %collective-permute-done.4 = f32[48,128]{1,0:T(8,128)S(1)} collective-permute-done((f32[48,128]{1,0:T(8,128)S(1)}, f32[48,128]{1,0:T(8,128)S(1)}, u32[]{:S(2)}, u32[]{:S(2)}) %collective-permute-start.4) | collective-permute-done | bytes 24608 | tf_op jit(solution)/shard_map/ppermute | solution.py:449
  17.6 1.3 %collective-permute-start.5 = (f32[48,128]{1,0:T(8,128)S(1)}, f32[48,128]{1,0:T(8,128)S(1)}, u32[]{:S(2)}, u32[]{:S(2)}) collective-permute-start(f32[48,128]{1,0:T(8,128)S(1)} %add.38), channel_id=1, source_target_pairs={{0,3},{1,2},{2,1},{3,0},{4,7},{5,6},{6,5},{7,4},{8,11},{9,10},{10,... | collective-permute-start | bytes 73736 | tf_op jit(solution)/shard_map/ppermute | solution.py:433
  18.9 2.0 %collective-permute-done.5 = f32[48,128]{1,0:T(8,128)S(1)} collective-permute-done((f32[48,128]{1,0:T(8,128)S(1)}, f32[48,128]{1,0:T(8,128)S(1)}, u32[]{:S(2)}, u32[]{:S(2)}) %collective-permute-start.5) | collective-permute-done | bytes 24608 | tf_op jit(solution)/shard_map/ppermute | solution.py:433
  20.9 0.2 collective-permute-start.7
  21.1 2.0 %collective-permute-start.6 = (f32[48,128]{1,0:T(8,128)S(1)}, f32[48,128]{1,0:T(8,128)S(1)}, u32[]{:S(2)}, u32[]{:S(2)}) collective-permute-start(f32[48,128]{1,0:T(8,128)S(1)} %add.39.own), channel_id=1, source_target_pairs={{0,5},{1,4},{4,1},{5,0},{8,13},{9,12},{12,9},{13,8},{2,7},{3,6},{6... | collective-permute-start | bytes 73736 | tf_op jit(solution)/shard_map/ppermute | solution.py:433
  23.1 0.0 collective-permute-done.7.odd_in
  23.1 1.5 %collective-permute-done.6.even_in = f32[48,128]{1,0:T(8,128)S(1)} collective-permute-done((f32[48,128]{1,0:T(8,128)S(1)}, f32[48,128]{1,0:T(8,128)S(1)}, u32[]{:S(2)}, u32[]{:S(2)}) %collective-permute-start.6) | collective-permute-done | bytes 24608 | tf_op jit(solution)/shard_map/ppermute | solution.py:433
  24.6 0.4 shard_map.80
  25.0 0.2 collective-permute-start.8
  25.2 1.0 %collective-permute-done.8 = f32[48,128]{1,0:T(8,128)S(1)} collective-permute-done((f32[48,128]{1,0:T(8,128)S(1)}, f32[48,128]{1,0:T(8,128)S(1)}, u32[]{:S(2)}, u32[]{:S(2)}) %collective-permute-start.8) | collective-permute-done | bytes 24608 | tf_op jit(solution)/shard_map/ppermute | solution.py:449
  26.3 1.3 %collective-permute-start.9 = (f32[48,128]{1,0:T(8,128)S(1)}, f32[48,128]{1,0:T(8,128)S(1)}, u32[]{:S(2)}, u32[]{:S(2)}) collective-permute-start(f32[48,128]{1,0:T(8,128)S(1)} %add.40), channel_id=1, source_target_pairs={{0,3},{1,2},{2,1},{3,0},{4,7},{5,6},{6,5},{7,4},{8,11},{9,10},{10,... | collective-permute-start | bytes 73736 | tf_op jit(solution)/shard_map/ppermute | solution.py:433
  27.5 2.0 %collective-permute-done.9 = f32[48,128]{1,0:T(8,128)S(1)} collective-permute-done((f32[48,128]{1,0:T(8,128)S(1)}, f32[48,128]{1,0:T(8,128)S(1)}, u32[]{:S(2)}, u32[]{:S(2)}) %collective-permute-start.9) | collective-permute-done | bytes 24608 | tf_op jit(solution)/shard_map/ppermute | solution.py:433
  29.5 0.2 collective-permute-start.11
  29.7 2.9 %collective-permute-start.10 = (f32[48,128]{1,0:T(8,128)S(1)}, f32[48,128]{1,0:T(8,128)S(1)}, u32[]{:S(2)}, u32[]{:S(2)}) collective-permute-start(f32[48,128]{1,0:T(8,128)S(1)} %add.41.own), channel_id=1, source_target_pairs={{0,5},{1,4},{4,1},{5,0},{8,13},{9,12},{12,9},{13,8},{2,7},{3,6},{6... | collective-permute-start | bytes 73736 | tf_op jit(solution)/shard_map/ppermute | solution.py:433
  32.6 0.0 collective-permute-done.11.odd_in
  32.6 1.5 %collective-permute-done.10.even_in = f32[48,128]{1,0:T(8,128)S(1)} collective-permute-done((f32[48,128]{1,0:T(8,128)S(1)}, f32[48,128]{1,0:T(8,128)S(1)}, u32[]{:S(2)}, u32[]{:S(2)}) %collective-permute-start.10) | collective-permute-done | bytes 24608 | tf_op jit(solution)/shard_map/ppermute | solution.py:433
  34.1 0.8 %shard_map.81 = (f32[4,2,48,128]{3,2,1,0:T(8,128)S(1)}, f32[4,2,48,128]{3,2,1,0:T(8,128)S(1)}, f32[48,128]{1,0:T(8,128)S(1)}) custom-call(s32[2,4]{1,0:T(2,128)S(1)} %get-tuple-element.30.delays, s32[2,4]{1,0:T(2,128)S(1)} %get-tuple-element.29.shifts, f32[2,4]{1,0:T(2,128)S(1)} %get-tuple-element.31.gains, f32[4,2,48,128]{3,2,1,0:T(8,128)S(1)} %get-tuple-element.42.turned1, ...), custom_call_target="tpu_custom_call" | custom-call | flops 200000000 | bytes 6000000 | tf_op jit(solution)/shard_map/pallas_call | solution.py:410
  35.0 0.4 collective-permute-start.12
  35.4 0.9 %collective-permute-done.12 = f32[48,128]{1,0:T(8,128)S(1)} collective-permute-done((f32[48,128]{1,0:T(8,128)S(1)}, f32[48,128]{1,0:T(8,128)S(1)}, u32[]{:S(2)}, u32[]{:S(2)}) %collective-permute-start.12) | collective-permute-done | bytes 24608 | tf_op jit(solution)/shard_map/ppermute | solution.py:449
  36.2 1.4 %collective-permute-start.13 = (f32[48,128]{1,0:T(8,128)S(1)}, f32[48,128]{1,0:T(8,128)S(1)}, u32[]{:S(2)}, u32[]{:S(2)}) collective-permute-start(f32[48,128]{1,0:T(8,128)S(1)} %add.42), channel_id=1, source_target_pairs={{0,3},{1,2},{2,1},{3,0},{4,7},{5,6},{6,5},{7,4},{8,11},{9,10},{10,... | collective-permute-start | bytes 73736 | tf_op jit(solution)/shard_map/ppermute | solution.py:433
  37.7 1.8 %collective-permute-done.13 = f32[48,128]{1,0:T(8,128)S(1)} collective-permute-done((f32[48,128]{1,0:T(8,128)S(1)}, f32[48,128]{1,0:T(8,128)S(1)}, u32[]{:S(2)}, u32[]{:S(2)}) %collective-permute-start.13) | collective-permute-done | bytes 24608 | tf_op jit(solution)/shard_map/ppermute | solution.py:433
  39.5 0.3 collective-permute-start.15
  39.8 1.8 %collective-permute-start.14 = (f32[48,128]{1,0:T(8,128)S(1)}, f32[48,128]{1,0:T(8,128)S(1)}, u32[]{:S(2)}, u32[]{:S(2)}) collective-permute-start(f32[48,128]{1,0:T(8,128)S(1)} %add.43.own), channel_id=1, source_target_pairs={{0,5},{1,4},{4,1},{5,0},{8,13},{9,12},{12,9},{13,8},{2,7},{3,6},{6... | collective-permute-start | bytes 73736 | tf_op jit(solution)/shard_map/ppermute | solution.py:433
  41.6 1.1 %shard_map.82.taps1 = f32[8,128]{1,0:T(8,128)S(1)} custom-call(f32[4,2,48,128]{3,2,1,0:T(8,128)S(1)} %get-tuple-element.50.shifted, f32[4,2,48,128]{3,2,1,0:T(8,128)S(1)} %get-tuple-element.51.grad), custom_call_target="tpu_custom_call" | custom-call | flops 200000000 | bytes 6000000 | tf_op jit(solution)/shard_map/pallas_call | solution.py:410
  42.7 0.0 collective-permute-done.15.odd_in
  42.7 0.4 collective-permute-done.14.even_in
  43.1 1.0 %shard_map.83 = (f32[4,2,48,128]{3,2,1,0:T(8,128)S(1)}, f32[16,128]{1,0:T(8,128)S(1)}) custom-call(s32[2,4]{1,0:T(2,128)S(1)} %get-tuple-element.30.delays, f32[4,2,48,128]{3,2,1,0:T(8,128)S(1)} %get-tuple-element.47.turned0, f32[4,2,48,128]{3,2,1,0:T(8,128)S(1)} %get-tuple-element.35.linear0, f32[48,128]{1,0:T(8,128)S(1)} %add.43.own, ...), custom_call_target="tpu_custom_call" | custom-call | flops 200000000 | bytes 6000000 | tf_op jit(solution)/shard_map/pallas_call | solution.py:410
  44.2 0.2 collective-permute-start.16
  44.4 1.0 %collective-permute-done.16 = f32[16,128]{1,0:T(8,128)S(1)} collective-permute-done((f32[16,128]{1,0:T(8,128)S(1)}, f32[16,128]{1,0:T(8,128)S(1)}, u32[]{:S(2)}, u32[]{:S(2)}) %collective-permute-start.16) | collective-permute-done | bytes 8224 | tf_op jit(solution)/shard_map/ppermute | solution.py:449
  45.4 2.2 %collective-permute-start.19 = (f32[16,128]{1,0:T(8,128)S(1)}, f32[16,128]{1,0:T(8,128)S(1)}, u32[]{:S(2)}, u32[]{:S(2)}) collective-permute-start(f32[16,128]{1,0:T(8,128)S(1)} %add.44), channel_id=1, source_target_pairs={{0,13},{1,12},{4,9},{5,8},{8,5},{9,4},{12,1},{13,0},{2,15},{3,14},... | collective-permute-start | bytes 24584 | tf_op jit(solution)/shard_map/ppermute | solution.py:433
  47.6 0.7 %collective-permute-start.18 = (f32[16,128]{1,0:T(8,128)S(1)}, f32[16,128]{1,0:T(8,128)S(1)}, u32[]{:S(2)}, u32[]{:S(2)}) collective-permute-start(f32[16,128]{1,0:T(8,128)S(1)} %add.44), channel_id=1, source_target_pairs={{0,9},{1,8},{4,13},{5,12},{8,1},{9,0},{12,5},{13,4},{2,11},{3,10},... | collective-permute-start | bytes 24584 | tf_op jit(solution)/shard_map/ppermute | solution.py:433
  48.4 0.9 %collective-permute-start.17 = (f32[16,128]{1,0:T(8,128)S(1)}, f32[16,128]{1,0:T(8,128)S(1)}, u32[]{:S(2)}, u32[]{:S(2)}) collective-permute-start(f32[16,128]{1,0:T(8,128)S(1)} %add.44), channel_id=1, source_target_pairs={{0,5},{1,4},{4,1},{5,0},{8,13},{9,12},{12,9},{13,8},{2,7},{3,6},{6... | collective-permute-start | bytes 24584 | tf_op jit(solution)/shard_map/ppermute | solution.py:433
  49.3 1.2 %shard_map.84 = f32[4,1,2,4096]{3,2,1,0:T(2,128)} custom-call(s32[2,4]{1,0:T(2,128)S(1)} %get-tuple-element.29.shifts, f32[4,2,48,128]{3,2,1,0:T(8,128)S(1)} %get-tuple-element.52.grad0, bf16[4,256,512]{2,1,0:T(8,128)(2,1)S(1)} %get-tuple-element.33.high, bf16[4,256,512]{2,1,0:T(8,128)(2,1)S(1)} %get-tuple-element.34.low), custom_call_target="tpu_custom_call" | custom-call | flops 200000000 | bytes 6000000 | tf_op jit(solution)/shard_map/pallas_call | solution.py:410
  50.5 0.0 collective-permute-done.19
  50.5 1.1 %collective-permute-done.18 = f32[16,128]{1,0:T(8,128)S(1)} collective-permute-done((f32[16,128]{1,0:T(8,128)S(1)}, f32[16,128]{1,0:T(8,128)S(1)}, u32[]{:S(2)}, u32[]{:S(2)}) %collective-permute-start.18) | collective-permute-done | bytes 8224 | tf_op jit(solution)/shard_map/ppermute | solution.py:433
  51.6 0.0 collective-permute-done.17
  51.6 0.6 %add_add_fusion = f32[16,128]{1,0:T(8,128)} fusion(f32[16,128]{1,0:T(8,128)S(1)} %collective-permute-done.18, f32[16,128]{1,0:T(8,128)S(1)} %collective-permute-done.19, f32[16,128]{1,0:T(8,128)S(1)} %add.44, f32[16,128]{1,0:T(8,128)S(1)} %collective-permute-done.17), kind=kLoop, calls=%fused_computation.4 | loop fusion | flops 6144 | bytes 40960 | tf_op jit(solution)/shard_map/add | solution.py:462
  (9 shorter events, 0.0 us)
Async XLA Ops:
  2.4 4.8 %copy-start = (f32[4,1,2,4096]{3,2,1,0:T(2,128)S(1)}, f32[4,1,2,4096]{3,2,1,0:T(2,128)}, u32[]{:S(2)}) copy-start(f32[4,1,2,4096]{3,2,1,0:T(2,128)} %signal.1) | copy-start | bytes 393220
  2.4 4.8 %copy-start.1 = (f32[4,1,2,4096]{3,2,1,0:T(2,128)S(1)}, f32[4,1,2,4096]{3,2,1,0:T(2,128)}, u32[]{:S(2)}) copy-start(f32[4,1,2,4096]{3,2,1,0:T(2,128)} %cotangent.1) | copy-start | bytes 393220
  2.4 4.8 %copy-start.2 = (f32[2,4,2,128]{3,2,1,0:T(2,128)S(1)}, f32[2,4,2,128]{3,2,1,0:T(2,128)}, u32[]{:S(2)}) copy-start(f32[2,4,2,128]{3,2,1,0:T(2,128)} %taps) | copy-start | bytes 24580
  2.5 4.7 %copy-start.4 = (s32[2,4]{1,0:T(2,128)S(1)}, s32[2,4]{1,0:T(2,128)}, u32[]{:S(2)}) copy-start(s32[2,4]{1,0:T(2,128)} %shifts.1) | copy-start | bytes 100
  2.5 4.7 %copy-start.5 = (f32[2,4]{1,0:T(2,128)S(1)}, f32[2,4]{1,0:T(2,128)}, u32[]{:S(2)}) copy-start(f32[2,4]{1,0:T(2,128)} %gains.1) | copy-start | bytes 100
  2.5 4.7 %copy-start.3 = (s32[2,4]{1,0:T(2,128)S(1)}, s32[2,4]{1,0:T(2,128)}, u32[]{:S(2)}) copy-start(s32[2,4]{1,0:T(2,128)} %delays.1) | copy-start | bytes 100
  2.5 5.5 %collective-permute-start.1 = (f32[4,2,3072]{2,1,0:T(2,128)S(1)}, f32[4,2,3072]{2,1,0:T(2,128)S(1)}, u32[]{:S(2)}, u32[]{:S(2)}) collective-permute-start(f32[4,2,3072]{2,1,0:T(2,128)S(1)} %get-tuple-element.54), channel_id=1, source_target_pairs={{0,1},{1,0},{4,8},{5,9},{8,4},{9,5},{12,13},{13,12},{2,3},{3,2},{6... | collective-permute-start | bytes 294920 | tf_op jit(solution)/shard_map/ppermute | solution.py:433
  3.0 6.7 %collective-permute-start = (f32[4,2,3072]{2,1,0:T(2,128)S(1)}, f32[4,2,3072]{2,1,0:T(2,128)S(1)}, u32[]{:S(2)}, u32[]{:S(2)}) collective-permute-start(f32[4,2,3072]{2,1,0:T(2,128)S(1)} %get-tuple-element.55), channel_id=1, source_target_pairs={{0,4},{1,5},{4,0},{5,1},{8,12},{9,13},{12,8},{13,9},{2,6},{3,7},{6... | collective-permute-start | bytes 294920 | tf_op jit(solution)/shard_map/ppermute | solution.py:433
  10.7 1.3 %collective-permute-start.2 = (f32[64,128]{1,0:T(8,128)S(1)}, f32[64,128]{1,0:T(8,128)S(1)}, u32[]{:S(2)}, u32[]{:S(2)}) collective-permute-start(f32[64,128]{1,0:T(8,128)S(1)} %get-tuple-element.36), channel_id=1, source_target_pairs={{0,1},{1,0},{2,3},{3,2},{4,5},{5,4},{6,7},{7,6},{8,9},{9,8},{10,11... | collective-permute-start | bytes 98312 | tf_op jit(solution)/shard_map/ppermute | solution.py:449
  12.0 3.3 %collective-permute-start.3 = (f32[64,128]{1,0:T(8,128)S(1)}, f32[64,128]{1,0:T(8,128)S(1)}, u32[]{:S(2)}, u32[]{:S(2)}) collective-permute-start(f32[64,128]{1,0:T(8,128)S(1)} %add.36), channel_id=1, source_target_pairs={{0,3},{1,2},{2,1},{3,0},{4,7},{5,6},{6,5},{7,4},{8,11},{9,10},{10,... | collective-permute-start | bytes 98312 | tf_op jit(solution)/shard_map/ppermute | solution.py:433
  16.4 1.3 %collective-permute-start.4 = (f32[48,128]{1,0:T(8,128)S(1)}, f32[48,128]{1,0:T(8,128)S(1)}, u32[]{:S(2)}, u32[]{:S(2)}) collective-permute-start(f32[48,128]{1,0:T(8,128)S(1)} %get-tuple-element.40), channel_id=1, source_target_pairs={{0,1},{1,0},{2,3},{3,2},{4,5},{5,4},{6,7},{7,6},{8,9},{9,8},{10,11... | collective-permute-start | bytes 73736 | tf_op jit(solution)/shard_map/ppermute | solution.py:449
  17.6 3.3 %collective-permute-start.5 = (f32[48,128]{1,0:T(8,128)S(1)}, f32[48,128]{1,0:T(8,128)S(1)}, u32[]{:S(2)}, u32[]{:S(2)}) collective-permute-start(f32[48,128]{1,0:T(8,128)S(1)} %add.38), channel_id=1, source_target_pairs={{0,3},{1,2},{2,1},{3,0},{4,7},{5,6},{6,5},{7,4},{8,11},{9,10},{10,... | collective-permute-start | bytes 73736 | tf_op jit(solution)/shard_map/ppermute | solution.py:433
  20.9 2.2 %collective-permute-start.7 = (f32[48,128]{1,0:T(8,128)S(1)}, f32[48,128]{1,0:T(8,128)S(1)}, u32[]{:S(2)}, u32[]{:S(2)}) collective-permute-start(f32[48,128]{1,0:T(8,128)S(1)} %add.39.own), channel_id=1, source_target_pairs={{0,1},{1,0},{4,9},{5,8},{8,5},{9,4},{12,13},{13,12},{2,3},{3,2},{6... | collective-permute-start | bytes 73736 | tf_op jit(solution)/shard_map/ppermute | solution.py:433
  21.1 3.5 %collective-permute-start.6 = (f32[48,128]{1,0:T(8,128)S(1)}, f32[48,128]{1,0:T(8,128)S(1)}, u32[]{:S(2)}, u32[]{:S(2)}) collective-permute-start(f32[48,128]{1,0:T(8,128)S(1)} %add.39.own), channel_id=1, source_target_pairs={{0,5},{1,4},{4,1},{5,0},{8,13},{9,12},{12,9},{13,8},{2,7},{3,6},{6... | collective-permute-start | bytes 73736 | tf_op jit(solution)/shard_map/ppermute | solution.py:433
  25.0 1.2 %collective-permute-start.8 = (f32[48,128]{1,0:T(8,128)S(1)}, f32[48,128]{1,0:T(8,128)S(1)}, u32[]{:S(2)}, u32[]{:S(2)}) collective-permute-start(f32[48,128]{1,0:T(8,128)S(1)} %get-tuple-element.43), channel_id=1, source_target_pairs={{0,1},{1,0},{2,3},{3,2},{4,5},{5,4},{6,7},{7,6},{8,9},{9,8},{10,11... | collective-permute-start | bytes 73736 | tf_op jit(solution)/shard_map/ppermute | solution.py:449
  26.3 3.3 %collective-permute-start.9 = (f32[48,128]{1,0:T(8,128)S(1)}, f32[48,128]{1,0:T(8,128)S(1)}, u32[]{:S(2)}, u32[]{:S(2)}) collective-permute-start(f32[48,128]{1,0:T(8,128)S(1)} %add.40), channel_id=1, source_target_pairs={{0,3},{1,2},{2,1},{3,0},{4,7},{5,6},{6,5},{7,4},{8,11},{9,10},{10,... | collective-permute-start | bytes 73736 | tf_op jit(solution)/shard_map/ppermute | solution.py:433
  29.5 3.1 %collective-permute-start.11 = (f32[48,128]{1,0:T(8,128)S(1)}, f32[48,128]{1,0:T(8,128)S(1)}, u32[]{:S(2)}, u32[]{:S(2)}) collective-permute-start(f32[48,128]{1,0:T(8,128)S(1)} %add.41.own), channel_id=1, source_target_pairs={{0,1},{1,0},{4,9},{5,8},{8,5},{9,4},{12,13},{13,12},{2,3},{3,2},{6... | collective-permute-start | bytes 73736 | tf_op jit(solution)/shard_map/ppermute | solution.py:433
  29.7 4.4 %collective-permute-start.10 = (f32[48,128]{1,0:T(8,128)S(1)}, f32[48,128]{1,0:T(8,128)S(1)}, u32[]{:S(2)}, u32[]{:S(2)}) collective-permute-start(f32[48,128]{1,0:T(8,128)S(1)} %add.41.own), channel_id=1, source_target_pairs={{0,5},{1,4},{4,1},{5,0},{8,13},{9,12},{12,9},{13,8},{2,7},{3,6},{6... | collective-permute-start | bytes 73736 | tf_op jit(solution)/shard_map/ppermute | solution.py:433
  35.0 1.3 %collective-permute-start.12 = (f32[48,128]{1,0:T(8,128)S(1)}, f32[48,128]{1,0:T(8,128)S(1)}, u32[]{:S(2)}, u32[]{:S(2)}) collective-permute-start(f32[48,128]{1,0:T(8,128)S(1)} %get-tuple-element.48), channel_id=1, source_target_pairs={{0,1},{1,0},{2,3},{3,2},{4,5},{5,4},{6,7},{7,6},{8,9},{9,8},{10,11... | collective-permute-start | bytes 73736 | tf_op jit(solution)/shard_map/ppermute | solution.py:449
  36.2 3.3 %collective-permute-start.13 = (f32[48,128]{1,0:T(8,128)S(1)}, f32[48,128]{1,0:T(8,128)S(1)}, u32[]{:S(2)}, u32[]{:S(2)}) collective-permute-start(f32[48,128]{1,0:T(8,128)S(1)} %add.42), channel_id=1, source_target_pairs={{0,3},{1,2},{2,1},{3,0},{4,7},{5,6},{6,5},{7,4},{8,11},{9,10},{10,... | collective-permute-start | bytes 73736 | tf_op jit(solution)/shard_map/ppermute | solution.py:433
  39.5 3.2 %collective-permute-start.15 = (f32[48,128]{1,0:T(8,128)S(1)}, f32[48,128]{1,0:T(8,128)S(1)}, u32[]{:S(2)}, u32[]{:S(2)}) collective-permute-start(f32[48,128]{1,0:T(8,128)S(1)} %add.43.own), channel_id=1, source_target_pairs={{0,1},{1,0},{4,9},{5,8},{8,5},{9,4},{12,13},{13,12},{2,3},{3,2},{6... | collective-permute-start | bytes 73736 | tf_op jit(solution)/shard_map/ppermute | solution.py:433
  39.8 3.3 %collective-permute-start.14 = (f32[48,128]{1,0:T(8,128)S(1)}, f32[48,128]{1,0:T(8,128)S(1)}, u32[]{:S(2)}, u32[]{:S(2)}) collective-permute-start(f32[48,128]{1,0:T(8,128)S(1)} %add.43.own), channel_id=1, source_target_pairs={{0,5},{1,4},{4,1},{5,0},{8,13},{9,12},{12,9},{13,8},{2,7},{3,6},{6... | collective-permute-start | bytes 73736 | tf_op jit(solution)/shard_map/ppermute | solution.py:433
  44.2 1.2 %collective-permute-start.16 = (f32[16,128]{1,0:T(8,128)S(1)}, f32[16,128]{1,0:T(8,128)S(1)}, u32[]{:S(2)}, u32[]{:S(2)}) collective-permute-start(f32[16,128]{1,0:T(8,128)S(1)} %get-tuple-element.53), channel_id=1, source_target_pairs={{0,1},{1,0},{2,3},{3,2},{4,5},{5,4},{6,7},{7,6},{8,9},{9,8},{10,11... | collective-permute-start | bytes 24584 | tf_op jit(solution)/shard_map/ppermute | solution.py:449
  45.4 5.1 %collective-permute-start.19 = (f32[16,128]{1,0:T(8,128)S(1)}, f32[16,128]{1,0:T(8,128)S(1)}, u32[]{:S(2)}, u32[]{:S(2)}) collective-permute-start(f32[16,128]{1,0:T(8,128)S(1)} %add.44), channel_id=1, source_target_pairs={{0,13},{1,12},{4,9},{5,8},{8,5},{9,4},{12,1},{13,0},{2,15},{3,14},... | collective-permute-start | bytes 24584 | tf_op jit(solution)/shard_map/ppermute | solution.py:433
  47.6 4.0 %collective-permute-start.18 = (f32[16,128]{1,0:T(8,128)S(1)}, f32[16,128]{1,0:T(8,128)S(1)}, u32[]{:S(2)}, u32[]{:S(2)}) collective-permute-start(f32[16,128]{1,0:T(8,128)S(1)} %add.44), channel_id=1, source_target_pairs={{0,9},{1,8},{4,13},{5,12},{8,1},{9,0},{12,5},{13,4},{2,11},{3,10},... | collective-permute-start | bytes 24584 | tf_op jit(solution)/shard_map/ppermute | solution.py:433
  48.4 3.3 %collective-permute-start.17 = (f32[16,128]{1,0:T(8,128)S(1)}, f32[16,128]{1,0:T(8,128)S(1)}, u32[]{:S(2)}, u32[]{:S(2)}) collective-permute-start(f32[16,128]{1,0:T(8,128)S(1)} %add.44), channel_id=1, source_target_pairs={{0,5},{1,4},{4,1},{5,0},{8,13},{9,12},{12,9},{13,8},{2,7},{3,6},{6... | collective-permute-start | bytes 24584 | tf_op jit(solution)/shard_map/ppermute | solution.py:433

commit v3 on v2

--- a/solution.py
+++ b/solution.py
@@ -65,6 +65,11 @@
     return jnp.where(lanes_of(x.shape) + amount < LANES, rolled, follow)
 
 
+def at(table, step, b):
+    own = table.shape[2]
+    return table[b // own, step, b % own]
+
+
 def is_even():
     return lax.rem(lax.axis_index("tm"), 2) == 0
 
@@ -87,22 +92,29 @@
     return before, after
 
 
-def extend(out, own, even_in, odd_in, first, edge):
-    bands, _, rows, _ = own.shape
-    pad = (out.shape[2] - rows) // 2
-    for b in range(bands):
+def extend(out, b, even_in, odd_in, first, edge):
+    own = even_in.shape[0]
+    rows = out.shape[2]
+    pad = edge + 4
+    for c in range(2):
+        out[b, c, 0:8, :] = jnp.zeros((8, LANES), F32)
+        out[b, c, rows - 8 :, :] = jnp.zeros((8, LANES), F32)
+    for r in range(edge):
+        lanes = slice((first + r) * LANES, (first + r + 1) * LANES)
+        before, after = from_sides(even_in[b % own, :, lanes], odd_in[b % own, :, lanes])
         for c in range(2):
-            out[b, c, 0:pad, :] = jnp.zeros((pad, LANES), F32)
-            out[b, c, pad : pad + rows, :] = own[b, c]
-            out[b, c, pad + rows :, :] = jnp.zeros((pad, LANES), F32)
-        for r in range(edge):
-            lanes = slice((first + r) * LANES, (first + r + 1) * LANES)
-            before, after = from_sides(even_in[b, :, lanes], odd_in[b, :, lanes])
-            for c in range(2):
-                above = pad - edge + r
-                below = pad + rows + r
-                out[b, c, above : above + 1, :] = before[c : c + 1]
-                out[b, c, below : below + 1, :] = after[c : c + 1]
+            above = pad - edge + r
+            below = rows - pad + r
+            out[b, c, above : above + 1, :] = before[c : c + 1]
+            out[b, c, below : below + 1, :] = after[c : c + 1]
+
+
+def lay_rows(source, target, b, first, rows):
+    own = source.shape[0]
+    for r in range(rows):
+        pair = source[b % own, 0, :, r * LANES : (r + 1) * LANES]
+        for c in range(2):
+            target[b, c, first + r : first + r + 1, :] = pair[c : c + 1]
 
 
 def fir(real, imag, high, low):
@@ -137,7 +149,7 @@
     lane = lanes_of((total, LANES))
     acc = None
     for b in range(bands):
-        delay = delays[step, b]
+        delay = at(delays, step, b)
         q = lax.shift_right_logical(delay, 7)
         s = delay & (LANES - 1)
         held[b, 0:base, :] = jnp.zeros((base, LANES), F32)
@@ -156,7 +168,7 @@
     lane = lanes_of((total, LANES))
     acc = None
     for b in range(bands):
-        delay = delays[step, b]
+        delay = at(delays, step, b)
         q = lax.shift_right_logical(delay, 7)
         s = delay & (LANES - 1)
         held[b, 0:8, :] = jnp.zeros((8, LANES), F32)
@@ -197,31 +209,30 @@
     return jnp.where(lanes_of((count, LANES)) + s < LANES, near, far)
 
 
-def k_setup(
-    signal, cotangent, taps, delays, shifts, gains,
-    sig_rows, cot_rows, delays_out, shifts_out, gains_out, *tables,
-):
-    steps, bands = taps.shape[:2]
+def k_setup(groups, steps, *refs):
+    signals, packs = refs[:groups], refs[groups : 2 * groups]
+    sig_rows, delays, shifts, gains = refs[2 * groups : 2 * groups + 4]
+    tables = refs[2 * groups + 4 :]
     rows = sig_rows.shape[2]
-    for source, target in ((signal, sig_rows), (cotangent, cot_rows)):
-        for b in range(bands):
-            for r in range(rows):
-                pair = source[b, 0, :, r * LANES : (r + 1) * LANES]
-                target[b, 0, r : r + 1, :] = pair[0:1]
-                target[b, 1, r : r + 1, :] = pair[1:2]
-    delays_out[...] = delays[...]
-    shifts_out[...] = shifts[...]
-    gains_out[...] = gains[...]
+    own = delays.shape[2]
     shape = (LANES, LANES)
     diagonal = lanes_of(shape) >= lax.broadcasted_iota(jnp.int32, shape, 0)
-    for step in range(steps):
-        high, low = tables[2 * step : 2 * step + 2]
-        for b in range(bands):
+    first = 2 * steps * own
+    for k, pack in enumerate(packs):
+        for n, target in enumerate((delays, shifts, gains)):
+            row = first + n * steps
+            target[k] = pack[row : row + steps, 0:own].astype(target.dtype)
+    for b in range(groups * own):
+        lay_rows(signals[b // own], sig_rows, b, 0, rows)
+        pack = packs[b // own]
+        for step in range(steps):
+            high, low = tables[2 * step : 2 * step + 2]
             for c in range(2):
-                row = jnp.broadcast_to(taps[step, b, c : c + 1, :], shape)
+                tap = 2 * (step * own + b % own) + c
+                row = jnp.broadcast_to(pack[tap : tap + 1, :], shape)
                 ring = pltpu.roll(row, 0, 1, stride=1, stride_axis=0)
-                first = jnp.where(diagonal, ring, 0.0)
-                for place, half in ((0, first), (1, ring - first)):
+                near = jnp.where(diagonal, ring, 0.0)
+                for place, half in ((0, near), (1, ring - near)):
                     for target, value in zip((high, low), split(half)):
                         a = place * LANES
                         d = (2 + place) * LANES
@@ -233,17 +244,34 @@
                             target[b, 0:LANES, d : d + LANES] = -value
 
 
-def k_first(delays, shifts, sig_rows, even_in, odd_in, high, low, shifted, linear, out, ext, held):
+def k_cotangent(groups, *refs):
+    out = refs[-1]
+    own = refs[0].shape[0]
+    rows = out.shape[2] - 2 * PAD
+    for b in range(out.shape[0]):
+        k = b // own
+        extend(out, b, refs[groups + 2 * k], refs[groups + 2 * k + 1], WIDE, EDGE)
+        lay_rows(refs[k], out, b, PAD, rows)
+
+
+def k_first(groups, delays, shifts, sig_rows, *refs):
+    sides = refs[: 2 * groups]
+    high, low, shifted, linear, out, ext, held = refs[2 * groups :]
     bands, _, rows, _ = sig_rows.shape
-    extend(ext, sig_rows, even_in, odd_in, 0, WIDE)
+    own = shifted.shape[0]
     middle = slice(WIDE_PAD - PAD, WIDE_PAD + rows + PAD)
     powers = []
     for b in range(bands):
-        amount = LANES // 2 - shifts[0, b]
+        k = b // own
+        extend(ext, b, sides[2 * k], sides[2 * k + 1], 0, WIDE)
+        for c in range(2):
+            ext[b, c, WIDE_PAD : WIDE_PAD + rows, :] = sig_rows[b, c]
+        amount = LANES // 2 - at(shifts, 0, b)
         real = later(ext[b, 0], amount)
         imag = later(ext[b, 1], amount)
-        shifted[b, 0] = real[middle]
-        shifted[b, 1] = imag[middle]
+        if b < own:
+            shifted[b, 0] = real[middle]
+            shifted[b, 1] = imag[middle]
         lr, li = fir(real, imag, high[b], low[b])
         linear[b, 0] = lr[middle]
         linear[b, 1] = li[middle]
@@ -260,20 +288,21 @@
     values = end_at_last(own[...], rows)
     powers = []
     for b in range(bands):
-        phase = gains[0, b] * read_spread(values, delays[0, b], held, b, rows)
-        sine, cosine = sine_cosine(phase)
-        cosine0[b] = cosine
-        sine0[b] = sine
+        spread = read_spread(values, at(delays, 0, b), held, b, rows)
+        sine, cosine = sine_cosine(at(gains, 0, b) * spread)
         lr, li = linear0[b, 0], linear0[b, 1]
         fr = keep_inside(lr * cosine - li * sine, rows)
         fi = keep_inside(lr * sine + li * cosine, rows)
         field1[b, 0] = fr
         field1[b, 1] = fi
-        amount = LANES // 2 - shifts[1, b]
+        amount = LANES // 2 - at(shifts, 1, b)
         real = later(fr, amount)
         imag = later(fi, amount)
-        shifted[b, 0] = real
-        shifted[b, 1] = imag
+        if b < shifted.shape[0]:
+            cosine0[b] = cosine
+            sine0[b] = sine
+            shifted[b, 0] = real
+            shifted[b, 1] = imag
         lr, li = fir(real, imag, high[b], low[b])
         linear1[b, 0] = lr
         linear1[b, 1] = li
@@ -283,24 +312,23 @@
 
 
 def k_third(
-    delays, gains, linear1, own, even_in, odd_in, cot_rows, even_edge, odd_edge,
-    turned1, out, ext, spread, held, held_out,
+    delays, gains, linear1, own, even_in, odd_in, cotangent, turned1, out, spread, held, held_out
 ):
     bands = linear1.shape[0]
     rows = linear1.shape[2] - 2 * PAD
-    extend(ext, cot_rows, even_edge, odd_edge, WIDE, EDGE)
     values = gather_spread(own, even_in, odd_in, spread, rows)
     terms = []
     for b in range(bands):
-        phase = gains[1, b] * read_spread(values, delays[1, b], held, b, rows)
+        gain = at(gains, 1, b)
+        phase = gain * read_spread(values, at(delays, 1, b), held, b, rows)
         sine, cosine = sine_cosine(phase)
-        gr, gi = ext[b, 0], ext[b, 1]
+        gr, gi = cotangent[b, 0], cotangent[b, 1]
         er = gr * cosine + gi * sine
         ei = gi * cosine - gr * sine
         turned1[b, 0] = er
         turned1[b, 1] = ei
         term = ei * linear1[b, 0] - er * linear1[b, 1]
-        terms.append(gains[1, b] * term[PAD : PAD + rows])
+        terms.append(gain * term[PAD : PAD + rows])
     scatter_delayed(terms, delays, 1, held_out, out)
 
 
@@ -313,20 +341,22 @@
     values = gather_spread(own, even_in, odd_in, spread, rows)
     terms = []
     for b in range(bands):
-        twice = 2.0 * read_spread(values, delays[1, b], held, b, rows)
+        twice = 2.0 * read_spread(values, at(delays, 1, b), held, b, rows)
         gr = keep_inside(turned1[b, 0] + linear1[b, 0] * twice, rows)
         gi = keep_inside(turned1[b, 1] + linear1[b, 1] * twice, rows)
-        grad1[b, 0] = gr
-        grad1[b, 1] = gi
+        if b < grad1.shape[0]:
+            grad1[b, 0] = gr
+            grad1[b, 1] = gi
         gr, gi = fir_adjoint(gr, gi, high[b], low[b])
-        amount = LANES // 2 - shifts[1, b]
+        amount = LANES // 2 - at(shifts, 1, b)
         gr = earlier(gr, amount)
         gi = earlier(gi, amount)
-        cosine, sine = cosine0[b], sine0[b]
-        turned0[b, 0] = gr * cosine + gi * sine
-        turned0[b, 1] = gi * cosine - gr * sine
+        if b < grad1.shape[0]:
+            cosine, sine = cosine0[b], sine0[b]
+            turned0[b, 0] = gr * cosine + gi * sine
+            turned0[b, 1] = gi * cosine - gr * sine
         term = gi * field1[b, 0] - gr * field1[b, 1]
-        terms.append(gains[0, b] * term[PAD : PAD + rows])
+        terms.append(at(gains, 0, b) * term[PAD : PAD + rows])
     scatter_delayed(terms, delays, 0, held_out, out)
 
 
@@ -377,11 +407,11 @@
     scale, delays, turned0, linear0, own, even_in, odd_in, shifted, taps1,
     grad0, out, spread, held,
 ):
-    bands = linear0.shape[0]
-    rows = linear0.shape[2] - 2 * PAD
+    bands = turned0.shape[0]
+    rows = turned0.shape[2] - 2 * PAD
     values = gather_spread(own, even_in, odd_in, spread, rows)
     for b in range(bands):
-        twice = 2.0 * read_spread(values, delays[0, b], held, b, rows)
+        twice = 2.0 * read_spread(values, at(delays, 0, b), held, b, rows)
         gr = keep_inside(turned0[b, 0] + linear0[b, 0] * twice, rows)
         gi = keep_inside(turned0[b, 1] + linear0[b, 1] * twice, rows)
         grad0[b, 0] = gr
@@ -397,7 +427,7 @@
     rows = grad0.shape[2] - 2 * PAD
     for b in range(bands):
         gr, gi = fir_adjoint(grad0[b, 0], grad0[b, 1], high[b], low[b])
-        amount = LANES // 2 - shifts[0, b]
+        amount = LANES // 2 - at(shifts, 0, b)
         gr = earlier(gr, amount)[PAD : PAD + rows]
         gi = earlier(gi, amount)[PAD : PAD + rows]
         for r in range(rows):
@@ -405,19 +435,19 @@
             result[b, 0, 1:2, r * LANES : (r + 1) * LANES] = gi[r : r + 1]
 
 
-def call(kernel, scalars, arrays, shapes, scratch=(), micros=2.0):
+def call(kernel, arrays, shapes, scratch=(), micros=2.0):
     vmem = pl.BlockSpec(memory_space=pltpu.VMEM)
     return pl.pallas_call(
         kernel,
         out_shape=shapes,
-        in_specs=[vmem] * (len(scalars) + len(arrays)),
+        in_specs=[vmem] * len(arrays),
         out_specs=[vmem] * len(shapes),
         scratch_shapes=[pltpu.VMEM(s, F32) for s in scratch],
         compiler_params=pltpu.CompilerParams(vmem_limit_bytes=24 * 1024 * 1024),
         cost_estimate=pl.CostEstimate(
             flops=int(micros * 1e8), bytes_accessed=int(micros * 3e6), transcendentals=0
         ),
-    )(*scalars, *arrays)
+    )(*arrays)
 
 
 def swapped(x, axis, partner, cross):
@@ -449,10 +479,33 @@
     return x + lax.ppermute(x, "pol", [(p, cores - 1 - p) for p in range(cores)])
 
 
+def evenly(i):
+    return i ^ 1
+
+
+def oddly(i):
+    return ((i + 1) ^ 1) - 1
+
+
 def neighbours(even_out, odd_out, cross):
-    odd_in = swapped(odd_out, "tm", lambda i: ((i + 1) ^ 1) - 1, cross)
-    even_in = swapped(even_out, "tm", lambda i: i ^ 1, cross)
+    odd_in = swapped(odd_out, "tm", oddly, cross)
+    even_in = swapped(even_out, "tm", evenly, cross)
     return even_in, odd_in
+
+
+def aslant(x, partner):
+    size, cores = lax.axis_size("tm"), lax.axis_size("pol")
+    pairs = []
+    for i in range(size):
+        for b in range(2):
+            for p in range(cores):
+                here = (i * 2 + b) * cores
+                j = partner(i)
+                if 0 <= j < size:
+                    pairs.append((here + p, (j * 2 + 1 - b) * cores + p))
+                else:
+                    pairs.append((here + p, here + cores - 1 - p))
+    return lax.ppermute(x, ("tm", "band", "pol"), pairs)
 
 
 def over_tm(x):
@@ -462,12 +515,13 @@
     return (x + others[0]) + (others[1] + others[2])
 
 
-def over_powers(part):
-    return summed(over_cores(part), "band")
-
-
-def exchanged(part):
-    part = over_powers(part)
+def over_powers(part, doubled):
+    part = over_cores(part)
+    return part if doubled else summed(part, "band")
+
+
+def exchanged(part, doubled):
+    part = over_powers(part, doubled)
     return (part,) + neighbours(part, part, True)
 
 
@@ -480,65 +534,80 @@
 
 
 def on_device(signal, cotangent, taps, gains, walk_off, tap_shift):
-    bands, _, _, length = signal.shape
+    own, _, _, length = signal.shape
     steps = taps.shape[0]
     rows = length // LANES
     held_rows = rows + 2 * PAD
+    doubled = lax.axis_size("band") == 2
+    groups = 2 if doubled else 1
+    bands = groups * own
 
     def shape(*dims, dtype=F32):
         return jax.ShapeDtypeStruct(dims, dtype)
 
-    own = shape(bands, 2, rows, LANES)
     field = shape(bands, 2, held_rows, LANES)
-    angle = shape(bands, held_rows, LANES)
+    own_field = shape(own, 2, held_rows, LANES)
+    angle = shape(own, held_rows, LANES)
     wide_part = shape(rows + REACH + 2 * PAD, LANES)
     part = shape(rows + REACH, LANES)
     table = shape(bands, 2 * LANES, 4 * LANES, dtype=BF16)
-    ext = (bands, 2, held_rows, LANES)
     ext_wide = (bands, 2, rows + 2 * WIDE_PAD, LANES)
     held_wide = (bands, rows + 2 * WIDE_PAD + 8, LANES)
     spread = (rows + REACH + 2 * PAD, LANES)
     held_in = (bands, rows + REACH + 3 * PAD, LANES)
     held_out = (bands, rows + 3 * REACH, LANES)
 
+    signals, cotangents = [signal], [cotangent]
+    small = jnp.concatenate([walk_off.astype(F32), tap_shift.astype(F32), gains])
+    small = jnp.pad(small, ((0, -3 * steps % 8), (0, LANES - own)))
+    small = jnp.concatenate([taps.reshape(2 * steps * own, LANES), small])
     even_out, odd_out = edges(signal[:, 0], cotangent[:, 0])
-    even_edge, odd_edge = neighbours(even_out, odd_out, False)
-    taps, even_out = lax.optimization_barrier((taps, even_out))
-    small = [shape(*a.shape, dtype=a.dtype) for a in (walk_off, tap_shift, gains)]
-    sig_rows, cot_rows, walk_off, tap_shift, gains, high0, low0, high1, low1 = call(
-        k_setup, (), (signal, cotangent, taps, walk_off, tap_shift, gains),
-        [own, own] + small + [table] * (2 * steps),
+    small, _ = lax.optimization_barrier((small, even_out))
+    packs = [small]
+    sides = list(neighbours(even_out, odd_out, False))
+    if doubled:
+        signals.append(swapped(signal, "band", evenly, False))
+        packs.append(swapped(packs[0], "band", evenly, False))
+        sides += [aslant(even_out, evenly), aslant(odd_out, oddly)]
+        cotangents.append(swapped(cotangent, "band", evenly, False))
+    tiny = [shape(groups, steps, own, dtype=d) for d in (jnp.int32, jnp.int32, F32)]
+    sig_rows, delays, shifts, gains, high0, low0, high1, low1 = call(
+        functools.partial(k_setup, groups, steps), (*signals, *packs),
+        [shape(bands, 2, rows, LANES)] + tiny + [table] * (2 * steps),
+    )
+    (cot_rows,) = call(
+        functools.partial(k_cotangent, groups), (*cotangents, *sides), [field]
     )
     shifted0, linear0, sent = call(
-        k_first, (walk_off, tap_shift), (sig_rows, even_edge, odd_edge, high0, low0),
-        [field, field, wide_part], (ext_wide, held_wide),
+        functools.partial(k_first, groups), (delays, shifts, sig_rows, *sides, high0, low0),
+        [own_field, field, wide_part], (ext_wide, held_wide),
     )
     cosine0, sine0, field1, shifted1, linear1, sent = call(
-        k_second, (walk_off, tap_shift, gains), (linear0, over_powers(sent), high1, low1),
-        [angle, angle, field, field, field, part], (held_in, held_out),
+        k_second, (delays, shifts, gains, linear0, over_powers(sent, doubled), high1, low1),
+        [angle, angle, field, own_field, field, part], (held_in, held_out),
     )
     turned1, sent = call(
-        k_third, (walk_off, gains),
-        (linear1, *exchanged(sent), cot_rows, even_edge, odd_edge),
-        [field, part], (ext, spread, held_in, held_out),
+        k_third, (delays, gains, linear1, *exchanged(sent, doubled), cot_rows),
+        [field, part], (spread, held_in, held_out),
     )
     grad1, turned0, sent = call(
-        k_fourth, (walk_off, tap_shift, gains),
-        (turned1, linear1, *exchanged(sent), high1, low1, cosine0, sine0, field1),
-        [field, field, part], (spread, held_in, held_out),
-    )
-    (taps1,) = call(k_taps, (), (shifted1, grad1), [shape(2 * bands, LANES)])
+        k_fourth,
+        (delays, shifts, gains, turned1, linear1, *exchanged(sent, doubled), high1, low1,
+         cosine0, sine0, field1),
+        [own_field, own_field, part], (spread, held_in, held_out),
+    )
+    (taps1,) = call(k_taps, (shifted1, grad1), [shape(2 * own, LANES)])
     scale = 1.0 / math.sqrt(2.0 * length * lax.axis_size("tm"))
     grad0, grad_taps = call(
         functools.partial(k_fifth, scale),
-        (walk_off,), (turned0, linear0, *exchanged(sent), shifted0, taps1),
-        [field, shape(steps * 2 * bands, LANES)], (spread, held_in),
+        (delays, turned0, linear0, *exchanged(sent, doubled), shifted0, taps1),
+        [own_field, shape(steps * 2 * own, LANES)], (spread, held_in),
     )
     (grad_signal,) = call(
-        k_last, (tap_shift,), (grad0, high0, low0), [shape(bands, 1, 2, length)]
+        k_last, (shifts, grad0, high0, low0), [shape(own, 1, 2, length)]
     )
     grad_taps = over_tm(over_cores(grad_taps))
-    return grad_signal, grad_taps.reshape(steps, bands, 2, LANES)
+    return grad_signal, grad_taps.reshape(steps, own, 2, LANES)
 
 
 def solution(mesh):

time: 52.4 us -> 49.6 us (0.947)
  waiting for transfers between devices: 19.4 us -> 10.2 us
  other arithmetic: 0.73 us -> 3.47 us
  Pallas kernels: 7.24 us -> 9.97 us
  local copies, waits for them, and re-layouts: 1.75 us -> 2.62 us
    ppermute x15 -> x14, waiting for transfers between devices: 14.3 us -> 5.05 us  [swapped(): return lax.ppermute(x, (axis, 'pol'), pairs)]
    ppermute x15 -> x14, starting transfers between devices: 21.2 us -> 16.6 us  [swapped(): return lax.ppermute(x, (axis, 'pol'), pairs)]
    ppermute x0 -> x2, starting transfers between devices: none -> 4.5 us  [aslant(): return lax.ppermute(x, ('tm', 'band', 'pol'), pairs)]
    pallas_call x8 -> x9, Pallas kernels: 7.24 us -> 9.97 us  [call(): pl.pallas_call(kernel, out_shape=shapes, in_specs=[vmem] * len(arrays), o...]
    concatenate x0 -> x2, other arithmetic: none -> 1.39 us  [the longest x1 0.7 us: on_device(): small = jnp.concatenate([taps.reshape(2 * steps * own, LANES), small])]
    convert_element_type x0 -> x2, other arithmetic: none -> 1.36 us  [the longest x1 0.68 us: on_device(): walk_off.astype(F32)]
    unnamed x12 -> x4, local copies, waits for them, and re-layouts: 0.04 us -> 0.91 us
  transfers between devices with their start and end apart: 20 -> 21, of which waited for: 14 -> 10; matrix products, arithmetic and copies ran while one was open for 0% -> 9% of each run, Pallas kernels for 6% -> 14%
where the time goes in v3:
time: 49.6 us; the launch traced here: 49.3 us
  starting transfers between devices  22.3 us (45%)
  waiting for transfers between devices  10.2 us (21%)
  Pallas kernels  9.97 us (20%)
  other arithmetic  3.47 us (7%)
  local copies, waits for them, and re-layouts  2.62 us (5%)
  between operations  0.75 us (2%)
    ppermute x14, starting transfers between devices, swapped(): return lax.ppermute(x, (axis, 'pol'), pairs)  16.6 us
    pallas_call x9, Pallas kernels, call(): pl.pallas_call(kernel, out_shape=shapes, in_specs=[vmem] * len(arrays), o...  9.97 us
    ppermute x5, waiting for transfers between devices, over_cores(): lax.ppermute(x, 'pol', [(p, cores - 1 - p) for p in range(cores)])  5.16 us
    ppermute x14, waiting for transfers between devices, swapped(): return lax.ppermute(x, (axis, 'pol'), pairs)  5.05 us
    ppermute x2, starting transfers between devices, aslant(): return lax.ppermute(x, ('tm', 'band', 'pol'), pairs)  4.5 us
    slice x2, local copies, waits for them, and re-layouts, edges(): right = jnp.concatenate([signal[..., -wide:], cotangent[..., -edge:]], -1)  1.71 us
    ppermute x5, starting transfers between devices, over_cores(): lax.ppermute(x, 'pol', [(p, cores - 1 - p) for p in range(cores)])  1.12 us
  transfers between devices with their start and end apart: 21, of which 10 were waited for; matrix products, arithmetic and copies ran while one was open for 9% of the time, Pallas kernels for 14%

profile of v3, /device:TPU:0, one launch (start us, length us, event | category | flops | bytes accessed | tf_op | source)
XLA Modules:
  0.0 49.3 jit_solution(2351027454258123052)
XLA Ops:
  0.6 3.0 %collective-permute-start = (f32[4,1,2,4096]{3,2,1,0:T(2,128)}, f32[4,1,2,4096]{3,2,1,0:T(2,128)S(1)}, u32[]{:S(2)}, u32[]{:S(2)}) collective-permute-start(f32[4,1,2,4096]{3,2,1,0:T(2,128)} %refs_0_.2), channel_id=1, source_target_pairs={{0,2},{1,3},{2,0},{3,1},{4,6},{5,7},{6,4},{7,5},{8,10},{9,11},{10,... | collective-permute-start | bytes 393224 | tf_op jit(solution)/shard_map/ppermute | solution.py:463
  3.6 0.7 %convert_element_type.8 = f32[2,4]{1,0:T(2,128)S(1)} convert(s32[2,4]{1,0:T(2,128)} %param.10) | non-fusion elementwise | flops 8 | bytes 64 | tf_op jit(solution)/shard_map/convert_element_type | solution.py:561
  4.3 0.7 %convert_element_type.9 = f32[2,4]{1,0:T(2,128)S(1)} convert(s32[2,4]{1,0:T(2,128)} %param.11) | non-fusion elementwise | flops 8 | bytes 64 | tf_op jit(solution)/shard_map/convert_element_type | solution.py:561
  5.0 0.7 %fusion.1 = (f32[4,2,512]{2,1,0:T(2,128)S(1)}, f32[4,2,512]{2,1,0:T(2,128)S(1)}) fusion(f32[4,2,4096]{2,1,0:T(2,128)} %bitcast.5), kind=kLoop, calls=%fused_computation.11 | loop fusion | bytes 65536 | tf_op jit(solution)/shard_map/slice | solution.py:531
  5.7 1.0 %fusion = (f32[4,2,2560]{2,1,0:T(2,128)S(1)}, f32[4,2,2560]{2,1,0:T(2,128)S(1)}) fusion(f32[4,2,4096]{2,1,0:T(2,128)} %bitcast.4), kind=kLoop, calls=%fused_computation.10 | loop fusion | bytes 327680 | tf_op jit(solution)/shard_map/slice | solution.py:531
  6.7 0.7 %select_maximum_fusion = f32[8,128]{1,0:T(8,128)S(1)} fusion(f32[2,4]{1,0:T(2,128)} %param.9, f32[2,4]{1,0:T(2,128)S(1)} %convert_element_type.9, f32[2,4]{1,0:T(2,128)S(1)} %convert_element_type.8), kind=kLoop, calls=%fused_computation.6 | loop fusion | flops 11264 | bytes 4192 | tf_op jit(solution)/shard_map/concatenate | solution.py:561
  7.4 0.1 broadcast_select_fusion
  7.5 0.7 %pad_maximum_fusion.2.refs_2_ = f32[24,128]{1,0:T(8,128)S(1)} fusion(f32[8,128]{1,0:T(8,128)S(1)} %select_maximum_fusion, f32[16,128]{1,0:T(8,128)} %bitcast.6), kind=kLoop, calls=%fused_computation.4 | loop fusion | flops 3072 | bytes 24576 | tf_op jit(solution)/shard_map/concatenate | solution.py:563
  8.2 0.0 collective-permute-start.1
  8.2 0.0 collective-permute-start.5
  8.2 0.5 %collective-permute-start.3 = (f32[4,2,3072]{2,1,0:T(2,128)S(1)}, f32[4,2,3072]{2,1,0:T(2,128)S(1)}, u32[]{:S(2)}, u32[]{:S(2)}) collective-permute-start(f32[4,2,3072]{2,1,0:T(2,128)S(1)} %get-tuple-element.52), channel_id=1, source_target_pairs={{0,1},{1,0},{4,8},{5,9},{8,4},{9,5},{12,13},{13,12},{2,3},{3,2},{6... | collective-permute-start | bytes 294920 | tf_op jit(solution)/shard_map/ppermute | solution.py:463
  8.7 4.5 %collective-permute-start.4 = (f32[4,2,3072]{2,1,0:T(2,128)S(1)}, f32[4,2,3072]{2,1,0:T(2,128)S(1)}, u32[]{:S(2)}, u32[]{:S(2)}) collective-permute-start(f32[4,2,3072]{2,1,0:T(2,128)S(1)} %get-tuple-element.53), channel_id=1, source_target_pairs={{0,6},{1,7},{2,4},{3,5},{4,2},{5,3},{6,0},{7,1},{8,14},{9,15},{10,... | collective-permute-start | bytes 294920 | tf_op jit(solution)/shard_map/ppermute | solution.py:508
  13.2 0.0 collective-permute-done.1.refs_3_
  13.2 1.0 %collective-permute-start.2 = (f32[4,2,3072]{2,1,0:T(2,128)S(1)}, f32[4,2,3072]{2,1,0:T(2,128)S(1)}, u32[]{:S(2)}, u32[]{:S(2)}) collective-permute-start(f32[4,2,3072]{2,1,0:T(2,128)S(1)} %get-tuple-element.53), channel_id=1, source_target_pairs={{0,4},{1,5},{4,0},{5,1},{8,12},{9,13},{12,8},{13,9},{2,6},{3,7},{6... | collective-permute-start | bytes 294920 | tf_op jit(solution)/shard_map/ppermute | solution.py:463
  14.3 0.0 collective-permute-done.refs_1_
  14.3 0.5 %collective-permute-start.10 = (f32[4,1,2,4096]{3,2,1,0:T(2,128)}, f32[4,1,2,4096]{3,2,1,0:T(2,128)S(1)}, u32[]{:S(2)}, u32[]{:S(2)}) collective-permute-start(f32[4,1,2,4096]{3,2,1,0:T(2,128)} %refs_0_.3), channel_id=1, source_target_pairs={{0,2},{1,3},{2,0},{3,1},{4,6},{5,7},{6,4},{7,5},{8,10},{9,11},{10,... | collective-permute-start | bytes 393224 | tf_op jit(solution)/shard_map/ppermute | solution.py:463
  14.8 0.0 copy-start
  14.8 0.9 %copy-done = f32[4,1,2,4096]{3,2,1,0:T(2,128)S(1)} copy-done((f32[4,1,2,4096]{3,2,1,0:T(2,128)S(1)}, f32[4,1,2,4096]{3,2,1,0:T(2,128)}, u32[]{:S(2)}) %copy-start) | copy-done | bytes 131096
  15.7 1.3 %shard_map.77 = (f32[8,2,32,128]{3,2,1,0:T(8,128)S(1)}, s32[2,2,4]{2,1,0:T(2,128)S(1)}, s32[2,2,4]{2,1,0:T(2,128)S(1)}, f32[2,2,4]{2,1,0:T(2,128)S(1)}, bf16[8,2...) custom-call(f32[4,1,2,4096]{3,2,1,0:T(2,128)S(1)} %copy-done, ...), custom_call_target="tpu_custom_call" | custom-call | flops 200000000 | bytes 6000000 | tf_op jit(solution)/shard_map/pallas_call | solution.py:440
  17.0 0.0 collective-permute-done.5.refs_3_.refs_5_
  17.0 0.0 collective-permute-done.3.refs_1_.refs_3_
  17.0 0.0 collective-permute-done.4.refs_2_.refs_4_
  17.0 0.8 %collective-permute-done.2.refs_0_.refs_2_ = f32[4,2,3072]{2,1,0:T(2,128)S(1)} collective-permute-done((f32[4,2,3072]{2,1,0:T(2,128)S(1)}, f32[4,2,3072]{2,1,0:T(2,128)S(1)}, u32[]{:S(2)}, u32[]{:S(2)}) %collective-permute-start.2) | collective-permute-done | bytes 98336 | tf_op jit(solution)/shard_map/ppermute | solution.py:463
  17.9 1.6 %shard_map.78 = (f32[4,2,48,128]{3,2,1,0:T(8,128)S(1)}, f32[8,2,48,128]{3,2,1,0:T(8,128)S(1)}, f32[64,128]{1,0:T(8,128)S(1)}) custom-call(s32[2,2,4]{2,1,0:T(2,128)S(1)} %get-tuple-element.29.delays, s32[2,2,4]{2,1,0:T(2,128)S(1)} %get-tuple-element.28.shifts, f32[8,2,32,128]{3,2,1,0:T(8,128)S(1)} %get-tuple-element.31.sig_rows, ...), custom_call_target="tpu_custom_call" | custom-call | flops 200000000 | bytes 6000000 | tf_op jit(solution)/shard_map/pallas_call | solution.py:440
  19.5 0.1 collective-permute-start.6
  19.6 1.2 %collective-permute-done.6 = f32[64,128]{1,0:T(8,128)S(1)} collective-permute-done((f32[64,128]{1,0:T(8,128)S(1)}, f32[64,128]{1,0:T(8,128)S(1)}, u32[]{:S(2)}, u32[]{:S(2)}) %collective-permute-start.6) | collective-permute-done | bytes 32800 | tf_op jit(solution)/shard_map/ppermute | solution.py:479
  20.8 0.0 copy-start.1
  20.8 1.7 %shard_map.79 = (f32[4,48,128]{2,1,0:T(8,128)S(1)}, f32[4,48,128]{2,1,0:T(8,128)S(1)}, f32[8,2,48,128]{3,2,1,0:T(8,128)S(1)}, f32[4,2,48,128]{3,2,1,0:T(8,128)S(...) custom-call(s32[2,2,4]{2,1,0:T(2,128)S(1)} %get-tuple-element.29.delays, ...), custom_call_target="tpu_custom_call" | custom-call | flops 200000000 | bytes 6000000 | tf_op jit(solution)/shard_map/pallas_call | solution.py:440
  22.4 0.2 collective-permute-start.7
  22.6 1.0 %collective-permute-done.7 = f32[48,128]{1,0:T(8,128)S(1)} collective-permute-done((f32[48,128]{1,0:T(8,128)S(1)}, f32[48,128]{1,0:T(8,128)S(1)}, u32[]{:S(2)}, u32[]{:S(2)}) %collective-permute-start.7) | collective-permute-done | bytes 24608 | tf_op jit(solution)/shard_map/ppermute | solution.py:479
  23.7 0.2 collective-permute-start.9
  23.9 2.3 %collective-permute-start.8 = (f32[48,128]{1,0:T(8,128)S(1)}, f32[48,128]{1,0:T(8,128)S(1)}, u32[]{:S(2)}, u32[]{:S(2)}) collective-permute-start(f32[48,128]{1,0:T(8,128)S(1)} %add.27.own), channel_id=1, source_target_pairs={{0,5},{1,4},{4,1},{5,0},{8,13},{9,12},{12,9},{13,8},{2,7},{3,6},{6... | collective-permute-start | bytes 73736 | tf_op jit(solution)/shard_map/ppermute | solution.py:463
  26.2 0.0 collective-permute-done.10.refs_1_
  26.2 0.0 copy-done.1
  26.2 0.2 shard_map.80.cotangent
  26.3 0.0 collective-permute-done.9.odd_in
  26.4 1.3 %collective-permute-done.8.even_in = f32[48,128]{1,0:T(8,128)S(1)} collective-permute-done((f32[48,128]{1,0:T(8,128)S(1)}, f32[48,128]{1,0:T(8,128)S(1)}, u32[]{:S(2)}, u32[]{:S(2)}) %collective-permute-start.8) | collective-permute-done | bytes 24608 | tf_op jit(solution)/shard_map/ppermute | solution.py:463
  27.7 0.6 %shard_map.81 = (f32[8,2,48,128]{3,2,1,0:T(8,128)S(1)}, f32[48,128]{1,0:T(8,128)S(1)}) custom-call(s32[2,2,4]{2,1,0:T(2,128)S(1)} %get-tuple-element.29.delays, f32[2,2,4]{2,1,0:T(2,128)S(1)} %get-tuple-element.30.gains, f32[8,2,48,128]{3,2,1,0:T(8,128)S(1)} %get-tuple-element.38.linear1, f32[48,128]{1,0:T(8,128)S(1)} %add.27.own, ...), custom_call_target="tpu_custom_call" | custom-call | flops 200000000 | bytes 6000000 | tf_op jit(solution)/shard_map/pallas_call | solution.py:440
  28.3 0.2 collective-permute-start.11
  28.5 1.0 %collective-permute-done.11 = f32[48,128]{1,0:T(8,128)S(1)} collective-permute-done((f32[48,128]{1,0:T(8,128)S(1)}, f32[48,128]{1,0:T(8,128)S(1)}, u32[]{:S(2)}, u32[]{:S(2)}) %collective-permute-start.11) | collective-permute-done | bytes 24608 | tf_op jit(solution)/shard_map/ppermute | solution.py:479
  29.5 0.2 collective-permute-start.13
  29.7 1.8 %collective-permute-start.12 = (f32[48,128]{1,0:T(8,128)S(1)}, f32[48,128]{1,0:T(8,128)S(1)}, u32[]{:S(2)}, u32[]{:S(2)}) collective-permute-start(f32[48,128]{1,0:T(8,128)S(1)} %add.28.own), channel_id=1, source_target_pairs={{0,5},{1,4},{4,1},{5,0},{8,13},{9,12},{12,9},{13,8},{2,7},{3,6},{6... | collective-permute-start | bytes 73736 | tf_op jit(solution)/shard_map/ppermute | solution.py:463
  31.5 0.0 collective-permute-done.13.odd_in
  31.5 1.5 %collective-permute-done.12.even_in = f32[48,128]{1,0:T(8,128)S(1)} collective-permute-done((f32[48,128]{1,0:T(8,128)S(1)}, f32[48,128]{1,0:T(8,128)S(1)}, u32[]{:S(2)}, u32[]{:S(2)}) %collective-permute-start.12) | collective-permute-done | bytes 24608 | tf_op jit(solution)/shard_map/ppermute | solution.py:463
  33.0 1.3 %shard_map.82 = (f32[4,2,48,128]{3,2,1,0:T(8,128)S(1)}, f32[4,2,48,128]{3,2,1,0:T(8,128)S(1)}, f32[48,128]{1,0:T(8,128)S(1)}) custom-call(s32[2,2,4]{2,1,0:T(2,128)S(1)} %get-tuple-element.29.delays, s32[2,2,4]{2,1,0:T(2,128)S(1)} %get-tuple-element.28.shifts, f32[2,2,4]{2,1,0:T(2,128)S(1)} %get-tuple-element.30.gains, ...), custom_call_target="tpu_custom_call" | custom-call | flops 200000000 | bytes 6000000 | tf_op jit(solution)/shard_map/pallas_call | solution.py:440
  34.3 0.4 collective-permute-start.14
  34.7 0.9 %collective-permute-done.14 = f32[48,128]{1,0:T(8,128)S(1)} collective-permute-done((f32[48,128]{1,0:T(8,128)S(1)}, f32[48,128]{1,0:T(8,128)S(1)}, u32[]{:S(2)}, u32[]{:S(2)}) %collective-permute-start.14) | collective-permute-done | bytes 24608 | tf_op jit(solution)/shard_map/ppermute | solution.py:479
  35.6 0.3 collective-permute-start.16
  35.9 2.9 %collective-permute-start.15 = (f32[48,128]{1,0:T(8,128)S(1)}, f32[48,128]{1,0:T(8,128)S(1)}, u32[]{:S(2)}, u32[]{:S(2)}) collective-permute-start(f32[48,128]{1,0:T(8,128)S(1)} %add.29.own), channel_id=1, source_target_pairs={{0,5},{1,4},{4,1},{5,0},{8,13},{9,12},{12,9},{13,8},{2,7},{3,6},{6... | collective-permute-start | bytes 73736 | tf_op jit(solution)/shard_map/ppermute | solution.py:463
  38.8 1.1 %shard_map.83.taps1 = f32[8,128]{1,0:T(8,128)S(1)} custom-call(f32[4,2,48,128]{3,2,1,0:T(8,128)S(1)} %get-tuple-element.48.shifted, f32[4,2,48,128]{3,2,1,0:T(8,128)S(1)} %get-tuple-element.49.grad), custom_call_target="tpu_custom_call" | custom-call | flops 200000000 | bytes 6000000 | tf_op jit(solution)/shard_map/pallas_call | solution.py:440
  39.9 0.0 collective-permute-done.16.odd_in
  39.9 0.4 collective-permute-done.15.even_in
  40.4 1.0 %shard_map.84 = (f32[4,2,48,128]{3,2,1,0:T(8,128)S(1)}, f32[16,128]{1,0:T(8,128)S(1)}) custom-call(s32[2,2,4]{2,1,0:T(2,128)S(1)} %get-tuple-element.29.delays, f32[4,2,48,128]{3,2,1,0:T(8,128)S(1)} %get-tuple-element.45.turned0, f32[8,2,48,128]{3,2,1,0:T(8,128)S(1)} %get-tuple-element.34.linear0, f32[48,128]{1,0:T(8,128)S(1)} %add.29.own, ...), custom_call_target="tpu_custom_call" | custom-call | flops 200000000 | bytes 6000000 | tf_op jit(solution)/shard_map/pallas_call | solution.py:440
  41.4 0.2 collective-permute-start.17
  41.6 1.0 %collective-permute-done.17 = f32[16,128]{1,0:T(8,128)S(1)} collective-permute-done((f32[16,128]{1,0:T(8,128)S(1)}, f32[16,128]{1,0:T(8,128)S(1)}, u32[]{:S(2)}, u32[]{:S(2)}) %collective-permute-start.17) | collective-permute-done | bytes 8224 | tf_op jit(solution)/shard_map/ppermute | solution.py:479
  42.6 1.1 %collective-permute-start.20 = (f32[16,128]{1,0:T(8,128)S(1)}, f32[16,128]{1,0:T(8,128)S(1)}, u32[]{:S(2)}, u32[]{:S(2)}) collective-permute-start(f32[16,128]{1,0:T(8,128)S(1)} %add.30), channel_id=1, source_target_pairs={{0,13},{1,12},{4,9},{5,8},{8,5},{9,4},{12,1},{13,0},{2,15},{3,14},... | collective-permute-start | bytes 24584 | tf_op jit(solution)/shard_map/ppermute | solution.py:463
  43.7 1.8 %collective-permute-start.19 = (f32[16,128]{1,0:T(8,128)S(1)}, f32[16,128]{1,0:T(8,128)S(1)}, u32[]{:S(2)}, u32[]{:S(2)}) collective-permute-start(f32[16,128]{1,0:T(8,128)S(1)} %add.30), channel_id=1, source_target_pairs={{0,9},{1,8},{4,13},{5,12},{8,1},{9,0},{12,5},{13,4},{2,11},{3,10},... | collective-permute-start | bytes 24584 | tf_op jit(solution)/shard_map/ppermute | solution.py:463
  45.6 0.9 %collective-permute-start.18 = (f32[16,128]{1,0:T(8,128)S(1)}, f32[16,128]{1,0:T(8,128)S(1)}, u32[]{:S(2)}, u32[]{:S(2)}) collective-permute-start(f32[16,128]{1,0:T(8,128)S(1)} %add.30), channel_id=1, source_target_pairs={{0,5},{1,4},{4,1},{5,0},{8,13},{9,12},{12,9},{13,8},{2,7},{3,6},{6... | collective-permute-start | bytes 24584 | tf_op jit(solution)/shard_map/ppermute | solution.py:463
  46.5 1.2 %shard_map.85 = f32[4,1,2,4096]{3,2,1,0:T(2,128)} custom-call(s32[2,2,4]{2,1,0:T(2,128)S(1)} %get-tuple-element.28.shifts, f32[4,2,48,128]{3,2,1,0:T(8,128)S(1)} %get-tuple-element.50.grad0, bf16[8,256,512]{2,1,0:T(8,128)(2,1)S(1)} %get-tuple-element.32.refs_4_.high, bf16[8,256,512]{2,1,0:T(8,128)(2,1)S(1)} %get-tuple-element.33.refs_5_.low), custom_call_target="tpu_custom_call" | custom-call | flops 200000000 | bytes 6000000 | tf_op jit(solution)/shard_map/pallas_call | solution.py:440
  47.7 0.0 collective-permute-done.20
  47.7 0.0 collective-permute-done.19
  47.7 0.9 %collective-permute-done.18 = f32[16,128]{1,0:T(8,128)S(1)} collective-permute-done((f32[16,128]{1,0:T(8,128)S(1)}, f32[16,128]{1,0:T(8,128)S(1)}, u32[]{:S(2)}, u32[]{:S(2)}) %collective-permute-start.18) | collective-permute-done | bytes 8224 | tf_op jit(solution)/shard_map/ppermute | solution.py:463
  48.7 0.6 %add_add_fusion = f32[16,128]{1,0:T(8,128)} fusion(f32[16,128]{1,0:T(8,128)S(1)} %collective-permute-done.19, f32[16,128]{1,0:T(8,128)S(1)} %collective-permute-done.20, f32[16,128]{1,0:T(8,128)S(1)} %add.30, f32[16,128]{1,0:T(8,128)S(1)} %collective-permute-done.18), kind=kLoop, calls=%fused_computation.5 | loop fusion | flops 6144 | bytes 40960 | tf_op jit(solution)/shard_map/add | solution.py:515
  (5 shorter events, 0.0 us)
Async XLA Ops:
  0.6 13.6 %collective-permute-start = (f32[4,1,2,4096]{3,2,1,0:T(2,128)}, f32[4,1,2,4096]{3,2,1,0:T(2,128)S(1)}, u32[]{:S(2)}, u32[]{:S(2)}) collective-permute-start(f32[4,1,2,4096]{3,2,1,0:T(2,128)} %refs_0_.2), channel_id=1, source_target_pairs={{0,2},{1,3},{2,0},{3,1},{4,6},{5,7},{6,4},{7,5},{8,10},{9,11},{10,... | collective-permute-start | bytes 393224 | tf_op jit(solution)/shard_map/ppermute | solution.py:463
  8.2 5.0 %collective-permute-start.1 = (f32[24,128]{1,0:T(8,128)S(1)}, f32[24,128]{1,0:T(8,128)S(1)}, u32[]{:S(2)}, u32[]{:S(2)}) collective-permute-start(f32[24,128]{1,0:T(8,128)S(1)} %pad_maximum_fusion.2.refs_2_), channel_id=1, source_target_pairs={{0,2},{1,3},{2,0},{3,1},{4,6},{5,7},{6,4},{7,5},{8,10},{9,11},{10,... | collective-permute-start | bytes 36872 | tf_op jit(solution)/shard_map/ppermute | solution.py:463
  8.2 8.8 %collective-permute-start.5 = (f32[4,2,3072]{2,1,0:T(2,128)S(1)}, f32[4,2,3072]{2,1,0:T(2,128)S(1)}, u32[]{:S(2)}, u32[]{:S(2)}) collective-permute-start(f32[4,2,3072]{2,1,0:T(2,128)S(1)} %get-tuple-element.52), channel_id=1, source_target_pairs={{0,1},{1,0},{2,3},{3,2},{4,10},{5,11},{6,8},{7,9},{8,6},{9,7},{10,... | collective-permute-start | bytes 294920 | tf_op jit(solution)/shard_map/ppermute | solution.py:508
  8.2 8.8 %collective-permute-start.3 = (f32[4,2,3072]{2,1,0:T(2,128)S(1)}, f32[4,2,3072]{2,1,0:T(2,128)S(1)}, u32[]{:S(2)}, u32[]{:S(2)}) collective-permute-start(f32[4,2,3072]{2,1,0:T(2,128)S(1)} %get-tuple-element.52), channel_id=1, source_target_pairs={{0,1},{1,0},{4,8},{5,9},{8,4},{9,5},{12,13},{13,12},{2,3},{3,2},{6... | collective-permute-start | bytes 294920 | tf_op jit(solution)/shard_map/ppermute | solution.py:463
  8.7 8.3 %collective-permute-start.4 = (f32[4,2,3072]{2,1,0:T(2,128)S(1)}, f32[4,2,3072]{2,1,0:T(2,128)S(1)}, u32[]{:S(2)}, u32[]{:S(2)}) collective-permute-start(f32[4,2,3072]{2,1,0:T(2,128)S(1)} %get-tuple-element.53), channel_id=1, source_target_pairs={{0,6},{1,7},{2,4},{3,5},{4,2},{5,3},{6,0},{7,1},{8,14},{9,15},{10,... | collective-permute-start | bytes 294920 | tf_op jit(solution)/shard_map/ppermute | solution.py:508
  13.2 4.6 %collective-permute-start.2 = (f32[4,2,3072]{2,1,0:T(2,128)S(1)}, f32[4,2,3072]{2,1,0:T(2,128)S(1)}, u32[]{:S(2)}, u32[]{:S(2)}) collective-permute-start(f32[4,2,3072]{2,1,0:T(2,128)S(1)} %get-tuple-element.53), channel_id=1, source_target_pairs={{0,4},{1,5},{4,0},{5,1},{8,12},{9,13},{12,8},{13,9},{2,6},{3,7},{6... | collective-permute-start | bytes 294920 | tf_op jit(solution)/shard_map/ppermute | solution.py:463
  14.3 11.9 %collective-permute-start.10 = (f32[4,1,2,4096]{3,2,1,0:T(2,128)}, f32[4,1,2,4096]{3,2,1,0:T(2,128)S(1)}, u32[]{:S(2)}, u32[]{:S(2)}) collective-permute-start(f32[4,1,2,4096]{3,2,1,0:T(2,128)} %refs_0_.3), channel_id=1, source_target_pairs={{0,2},{1,3},{2,0},{3,1},{4,6},{5,7},{6,4},{7,5},{8,10},{9,11},{10,... | collective-permute-start | bytes 393224 | tf_op jit(solution)/shard_map/ppermute | solution.py:463
  14.8 0.9 %copy-start = (f32[4,1,2,4096]{3,2,1,0:T(2,128)S(1)}, f32[4,1,2,4096]{3,2,1,0:T(2,128)}, u32[]{:S(2)}) copy-start(f32[4,1,2,4096]{3,2,1,0:T(2,128)} %refs_0_.2) | copy-start | bytes 393220
  19.5 1.3 %collective-permute-start.6 = (f32[64,128]{1,0:T(8,128)S(1)}, f32[64,128]{1,0:T(8,128)S(1)}, u32[]{:S(2)}, u32[]{:S(2)}) collective-permute-start(f32[64,128]{1,0:T(8,128)S(1)} %get-tuple-element.35), channel_id=1, source_target_pairs={{0,1},{1,0},{2,3},{3,2},{4,5},{5,4},{6,7},{7,6},{8,9},{9,8},{10,11... | collective-permute-start | bytes 98312 | tf_op jit(solution)/shard_map/ppermute | solution.py:479
  20.8 5.4 %copy-start.1 = (f32[4,1,2,4096]{3,2,1,0:T(2,128)S(1)}, f32[4,1,2,4096]{3,2,1,0:T(2,128)}, u32[]{:S(2)}) copy-start(f32[4,1,2,4096]{3,2,1,0:T(2,128)} %refs_0_.3) | copy-start | bytes 393220
  22.4 1.3 %collective-permute-start.7 = (f32[48,128]{1,0:T(8,128)S(1)}, f32[48,128]{1,0:T(8,128)S(1)}, u32[]{:S(2)}, u32[]{:S(2)}) collective-permute-start(f32[48,128]{1,0:T(8,128)S(1)} %get-tuple-element.39), channel_id=1, source_target_pairs={{0,1},{1,0},{2,3},{3,2},{4,5},{5,4},{6,7},{7,6},{8,9},{9,8},{10,11... | collective-permute-start | bytes 73736 | tf_op jit(solution)/shard_map/ppermute | solution.py:479
  23.7 2.6 %collective-permute-start.9 = (f32[48,128]{1,0:T(8,128)S(1)}, f32[48,128]{1,0:T(8,128)S(1)}, u32[]{:S(2)}, u32[]{:S(2)}) collective-permute-start(f32[48,128]{1,0:T(8,128)S(1)} %add.27.own), channel_id=1, source_target_pairs={{0,1},{1,0},{4,9},{5,8},{8,5},{9,4},{12,13},{13,12},{2,3},{3,2},{6... | collective-permute-start | bytes 73736 | tf_op jit(solution)/shard_map/ppermute | solution.py:463
  23.9 3.8 %collective-permute-start.8 = (f32[48,128]{1,0:T(8,128)S(1)}, f32[48,128]{1,0:T(8,128)S(1)}, u32[]{:S(2)}, u32[]{:S(2)}) collective-permute-start(f32[48,128]{1,0:T(8,128)S(1)} %add.27.own), channel_id=1, source_target_pairs={{0,5},{1,4},{4,1},{5,0},{8,13},{9,12},{12,9},{13,8},{2,7},{3,6},{6... | collective-permute-start | bytes 73736 | tf_op jit(solution)/shard_map/ppermute | solution.py:463
  28.3 1.3 %collective-permute-start.11 = (f32[48,128]{1,0:T(8,128)S(1)}, f32[48,128]{1,0:T(8,128)S(1)}, u32[]{:S(2)}, u32[]{:S(2)}) collective-permute-start(f32[48,128]{1,0:T(8,128)S(1)} %get-tuple-element.41), channel_id=1, source_target_pairs={{0,1},{1,0},{2,3},{3,2},{4,5},{5,4},{6,7},{7,6},{8,9},{9,8},{10,11... | collective-permute-start | bytes 73736 | tf_op jit(solution)/shard_map/ppermute | solution.py:479
  29.5 2.0 %collective-permute-start.13 = (f32[48,128]{1,0:T(8,128)S(1)}, f32[48,128]{1,0:T(8,128)S(1)}, u32[]{:S(2)}, u32[]{:S(2)}) collective-permute-start(f32[48,128]{1,0:T(8,128)S(1)} %add.28.own), channel_id=1, source_target_pairs={{0,1},{1,0},{4,9},{5,8},{8,5},{9,4},{12,13},{13,12},{2,3},{3,2},{6... | collective-permute-start | bytes 73736 | tf_op jit(solution)/shard_map/ppermute | solution.py:463
  29.7 3.3 %collective-permute-start.12 = (f32[48,128]{1,0:T(8,128)S(1)}, f32[48,128]{1,0:T(8,128)S(1)}, u32[]{:S(2)}, u32[]{:S(2)}) collective-permute-start(f32[48,128]{1,0:T(8,128)S(1)} %add.28.own), channel_id=1, source_target_pairs={{0,5},{1,4},{4,1},{5,0},{8,13},{9,12},{12,9},{13,8},{2,7},{3,6},{6... | collective-permute-start | bytes 73736 | tf_op jit(solution)/shard_map/ppermute | solution.py:463
  34.3 1.3 %collective-permute-start.14 = (f32[48,128]{1,0:T(8,128)S(1)}, f32[48,128]{1,0:T(8,128)S(1)}, u32[]{:S(2)}, u32[]{:S(2)}) collective-permute-start(f32[48,128]{1,0:T(8,128)S(1)} %get-tuple-element.46), channel_id=1, source_target_pairs={{0,1},{1,0},{2,3},{3,2},{4,5},{5,4},{6,7},{7,6},{8,9},{9,8},{10,11... | collective-permute-start | bytes 73736 | tf_op jit(solution)/shard_map/ppermute | solution.py:479
  35.6 4.3 %collective-permute-start.16 = (f32[48,128]{1,0:T(8,128)S(1)}, f32[48,128]{1,0:T(8,128)S(1)}, u32[]{:S(2)}, u32[]{:S(2)}) collective-permute-start(f32[48,128]{1,0:T(8,128)S(1)} %add.29.own), channel_id=1, source_target_pairs={{0,1},{1,0},{4,9},{5,8},{8,5},{9,4},{12,13},{13,12},{2,3},{3,2},{6... | collective-permute-start | bytes 73736 | tf_op jit(solution)/shard_map/ppermute | solution.py:463
  35.9 4.5 %collective-permute-start.15 = (f32[48,128]{1,0:T(8,128)S(1)}, f32[48,128]{1,0:T(8,128)S(1)}, u32[]{:S(2)}, u32[]{:S(2)}) collective-permute-start(f32[48,128]{1,0:T(8,128)S(1)} %add.29.own), channel_id=1, source_target_pairs={{0,5},{1,4},{4,1},{5,0},{8,13},{9,12},{12,9},{13,8},{2,7},{3,6},{6... | collective-permute-start | bytes 73736 | tf_op jit(solution)/shard_map/ppermute | solution.py:463
  41.4 1.2 %collective-permute-start.17 = (f32[16,128]{1,0:T(8,128)S(1)}, f32[16,128]{1,0:T(8,128)S(1)}, u32[]{:S(2)}, u32[]{:S(2)}) collective-permute-start(f32[16,128]{1,0:T(8,128)S(1)} %get-tuple-element.51), channel_id=1, source_target_pairs={{0,1},{1,0},{2,3},{3,2},{4,5},{5,4},{6,7},{7,6},{8,9},{9,8},{10,11... | collective-permute-start | bytes 24584 | tf_op jit(solution)/shard_map/ppermute | solution.py:479
  42.6 5.1 %collective-permute-start.20 = (f32[16,128]{1,0:T(8,128)S(1)}, f32[16,128]{1,0:T(8,128)S(1)}, u32[]{:S(2)}, u32[]{:S(2)}) collective-permute-start(f32[16,128]{1,0:T(8,128)S(1)} %add.30), channel_id=1, source_target_pairs={{0,13},{1,12},{4,9},{5,8},{8,5},{9,4},{12,1},{13,0},{2,15},{3,14},... | collective-permute-start | bytes 24584 | tf_op jit(solution)/shard_map/ppermute | solution.py:463
  43.7 4.0 %collective-permute-start.19 = (f32[16,128]{1,0:T(8,128)S(1)}, f32[16,128]{1,0:T(8,128)S(1)}, u32[]{:S(2)}, u32[]{:S(2)}) collective-permute-start(f32[16,128]{1,0:T(8,128)S(1)} %add.30), channel_id=1, source_target_pairs={{0,9},{1,8},{4,13},{5,12},{8,1},{9,0},{12,5},{13,4},{2,11},{3,10},... | collective-permute-start | bytes 24584 | tf_op jit(solution)/shard_map/ppermute | solution.py:463
  45.6 3.1 %collective-permute-start.18 = (f32[16,128]{1,0:T(8,128)S(1)}, f32[16,128]{1,0:T(8,128)S(1)}, u32[]{:S(2)}, u32[]{:S(2)}) collective-permute-start(f32[16,128]{1,0:T(8,128)S(1)} %add.30), channel_id=1, source_target_pairs={{0,5},{1,4},{4,1},{5,0},{8,13},{9,12},{12,9},{13,8},{2,7},{3,6},{6... | collective-permute-start | bytes 24584 | tf_op jit(solution)/shard_map/ppermute | solution.py:463

commit v4 on v3

--- a/solution.py
+++ b/solution.py
@@ -109,14 +109,6 @@
             out[b, c, below : below + 1, :] = after[c : c + 1]
 
 
-def lay_rows(source, target, b, first, rows):
-    own = source.shape[0]
-    for r in range(rows):
-        pair = source[b % own, 0, :, r * LANES : (r + 1) * LANES]
-        for c in range(2):
-            target[b, c, first + r : first + r + 1, :] = pair[c : c + 1]
-
-
 def fir(real, imag, high, low):
     rows = real.shape[0]
     x = jnp.concatenate(
@@ -209,26 +201,68 @@
     return jnp.where(lanes_of((count, LANES)) + s < LANES, near, far)
 
 
-def k_setup(groups, steps, *refs):
-    signals, packs = refs[:groups], refs[groups : 2 * groups]
-    sig_rows, delays, shifts, gains = refs[2 * groups : 2 * groups + 4]
-    tables = refs[2 * groups + 4 :]
-    rows = sig_rows.shape[2]
+def k_begin(
+    signal, cotangent, taps, delays, shifts, gains, even_out, odd_out, sent, cot_rows,
+    sig_held, cot_held, taps_held, delays_held, shifts_held, gains_held, done,
+):
+    steps, bands = taps.shape[:2]
+    rows = cot_rows.shape[2]
+    pairs = (
+        (signal, sig_held), (cotangent, cot_held), (taps, taps_held),
+        (delays, delays_held), (shifts, shifts_held), (gains, gains_held),
+    )
+    copies = [pltpu.make_async_copy(a, b, done.at[n]) for n, (a, b) in enumerate(pairs)]
+    for copy in copies:
+        copy.start()
+    for copy in copies:
+        copy.wait()
+    even = is_even()
+    length, wide, edge = rows * LANES, WIDE * LANES, EDGE * LANES
+    for b in range(bands):
+        for held, first, width in ((sig_held, 0, wide), (cot_held, wide, edge)):
+            left = held[b, 0, :, 0:width]
+            right = held[b, 0, :, length - width : length]
+            even_out[b, :, first : first + width] = jnp.where(even, right, left)
+            odd_out[b, :, first : first + width] = jnp.where(even, left, right)
+        for r in range(rows):
+            lanes = slice(r * LANES, (r + 1) * LANES)
+            pair = sig_held[b, 0, :, lanes]
+            other = cot_held[b, 0, :, lanes]
+            for c in range(2):
+                row = (2 * b + c) * rows + r
+                sent[row : row + 1, :] = pair[c : c + 1]
+                cot_rows[b, c, r : r + 1, :] = other[c : c + 1]
+    first = 2 * bands * rows
+    for step in range(steps):
+        for b in range(bands):
+            row = first + 2 * (step * bands + b)
+            sent[row : row + 2, :] = taps_held[step, b]
+    first = first + 2 * steps * bands
+    sent[first:, :] = jnp.zeros((sent.shape[0] - first, LANES), F32)
+    for k, held in enumerate((delays_held, shifts_held, gains_held)):
+        row = first + k * steps
+        sent[row : row + steps, 0:bands] = held[...].astype(F32)
+
+
+def k_setup(groups, steps, rows, *refs):
+    packs = refs[:groups]
+    delays, shifts, gains = refs[groups : groups + 3]
+    tables = refs[groups + 3 :]
     own = delays.shape[2]
     shape = (LANES, LANES)
     diagonal = lanes_of(shape) >= lax.broadcasted_iota(jnp.int32, shape, 0)
-    first = 2 * steps * own
+    base = 2 * own * rows
+    first = base + 2 * steps * own
     for k, pack in enumerate(packs):
         for n, target in enumerate((delays, shifts, gains)):
             row = first + n * steps
             target[k] = pack[row : row + steps, 0:own].astype(target.dtype)
     for b in range(groups * own):
-        lay_rows(signals[b // own], sig_rows, b, 0, rows)
         pack = packs[b // own]
         for step in range(steps):
             high, low = tables[2 * step : 2 * step + 2]
             for c in range(2):
-                tap = 2 * (step * own + b % own) + c
+                tap = base + 2 * (step * own + b % own) + c
                 row = jnp.broadcast_to(pack[tap : tap + 1, :], shape)
                 ring = pltpu.roll(row, 0, 1, stride=1, stride_axis=0)
                 near = jnp.where(diagonal, ring, 0.0)
@@ -251,13 +285,15 @@
     for b in range(out.shape[0]):
         k = b // own
         extend(out, b, refs[groups + 2 * k], refs[groups + 2 * k + 1], WIDE, EDGE)
-        lay_rows(refs[k], out, b, PAD, rows)
-
-
-def k_first(groups, delays, shifts, sig_rows, *refs):
-    sides = refs[: 2 * groups]
-    high, low, shifted, linear, out, ext, held = refs[2 * groups :]
-    bands, _, rows, _ = sig_rows.shape
+        for c in range(2):
+            out[b, c, PAD : PAD + rows, :] = refs[k][b % own, c]
+
+
+def k_first(groups, delays, shifts, *refs):
+    packs, sides = refs[:groups], refs[groups : 3 * groups]
+    high, low, shifted, linear, out, ext, held = refs[3 * groups :]
+    bands = linear.shape[0]
+    rows = linear.shape[2] - 2 * PAD
     own = shifted.shape[0]
     middle = slice(WIDE_PAD - PAD, WIDE_PAD + rows + PAD)
     powers = []
@@ -265,7 +301,8 @@
         k = b // own
         extend(ext, b, sides[2 * k], sides[2 * k + 1], 0, WIDE)
         for c in range(2):
-            ext[b, c, WIDE_PAD : WIDE_PAD + rows, :] = sig_rows[b, c]
+            row = (2 * (b % own) + c) * rows
+            ext[b, c, WIDE_PAD : WIDE_PAD + rows, :] = packs[k][row : row + rows, :]
         amount = LANES // 2 - at(shifts, 0, b)
         real = later(ext[b, 0], amount)
         imag = later(ext[b, 1], amount)
@@ -525,14 +562,6 @@
     return (part,) + neighbours(part, part, True)
 
 
-def edges(signal, cotangent):
-    wide, edge = WIDE * LANES, EDGE * LANES
-    left = jnp.concatenate([signal[..., :wide], cotangent[..., :edge]], -1)
-    right = jnp.concatenate([signal[..., -wide:], cotangent[..., -edge:]], -1)
-    even = is_even()
-    return jnp.where(even, right, left), jnp.where(even, left, right)
-
-
 def on_device(signal, cotangent, taps, gains, walk_off, tap_shift):
     own, _, _, length = signal.shape
     steps = taps.shape[0]
@@ -557,29 +586,36 @@
     held_in = (bands, rows + REACH + 3 * PAD, LANES)
     held_out = (bands, rows + 3 * REACH, LANES)
 
-    signals, cotangents = [signal], [cotangent]
-    small = jnp.concatenate([walk_off.astype(F32), tap_shift.astype(F32), gains])
-    small = jnp.pad(small, ((0, -3 * steps % 8), (0, LANES - own)))
-    small = jnp.concatenate([taps.reshape(2 * steps * own, LANES), small])
-    even_out, odd_out = edges(signal[:, 0], cotangent[:, 0])
-    small, _ = lax.optimization_barrier((small, even_out))
-    packs = [small]
+    inputs = (signal, cotangent, taps, walk_off, tap_shift, gains)
+    hbm, vmem = (pl.BlockSpec(memory_space=m) for m in (pltpu.HBM, pltpu.VMEM))
+    cut = shape(own, 2, (WIDE + EDGE) * LANES)
+    pack_rows = 2 * own * rows + 2 * steps * own + 3 * steps
+    pack = shape(pack_rows + -pack_rows % 8, LANES)
+    even_out, odd_out, pack_out, cot_out = pl.pallas_call(
+        k_begin,
+        out_shape=[cut, cut, pack, shape(own, 2, rows, LANES)],
+        in_specs=[hbm] * len(inputs),
+        out_specs=[vmem] * 4,
+        scratch_shapes=[pltpu.VMEM(a.shape, a.dtype) for a in inputs]
+        + [pltpu.SemaphoreType.DMA((len(inputs),))],
+        compiler_params=pltpu.CompilerParams(vmem_limit_bytes=24 * 1024 * 1024),
+        cost_estimate=pl.CostEstimate(flops=10**9, bytes_accessed=0, transcendentals=0),
+    )(*(pltpu.with_memory_space_constraint(a, pltpu.HBM) for a in inputs))
+    packs, cots = [pack_out], [cot_out]
+    if doubled:
+        packs.append(swapped(pack_out, "band", evenly, False))
     sides = list(neighbours(even_out, odd_out, False))
     if doubled:
-        signals.append(swapped(signal, "band", evenly, False))
-        packs.append(swapped(packs[0], "band", evenly, False))
         sides += [aslant(even_out, evenly), aslant(odd_out, oddly)]
-        cotangents.append(swapped(cotangent, "band", evenly, False))
+        cots.append(swapped(cot_out, "band", evenly, False))
     tiny = [shape(groups, steps, own, dtype=d) for d in (jnp.int32, jnp.int32, F32)]
-    sig_rows, delays, shifts, gains, high0, low0, high1, low1 = call(
-        functools.partial(k_setup, groups, steps), (*signals, *packs),
-        [shape(bands, 2, rows, LANES)] + tiny + [table] * (2 * steps),
-    )
-    (cot_rows,) = call(
-        functools.partial(k_cotangent, groups), (*cotangents, *sides), [field]
-    )
+    delays, shifts, gains, high0, low0, high1, low1 = call(
+        functools.partial(k_setup, groups, steps, rows), tuple(packs),
+        tiny + [table] * (2 * steps),
+    )
+    (cot_rows,) = call(functools.partial(k_cotangent, groups), (*cots, *sides), [field])
     shifted0, linear0, sent = call(
-        functools.partial(k_first, groups), (delays, shifts, sig_rows, *sides, high0, low0),
+        functools.partial(k_first, groups), (delays, shifts, *packs, *sides, high0, low0),
         [own_field, field, wide_part], (ext_wide, held_wide),
     )
     cosine0, sine0, field1, shifted1, linear1, sent = call(

time: 49.6 us -> 48.2 us (0.972)
  other arithmetic: 3.47 us -> 0.63 us
  local copies, waits for them, and re-layouts: 2.62 us -> 0 us
  waiting for transfers between devices: 10.2 us -> 12.6 us
  Pallas kernels: 9.97 us -> 10.9 us
  starting transfers between devices: 22.3 us -> 23.2 us
    ppermute x14 -> x13, starting transfers between devices: 16.6 us -> 20.5 us  [swapped(): return lax.ppermute(x, (axis, 'pol'), pairs)]
    ppermute x2, starting transfers between devices: 4.5 us -> 1.55 us  [aslant(): return lax.ppermute(x, ('tm', 'band', 'pol'), pairs)]
    ppermute x14 -> x13, waiting for transfers between devices: 5.05 us -> 7.44 us  [swapped(): return lax.ppermute(x, (axis, 'pol'), pairs)]
    slice x2 -> x0, local copies, waits for them, and re-layouts: 1.71 us -> none  [edges(): right = jnp.concatenate([signal[..., -wide:], cotangent[..., -edge:]], -1)]
    concatenate x2 -> x0, other arithmetic: 1.39 us -> none  [the longest x1 0.7 us: on_device(): small = jnp.concatenate([taps.reshape(2 * steps * own, LANES), small])]
    convert_element_type x2 -> x0, other arithmetic: 1.36 us -> none  [the longest x1 0.68 us: on_device(): walk_off.astype(F32)]
    pallas_call x0 -> x1, Pallas kernels: none -> 1.18 us  [on_device(): pl.pallas_call(k_begin, out_shape=[cut, cut, pack, shape(own, 2, rows, LA...]
    unnamed x4 -> x0, local copies, waits for them, and re-layouts: 0.91 us -> none
  transfers between devices with their start and end apart: 21 -> 20, of which waited for: 10 -> 10; matrix products, arithmetic and copies ran while one was open for 9% -> 0% of each run, Pallas kernels for 14% -> 14%
where the time goes in v4:
time: 48.2 us; the launch traced here: 48.1 us
  starting transfers between devices  23.2 us (48%)
  waiting for transfers between devices  12.6 us (26%)
  Pallas kernels  10.9 us (23%)
  between operations  0.75 us (2%)
  other arithmetic  0.63 us (1%)
    ppermute x13, starting transfers between devices, swapped(): return lax.ppermute(x, (axis, 'pol'), pairs)  20.5 us
    pallas_call x9, Pallas kernels, call(): pl.pallas_call(kernel, out_shape=shapes, in_specs=[vmem] * len(arrays), o...  9.72 us
    ppermute x13, waiting for transfers between devices, swapped(): return lax.ppermute(x, (axis, 'pol'), pairs)  7.44 us
    ppermute x5, waiting for transfers between devices, over_cores(): lax.ppermute(x, 'pol', [(p, cores - 1 - p) for p in range(cores)])  5.14 us
    ppermute x2, starting transfers between devices, aslant(): return lax.ppermute(x, ('tm', 'band', 'pol'), pairs)  1.55 us
    pallas_call x1, Pallas kernels, on_device(): pl.pallas_call(k_begin, out_shape=[cut, cut, pack, shape(own, 2, rows, LA...  1.18 us
    ppermute x5, starting transfers between devices, over_cores(): lax.ppermute(x, 'pol', [(p, cores - 1 - p) for p in range(cores)])  1.13 us
  transfers between devices with their start and end apart: 20, of which 10 were waited for; matrix products, arithmetic and copies ran while one was open for 0% of the time, Pallas kernels for 14%

profile of v4, /device:TPU:0, one launch (start us, length us, event | category | flops | bytes accessed | tf_op | source)
XLA Modules:
  0.0 48.1 jit_solution(6296812462025424528)
XLA Ops:
  0.6 1.2 %shard_map.77 = (f32[4,2,3072]{2,1,0:T(2,128)S(1)}, f32[4,2,3072]{2,1,0:T(2,128)S(1)}, f32[280,128]{1,0:T(8,128)S(1)}, f32[4,2,32,128]{3,2,1,0:T(8,128)S(1)}) custom-call(f32[4,1,2,4096]{3,2,1,0:T(2,128)} %signal.1, f32[4,1,2,4096]{3,2,1,0:T(2,128)} %cotangent.1, f32[2,4,2,128]{3,2,1,0:T(2,128)} %taps.1, s32[2,4]{1,0:T(2,128)} %delays.1, s32[2,4]{1,0:T(2,128)} %shifts.1, ...), custom_call_target="tpu_custom_call" | custom-call | flops 1000000000 | tf_op jit(solution)/shard_map/pallas_call | solution.py:594
  1.8 3.0 %collective-permute-start = (f32[280,128]{1,0:T(8,128)S(1)}, f32[280,128]{1,0:T(8,128)S(1)}, u32[]{:S(2)}, u32[]{:S(2)}) collective-permute-start(f32[280,128]{1,0:T(8,128)S(1)} %get-tuple-element.29.refs_0_), channel_id=1, source_target_pairs={{0,2},{1,3},{2,0},{3,1},{4,6},{5,7},{6,4},{7,5},{8,10},{9,11},{10,... | collective-permute-start | bytes 430088 | tf_op jit(solution)/shard_map/ppermute | solution.py:500
  4.8 1.5 %collective-permute-start.3 = (f32[4,2,3072]{2,1,0:T(2,128)S(1)}, f32[4,2,3072]{2,1,0:T(2,128)S(1)}, u32[]{:S(2)}, u32[]{:S(2)}) collective-permute-start(f32[4,2,3072]{2,1,0:T(2,128)S(1)} %get-tuple-element.33), channel_id=1, source_target_pairs={{0,6},{1,7},{2,4},{3,5},{4,2},{5,3},{6,0},{7,1},{8,14},{9,15},{10,... | collective-permute-start | bytes 294920 | tf_op jit(solution)/shard_map/ppermute | solution.py:545
  6.4 0.0 collective-permute-start.1
  6.4 0.0 collective-permute-start.4
  6.4 0.5 %collective-permute-start.2 = (f32[4,2,3072]{2,1,0:T(2,128)S(1)}, f32[4,2,3072]{2,1,0:T(2,128)S(1)}, u32[]{:S(2)}, u32[]{:S(2)}) collective-permute-start(f32[4,2,3072]{2,1,0:T(2,128)S(1)} %get-tuple-element.34), channel_id=1, source_target_pairs={{0,1},{1,0},{4,8},{5,9},{8,4},{9,5},{12,13},{13,12},{2,3},{3,2},{6... | collective-permute-start | bytes 294920 | tf_op jit(solution)/shard_map/ppermute | solution.py:500
  6.9 3.1 %collective-permute-done.refs_1_ = f32[280,128]{1,0:T(8,128)S(1)} collective-permute-done((f32[280,128]{1,0:T(8,128)S(1)}, f32[280,128]{1,0:T(8,128)S(1)}, u32[]{:S(2)}, u32[]{:S(2)}) %collective-permute-start) | collective-permute-done | bytes 143392 | tf_op jit(solution)/shard_map/ppermute | solution.py:500
  10.0 2.4 %collective-permute-start.9 = (f32[4,2,32,128]{3,2,1,0:T(8,128)S(1)}, f32[4,2,32,128]{3,2,1,0:T(8,128)S(1)}, u32[]{:S(2)}, u32[]{:S(2)}) collective-permute-start(f32[4,2,32,128]{3,2,1,0:T(8,128)S(1)} %get-tuple-element.43.refs_0_), channel_id=1, source_target_pairs={{0,2},{1,3},{2,0},{3,1},{4,6},{5,7},{6,4},{7,5},{8,10},{9,11},{10,... | collective-permute-start | bytes 393224 | tf_op jit(solution)/shard_map/ppermute | solution.py:500
  12.4 1.2 %shard_map.78 = (s32[2,2,4]{2,1,0:T(2,128)S(1)}, s32[2,2,4]{2,1,0:T(2,128)S(1)}, f32[2,2,4]{2,1,0:T(2,128)S(1)}, bf16[8,256,512]{2,1,0:T(8,128)(2,1)S(1)}, bf16[...) custom-call(f32[280,128]{1,0:T(8,128)S(1)} %get-tuple-element.29.refs_0_, ...), custom_call_target="tpu_custom_call" | custom-call | flops 200000000 | bytes 6000000 | tf_op jit(solution)/shard_map/pallas_call | solution.py:477
  13.6 0.0 collective-permute-done.3.refs_4_
  13.6 0.0 collective-permute-done.1.refs_2_
  13.6 0.0 collective-permute-done.4.refs_5_
  13.6 0.0 collective-permute-done.2.refs_3_
  13.6 1.6 %shard_map.79 = (f32[4,2,48,128]{3,2,1,0:T(8,128)S(1)}, f32[8,2,48,128]{3,2,1,0:T(8,128)S(1)}, f32[64,128]{1,0:T(8,128)S(1)}) custom-call(s32[2,2,4]{2,1,0:T(2,128)S(1)} %get-tuple-element.31.delays, s32[2,2,4]{2,1,0:T(2,128)S(1)} %get-tuple-element.30.shifts, f32[280,128]{1,0:T(8,128)S(1)} %get-tuple-element.29.refs_0_, ...), custom_call_target="tpu_custom_call" | custom-call | flops 200000000 | bytes 6000000 | tf_op jit(solution)/shard_map/pallas_call | solution.py:477
  15.3 0.1 collective-permute-start.5
  15.3 1.2 %collective-permute-done.5 = f32[64,128]{1,0:T(8,128)S(1)} collective-permute-done((f32[64,128]{1,0:T(8,128)S(1)}, f32[64,128]{1,0:T(8,128)S(1)}, u32[]{:S(2)}, u32[]{:S(2)}) %collective-permute-start.5) | collective-permute-done | bytes 32800 | tf_op jit(solution)/shard_map/ppermute | solution.py:516
  16.5 1.7 %shard_map.80 = (f32[4,48,128]{2,1,0:T(8,128)S(1)}, f32[4,48,128]{2,1,0:T(8,128)S(1)}, f32[8,2,48,128]{3,2,1,0:T(8,128)S(1)}, f32[4,2,48,128]{3,2,1,0:T(8,128)S(...) custom-call(s32[2,2,4]{2,1,0:T(2,128)S(1)} %get-tuple-element.31.delays, ...), custom_call_target="tpu_custom_call" | custom-call | flops 200000000 | bytes 6000000 | tf_op jit(solution)/shard_map/pallas_call | solution.py:477
  18.2 0.2 collective-permute-start.6
  18.4 1.0 %collective-permute-done.6 = f32[48,128]{1,0:T(8,128)S(1)} collective-permute-done((f32[48,128]{1,0:T(8,128)S(1)}, f32[48,128]{1,0:T(8,128)S(1)}, u32[]{:S(2)}, u32[]{:S(2)}) %collective-permute-start.6) | collective-permute-done | bytes 24608 | tf_op jit(solution)/shard_map/ppermute | solution.py:516
  19.5 0.2 collective-permute-start.8
  19.6 5.3 %collective-permute-start.7 = (f32[48,128]{1,0:T(8,128)S(1)}, f32[48,128]{1,0:T(8,128)S(1)}, u32[]{:S(2)}, u32[]{:S(2)}) collective-permute-start(f32[48,128]{1,0:T(8,128)S(1)} %add.25.own), channel_id=1, source_target_pairs={{0,5},{1,4},{4,1},{5,0},{8,13},{9,12},{12,9},{13,8},{2,7},{3,6},{6... | collective-permute-start | bytes 73736 | tf_op jit(solution)/shard_map/ppermute | solution.py:500
  24.9 0.0 collective-permute-done.9.refs_1_
  24.9 0.1 shard_map.81.cotangent
  25.0 0.0 collective-permute-done.8.odd_in
  25.0 1.4 %collective-permute-done.7.even_in = f32[48,128]{1,0:T(8,128)S(1)} collective-permute-done((f32[48,128]{1,0:T(8,128)S(1)}, f32[48,128]{1,0:T(8,128)S(1)}, u32[]{:S(2)}, u32[]{:S(2)}) %collective-permute-start.7) | collective-permute-done | bytes 24608 | tf_op jit(solution)/shard_map/ppermute | solution.py:500
  26.5 0.6 %shard_map.82 = (f32[8,2,48,128]{3,2,1,0:T(8,128)S(1)}, f32[48,128]{1,0:T(8,128)S(1)}) custom-call(s32[2,2,4]{2,1,0:T(2,128)S(1)} %get-tuple-element.31.delays, f32[2,2,4]{2,1,0:T(2,128)S(1)} %get-tuple-element.32.gains, f32[8,2,48,128]{3,2,1,0:T(8,128)S(1)} %get-tuple-element.41.linear1, f32[48,128]{1,0:T(8,128)S(1)} %add.25.own, ...), custom_call_target="tpu_custom_call" | custom-call | flops 200000000 | bytes 6000000 | tf_op jit(solution)/shard_map/pallas_call | solution.py:477
  27.0 0.2 collective-permute-start.10
  27.3 1.0 %collective-permute-done.10 = f32[48,128]{1,0:T(8,128)S(1)} collective-permute-done((f32[48,128]{1,0:T(8,128)S(1)}, f32[48,128]{1,0:T(8,128)S(1)}, u32[]{:S(2)}, u32[]{:S(2)}) %collective-permute-start.10) | collective-permute-done | bytes 24608 | tf_op jit(solution)/shard_map/ppermute | solution.py:516
  28.3 0.2 collective-permute-start.12
  28.5 1.7 %collective-permute-start.11 = (f32[48,128]{1,0:T(8,128)S(1)}, f32[48,128]{1,0:T(8,128)S(1)}, u32[]{:S(2)}, u32[]{:S(2)}) collective-permute-start(f32[48,128]{1,0:T(8,128)S(1)} %add.26.own), channel_id=1, source_target_pairs={{0,5},{1,4},{4,1},{5,0},{8,13},{9,12},{12,9},{13,8},{2,7},{3,6},{6... | collective-permute-start | bytes 73736 | tf_op jit(solution)/shard_map/ppermute | solution.py:500
  30.2 0.0 collective-permute-done.12.odd_in
  30.2 1.5 %collective-permute-done.11.even_in = f32[48,128]{1,0:T(8,128)S(1)} collective-permute-done((f32[48,128]{1,0:T(8,128)S(1)}, f32[48,128]{1,0:T(8,128)S(1)}, u32[]{:S(2)}, u32[]{:S(2)}) %collective-permute-start.11) | collective-permute-done | bytes 24608 | tf_op jit(solution)/shard_map/ppermute | solution.py:500
  31.7 1.3 %shard_map.83 = (f32[4,2,48,128]{3,2,1,0:T(8,128)S(1)}, f32[4,2,48,128]{3,2,1,0:T(8,128)S(1)}, f32[48,128]{1,0:T(8,128)S(1)}) custom-call(s32[2,2,4]{2,1,0:T(2,128)S(1)} %get-tuple-element.31.delays, s32[2,2,4]{2,1,0:T(2,128)S(1)} %get-tuple-element.30.shifts, f32[2,2,4]{2,1,0:T(2,128)S(1)} %get-tuple-element.32.gains, ...), custom_call_target="tpu_custom_call" | custom-call | flops 200000000 | bytes 6000000 | tf_op jit(solution)/shard_map/pallas_call | solution.py:477
  33.1 0.4 collective-permute-start.13
  33.5 0.9 %collective-permute-done.13 = f32[48,128]{1,0:T(8,128)S(1)} collective-permute-done((f32[48,128]{1,0:T(8,128)S(1)}, f32[48,128]{1,0:T(8,128)S(1)}, u32[]{:S(2)}, u32[]{:S(2)}) %collective-permute-start.13) | collective-permute-done | bytes 24608 | tf_op jit(solution)/shard_map/ppermute | solution.py:516
  34.3 0.3 collective-permute-start.15
  34.7 3.0 %collective-permute-start.14 = (f32[48,128]{1,0:T(8,128)S(1)}, f32[48,128]{1,0:T(8,128)S(1)}, u32[]{:S(2)}, u32[]{:S(2)}) collective-permute-start(f32[48,128]{1,0:T(8,128)S(1)} %add.27.own), channel_id=1, source_target_pairs={{0,5},{1,4},{4,1},{5,0},{8,13},{9,12},{12,9},{13,8},{2,7},{3,6},{6... | collective-permute-start | bytes 73736 | tf_op jit(solution)/shard_map/ppermute | solution.py:500
  37.6 1.1 %shard_map.84.taps1 = f32[8,128]{1,0:T(8,128)S(1)} custom-call(f32[4,2,48,128]{3,2,1,0:T(8,128)S(1)} %get-tuple-element.52.shifted, f32[4,2,48,128]{3,2,1,0:T(8,128)S(1)} %get-tuple-element.53.grad), custom_call_target="tpu_custom_call" | custom-call | flops 200000000 | bytes 6000000 | tf_op jit(solution)/shard_map/pallas_call | solution.py:477
  38.7 0.0 collective-permute-done.15.odd_in
  38.7 0.4 collective-permute-done.14.even_in
  39.2 1.0 %shard_map.85 = (f32[4,2,48,128]{3,2,1,0:T(8,128)S(1)}, f32[16,128]{1,0:T(8,128)S(1)}) custom-call(s32[2,2,4]{2,1,0:T(2,128)S(1)} %get-tuple-element.31.delays, f32[4,2,48,128]{3,2,1,0:T(8,128)S(1)} %get-tuple-element.49.turned0, f32[8,2,48,128]{3,2,1,0:T(8,128)S(1)} %get-tuple-element.37.linear0, f32[48,128]{1,0:T(8,128)S(1)} %add.27.own, ...), custom_call_target="tpu_custom_call" | custom-call | flops 200000000 | bytes 6000000 | tf_op jit(solution)/shard_map/pallas_call | solution.py:477
  40.2 0.2 collective-permute-start.16
  40.4 1.0 %collective-permute-done.16 = f32[16,128]{1,0:T(8,128)S(1)} collective-permute-done((f32[16,128]{1,0:T(8,128)S(1)}, f32[16,128]{1,0:T(8,128)S(1)}, u32[]{:S(2)}, u32[]{:S(2)}) %collective-permute-start.16) | collective-permute-done | bytes 8224 | tf_op jit(solution)/shard_map/ppermute | solution.py:516
  41.4 1.1 %collective-permute-start.19 = (f32[16,128]{1,0:T(8,128)S(1)}, f32[16,128]{1,0:T(8,128)S(1)}, u32[]{:S(2)}, u32[]{:S(2)}) collective-permute-start(f32[16,128]{1,0:T(8,128)S(1)} %add.28), channel_id=1, source_target_pairs={{0,13},{1,12},{4,9},{5,8},{8,5},{9,4},{12,1},{13,0},{2,15},{3,14},... | collective-permute-start | bytes 24584 | tf_op jit(solution)/shard_map/ppermute | solution.py:500
  42.5 1.9 %collective-permute-start.18 = (f32[16,128]{1,0:T(8,128)S(1)}, f32[16,128]{1,0:T(8,128)S(1)}, u32[]{:S(2)}, u32[]{:S(2)}) collective-permute-start(f32[16,128]{1,0:T(8,128)S(1)} %add.28), channel_id=1, source_target_pairs={{0,9},{1,8},{4,13},{5,12},{8,1},{9,0},{12,5},{13,4},{2,11},{3,10},... | collective-permute-start | bytes 24584 | tf_op jit(solution)/shard_map/ppermute | solution.py:500
  44.4 0.9 %collective-permute-start.17 = (f32[16,128]{1,0:T(8,128)S(1)}, f32[16,128]{1,0:T(8,128)S(1)}, u32[]{:S(2)}, u32[]{:S(2)}) collective-permute-start(f32[16,128]{1,0:T(8,128)S(1)} %add.28), channel_id=1, source_target_pairs={{0,5},{1,4},{4,1},{5,0},{8,13},{9,12},{12,9},{13,8},{2,7},{3,6},{6... | collective-permute-start | bytes 24584 | tf_op jit(solution)/shard_map/ppermute | solution.py:500
  45.3 1.2 %shard_map.86 = f32[4,1,2,4096]{3,2,1,0:T(2,128)} custom-call(s32[2,2,4]{2,1,0:T(2,128)S(1)} %get-tuple-element.30.shifts, f32[4,2,48,128]{3,2,1,0:T(8,128)S(1)} %get-tuple-element.54.grad0, bf16[8,256,512]{2,1,0:T(8,128)(2,1)S(1)} %get-tuple-element.35.refs_6_.high, bf16[8,256,512]{2,1,0:T(8,128)(2,1)S(1)} %get-tuple-element.36.refs_7_.low), custom_call_target="tpu_custom_call" | custom-call | flops 200000000 | bytes 6000000 | tf_op jit(solution)/shard_map/pallas_call | solution.py:477
  46.5 0.0 collective-permute-done.19
  46.5 0.0 collective-permute-done.18
  46.5 1.0 %collective-permute-done.17 = f32[16,128]{1,0:T(8,128)S(1)} collective-permute-done((f32[16,128]{1,0:T(8,128)S(1)}, f32[16,128]{1,0:T(8,128)S(1)}, u32[]{:S(2)}, u32[]{:S(2)}) %collective-permute-start.17) | collective-permute-done | bytes 8224 | tf_op jit(solution)/shard_map/ppermute | solution.py:500
  47.5 0.6 %add_add_fusion = f32[16,128]{1,0:T(8,128)} fusion(f32[16,128]{1,0:T(8,128)S(1)} %collective-permute-done.18, f32[16,128]{1,0:T(8,128)S(1)} %collective-permute-done.19, f32[16,128]{1,0:T(8,128)S(1)} %add.28, f32[16,128]{1,0:T(8,128)S(1)} %collective-permute-done.17), kind=kLoop, calls=%fused_computation | loop fusion | flops 6144 | bytes 40960 | tf_op jit(solution)/shard_map/add | solution.py:552
  (5 shorter events, 0.0 us)
Async XLA Ops:
  1.8 8.2 %collective-permute-start = (f32[280,128]{1,0:T(8,128)S(1)}, f32[280,128]{1,0:T(8,128)S(1)}, u32[]{:S(2)}, u32[]{:S(2)}) collective-permute-start(f32[280,128]{1,0:T(8,128)S(1)} %get-tuple-element.29.refs_0_), channel_id=1, source_target_pairs={{0,2},{1,3},{2,0},{3,1},{4,6},{5,7},{6,4},{7,5},{8,10},{9,11},{10,... | collective-permute-start | bytes 430088 | tf_op jit(solution)/shard_map/ppermute | solution.py:500
  4.8 8.8 %collective-permute-start.3 = (f32[4,2,3072]{2,1,0:T(2,128)S(1)}, f32[4,2,3072]{2,1,0:T(2,128)S(1)}, u32[]{:S(2)}, u32[]{:S(2)}) collective-permute-start(f32[4,2,3072]{2,1,0:T(2,128)S(1)} %get-tuple-element.33), channel_id=1, source_target_pairs={{0,6},{1,7},{2,4},{3,5},{4,2},{5,3},{6,0},{7,1},{8,14},{9,15},{10,... | collective-permute-start | bytes 294920 | tf_op jit(solution)/shard_map/ppermute | solution.py:545
  6.4 7.2 %collective-permute-start.1 = (f32[4,2,3072]{2,1,0:T(2,128)S(1)}, f32[4,2,3072]{2,1,0:T(2,128)S(1)}, u32[]{:S(2)}, u32[]{:S(2)}) collective-permute-start(f32[4,2,3072]{2,1,0:T(2,128)S(1)} %get-tuple-element.33), channel_id=1, source_target_pairs={{0,4},{1,5},{4,0},{5,1},{8,12},{9,13},{12,8},{13,9},{2,6},{3,7},{6... | collective-permute-start | bytes 294920 | tf_op jit(solution)/shard_map/ppermute | solution.py:500
  6.4 7.2 %collective-permute-start.4 = (f32[4,2,3072]{2,1,0:T(2,128)S(1)}, f32[4,2,3072]{2,1,0:T(2,128)S(1)}, u32[]{:S(2)}, u32[]{:S(2)}) collective-permute-start(f32[4,2,3072]{2,1,0:T(2,128)S(1)} %get-tuple-element.34), channel_id=1, source_target_pairs={{0,1},{1,0},{2,3},{3,2},{4,10},{5,11},{6,8},{7,9},{8,6},{9,7},{10,... | collective-permute-start | bytes 294920 | tf_op jit(solution)/shard_map/ppermute | solution.py:545
  6.4 7.2 %collective-permute-start.2 = (f32[4,2,3072]{2,1,0:T(2,128)S(1)}, f32[4,2,3072]{2,1,0:T(2,128)S(1)}, u32[]{:S(2)}, u32[]{:S(2)}) collective-permute-start(f32[4,2,3072]{2,1,0:T(2,128)S(1)} %get-tuple-element.34), channel_id=1, source_target_pairs={{0,1},{1,0},{4,8},{5,9},{8,4},{9,5},{12,13},{13,12},{2,3},{3,2},{6... | collective-permute-start | bytes 294920 | tf_op jit(solution)/shard_map/ppermute | solution.py:500
  10.0 15.0 %collective-permute-start.9 = (f32[4,2,32,128]{3,2,1,0:T(8,128)S(1)}, f32[4,2,32,128]{3,2,1,0:T(8,128)S(1)}, u32[]{:S(2)}, u32[]{:S(2)}) collective-permute-start(f32[4,2,32,128]{3,2,1,0:T(8,128)S(1)} %get-tuple-element.43.refs_0_), channel_id=1, source_target_pairs={{0,2},{1,3},{2,0},{3,1},{4,6},{5,7},{6,4},{7,5},{8,10},{9,11},{10,... | collective-permute-start | bytes 393224 | tf_op jit(solution)/shard_map/ppermute | solution.py:500
  15.3 1.3 %collective-permute-start.5 = (f32[64,128]{1,0:T(8,128)S(1)}, f32[64,128]{1,0:T(8,128)S(1)}, u32[]{:S(2)}, u32[]{:S(2)}) collective-permute-start(f32[64,128]{1,0:T(8,128)S(1)} %get-tuple-element.38), channel_id=1, source_target_pairs={{0,1},{1,0},{2,3},{3,2},{4,5},{5,4},{6,7},{7,6},{8,9},{9,8},{10,11... | collective-permute-start | bytes 98312 | tf_op jit(solution)/shard_map/ppermute | solution.py:516
  18.2 1.3 %collective-permute-start.6 = (f32[48,128]{1,0:T(8,128)S(1)}, f32[48,128]{1,0:T(8,128)S(1)}, u32[]{:S(2)}, u32[]{:S(2)}) collective-permute-start(f32[48,128]{1,0:T(8,128)S(1)} %get-tuple-element.42), channel_id=1, source_target_pairs={{0,1},{1,0},{2,3},{3,2},{4,5},{5,4},{6,7},{7,6},{8,9},{9,8},{10,11... | collective-permute-start | bytes 73736 | tf_op jit(solution)/shard_map/ppermute | solution.py:516
  19.5 5.5 %collective-permute-start.8 = (f32[48,128]{1,0:T(8,128)S(1)}, f32[48,128]{1,0:T(8,128)S(1)}, u32[]{:S(2)}, u32[]{:S(2)}) collective-permute-start(f32[48,128]{1,0:T(8,128)S(1)} %add.25.own), channel_id=1, source_target_pairs={{0,1},{1,0},{4,9},{5,8},{8,5},{9,4},{12,13},{13,12},{2,3},{3,2},{6... | collective-permute-start | bytes 73736 | tf_op jit(solution)/shard_map/ppermute | solution.py:500
  19.6 6.8 %collective-permute-start.7 = (f32[48,128]{1,0:T(8,128)S(1)}, f32[48,128]{1,0:T(8,128)S(1)}, u32[]{:S(2)}, u32[]{:S(2)}) collective-permute-start(f32[48,128]{1,0:T(8,128)S(1)} %add.25.own), channel_id=1, source_target_pairs={{0,5},{1,4},{4,1},{5,0},{8,13},{9,12},{12,9},{13,8},{2,7},{3,6},{6... | collective-permute-start | bytes 73736 | tf_op jit(solution)/shard_map/ppermute | solution.py:500
  27.0 1.3 %collective-permute-start.10 = (f32[48,128]{1,0:T(8,128)S(1)}, f32[48,128]{1,0:T(8,128)S(1)}, u32[]{:S(2)}, u32[]{:S(2)}) collective-permute-start(f32[48,128]{1,0:T(8,128)S(1)} %get-tuple-element.45), channel_id=1, source_target_pairs={{0,1},{1,0},{2,3},{3,2},{4,5},{5,4},{6,7},{7,6},{8,9},{9,8},{10,11... | collective-permute-start | bytes 73736 | tf_op jit(solution)/shard_map/ppermute | solution.py:516
  28.3 1.9 %collective-permute-start.12 = (f32[48,128]{1,0:T(8,128)S(1)}, f32[48,128]{1,0:T(8,128)S(1)}, u32[]{:S(2)}, u32[]{:S(2)}) collective-permute-start(f32[48,128]{1,0:T(8,128)S(1)} %add.26.own), channel_id=1, source_target_pairs={{0,1},{1,0},{4,9},{5,8},{8,5},{9,4},{12,13},{13,12},{2,3},{3,2},{6... | collective-permute-start | bytes 73736 | tf_op jit(solution)/shard_map/ppermute | solution.py:500
  28.5 3.3 %collective-permute-start.11 = (f32[48,128]{1,0:T(8,128)S(1)}, f32[48,128]{1,0:T(8,128)S(1)}, u32[]{:S(2)}, u32[]{:S(2)}) collective-permute-start(f32[48,128]{1,0:T(8,128)S(1)} %add.26.own), channel_id=1, source_target_pairs={{0,5},{1,4},{4,1},{5,0},{8,13},{9,12},{12,9},{13,8},{2,7},{3,6},{6... | collective-permute-start | bytes 73736 | tf_op jit(solution)/shard_map/ppermute | solution.py:500
  33.1 1.3 %collective-permute-start.13 = (f32[48,128]{1,0:T(8,128)S(1)}, f32[48,128]{1,0:T(8,128)S(1)}, u32[]{:S(2)}, u32[]{:S(2)}) collective-permute-start(f32[48,128]{1,0:T(8,128)S(1)} %get-tuple-element.50), channel_id=1, source_target_pairs={{0,1},{1,0},{2,3},{3,2},{4,5},{5,4},{6,7},{7,6},{8,9},{9,8},{10,11... | collective-permute-start | bytes 73736 | tf_op jit(solution)/shard_map/ppermute | solution.py:516
  34.3 4.4 %collective-permute-start.15 = (f32[48,128]{1,0:T(8,128)S(1)}, f32[48,128]{1,0:T(8,128)S(1)}, u32[]{:S(2)}, u32[]{:S(2)}) collective-permute-start(f32[48,128]{1,0:T(8,128)S(1)} %add.27.own), channel_id=1, source_target_pairs={{0,1},{1,0},{4,9},{5,8},{8,5},{9,4},{12,13},{13,12},{2,3},{3,2},{6... | collective-permute-start | bytes 73736 | tf_op jit(solution)/shard_map/ppermute | solution.py:500
  34.7 4.5 %collective-permute-start.14 = (f32[48,128]{1,0:T(8,128)S(1)}, f32[48,128]{1,0:T(8,128)S(1)}, u32[]{:S(2)}, u32[]{:S(2)}) collective-permute-start(f32[48,128]{1,0:T(8,128)S(1)} %add.27.own), channel_id=1, source_target_pairs={{0,5},{1,4},{4,1},{5,0},{8,13},{9,12},{12,9},{13,8},{2,7},{3,6},{6... | collective-permute-start | bytes 73736 | tf_op jit(solution)/shard_map/ppermute | solution.py:500
  40.2 1.2 %collective-permute-start.16 = (f32[16,128]{1,0:T(8,128)S(1)}, f32[16,128]{1,0:T(8,128)S(1)}, u32[]{:S(2)}, u32[]{:S(2)}) collective-permute-start(f32[16,128]{1,0:T(8,128)S(1)} %get-tuple-element.55), channel_id=1, source_target_pairs={{0,1},{1,0},{2,3},{3,2},{4,5},{5,4},{6,7},{7,6},{8,9},{9,8},{10,11... | collective-permute-start | bytes 24584 | tf_op jit(solution)/shard_map/ppermute | solution.py:516
  41.4 5.1 %collective-permute-start.19 = (f32[16,128]{1,0:T(8,128)S(1)}, f32[16,128]{1,0:T(8,128)S(1)}, u32[]{:S(2)}, u32[]{:S(2)}) collective-permute-start(f32[16,128]{1,0:T(8,128)S(1)} %add.28), channel_id=1, source_target_pairs={{0,13},{1,12},{4,9},{5,8},{8,5},{9,4},{12,1},{13,0},{2,15},{3,14},... | collective-permute-start | bytes 24584 | tf_op jit(solution)/shard_map/ppermute | solution.py:500
  42.5 4.0 %collective-permute-start.18 = (f32[16,128]{1,0:T(8,128)S(1)}, f32[16,128]{1,0:T(8,128)S(1)}, u32[]{:S(2)}, u32[]{:S(2)}) collective-permute-start(f32[16,128]{1,0:T(8,128)S(1)} %add.28), channel_id=1, source_target_pairs={{0,9},{1,8},{4,13},{5,12},{8,1},{9,0},{12,5},{13,4},{2,11},{3,10},... | collective-permute-start | bytes 24584 | tf_op jit(solution)/shard_map/ppermute | solution.py:500
  44.4 3.1 %collective-permute-start.17 = (f32[16,128]{1,0:T(8,128)S(1)}, f32[16,128]{1,0:T(8,128)S(1)}, u32[]{:S(2)}, u32[]{:S(2)}) collective-permute-start(f32[16,128]{1,0:T(8,128)S(1)} %add.28), channel_id=1, source_target_pairs={{0,5},{1,4},{4,1},{5,0},{8,13},{9,12},{12,9},{13,8},{2,7},{3,6},{6... | collective-permute-start | bytes 24584 | tf_op jit(solution)/shard_map/ppermute | solution.py:500

commit v5 on v4

--- a/solution.py
+++ b/solution.py
@@ -66,8 +66,13 @@
 
 
 def at(table, step, b):
-    own = table.shape[2]
-    return table[b // own, step, b % own]
+    own = table[0].shape[1]
+    return table[b // own][step, b % own]
+
+
+def of(groups, b):
+    own = groups[0].shape[0]
+    return groups[b // own].at[b % own]
 
 
 def is_even():
@@ -202,7 +207,8 @@
 
 
 def k_begin(
-    signal, cotangent, taps, delays, shifts, gains, even_out, odd_out, sent, cot_rows,
+    signal, cotangent, taps, delays, shifts, gains,
+    even_out, odd_out, even_near, odd_near, sent, cot_rows,
     sig_held, cot_held, taps_held, delays_held, shifts_held, gains_held, done,
 ):
     steps, bands = taps.shape[:2]
@@ -219,11 +225,16 @@
     even = is_even()
     length, wide, edge = rows * LANES, WIDE * LANES, EDGE * LANES
     for b in range(bands):
-        for held, first, width in ((sig_held, 0, wide), (cot_held, wide, edge)):
+        for targets, held, first, width in (
+            ((even_out, odd_out), sig_held, 0, wide),
+            ((even_out, odd_out), cot_held, wide, edge),
+            ((even_near, odd_near), sig_held, 0, edge),
+            ((even_near, odd_near), cot_held, edge, edge),
+        ):
             left = held[b, 0, :, 0:width]
             right = held[b, 0, :, length - width : length]
-            even_out[b, :, first : first + width] = jnp.where(even, right, left)
-            odd_out[b, :, first : first + width] = jnp.where(even, left, right)
+            targets[0][b, :, first : first + width] = jnp.where(even, right, left)
+            targets[1][b, :, first : first + width] = jnp.where(even, left, right)
         for r in range(rows):
             lanes = slice(r * LANES, (r + 1) * LANES)
             pair = sig_held[b, 0, :, lanes]
@@ -244,25 +255,20 @@
         sent[row : row + steps, 0:bands] = held[...].astype(F32)
 
 
-def k_setup(groups, steps, rows, *refs):
-    packs = refs[:groups]
-    delays, shifts, gains = refs[groups : groups + 3]
-    tables = refs[groups + 3 :]
-    own = delays.shape[2]
+def k_setup(steps, rows, pack, delays, shifts, gains, *tables):
+    bands = delays.shape[1]
     shape = (LANES, LANES)
     diagonal = lanes_of(shape) >= lax.broadcasted_iota(jnp.int32, shape, 0)
-    base = 2 * own * rows
-    first = base + 2 * steps * own
-    for k, pack in enumerate(packs):
-        for n, target in enumerate((delays, shifts, gains)):
-            row = first + n * steps
-            target[k] = pack[row : row + steps, 0:own].astype(target.dtype)
-    for b in range(groups * own):
-        pack = packs[b // own]
+    base = 2 * bands * rows
+    first = base + 2 * steps * bands
+    for n, target in enumerate((delays, shifts, gains)):
+        row = first + n * steps
+        target[...] = pack[row : row + steps, 0:bands].astype(target.dtype)
+    for b in range(bands):
         for step in range(steps):
             high, low = tables[2 * step : 2 * step + 2]
             for c in range(2):
-                tap = base + 2 * (step * own + b % own) + c
+                tap = base + 2 * (step * bands + b) + c
                 row = jnp.broadcast_to(pack[tap : tap + 1, :], shape)
                 ring = pltpu.roll(row, 0, 1, stride=1, stride_axis=0)
                 near = jnp.where(diagonal, ring, 0.0)
@@ -278,37 +284,37 @@
                             target[b, 0:LANES, d : d + LANES] = -value
 
 
-def k_cotangent(groups, *refs):
-    out = refs[-1]
-    own = refs[0].shape[0]
+def k_cotangent(cots, sides, first, out):
+    own = cots[0].shape[0]
     rows = out.shape[2] - 2 * PAD
     for b in range(out.shape[0]):
         k = b // own
-        extend(out, b, refs[groups + 2 * k], refs[groups + 2 * k + 1], WIDE, EDGE)
+        extend(out, b, *sides[k], first[k], EDGE)
         for c in range(2):
-            out[b, c, PAD : PAD + rows, :] = refs[k][b % own, c]
-
-
-def k_first(groups, delays, shifts, *refs):
-    packs, sides = refs[:groups], refs[groups : 3 * groups]
-    high, low, shifted, linear, out, ext, held = refs[3 * groups :]
+            out[b, c, PAD : PAD + rows, :] = cots[k][b % own, c]
+
+
+def widened(ext, pack, sides, edge, b):
+    pad = edge + 4
+    rows = ext.shape[2] - 2 * pad
+    extend(ext, b, *sides, 0, edge)
+    for c in range(2):
+        row = (2 * b + c) * rows
+        ext[b, c, pad : pad + rows, :] = pack[row : row + rows, :]
+
+
+def k_first(delays, shifts, pack, sides, high, low, shifted, linear, out, ext, held):
     bands = linear.shape[0]
     rows = linear.shape[2] - 2 * PAD
-    own = shifted.shape[0]
     middle = slice(WIDE_PAD - PAD, WIDE_PAD + rows + PAD)
     powers = []
     for b in range(bands):
-        k = b // own
-        extend(ext, b, sides[2 * k], sides[2 * k + 1], 0, WIDE)
-        for c in range(2):
-            row = (2 * (b % own) + c) * rows
-            ext[b, c, WIDE_PAD : WIDE_PAD + rows, :] = packs[k][row : row + rows, :]
+        widened(ext, pack, sides, WIDE, b)
         amount = LANES // 2 - at(shifts, 0, b)
         real = later(ext[b, 0], amount)
         imag = later(ext[b, 1], amount)
-        if b < own:
-            shifted[b, 0] = real[middle]
-            shifted[b, 1] = imag[middle]
+        shifted[b, 0] = real[middle]
+        shifted[b, 1] = imag[middle]
         lr, li = fir(real, imag, high[b], low[b])
         linear[b, 0] = lr[middle]
         linear[b, 1] = li[middle]
@@ -316,18 +322,30 @@
     delayed_sum(powers, delays, 0, held, out)
 
 
+def k_beside(shifts, pack, sides, high, low, linear, ext):
+    for b in range(linear.shape[0]):
+        widened(ext, pack, sides, EDGE, b)
+        amount = LANES // 2 - at(shifts, 0, b)
+        real = later(ext[b, 0], amount)
+        imag = later(ext[b, 1], amount)
+        lr, li = fir(real, imag, high[b], low[b])
+        linear[b, 0] = lr
+        linear[b, 1] = li
+
+
 def k_second(
     delays, shifts, gains, linear0, own, high, low,
     cosine0, sine0, field1, shifted, linear1, out, held, held_out,
 ):
-    bands = linear0.shape[0]
-    rows = linear0.shape[2] - 2 * PAD
+    bands = linear1.shape[0]
+    rows = linear1.shape[2] - 2 * PAD
     values = end_at_last(own[...], rows)
     powers = []
     for b in range(bands):
         spread = read_spread(values, at(delays, 0, b), held, b, rows)
         sine, cosine = sine_cosine(at(gains, 0, b) * spread)
-        lr, li = linear0[b, 0], linear0[b, 1]
+        linear = of(linear0, b)
+        lr, li = linear[0], linear[1]
         fr = keep_inside(lr * cosine - li * sine, rows)
         fi = keep_inside(lr * sine + li * cosine, rows)
         field1[b, 0] = fr
@@ -340,7 +358,7 @@
             sine0[b] = sine
             shifted[b, 0] = real
             shifted[b, 1] = imag
-        lr, li = fir(real, imag, high[b], low[b])
+        lr, li = fir(real, imag, of(high, b)[...], of(low, b)[...])
         linear1[b, 0] = lr
         linear1[b, 1] = li
         lr, li = lr[PAD : PAD + rows], li[PAD : PAD + rows]
@@ -384,7 +402,7 @@
         if b < grad1.shape[0]:
             grad1[b, 0] = gr
             grad1[b, 1] = gi
-        gr, gi = fir_adjoint(gr, gi, high[b], low[b])
+        gr, gi = fir_adjoint(gr, gi, of(high, b)[...], of(low, b)[...])
         amount = LANES // 2 - at(shifts, 1, b)
         gr = earlier(gr, amount)
         gi = earlier(gi, amount)
@@ -477,7 +495,7 @@
     return pl.pallas_call(
         kernel,
         out_shape=shapes,
-        in_specs=[vmem] * len(arrays),
+        in_specs=jax.tree.map(lambda _: vmem, arrays),
         out_specs=[vmem] * len(shapes),
         scratch_shapes=[pltpu.VMEM(s, F32) for s in scratch],
         compiler_params=pltpu.CompilerParams(vmem_limit_bytes=24 * 1024 * 1024),
@@ -552,13 +570,9 @@
     return (x + others[0]) + (others[1] + others[2])
 
 
-def over_powers(part, doubled):
+def exchanged(part, doubled):
     part = over_cores(part)
-    return part if doubled else summed(part, "band")
-
-
-def exchanged(part, doubled):
-    part = over_powers(part, doubled)
+    part = part if doubled else summed(part, "band")
     return (part,) + neighbours(part, part, True)
 
 
@@ -579,9 +593,9 @@
     angle = shape(own, held_rows, LANES)
     wide_part = shape(rows + REACH + 2 * PAD, LANES)
     part = shape(rows + REACH, LANES)
-    table = shape(bands, 2 * LANES, 4 * LANES, dtype=BF16)
-    ext_wide = (bands, 2, rows + 2 * WIDE_PAD, LANES)
-    held_wide = (bands, rows + 2 * WIDE_PAD + 8, LANES)
+    table = shape(own, 2 * LANES, 4 * LANES, dtype=BF16)
+    ext_wide = (own, 2, rows + 2 * WIDE_PAD, LANES)
+    held_wide = (own, rows + 2 * WIDE_PAD + 8, LANES)
     spread = (rows + REACH + 2 * PAD, LANES)
     held_in = (bands, rows + REACH + 3 * PAD, LANES)
     held_out = (bands, rows + 3 * REACH, LANES)
@@ -589,37 +603,48 @@
     inputs = (signal, cotangent, taps, walk_off, tap_shift, gains)
     hbm, vmem = (pl.BlockSpec(memory_space=m) for m in (pltpu.HBM, pltpu.VMEM))
     cut = shape(own, 2, (WIDE + EDGE) * LANES)
+    near = shape(own, 2, 2 * EDGE * LANES)
     pack_rows = 2 * own * rows + 2 * steps * own + 3 * steps
     pack = shape(pack_rows + -pack_rows % 8, LANES)
-    even_out, odd_out, pack_out, cot_out = pl.pallas_call(
+    even_out, odd_out, even_near, odd_near, pack_out, cot_out = pl.pallas_call(
         k_begin,
-        out_shape=[cut, cut, pack, shape(own, 2, rows, LANES)],
+        out_shape=[cut, cut, near, near, pack, shape(own, 2, rows, LANES)],
         in_specs=[hbm] * len(inputs),
-        out_specs=[vmem] * 4,
+        out_specs=[vmem] * 6,
         scratch_shapes=[pltpu.VMEM(a.shape, a.dtype) for a in inputs]
         + [pltpu.SemaphoreType.DMA((len(inputs),))],
         compiler_params=pltpu.CompilerParams(vmem_limit_bytes=24 * 1024 * 1024),
-        cost_estimate=pl.CostEstimate(flops=10**9, bytes_accessed=0, transcendentals=0),
+        cost_estimate=pl.CostEstimate(flops=10**8, bytes_accessed=10**6, transcendentals=0),
     )(*(pltpu.with_memory_space_constraint(a, pltpu.HBM) for a in inputs))
-    packs, cots = [pack_out], [cot_out]
+
+    packs, cots, first_cot = [pack_out], [cot_out], [WIDE]
+    sides = [neighbours(even_out, odd_out, False)]
     if doubled:
         packs.append(swapped(pack_out, "band", evenly, False))
-    sides = list(neighbours(even_out, odd_out, False))
+        sides.append((aslant(even_near, evenly), aslant(odd_near, oddly)))
+        cots.append(swapped(cot_out, "band", evenly, False))
+        first_cot.append(EDGE)
+    tiny = [shape(steps, own, dtype=d) for d in (jnp.int32, jnp.int32, F32)]
+    setup = functools.partial(k_setup, steps, rows)
+    made = [call(setup, (p,), tiny + [table] * (2 * steps)) for p in packs]
+    delays, shifts, gains, high0, low0, high1, low1 = (list(m) for m in zip(*made))
+
+    shifted0, linear, sent = call(
+        k_first, (delays[:1], shifts[:1], pack_out, sides[0], high0[0], low0[0]),
+        [own_field, own_field, wide_part], (ext_wide, held_wide),
+    )
+    spread0 = summed(over_cores(sent), "band")
+    linear0 = [linear]
     if doubled:
-        sides += [aslant(even_out, evenly), aslant(odd_out, oddly)]
-        cots.append(swapped(cot_out, "band", evenly, False))
-    tiny = [shape(groups, steps, own, dtype=d) for d in (jnp.int32, jnp.int32, F32)]
-    delays, shifts, gains, high0, low0, high1, low1 = call(
-        functools.partial(k_setup, groups, steps, rows), tuple(packs),
-        tiny + [table] * (2 * steps),
-    )
-    (cot_rows,) = call(functools.partial(k_cotangent, groups), (*cots, *sides), [field])
-    shifted0, linear0, sent = call(
-        functools.partial(k_first, groups), (delays, shifts, *packs, *sides, high0, low0),
-        [own_field, field, wide_part], (ext_wide, held_wide),
+        linear0 += call(
+            k_beside, (shifts[1:], packs[1], sides[1], high0[1], low0[1]), [own_field],
+            ((own, 2, held_rows, LANES),),
+        )
+    (cot_rows,) = call(
+        lambda c, s, out: k_cotangent(c, s, first_cot, out), (cots, sides), [field]
     )
     cosine0, sine0, field1, shifted1, linear1, sent = call(
-        k_second, (delays, shifts, gains, linear0, over_powers(sent, doubled), high1, low1),
+        k_second, (delays, shifts, gains, linear0, spread0, high1, low1),
         [angle, angle, field, own_field, field, part], (held_in, held_out),
     )
     turned1, sent = call(
@@ -636,11 +661,11 @@
     scale = 1.0 / math.sqrt(2.0 * length * lax.axis_size("tm"))
     grad0, grad_taps = call(
         functools.partial(k_fifth, scale),
-        (delays, turned0, linear0, *exchanged(sent, doubled), shifted0, taps1),
+        (delays[:1], turned0, linear, *exchanged(sent, doubled), shifted0, taps1),
         [own_field, shape(steps * 2 * own, LANES)], (spread, held_in),
     )
     (grad_signal,) = call(
-        k_last, (shifts, grad0, high0, low0), [shape(own, 1, 2, length)]
+        k_last, (shifts[:1], grad0, high0[0], low0[0]), [shape(own, 1, 2, length)]
     )
     grad_taps = over_tm(over_cores(grad_taps))
     return grad_signal, grad_taps.reshape(steps, own, 2, LANES)

time: 48.2 us -> 46.3 us (0.961)
  waiting for transfers between devices: 12.6 us -> 9.81 us
  starting transfers between devices: 23.2 us -> 23.9 us
    ppermute x2, starting transfers between devices: 1.55 us -> 4.19 us  [aslant(): return lax.ppermute(x, ('tm', 'band', 'pol'), pairs)]
    ppermute x13 -> x14, starting transfers between devices: 20.5 us -> 18.4 us  [swapped(): return lax.ppermute(x, (axis, 'pol'), pairs)]
    ppermute x13 -> x14, waiting for transfers between devices: 7.44 us -> 5.41 us  [swapped(): return lax.ppermute(x, (axis, 'pol'), pairs)]
    ppermute x5, waiting for transfers between devices: 5.14 us -> 3.77 us  [over_cores(): lax.ppermute(x, 'pol', [(p, cores - 1 - p) for p in range(cores)])]
    ppermute x2, waiting for transfers between devices: 0.01 us -> 0.63 us  [aslant(): return lax.ppermute(x, ('tm', 'band', 'pol'), pairs)]
    pallas_call x10 -> x12, Pallas kernels: 10.9 us -> 11 us  [the longest x11 9.85 us: call(): pl.pallas_call(kernel, out_shape=shapes, in_specs=jax.tree.map(lambda _:...]
  transfers between devices with their start and end apart: 20 -> 21, of which waited for: 10 -> 11; matrix products, arithmetic and copies ran while one was open for 0% -> 0% of each run, Pallas kernels for 14% -> 15%
where the time goes in v5:
time: 46.3 us; the launch traced here: 46.1 us
  starting transfers between devices  23.9 us (52%)
  Pallas kernels  11 us (24%)
  waiting for transfers between devices  9.81 us (21%)
  between operations  0.74 us (2%)
  other arithmetic  0.63 us (1%)
    ppermute x14, starting transfers between devices, swapped(): return lax.ppermute(x, (axis, 'pol'), pairs)  18.4 us
    pallas_call x11, Pallas kernels, call(): pl.pallas_call(kernel, out_shape=shapes, in_specs=jax.tree.map(lambda _:...  9.85 us
    ppermute x14, waiting for transfers between devices, swapped(): return lax.ppermute(x, (axis, 'pol'), pairs)  5.41 us
    ppermute x2, starting transfers between devices, aslant(): return lax.ppermute(x, ('tm', 'band', 'pol'), pairs)  4.19 us
    ppermute x5, waiting for transfers between devices, over_cores(): lax.ppermute(x, 'pol', [(p, cores - 1 - p) for p in range(cores)])  3.77 us
    ppermute x5, starting transfers between devices, over_cores(): lax.ppermute(x, 'pol', [(p, cores - 1 - p) for p in range(cores)])  1.32 us
    pallas_call x1, Pallas kernels, on_device(): pl.pallas_call(k_begin, out_shape=[cut, cut, near, near, pack, shape(own,...  1.18 us
  transfers between devices with their start and end apart: 21, of which 11 were waited for; matrix products, arithmetic and copies ran while one was open for 0% of the time, Pallas kernels for 15%

profile of v5, /device:TPU:0, one launch (start us, length us, event | category | flops | bytes accessed | tf_op | source)
XLA Modules:
  0.0 46.1 jit_solution(7948195665880498753)
XLA Ops:
  0.6 1.2 %shard_map.77 = (f32[4,2,3072]{2,1,0:T(2,128)S(1)}, f32[4,2,3072]{2,1,0:T(2,128)S(1)}, f32[4,2,1024]{2,1,0:T(2,128)S(1)}, f32[4,2,1024]{2,1,0:T(2,128)S(1)}, f32...) custom-call(f32[4,1,2,4096]{3,2,1,0:T(2,128)} %signal.1, f32[4,1,2,4096]{3,2,1,0:T(2,128)} %cotangent.1, ...), custom_call_target="tpu_custom_call" | custom-call | flops 100000000 | bytes 1000000 | tf_op jit(solution)/shard_map/pallas_call | solution.py:609
  1.8 3.1 %collective-permute-start.1 = (f32[4,2,3072]{2,1,0:T(2,128)S(1)}, f32[4,2,3072]{2,1,0:T(2,128)S(1)}, u32[]{:S(2)}, u32[]{:S(2)}) collective-permute-start(f32[4,2,3072]{2,1,0:T(2,128)S(1)} %get-tuple-element.45), channel_id=1, source_target_pairs={{0,4},{1,5},{4,0},{5,1},{8,12},{9,13},{12,8},{13,9},{2,6},{3,7},{6... | collective-permute-start | bytes 294920 | tf_op jit(solution)/shard_map/ppermute | solution.py:518
  4.9 0.0 collective-permute-start.2
  4.9 1.5 %collective-permute-start = (f32[280,128]{1,0:T(8,128)S(1)}, f32[280,128]{1,0:T(8,128)S(1)}, u32[]{:S(2)}, u32[]{:S(2)}) collective-permute-start(f32[280,128]{1,0:T(8,128)S(1)} %get-tuple-element.38.pack), channel_id=1, source_target_pairs={{0,2},{1,3},{2,0},{3,1},{4,6},{5,7},{6,4},{7,5},{8,10},{9,11},{10,... | collective-permute-start | bytes 430088 | tf_op jit(solution)/shard_map/ppermute | solution.py:518
  6.4 0.5 %collective-permute-start.10 = (f32[4,2,32,128]{3,2,1,0:T(8,128)S(1)}, f32[4,2,32,128]{3,2,1,0:T(8,128)S(1)}, u32[]{:S(2)}, u32[]{:S(2)}) collective-permute-start(f32[4,2,32,128]{3,2,1,0:T(8,128)S(1)} %get-tuple-element.61.c_0_), channel_id=1, source_target_pairs={{0,2},{1,3},{2,0},{3,1},{4,6},{5,7},{6,4},{7,5},{8,10},{9,11},{10,... | collective-permute-start | bytes 393224 | tf_op jit(solution)/shard_map/ppermute | solution.py:518
  6.9 0.6 %shard_map.78 = (s32[2,4]{1,0:T(2,128)S(1)}, s32[2,4]{1,0:T(2,128)S(1)}, f32[2,4]{1,0:T(2,128)S(1)}, bf16[4,256,512]{2,1,0:T(8,128)(2,1)S(1)}, bf16[4,256,512]{2...) custom-call(f32[280,128]{1,0:T(8,128)S(1)} %get-tuple-element.38.pack), custom_call_target="tpu_custom_call" | custom-call | flops 200000000 | bytes 6000000 | tf_op jit(solution)/shard_map/pallas_call | solution.py:495
  7.6 0.1 collective-permute-done.1.sides_0_.s_0__0_
  7.7 0.0 collective-permute-done.2.sides_1_.s_0__1_
  7.7 0.9 %shard_map.80 = (f32[4,2,48,128]{3,2,1,0:T(8,128)S(1)}, f32[4,2,48,128]{3,2,1,0:T(8,128)S(1)}, f32[64,128]{1,0:T(8,128)S(1)}) custom-call(s32[2,4]{1,0:T(2,128)S(1)} %get-tuple-element.40.delays_0_, s32[2,4]{1,0:T(2,128)S(1)} %get-tuple-element.39.shifts_0_, f32[280,128]{1,0:T(8,128)S(1)} %get-tuple-element.38.pack, ...), custom_call_target="tpu_custom_call" | custom-call | flops 200000000 | bytes 6000000 | tf_op jit(solution)/shard_map/pallas_call | solution.py:495
  8.7 0.1 collective-permute-start.5
  8.7 4.0 %collective-permute-start.3 = (f32[4,2,1024]{2,1,0:T(2,128)S(1)}, f32[4,2,1024]{2,1,0:T(2,128)S(1)}, u32[]{:S(2)}, u32[]{:S(2)}) collective-permute-start(f32[4,2,1024]{2,1,0:T(2,128)S(1)} %get-tuple-element.50), channel_id=1, source_target_pairs={{0,6},{1,7},{2,4},{3,5},{4,2},{5,3},{6,0},{7,1},{8,14},{9,15},{10,... | collective-permute-start | bytes 98312 | tf_op jit(solution)/shard_map/ppermute | solution.py:563
  12.8 0.2 collective-permute-start.4
  12.9 0.0 collective-permute-done.5
  12.9 0.6 %collective-permute-start.6 = (f32[64,128]{1,0:T(8,128)S(1)}, f32[64,128]{1,0:T(8,128)S(1)}, u32[]{:S(2)}, u32[]{:S(2)}) collective-permute-start(f32[64,128]{1,0:T(8,128)S(1)} %add.27), channel_id=1, source_target_pairs={{0,3},{1,2},{2,1},{3,0},{4,7},{5,6},{6,5},{7,4},{8,11},{9,10},{10,... | collective-permute-start | bytes 98312 | tf_op jit(solution)/shard_map/ppermute | solution.py:518
  13.5 0.0 collective-permute-done.pack
  13.5 0.6 %shard_map.79 = (s32[2,4]{1,0:T(2,128)S(1)}, s32[2,4]{1,0:T(2,128)S(1)}, f32[2,4]{1,0:T(2,128)S(1)}, bf16[4,256,512]{2,1,0:T(8,128)(2,1)S(1)}, bf16[4,256,512]{2...) custom-call(f32[280,128]{1,0:T(8,128)S(1)} %collective-permute-done.pack), custom_call_target="tpu_custom_call" | custom-call | flops 200000000 | bytes 6000000 | tf_op jit(solution)/shard_map/pallas_call | solution.py:495
  14.1 0.6 %collective-permute-done.3.sides_0_.s_1__0_ = f32[4,2,1024]{2,1,0:T(2,128)S(1)} collective-permute-done((f32[4,2,1024]{2,1,0:T(2,128)S(1)}, f32[4,2,1024]{2,1,0:T(2,128)S(1)}, u32[]{:S(2)}, u32[]{:S(2)}) %collective-permute-start.3) | collective-permute-done | bytes 32800 | tf_op jit(solution)/shard_map/ppermute | solution.py:563
  14.7 0.0 collective-permute-done.4.sides_1_.s_1__1_
  14.7 0.8 %shard_map.81.linear0_1_ = f32[4,2,48,128]{3,2,1,0:T(8,128)S(1)} custom-call(s32[2,4]{1,0:T(2,128)S(1)} %get-tuple-element.42.shifts_0_.shifts_1_, f32[280,128]{1,0:T(8,128)S(1)} %collective-permute-done.pack, f32[4,2,1024]{2,1,0:T(2,128)S(1)} %collective-permute-done.3.sides_0_.s_1__0_, f32[4,2,1024]{2,1,0:T(2,128)S(1)} %collective-permute-done.4.sides_1_.s_1__1_, ...), custom_call_target="tpu_custom_call" | custom-call | flops 200000000 | bytes 6000000 | tf_op jit(solution)/shard_map/pallas_call | solution.py:495
  15.5 0.8 %collective-permute-done.6 = f32[64,128]{1,0:T(8,128)S(1)} collective-permute-done((f32[64,128]{1,0:T(8,128)S(1)}, f32[64,128]{1,0:T(8,128)S(1)}, u32[]{:S(2)}, u32[]{:S(2)}) %collective-permute-start.6) | collective-permute-done | bytes 32800 | tf_op jit(solution)/shard_map/ppermute | solution.py:518
  16.4 1.7 %shard_map.82 = (f32[4,48,128]{2,1,0:T(8,128)S(1)}, f32[4,48,128]{2,1,0:T(8,128)S(1)}, f32[8,2,48,128]{3,2,1,0:T(8,128)S(1)}, f32[4,2,48,128]{3,2,1,0:T(8,128)S(...) custom-call(s32[2,4]{1,0:T(2,128)S(1)} %get-tuple-element.40.delays_0_, ...), custom_call_target="tpu_custom_call" | custom-call | flops 200000000 | bytes 6000000 | tf_op jit(solution)/shard_map/pallas_call | solution.py:495
  18.0 0.4 collective-permute-start.7
  18.4 0.9 %collective-permute-done.7 = f32[48,128]{1,0:T(8,128)S(1)} collective-permute-done((f32[48,128]{1,0:T(8,128)S(1)}, f32[48,128]{1,0:T(8,128)S(1)}, u32[]{:S(2)}, u32[]{:S(2)}) %collective-permute-start.7) | collective-permute-done | bytes 24608 | tf_op jit(solution)/shard_map/ppermute | solution.py:534
  19.3 0.3 collective-permute-start.9
  19.6 3.4 %collective-permute-start.8 = (f32[48,128]{1,0:T(8,128)S(1)}, f32[48,128]{1,0:T(8,128)S(1)}, u32[]{:S(2)}, u32[]{:S(2)}) collective-permute-start(f32[48,128]{1,0:T(8,128)S(1)} %add.29.own), channel_id=1, source_target_pairs={{0,5},{1,4},{4,1},{5,0},{8,13},{9,12},{12,9},{13,8},{2,7},{3,6},{6... | collective-permute-start | bytes 73736 | tf_op jit(solution)/shard_map/ppermute | solution.py:518
  23.0 0.0 collective-permute-done.10.c_1_
  23.0 0.1 shard_map.83.cotangent
  23.1 0.0 collective-permute-done.9.odd_in
  23.1 1.4 %collective-permute-done.8.even_in = f32[48,128]{1,0:T(8,128)S(1)} collective-permute-done((f32[48,128]{1,0:T(8,128)S(1)}, f32[48,128]{1,0:T(8,128)S(1)}, u32[]{:S(2)}, u32[]{:S(2)}) %collective-permute-start.8) | collective-permute-done | bytes 24608 | tf_op jit(solution)/shard_map/ppermute | solution.py:518
  24.5 0.6 %shard_map.84 = (f32[8,2,48,128]{3,2,1,0:T(8,128)S(1)}, f32[48,128]{1,0:T(8,128)S(1)}) custom-call(s32[2,4]{1,0:T(2,128)S(1)} %get-tuple-element.40.delays_0_, s32[2,4]{1,0:T(2,128)S(1)} %get-tuple-element.41.delays_1_, f32[2,4]{1,0:T(2,128)S(1)} %get-tuple-element.43.gains_0_, f32[2,4]{1,0:T(2,128)S(1)} %get-tuple-element.44.gains_1_, ...), custom_call_target="tpu_custom_call" | custom-call | flops 200000000 | bytes 6000000 | tf_op jit(solution)/shard_map/pallas_call | solution.py:495
  25.1 0.2 collective-permute-start.11
  25.3 1.0 %collective-permute-done.11 = f32[48,128]{1,0:T(8,128)S(1)} collective-permute-done((f32[48,128]{1,0:T(8,128)S(1)}, f32[48,128]{1,0:T(8,128)S(1)}, u32[]{:S(2)}, u32[]{:S(2)}) %collective-permute-start.11) | collective-permute-done | bytes 24608 | tf_op jit(solution)/shard_map/ppermute | solution.py:534
  26.4 0.2 collective-permute-start.13
  26.6 1.6 %collective-permute-start.12 = (f32[48,128]{1,0:T(8,128)S(1)}, f32[48,128]{1,0:T(8,128)S(1)}, u32[]{:S(2)}, u32[]{:S(2)}) collective-permute-start(f32[48,128]{1,0:T(8,128)S(1)} %add.30.own), channel_id=1, source_target_pairs={{0,5},{1,4},{4,1},{5,0},{8,13},{9,12},{12,9},{13,8},{2,7},{3,6},{6... | collective-permute-start | bytes 73736 | tf_op jit(solution)/shard_map/ppermute | solution.py:518
  28.2 0.0 collective-permute-done.13.odd_in
  28.2 1.6 %collective-permute-done.12.even_in = f32[48,128]{1,0:T(8,128)S(1)} collective-permute-done((f32[48,128]{1,0:T(8,128)S(1)}, f32[48,128]{1,0:T(8,128)S(1)}, u32[]{:S(2)}, u32[]{:S(2)}) %collective-permute-start.12) | collective-permute-done | bytes 24608 | tf_op jit(solution)/shard_map/ppermute | solution.py:518
  29.8 1.3 %shard_map.85 = (f32[4,2,48,128]{3,2,1,0:T(8,128)S(1)}, f32[4,2,48,128]{3,2,1,0:T(8,128)S(1)}, f32[48,128]{1,0:T(8,128)S(1)}) custom-call(s32[2,4]{1,0:T(2,128)S(1)} %get-tuple-element.40.delays_0_, s32[2,4]{1,0:T(2,128)S(1)} %get-tuple-element.41.delays_1_, s32[2,4]{1,0:T(2,128)S(1)} %get-tuple-element.39.shifts_0_, ...), custom_call_target="tpu_custom_call" | custom-call | flops 200000000 | bytes 6000000 | tf_op jit(solution)/shard_map/pallas_call | solution.py:495
  31.1 0.4 collective-permute-start.14
  31.5 0.9 %collective-permute-done.14 = f32[48,128]{1,0:T(8,128)S(1)} collective-permute-done((f32[48,128]{1,0:T(8,128)S(1)}, f32[48,128]{1,0:T(8,128)S(1)}, u32[]{:S(2)}, u32[]{:S(2)}) %collective-permute-start.14) | collective-permute-done | bytes 24608 | tf_op jit(solution)/shard_map/ppermute | solution.py:534
  32.4 0.3 collective-permute-start.16
  32.7 3.0 %collective-permute-start.15 = (f32[48,128]{1,0:T(8,128)S(1)}, f32[48,128]{1,0:T(8,128)S(1)}, u32[]{:S(2)}, u32[]{:S(2)}) collective-permute-start(f32[48,128]{1,0:T(8,128)S(1)} %add.31.own), channel_id=1, source_target_pairs={{0,5},{1,4},{4,1},{5,0},{8,13},{9,12},{12,9},{13,8},{2,7},{3,6},{6... | collective-permute-start | bytes 73736 | tf_op jit(solution)/shard_map/ppermute | solution.py:518
  35.7 1.1 %shard_map.86.taps1 = f32[8,128]{1,0:T(8,128)S(1)} custom-call(f32[4,2,48,128]{3,2,1,0:T(8,128)S(1)} %get-tuple-element.70.shifted, f32[4,2,48,128]{3,2,1,0:T(8,128)S(1)} %get-tuple-element.71.grad), custom_call_target="tpu_custom_call" | custom-call | flops 200000000 | bytes 6000000 | tf_op jit(solution)/shard_map/pallas_call | solution.py:495
  36.8 0.0 collective-permute-done.16.odd_in
  36.8 0.4 collective-permute-done.15.even_in
  37.2 1.0 %shard_map.87 = (f32[4,2,48,128]{3,2,1,0:T(8,128)S(1)}, f32[16,128]{1,0:T(8,128)S(1)}) custom-call(s32[2,4]{1,0:T(2,128)S(1)} %get-tuple-element.40.delays_0_, f32[4,2,48,128]{3,2,1,0:T(8,128)S(1)} %get-tuple-element.67.turned0, f32[4,2,48,128]{3,2,1,0:T(8,128)S(1)} %get-tuple-element.49.linear0_0_.linear0, f32[48,128]{1,0:T(8,128)S(1)} %add.31.own, ...), custom_call_target="tpu_custom_call" | custom-call | flops 200000000 | bytes 6000000 | tf_op jit(solution)/shard_map/pallas_call | solution.py:495
  38.3 0.2 collective-permute-start.17
  38.5 1.0 %collective-permute-done.17 = f32[16,128]{1,0:T(8,128)S(1)} collective-permute-done((f32[16,128]{1,0:T(8,128)S(1)}, f32[16,128]{1,0:T(8,128)S(1)}, u32[]{:S(2)}, u32[]{:S(2)}) %collective-permute-start.17) | collective-permute-done | bytes 8224 | tf_op jit(solution)/shard_map/ppermute | solution.py:534
  39.5 1.1 %collective-permute-start.20 = (f32[16,128]{1,0:T(8,128)S(1)}, f32[16,128]{1,0:T(8,128)S(1)}, u32[]{:S(2)}, u32[]{:S(2)}) collective-permute-start(f32[16,128]{1,0:T(8,128)S(1)} %add.32), channel_id=1, source_target_pairs={{0,13},{1,12},{4,9},{5,8},{8,5},{9,4},{12,1},{13,0},{2,15},{3,14},... | collective-permute-start | bytes 24584 | tf_op jit(solution)/shard_map/ppermute | solution.py:518
  40.6 1.9 %collective-permute-start.19 = (f32[16,128]{1,0:T(8,128)S(1)}, f32[16,128]{1,0:T(8,128)S(1)}, u32[]{:S(2)}, u32[]{:S(2)}) collective-permute-start(f32[16,128]{1,0:T(8,128)S(1)} %add.32), channel_id=1, source_target_pairs={{0,9},{1,8},{4,13},{5,12},{8,1},{9,0},{12,5},{13,4},{2,11},{3,10},... | collective-permute-start | bytes 24584 | tf_op jit(solution)/shard_map/ppermute | solution.py:518
  42.5 0.9 %collective-permute-start.18 = (f32[16,128]{1,0:T(8,128)S(1)}, f32[16,128]{1,0:T(8,128)S(1)}, u32[]{:S(2)}, u32[]{:S(2)}) collective-permute-start(f32[16,128]{1,0:T(8,128)S(1)} %add.32), channel_id=1, source_target_pairs={{0,5},{1,4},{4,1},{5,0},{8,13},{9,12},{12,9},{13,8},{2,7},{3,6},{6... | collective-permute-start | bytes 24584 | tf_op jit(solution)/shard_map/ppermute | solution.py:518
  43.4 1.2 %shard_map.88 = f32[4,1,2,4096]{3,2,1,0:T(2,128)} custom-call(s32[2,4]{1,0:T(2,128)S(1)} %get-tuple-element.39.shifts_0_, f32[4,2,48,128]{3,2,1,0:T(8,128)S(1)} %get-tuple-element.72.grad0, bf16[4,256,512]{2,1,0:T(8,128)(2,1)S(1)} %get-tuple-element.47.high, bf16[4,256,512]{2,1,0:T(8,128)(2,1)S(1)} %get-tuple-element.48.low), custom_call_target="tpu_custom_call" | custom-call | flops 200000000 | bytes 6000000 | tf_op jit(solution)/shard_map/pallas_call | solution.py:495
  44.6 0.0 collective-permute-done.20
  44.6 0.0 collective-permute-done.19
  44.6 1.0 %collective-permute-done.18 = f32[16,128]{1,0:T(8,128)S(1)} collective-permute-done((f32[16,128]{1,0:T(8,128)S(1)}, f32[16,128]{1,0:T(8,128)S(1)}, u32[]{:S(2)}, u32[]{:S(2)}) %collective-permute-start.18) | collective-permute-done | bytes 8224 | tf_op jit(solution)/shard_map/ppermute | solution.py:518
  45.5 0.6 %add_add_fusion = f32[16,128]{1,0:T(8,128)} fusion(f32[16,128]{1,0:T(8,128)S(1)} %collective-permute-done.19, f32[16,128]{1,0:T(8,128)S(1)} %collective-permute-done.20, f32[16,128]{1,0:T(8,128)S(1)} %add.32, f32[16,128]{1,0:T(8,128)S(1)} %collective-permute-done.18), kind=kLoop, calls=%fused_computation | loop fusion | flops 6144 | bytes 40960 | tf_op jit(solution)/shard_map/add | solution.py:570
  (6 shorter events, 0.0 us)
Async XLA Ops:
  1.8 5.9 %collective-permute-start.1 = (f32[4,2,3072]{2,1,0:T(2,128)S(1)}, f32[4,2,3072]{2,1,0:T(2,128)S(1)}, u32[]{:S(2)}, u32[]{:S(2)}) collective-permute-start(f32[4,2,3072]{2,1,0:T(2,128)S(1)} %get-tuple-element.45), channel_id=1, source_target_pairs={{0,4},{1,5},{4,0},{5,1},{8,12},{9,13},{12,8},{13,9},{2,6},{3,7},{6... | collective-permute-start | bytes 294920 | tf_op jit(solution)/shard_map/ppermute | solution.py:518
  4.9 2.8 %collective-permute-start.2 = (f32[4,2,3072]{2,1,0:T(2,128)S(1)}, f32[4,2,3072]{2,1,0:T(2,128)S(1)}, u32[]{:S(2)}, u32[]{:S(2)}) collective-permute-start(f32[4,2,3072]{2,1,0:T(2,128)S(1)} %get-tuple-element.46), channel_id=1, source_target_pairs={{0,1},{1,0},{4,8},{5,9},{8,4},{9,5},{12,13},{13,12},{2,3},{3,2},{6... | collective-permute-start | bytes 294920 | tf_op jit(solution)/shard_map/ppermute | solution.py:518
  4.9 8.6 %collective-permute-start = (f32[280,128]{1,0:T(8,128)S(1)}, f32[280,128]{1,0:T(8,128)S(1)}, u32[]{:S(2)}, u32[]{:S(2)}) collective-permute-start(f32[280,128]{1,0:T(8,128)S(1)} %get-tuple-element.38.pack), channel_id=1, source_target_pairs={{0,2},{1,3},{2,0},{3,1},{4,6},{5,7},{6,4},{7,5},{8,10},{9,11},{10,... | collective-permute-start | bytes 430088 | tf_op jit(solution)/shard_map/ppermute | solution.py:518
  6.4 16.6 %collective-permute-start.10 = (f32[4,2,32,128]{3,2,1,0:T(8,128)S(1)}, f32[4,2,32,128]{3,2,1,0:T(8,128)S(1)}, u32[]{:S(2)}, u32[]{:S(2)}) collective-permute-start(f32[4,2,32,128]{3,2,1,0:T(8,128)S(1)} %get-tuple-element.61.c_0_), channel_id=1, source_target_pairs={{0,2},{1,3},{2,0},{3,1},{4,6},{5,7},{6,4},{7,5},{8,10},{9,11},{10,... | collective-permute-start | bytes 393224 | tf_op jit(solution)/shard_map/ppermute | solution.py:518
  8.7 4.3 %collective-permute-start.5 = (f32[64,128]{1,0:T(8,128)S(1)}, f32[64,128]{1,0:T(8,128)S(1)}, u32[]{:S(2)}, u32[]{:S(2)}) collective-permute-start(f32[64,128]{1,0:T(8,128)S(1)} %get-tuple-element.54), channel_id=1, source_target_pairs={{0,1},{1,0},{2,3},{3,2},{4,5},{5,4},{6,7},{7,6},{8,9},{9,8},{10,11... | collective-permute-start | bytes 98312 | tf_op jit(solution)/shard_map/ppermute | solution.py:534
  8.7 6.0 %collective-permute-start.3 = (f32[4,2,1024]{2,1,0:T(2,128)S(1)}, f32[4,2,1024]{2,1,0:T(2,128)S(1)}, u32[]{:S(2)}, u32[]{:S(2)}) collective-permute-start(f32[4,2,1024]{2,1,0:T(2,128)S(1)} %get-tuple-element.50), channel_id=1, source_target_pairs={{0,6},{1,7},{2,4},{3,5},{4,2},{5,3},{6,0},{7,1},{8,14},{9,15},{10,... | collective-permute-start | bytes 98312 | tf_op jit(solution)/shard_map/ppermute | solution.py:563
  12.8 2.0 %collective-permute-start.4 = (f32[4,2,1024]{2,1,0:T(2,128)S(1)}, f32[4,2,1024]{2,1,0:T(2,128)S(1)}, u32[]{:S(2)}, u32[]{:S(2)}) collective-permute-start(f32[4,2,1024]{2,1,0:T(2,128)S(1)} %get-tuple-element.51), channel_id=1, source_target_pairs={{0,1},{1,0},{2,3},{3,2},{4,10},{5,11},{6,8},{7,9},{8,6},{9,7},{10,... | collective-permute-start | bytes 98312 | tf_op jit(solution)/shard_map/ppermute | solution.py:563
  12.9 3.4 %collective-permute-start.6 = (f32[64,128]{1,0:T(8,128)S(1)}, f32[64,128]{1,0:T(8,128)S(1)}, u32[]{:S(2)}, u32[]{:S(2)}) collective-permute-start(f32[64,128]{1,0:T(8,128)S(1)} %add.27), channel_id=1, source_target_pairs={{0,3},{1,2},{2,1},{3,0},{4,7},{5,6},{6,5},{7,4},{8,11},{9,10},{10,... | collective-permute-start | bytes 98312 | tf_op jit(solution)/shard_map/ppermute | solution.py:518
  18.0 1.3 %collective-permute-start.7 = (f32[48,128]{1,0:T(8,128)S(1)}, f32[48,128]{1,0:T(8,128)S(1)}, u32[]{:S(2)}, u32[]{:S(2)}) collective-permute-start(f32[48,128]{1,0:T(8,128)S(1)} %get-tuple-element.60), channel_id=1, source_target_pairs={{0,1},{1,0},{2,3},{3,2},{4,5},{5,4},{6,7},{7,6},{8,9},{9,8},{10,11... | collective-permute-start | bytes 73736 | tf_op jit(solution)/shard_map/ppermute | solution.py:534
  19.3 3.8 %collective-permute-start.9 = (f32[48,128]{1,0:T(8,128)S(1)}, f32[48,128]{1,0:T(8,128)S(1)}, u32[]{:S(2)}, u32[]{:S(2)}) collective-permute-start(f32[48,128]{1,0:T(8,128)S(1)} %add.29.own), channel_id=1, source_target_pairs={{0,1},{1,0},{4,9},{5,8},{8,5},{9,4},{12,13},{13,12},{2,3},{3,2},{6... | collective-permute-start | bytes 73736 | tf_op jit(solution)/shard_map/ppermute | solution.py:518
  19.6 4.9 %collective-permute-start.8 = (f32[48,128]{1,0:T(8,128)S(1)}, f32[48,128]{1,0:T(8,128)S(1)}, u32[]{:S(2)}, u32[]{:S(2)}) collective-permute-start(f32[48,128]{1,0:T(8,128)S(1)} %add.29.own), channel_id=1, source_target_pairs={{0,5},{1,4},{4,1},{5,0},{8,13},{9,12},{12,9},{13,8},{2,7},{3,6},{6... | collective-permute-start | bytes 73736 | tf_op jit(solution)/shard_map/ppermute | solution.py:518
  25.1 1.3 %collective-permute-start.11 = (f32[48,128]{1,0:T(8,128)S(1)}, f32[48,128]{1,0:T(8,128)S(1)}, u32[]{:S(2)}, u32[]{:S(2)}) collective-permute-start(f32[48,128]{1,0:T(8,128)S(1)} %get-tuple-element.63), channel_id=1, source_target_pairs={{0,1},{1,0},{2,3},{3,2},{4,5},{5,4},{6,7},{7,6},{8,9},{9,8},{10,11... | collective-permute-start | bytes 73736 | tf_op jit(solution)/shard_map/ppermute | solution.py:534
  26.4 1.8 %collective-permute-start.13 = (f32[48,128]{1,0:T(8,128)S(1)}, f32[48,128]{1,0:T(8,128)S(1)}, u32[]{:S(2)}, u32[]{:S(2)}) collective-permute-start(f32[48,128]{1,0:T(8,128)S(1)} %add.30.own), channel_id=1, source_target_pairs={{0,1},{1,0},{4,9},{5,8},{8,5},{9,4},{12,13},{13,12},{2,3},{3,2},{6... | collective-permute-start | bytes 73736 | tf_op jit(solution)/shard_map/ppermute | solution.py:518
  26.6 3.3 %collective-permute-start.12 = (f32[48,128]{1,0:T(8,128)S(1)}, f32[48,128]{1,0:T(8,128)S(1)}, u32[]{:S(2)}, u32[]{:S(2)}) collective-permute-start(f32[48,128]{1,0:T(8,128)S(1)} %add.30.own), channel_id=1, source_target_pairs={{0,5},{1,4},{4,1},{5,0},{8,13},{9,12},{12,9},{13,8},{2,7},{3,6},{6... | collective-permute-start | bytes 73736 | tf_op jit(solution)/shard_map/ppermute | solution.py:518
  31.1 1.3 %collective-permute-start.14 = (f32[48,128]{1,0:T(8,128)S(1)}, f32[48,128]{1,0:T(8,128)S(1)}, u32[]{:S(2)}, u32[]{:S(2)}) collective-permute-start(f32[48,128]{1,0:T(8,128)S(1)} %get-tuple-element.68), channel_id=1, source_target_pairs={{0,1},{1,0},{2,3},{3,2},{4,5},{5,4},{6,7},{7,6},{8,9},{9,8},{10,11... | collective-permute-start | bytes 73736 | tf_op jit(solution)/shard_map/ppermute | solution.py:534
  32.4 4.4 %collective-permute-start.16 = (f32[48,128]{1,0:T(8,128)S(1)}, f32[48,128]{1,0:T(8,128)S(1)}, u32[]{:S(2)}, u32[]{:S(2)}) collective-permute-start(f32[48,128]{1,0:T(8,128)S(1)} %add.31.own), channel_id=1, source_target_pairs={{0,1},{1,0},{4,9},{5,8},{8,5},{9,4},{12,13},{13,12},{2,3},{3,2},{6... | collective-permute-start | bytes 73736 | tf_op jit(solution)/shard_map/ppermute | solution.py:518
  32.7 4.5 %collective-permute-start.15 = (f32[48,128]{1,0:T(8,128)S(1)}, f32[48,128]{1,0:T(8,128)S(1)}, u32[]{:S(2)}, u32[]{:S(2)}) collective-permute-start(f32[48,128]{1,0:T(8,128)S(1)} %add.31.own), channel_id=1, source_target_pairs={{0,5},{1,4},{4,1},{5,0},{8,13},{9,12},{12,9},{13,8},{2,7},{3,6},{6... | collective-permute-start | bytes 73736 | tf_op jit(solution)/shard_map/ppermute | solution.py:518
  38.3 1.2 %collective-permute-start.17 = (f32[16,128]{1,0:T(8,128)S(1)}, f32[16,128]{1,0:T(8,128)S(1)}, u32[]{:S(2)}, u32[]{:S(2)}) collective-permute-start(f32[16,128]{1,0:T(8,128)S(1)} %get-tuple-element.73), channel_id=1, source_target_pairs={{0,1},{1,0},{2,3},{3,2},{4,5},{5,4},{6,7},{7,6},{8,9},{9,8},{10,11... | collective-permute-start | bytes 24584 | tf_op jit(solution)/shard_map/ppermute | solution.py:534
  39.5 5.1 %collective-permute-start.20 = (f32[16,128]{1,0:T(8,128)S(1)}, f32[16,128]{1,0:T(8,128)S(1)}, u32[]{:S(2)}, u32[]{:S(2)}) collective-permute-start(f32[16,128]{1,0:T(8,128)S(1)} %add.32), channel_id=1, source_target_pairs={{0,13},{1,12},{4,9},{5,8},{8,5},{9,4},{12,1},{13,0},{2,15},{3,14},... | collective-permute-start | bytes 24584 | tf_op jit(solution)/shard_map/ppermute | solution.py:518
  40.6 4.0 %collective-permute-start.19 = (f32[16,128]{1,0:T(8,128)S(1)}, f32[16,128]{1,0:T(8,128)S(1)}, u32[]{:S(2)}, u32[]{:S(2)}) collective-permute-start(f32[16,128]{1,0:T(8,128)S(1)} %add.32), channel_id=1, source_target_pairs={{0,9},{1,8},{4,13},{5,12},{8,1},{9,0},{12,5},{13,4},{2,11},{3,10},... | collective-permute-start | bytes 24584 | tf_op jit(solution)/shard_map/ppermute | solution.py:518
  42.5 3.1 %collective-permute-start.18 = (f32[16,128]{1,0:T(8,128)S(1)}, f32[16,128]{1,0:T(8,128)S(1)}, u32[]{:S(2)}, u32[]{:S(2)}) collective-permute-start(f32[16,128]{1,0:T(8,128)S(1)} %add.32), channel_id=1, source_target_pairs={{0,5},{1,4},{4,1},{5,0},{8,13},{9,12},{12,9},{13,8},{2,7},{3,6},{6... | collective-permute-start | bytes 24584 | tf_op jit(solution)/shard_map/ppermute | solution.py:518

commit v6 on v5

--- a/solution.py
+++ b/solution.py
@@ -633,6 +633,7 @@
         k_first, (delays[:1], shifts[:1], pack_out, sides[0], high0[0], low0[0]),
         [own_field, own_field, wide_part], (ext_wide, held_wide),
     )
+    sent, sides = lax.optimization_barrier((sent, sides))
     spread0 = summed(over_cores(sent), "band")
     linear0 = [linear]
     if doubled:

time: 46.3 us -> 44.9 us (0.970)
  starting transfers between devices: 23.9 us -> 22 us
  waiting for transfers between devices: 9.81 us -> 10.4 us
    ppermute x14, starting transfers between devices: 18.4 us -> 17.1 us  [swapped(): return lax.ppermute(x, (axis, 'pol'), pairs)]
    ppermute x2, starting transfers between devices: 4.19 us -> 3.12 us  [aslant(): return lax.ppermute(x, ('tm', 'band', 'pol'), pairs)]
    ppermute x5, waiting for transfers between devices: 3.77 us -> 4.51 us  [over_cores(): lax.ppermute(x, 'pol', [(p, cores - 1 - p) for p in range(cores)])]
    ppermute x2, waiting for transfers between devices: 0.63 us -> 0.01 us  [aslant(): return lax.ppermute(x, ('tm', 'band', 'pol'), pairs)]
  transfers between devices with their start and end apart: 21 -> 21, of which waited for: 11 -> 11; matrix products, arithmetic and copies ran while one was open for 0% -> 0% of each run, Pallas kernels for 15% -> 16%
where the time goes in v6:
time: 44.9 us; the launch traced here: 44.7 us
  starting transfers between devices  22 us (49%)
  Pallas kernels  11 us (24%)
  waiting for transfers between devices  10.4 us (23%)
  between operations  0.73 us (2%)
  other arithmetic  0.63 us (1%)
    ppermute x14, starting transfers between devices, swapped(): return lax.ppermute(x, (axis, 'pol'), pairs)  17.1 us
    pallas_call x11, Pallas kernels, call(): pl.pallas_call(kernel, out_shape=shapes, in_specs=jax.tree.map(lambda _:...  9.86 us
    ppermute x14, waiting for transfers between devices, swapped(): return lax.ppermute(x, (axis, 'pol'), pairs)  5.84 us
    ppermute x5, waiting for transfers between devices, over_cores(): lax.ppermute(x, 'pol', [(p, cores - 1 - p) for p in range(cores)])  4.51 us
    ppermute x2, starting transfers between devices, aslant(): return lax.ppermute(x, ('tm', 'band', 'pol'), pairs)  3.12 us
    ppermute x5, starting transfers between devices, over_cores(): lax.ppermute(x, 'pol', [(p, cores - 1 - p) for p in range(cores)])  1.77 us
    pallas_call x1, Pallas kernels, on_device(): pl.pallas_call(k_begin, out_shape=[cut, cut, near, near, pack, shape(own,...  1.18 us
  transfers between devices with their start and end apart: 21, of which 11 were waited for; matrix products, arithmetic and copies ran while one was open for 0% of the time, Pallas kernels for 16%

profile of v6, /device:TPU:0, one launch (start us, length us, event | category | flops | bytes accessed | tf_op | source)
XLA Modules:
  0.0 44.7 jit_solution(15651965854506495207)
XLA Ops:
  0.6 1.2 %shard_map.77 = (f32[4,2,3072]{2,1,0:T(2,128)S(1)}, f32[4,2,3072]{2,1,0:T(2,128)S(1)}, f32[4,2,1024]{2,1,0:T(2,128)S(1)}, f32[4,2,1024]{2,1,0:T(2,128)S(1)}, f32...) custom-call(f32[4,1,2,4096]{3,2,1,0:T(2,128)} %signal.1, f32[4,1,2,4096]{3,2,1,0:T(2,128)} %cotangent.1, ...), custom_call_target="tpu_custom_call" | custom-call | flops 100000000 | bytes 1000000 | tf_op jit(solution)/shard_map/pallas_call | solution.py:609
  1.8 3.1 %collective-permute-start.1 = (f32[4,2,3072]{2,1,0:T(2,128)S(1)}, f32[4,2,3072]{2,1,0:T(2,128)S(1)}, u32[]{:S(2)}, u32[]{:S(2)}) collective-permute-start(f32[4,2,3072]{2,1,0:T(2,128)S(1)} %get-tuple-element.50), channel_id=1, source_target_pairs={{0,4},{1,5},{4,0},{5,1},{8,12},{9,13},{12,8},{13,9},{2,6},{3,7},{6... | collective-permute-start | bytes 294920 | tf_op jit(solution)/shard_map/ppermute | solution.py:518
  4.9 0.0 collective-permute-start.2
  4.9 1.5 %collective-permute-start = (f32[280,128]{1,0:T(8,128)S(1)}, f32[280,128]{1,0:T(8,128)S(1)}, u32[]{:S(2)}, u32[]{:S(2)}) collective-permute-start(f32[280,128]{1,0:T(8,128)S(1)} %get-tuple-element.43.pack), channel_id=1, source_target_pairs={{0,2},{1,3},{2,0},{3,1},{4,6},{5,7},{6,4},{7,5},{8,10},{9,11},{10,... | collective-permute-start | bytes 430088 | tf_op jit(solution)/shard_map/ppermute | solution.py:518
  6.4 3.1 %collective-permute-start.3 = (f32[4,2,1024]{2,1,0:T(2,128)S(1)}, f32[4,2,1024]{2,1,0:T(2,128)S(1)}, u32[]{:S(2)}, u32[]{:S(2)}) collective-permute-start(f32[4,2,1024]{2,1,0:T(2,128)S(1)} %get-tuple-element.56), channel_id=1, source_target_pairs={{0,6},{1,7},{2,4},{3,5},{4,2},{5,3},{6,0},{7,1},{8,14},{9,15},{10,... | collective-permute-start | bytes 98312 | tf_op jit(solution)/shard_map/ppermute | solution.py:563
  9.5 0.0 collective-permute-start.4
  9.5 0.6 %shard_map.78 = (s32[2,4]{1,0:T(2,128)S(1)}, s32[2,4]{1,0:T(2,128)S(1)}, f32[2,4]{1,0:T(2,128)S(1)}, bf16[4,256,512]{2,1,0:T(8,128)(2,1)S(1)}, bf16[4,256,512]{2...) custom-call(f32[280,128]{1,0:T(8,128)S(1)} %get-tuple-element.43.pack), custom_call_target="tpu_custom_call" | custom-call | flops 200000000 | bytes 6000000 | tf_op jit(solution)/shard_map/pallas_call | solution.py:495
  10.2 0.0 collective-permute-done.1.sides_0_.s_0__0_
  10.2 1.6 %collective-permute-start.10 = (f32[4,2,32,128]{3,2,1,0:T(8,128)S(1)}, f32[4,2,32,128]{3,2,1,0:T(8,128)S(1)}, u32[]{:S(2)}, u32[]{:S(2)}) collective-permute-start(f32[4,2,32,128]{3,2,1,0:T(8,128)S(1)} %get-tuple-element.69.c_0_), channel_id=1, source_target_pairs={{0,2},{1,3},{2,0},{3,1},{4,6},{5,7},{6,4},{7,5},{8,10},{9,11},{10,... | collective-permute-start | bytes 393224 | tf_op jit(solution)/shard_map/ppermute | solution.py:518
  11.7 0.0 collective-permute-done.2.sides_1_.s_0__1_
  11.7 0.9 %shard_map.80 = (f32[4,2,48,128]{3,2,1,0:T(8,128)S(1)}, f32[4,2,48,128]{3,2,1,0:T(8,128)S(1)}, f32[64,128]{1,0:T(8,128)S(1)}) custom-call(s32[2,4]{1,0:T(2,128)S(1)} %get-tuple-element.45.delays_0_, s32[2,4]{1,0:T(2,128)S(1)} %get-tuple-element.44.shifts_0_, f32[280,128]{1,0:T(8,128)S(1)} %get-tuple-element.43.pack, ...), custom_call_target="tpu_custom_call" | custom-call | flops 200000000 | bytes 6000000 | tf_op jit(solution)/shard_map/pallas_call | solution.py:495
  12.7 0.0 collective-permute-done.3.sides_0_.s_1__0_
  12.7 0.0 collective-permute-done.4.sides_1_.s_1__1_
  12.7 0.3 collective-permute-start.5
  13.0 1.0 %collective-permute-done.5 = f32[64,128]{1,0:T(8,128)S(1)} collective-permute-done((f32[64,128]{1,0:T(8,128)S(1)}, f32[64,128]{1,0:T(8,128)S(1)}, u32[]{:S(2)}, u32[]{:S(2)}) %collective-permute-start.5) | collective-permute-done | bytes 32800 | tf_op jit(solution)/shard_map/ppermute | solution.py:534
  14.0 0.4 collective-permute-start.6
  14.3 0.0 collective-permute-done.pack
  14.4 0.6 %shard_map.79 = (s32[2,4]{1,0:T(2,128)S(1)}, s32[2,4]{1,0:T(2,128)S(1)}, f32[2,4]{1,0:T(2,128)S(1)}, bf16[4,256,512]{2,1,0:T(8,128)(2,1)S(1)}, bf16[4,256,512]{2...) custom-call(f32[280,128]{1,0:T(8,128)S(1)} %collective-permute-done.pack), custom_call_target="tpu_custom_call" | custom-call | flops 200000000 | bytes 6000000 | tf_op jit(solution)/shard_map/pallas_call | solution.py:495
  15.0 0.8 %shard_map.81.linear0_1_ = f32[4,2,48,128]{3,2,1,0:T(8,128)S(1)} custom-call(s32[2,4]{1,0:T(2,128)S(1)} %get-tuple-element.47.shifts_0_.shifts_1_, f32[280,128]{1,0:T(8,128)S(1)} %collective-permute-done.pack, f32[4,2,1024]{2,1,0:T(2,128)S(1)} %collective-permute-done.3.sides_0_.s_1__0_, f32[4,2,1024]{2,1,0:T(2,128)S(1)} %collective-permute-done.4.sides_1_.s_1__1_, ...), custom_call_target="tpu_custom_call" | custom-call | flops 200000000 | bytes 6000000 | tf_op jit(solution)/shard_map/pallas_call | solution.py:495
  15.8 1.6 %collective-permute-done.6 = f32[64,128]{1,0:T(8,128)S(1)} collective-permute-done((f32[64,128]{1,0:T(8,128)S(1)}, f32[64,128]{1,0:T(8,128)S(1)}, u32[]{:S(2)}, u32[]{:S(2)}) %collective-permute-start.6) | collective-permute-done | bytes 32800 | tf_op jit(solution)/shard_map/ppermute | solution.py:518
  17.3 1.7 %shard_map.82 = (f32[4,48,128]{2,1,0:T(8,128)S(1)}, f32[4,48,128]{2,1,0:T(8,128)S(1)}, f32[8,2,48,128]{3,2,1,0:T(8,128)S(1)}, f32[4,2,48,128]{3,2,1,0:T(8,128)S(...) custom-call(s32[2,4]{1,0:T(2,128)S(1)} %get-tuple-element.45.delays_0_, ...), custom_call_target="tpu_custom_call" | custom-call | flops 200000000 | bytes 6000000 | tf_op jit(solution)/shard_map/pallas_call | solution.py:495
  19.0 0.3 collective-permute-start.7
  19.3 1.0 %collective-permute-done.7 = f32[48,128]{1,0:T(8,128)S(1)} collective-permute-done((f32[48,128]{1,0:T(8,128)S(1)}, f32[48,128]{1,0:T(8,128)S(1)}, u32[]{:S(2)}, u32[]{:S(2)}) %collective-permute-start.7) | collective-permute-done | bytes 24608 | tf_op jit(solution)/shard_map/ppermute | solution.py:534
  20.2 1.8 %collective-permute-start.8 = (f32[48,128]{1,0:T(8,128)S(1)}, f32[48,128]{1,0:T(8,128)S(1)}, u32[]{:S(2)}, u32[]{:S(2)}) collective-permute-start(f32[48,128]{1,0:T(8,128)S(1)} %add.29.own), channel_id=1, source_target_pairs={{0,5},{1,4},{4,1},{5,0},{8,13},{9,12},{12,9},{13,8},{2,7},{3,6},{6... | collective-permute-start | bytes 73736 | tf_op jit(solution)/shard_map/ppermute | solution.py:518
  22.1 0.3 collective-permute-start.9
  22.4 0.0 collective-permute-done.10.c_1_
  22.4 0.1 shard_map.83.cotangent
  22.5 1.1 %collective-permute-done.8.even_in = f32[48,128]{1,0:T(8,128)S(1)} collective-permute-done((f32[48,128]{1,0:T(8,128)S(1)}, f32[48,128]{1,0:T(8,128)S(1)}, u32[]{:S(2)}, u32[]{:S(2)}) %collective-permute-start.8) | collective-permute-done | bytes 24608 | tf_op jit(solution)/shard_map/ppermute | solution.py:518
  23.6 0.0 collective-permute-done.9.odd_in
  23.6 0.6 %shard_map.84 = (f32[8,2,48,128]{3,2,1,0:T(8,128)S(1)}, f32[48,128]{1,0:T(8,128)S(1)}) custom-call(s32[2,4]{1,0:T(2,128)S(1)} %get-tuple-element.45.delays_0_, s32[2,4]{1,0:T(2,128)S(1)} %get-tuple-element.46.delays_1_, f32[2,4]{1,0:T(2,128)S(1)} %get-tuple-element.48.gains_0_, f32[2,4]{1,0:T(2,128)S(1)} %get-tuple-element.49.gains_1_, ...), custom_call_target="tpu_custom_call" | custom-call | flops 200000000 | bytes 6000000 | tf_op jit(solution)/shard_map/pallas_call | solution.py:495
  24.2 0.4 collective-permute-start.11
  24.6 0.9 %collective-permute-done.11 = f32[48,128]{1,0:T(8,128)S(1)} collective-permute-done((f32[48,128]{1,0:T(8,128)S(1)}, f32[48,128]{1,0:T(8,128)S(1)}, u32[]{:S(2)}, u32[]{:S(2)}) %collective-permute-start.11) | collective-permute-done | bytes 24608 | tf_op jit(solution)/shard_map/ppermute | solution.py:534
  25.5 1.8 %collective-permute-start.12 = (f32[48,128]{1,0:T(8,128)S(1)}, f32[48,128]{1,0:T(8,128)S(1)}, u32[]{:S(2)}, u32[]{:S(2)}) collective-permute-start(f32[48,128]{1,0:T(8,128)S(1)} %add.30.own), channel_id=1, source_target_pairs={{0,5},{1,4},{4,1},{5,0},{8,13},{9,12},{12,9},{13,8},{2,7},{3,6},{6... | collective-permute-start | bytes 73736 | tf_op jit(solution)/shard_map/ppermute | solution.py:518
  27.3 0.3 collective-permute-start.13
  27.6 1.2 %collective-permute-done.12.even_in = f32[48,128]{1,0:T(8,128)S(1)} collective-permute-done((f32[48,128]{1,0:T(8,128)S(1)}, f32[48,128]{1,0:T(8,128)S(1)}, u32[]{:S(2)}, u32[]{:S(2)}) %collective-permute-start.12) | collective-permute-done | bytes 24608 | tf_op jit(solution)/shard_map/ppermute | solution.py:518
  28.8 0.0 collective-permute-done.13.odd_in
  28.8 1.3 %shard_map.85 = (f32[4,2,48,128]{3,2,1,0:T(8,128)S(1)}, f32[4,2,48,128]{3,2,1,0:T(8,128)S(1)}, f32[48,128]{1,0:T(8,128)S(1)}) custom-call(s32[2,4]{1,0:T(2,128)S(1)} %get-tuple-element.45.delays_0_, s32[2,4]{1,0:T(2,128)S(1)} %get-tuple-element.46.delays_1_, s32[2,4]{1,0:T(2,128)S(1)} %get-tuple-element.44.shifts_0_, ...), custom_call_target="tpu_custom_call" | custom-call | flops 200000000 | bytes 6000000 | tf_op jit(solution)/shard_map/pallas_call | solution.py:495
  30.1 0.4 collective-permute-start.14
  30.5 0.9 %collective-permute-done.14 = f32[48,128]{1,0:T(8,128)S(1)} collective-permute-done((f32[48,128]{1,0:T(8,128)S(1)}, f32[48,128]{1,0:T(8,128)S(1)}, u32[]{:S(2)}, u32[]{:S(2)}) %collective-permute-start.14) | collective-permute-done | bytes 24608 | tf_op jit(solution)/shard_map/ppermute | solution.py:534
  31.4 1.8 %collective-permute-start.15 = (f32[48,128]{1,0:T(8,128)S(1)}, f32[48,128]{1,0:T(8,128)S(1)}, u32[]{:S(2)}, u32[]{:S(2)}) collective-permute-start(f32[48,128]{1,0:T(8,128)S(1)} %add.31.own), channel_id=1, source_target_pairs={{0,5},{1,4},{4,1},{5,0},{8,13},{9,12},{12,9},{13,8},{2,7},{3,6},{6... | collective-permute-start | bytes 73736 | tf_op jit(solution)/shard_map/ppermute | solution.py:518
  33.2 0.3 collective-permute-start.16
  33.5 1.1 %shard_map.86.taps1 = f32[8,128]{1,0:T(8,128)S(1)} custom-call(f32[4,2,48,128]{3,2,1,0:T(8,128)S(1)} %get-tuple-element.80.shifted, f32[4,2,48,128]{3,2,1,0:T(8,128)S(1)} %get-tuple-element.81.grad), custom_call_target="tpu_custom_call" | custom-call | flops 200000000 | bytes 6000000 | tf_op jit(solution)/shard_map/pallas_call | solution.py:495
  34.6 0.1 collective-permute-done.15.even_in
  34.7 0.0 collective-permute-done.16.odd_in
  34.7 1.0 %shard_map.87 = (f32[4,2,48,128]{3,2,1,0:T(8,128)S(1)}, f32[16,128]{1,0:T(8,128)S(1)}) custom-call(s32[2,4]{1,0:T(2,128)S(1)} %get-tuple-element.45.delays_0_, f32[4,2,48,128]{3,2,1,0:T(8,128)S(1)} %get-tuple-element.77.turned0, f32[4,2,48,128]{3,2,1,0:T(8,128)S(1)} %get-tuple-element.54.linear0_0_.linear0, f32[48,128]{1,0:T(8,128)S(1)} %add.31.own, ...), custom_call_target="tpu_custom_call" | custom-call | flops 200000000 | bytes 6000000 | tf_op jit(solution)/shard_map/pallas_call | solution.py:495
  35.7 0.4 collective-permute-start.17
  36.1 0.8 %collective-permute-done.17 = f32[16,128]{1,0:T(8,128)S(1)} collective-permute-done((f32[16,128]{1,0:T(8,128)S(1)}, f32[16,128]{1,0:T(8,128)S(1)}, u32[]{:S(2)}, u32[]{:S(2)}) %collective-permute-start.17) | collective-permute-done | bytes 8224 | tf_op jit(solution)/shard_map/ppermute | solution.py:534
  36.9 1.5 %collective-permute-start.19 = (f32[16,128]{1,0:T(8,128)S(1)}, f32[16,128]{1,0:T(8,128)S(1)}, u32[]{:S(2)}, u32[]{:S(2)}) collective-permute-start(f32[16,128]{1,0:T(8,128)S(1)} %add.32), channel_id=1, source_target_pairs={{0,9},{1,8},{4,13},{5,12},{8,1},{9,0},{12,5},{13,4},{2,11},{3,10},... | collective-permute-start | bytes 24584 | tf_op jit(solution)/shard_map/ppermute | solution.py:518
  38.4 2.6 %collective-permute-start.20 = (f32[16,128]{1,0:T(8,128)S(1)}, f32[16,128]{1,0:T(8,128)S(1)}, u32[]{:S(2)}, u32[]{:S(2)}) collective-permute-start(f32[16,128]{1,0:T(8,128)S(1)} %add.32), channel_id=1, source_target_pairs={{0,13},{1,12},{4,9},{5,8},{8,5},{9,4},{12,1},{13,0},{2,15},{3,14},... | collective-permute-start | bytes 24584 | tf_op jit(solution)/shard_map/ppermute | solution.py:518
  41.1 0.0 collective-permute-start.18
  41.1 1.2 %shard_map.88 = f32[4,1,2,4096]{3,2,1,0:T(2,128)} custom-call(s32[2,4]{1,0:T(2,128)S(1)} %get-tuple-element.44.shifts_0_, f32[4,2,48,128]{3,2,1,0:T(8,128)S(1)} %get-tuple-element.82.grad0, bf16[4,256,512]{2,1,0:T(8,128)(2,1)S(1)} %get-tuple-element.52.high, bf16[4,256,512]{2,1,0:T(8,128)(2,1)S(1)} %get-tuple-element.53.low), custom_call_target="tpu_custom_call" | custom-call | flops 200000000 | bytes 6000000 | tf_op jit(solution)/shard_map/pallas_call | solution.py:495
  42.3 0.0 collective-permute-done.19
  42.3 1.1 %collective-permute-done.20 = f32[16,128]{1,0:T(8,128)S(1)} collective-permute-done((f32[16,128]{1,0:T(8,128)S(1)}, f32[16,128]{1,0:T(8,128)S(1)}, u32[]{:S(2)}, u32[]{:S(2)}) %collective-permute-start.20) | collective-permute-done | bytes 8224 | tf_op jit(solution)/shard_map/ppermute | solution.py:518
  43.3 0.8 %collective-permute-done.18 = f32[16,128]{1,0:T(8,128)S(1)} collective-permute-done((f32[16,128]{1,0:T(8,128)S(1)}, f32[16,128]{1,0:T(8,128)S(1)}, u32[]{:S(2)}, u32[]{:S(2)}) %collective-permute-start.18) | collective-permute-done | bytes 8224 | tf_op jit(solution)/shard_map/ppermute | solution.py:518
  44.1 0.6 %add_add_fusion = f32[16,128]{1,0:T(8,128)} fusion(f32[16,128]{1,0:T(8,128)S(1)} %collective-permute-done.19, f32[16,128]{1,0:T(8,128)S(1)} %collective-permute-done.20, f32[16,128]{1,0:T(8,128)S(1)} %add.32, f32[16,128]{1,0:T(8,128)S(1)} %collective-permute-done.18), kind=kLoop, calls=%fused_computation | loop fusion | flops 6144 | bytes 40960 | tf_op jit(solution)/shard_map/add | solution.py:570
  (6 shorter events, 0.0 us)
Async XLA Ops:
  1.8 8.3 %collective-permute-start.1 = (f32[4,2,3072]{2,1,0:T(2,128)S(1)}, f32[4,2,3072]{2,1,0:T(2,128)S(1)}, u32[]{:S(2)}, u32[]{:S(2)}) collective-permute-start(f32[4,2,3072]{2,1,0:T(2,128)S(1)} %get-tuple-element.50), channel_id=1, source_target_pairs={{0,4},{1,5},{4,0},{5,1},{8,12},{9,13},{12,8},{13,9},{2,6},{3,7},{6... | collective-permute-start | bytes 294920 | tf_op jit(solution)/shard_map/ppermute | solution.py:518
  4.9 6.8 %collective-permute-start.2 = (f32[4,2,3072]{2,1,0:T(2,128)S(1)}, f32[4,2,3072]{2,1,0:T(2,128)S(1)}, u32[]{:S(2)}, u32[]{:S(2)}) collective-permute-start(f32[4,2,3072]{2,1,0:T(2,128)S(1)} %get-tuple-element.51), channel_id=1, source_target_pairs={{0,1},{1,0},{4,8},{5,9},{8,4},{9,5},{12,13},{13,12},{2,3},{3,2},{6... | collective-permute-start | bytes 294920 | tf_op jit(solution)/shard_map/ppermute | solution.py:518
  4.9 9.4 %collective-permute-start = (f32[280,128]{1,0:T(8,128)S(1)}, f32[280,128]{1,0:T(8,128)S(1)}, u32[]{:S(2)}, u32[]{:S(2)}) collective-permute-start(f32[280,128]{1,0:T(8,128)S(1)} %get-tuple-element.43.pack), channel_id=1, source_target_pairs={{0,2},{1,3},{2,0},{3,1},{4,6},{5,7},{6,4},{7,5},{8,10},{9,11},{10,... | collective-permute-start | bytes 430088 | tf_op jit(solution)/shard_map/ppermute | solution.py:518
  6.4 6.3 %collective-permute-start.3 = (f32[4,2,1024]{2,1,0:T(2,128)S(1)}, f32[4,2,1024]{2,1,0:T(2,128)S(1)}, u32[]{:S(2)}, u32[]{:S(2)}) collective-permute-start(f32[4,2,1024]{2,1,0:T(2,128)S(1)} %get-tuple-element.56), channel_id=1, source_target_pairs={{0,6},{1,7},{2,4},{3,5},{4,2},{5,3},{6,0},{7,1},{8,14},{9,15},{10,... | collective-permute-start | bytes 98312 | tf_op jit(solution)/shard_map/ppermute | solution.py:563
  9.5 3.2 %collective-permute-start.4 = (f32[4,2,1024]{2,1,0:T(2,128)S(1)}, f32[4,2,1024]{2,1,0:T(2,128)S(1)}, u32[]{:S(2)}, u32[]{:S(2)}) collective-permute-start(f32[4,2,1024]{2,1,0:T(2,128)S(1)} %get-tuple-element.57), channel_id=1, source_target_pairs={{0,1},{1,0},{2,3},{3,2},{4,10},{5,11},{6,8},{7,9},{8,6},{9,7},{10,... | collective-permute-start | bytes 98312 | tf_op jit(solution)/shard_map/ppermute | solution.py:563
  10.2 12.3 %collective-permute-start.10 = (f32[4,2,32,128]{3,2,1,0:T(8,128)S(1)}, f32[4,2,32,128]{3,2,1,0:T(8,128)S(1)}, u32[]{:S(2)}, u32[]{:S(2)}) collective-permute-start(f32[4,2,32,128]{3,2,1,0:T(8,128)S(1)} %get-tuple-element.69.c_0_), channel_id=1, source_target_pairs={{0,2},{1,3},{2,0},{3,1},{4,6},{5,7},{6,4},{7,5},{8,10},{9,11},{10,... | collective-permute-start | bytes 393224 | tf_op jit(solution)/shard_map/ppermute | solution.py:518
  12.7 1.3 %collective-permute-start.5 = (f32[64,128]{1,0:T(8,128)S(1)}, f32[64,128]{1,0:T(8,128)S(1)}, u32[]{:S(2)}, u32[]{:S(2)}) collective-permute-start(f32[64,128]{1,0:T(8,128)S(1)} %get-tuple-element.62), channel_id=1, source_target_pairs={{0,1},{1,0},{2,3},{3,2},{4,5},{5,4},{6,7},{7,6},{8,9},{9,8},{10,11... | collective-permute-start | bytes 98312 | tf_op jit(solution)/shard_map/ppermute | solution.py:534
  14.0 3.3 %collective-permute-start.6 = (f32[64,128]{1,0:T(8,128)S(1)}, f32[64,128]{1,0:T(8,128)S(1)}, u32[]{:S(2)}, u32[]{:S(2)}) collective-permute-start(f32[64,128]{1,0:T(8,128)S(1)} %add.27), channel_id=1, source_target_pairs={{0,3},{1,2},{2,1},{3,0},{4,7},{5,6},{6,5},{7,4},{8,11},{9,10},{10,... | collective-permute-start | bytes 98312 | tf_op jit(solution)/shard_map/ppermute | solution.py:518
  19.0 1.3 %collective-permute-start.7 = (f32[48,128]{1,0:T(8,128)S(1)}, f32[48,128]{1,0:T(8,128)S(1)}, u32[]{:S(2)}, u32[]{:S(2)}) collective-permute-start(f32[48,128]{1,0:T(8,128)S(1)} %get-tuple-element.68), channel_id=1, source_target_pairs={{0,1},{1,0},{2,3},{3,2},{4,5},{5,4},{6,7},{7,6},{8,9},{9,8},{10,11... | collective-permute-start | bytes 73736 | tf_op jit(solution)/shard_map/ppermute | solution.py:534
  20.2 3.4 %collective-permute-start.8 = (f32[48,128]{1,0:T(8,128)S(1)}, f32[48,128]{1,0:T(8,128)S(1)}, u32[]{:S(2)}, u32[]{:S(2)}) collective-permute-start(f32[48,128]{1,0:T(8,128)S(1)} %add.29.own), channel_id=1, source_target_pairs={{0,5},{1,4},{4,1},{5,0},{8,13},{9,12},{12,9},{13,8},{2,7},{3,6},{6... | collective-permute-start | bytes 73736 | tf_op jit(solution)/shard_map/ppermute | solution.py:518
  22.1 1.5 %collective-permute-start.9 = (f32[48,128]{1,0:T(8,128)S(1)}, f32[48,128]{1,0:T(8,128)S(1)}, u32[]{:S(2)}, u32[]{:S(2)}) collective-permute-start(f32[48,128]{1,0:T(8,128)S(1)} %add.29.own), channel_id=1, source_target_pairs={{0,1},{1,0},{4,9},{5,8},{8,5},{9,4},{12,13},{13,12},{2,3},{3,2},{6... | collective-permute-start | bytes 73736 | tf_op jit(solution)/shard_map/ppermute | solution.py:518
  24.2 1.3 %collective-permute-start.11 = (f32[48,128]{1,0:T(8,128)S(1)}, f32[48,128]{1,0:T(8,128)S(1)}, u32[]{:S(2)}, u32[]{:S(2)}) collective-permute-start(f32[48,128]{1,0:T(8,128)S(1)} %get-tuple-element.73), channel_id=1, source_target_pairs={{0,1},{1,0},{2,3},{3,2},{4,5},{5,4},{6,7},{7,6},{8,9},{9,8},{10,11... | collective-permute-start | bytes 73736 | tf_op jit(solution)/shard_map/ppermute | solution.py:534
  25.5 3.3 %collective-permute-start.12 = (f32[48,128]{1,0:T(8,128)S(1)}, f32[48,128]{1,0:T(8,128)S(1)}, u32[]{:S(2)}, u32[]{:S(2)}) collective-permute-start(f32[48,128]{1,0:T(8,128)S(1)} %add.30.own), channel_id=1, source_target_pairs={{0,5},{1,4},{4,1},{5,0},{8,13},{9,12},{12,9},{13,8},{2,7},{3,6},{6... | collective-permute-start | bytes 73736 | tf_op jit(solution)/shard_map/ppermute | solution.py:518
  27.3 1.5 %collective-permute-start.13 = (f32[48,128]{1,0:T(8,128)S(1)}, f32[48,128]{1,0:T(8,128)S(1)}, u32[]{:S(2)}, u32[]{:S(2)}) collective-permute-start(f32[48,128]{1,0:T(8,128)S(1)} %add.30.own), channel_id=1, source_target_pairs={{0,1},{1,0},{4,9},{5,8},{8,5},{9,4},{12,13},{13,12},{2,3},{3,2},{6... | collective-permute-start | bytes 73736 | tf_op jit(solution)/shard_map/ppermute | solution.py:518
  30.1 1.3 %collective-permute-start.14 = (f32[48,128]{1,0:T(8,128)S(1)}, f32[48,128]{1,0:T(8,128)S(1)}, u32[]{:S(2)}, u32[]{:S(2)}) collective-permute-start(f32[48,128]{1,0:T(8,128)S(1)} %get-tuple-element.78), channel_id=1, source_target_pairs={{0,1},{1,0},{2,3},{3,2},{4,5},{5,4},{6,7},{7,6},{8,9},{9,8},{10,11... | collective-permute-start | bytes 73736 | tf_op jit(solution)/shard_map/ppermute | solution.py:534
  31.4 3.3 %collective-permute-start.15 = (f32[48,128]{1,0:T(8,128)S(1)}, f32[48,128]{1,0:T(8,128)S(1)}, u32[]{:S(2)}, u32[]{:S(2)}) collective-permute-start(f32[48,128]{1,0:T(8,128)S(1)} %add.31.own), channel_id=1, source_target_pairs={{0,5},{1,4},{4,1},{5,0},{8,13},{9,12},{12,9},{13,8},{2,7},{3,6},{6... | collective-permute-start | bytes 73736 | tf_op jit(solution)/shard_map/ppermute | solution.py:518
  33.2 1.5 %collective-permute-start.16 = (f32[48,128]{1,0:T(8,128)S(1)}, f32[48,128]{1,0:T(8,128)S(1)}, u32[]{:S(2)}, u32[]{:S(2)}) collective-permute-start(f32[48,128]{1,0:T(8,128)S(1)} %add.31.own), channel_id=1, source_target_pairs={{0,1},{1,0},{4,9},{5,8},{8,5},{9,4},{12,13},{13,12},{2,3},{3,2},{6... | collective-permute-start | bytes 73736 | tf_op jit(solution)/shard_map/ppermute | solution.py:518
  35.7 1.2 %collective-permute-start.17 = (f32[16,128]{1,0:T(8,128)S(1)}, f32[16,128]{1,0:T(8,128)S(1)}, u32[]{:S(2)}, u32[]{:S(2)}) collective-permute-start(f32[16,128]{1,0:T(8,128)S(1)} %get-tuple-element.83), channel_id=1, source_target_pairs={{0,1},{1,0},{2,3},{3,2},{4,5},{5,4},{6,7},{7,6},{8,9},{9,8},{10,11... | collective-permute-start | bytes 24584 | tf_op jit(solution)/shard_map/ppermute | solution.py:534
  36.9 5.3 %collective-permute-start.19 = (f32[16,128]{1,0:T(8,128)S(1)}, f32[16,128]{1,0:T(8,128)S(1)}, u32[]{:S(2)}, u32[]{:S(2)}) collective-permute-start(f32[16,128]{1,0:T(8,128)S(1)} %add.32), channel_id=1, source_target_pairs={{0,9},{1,8},{4,13},{5,12},{8,1},{9,0},{12,5},{13,4},{2,11},{3,10},... | collective-permute-start | bytes 24584 | tf_op jit(solution)/shard_map/ppermute | solution.py:518
  38.4 4.9 %collective-permute-start.20 = (f32[16,128]{1,0:T(8,128)S(1)}, f32[16,128]{1,0:T(8,128)S(1)}, u32[]{:S(2)}, u32[]{:S(2)}) collective-permute-start(f32[16,128]{1,0:T(8,128)S(1)} %add.32), channel_id=1, source_target_pairs={{0,13},{1,12},{4,9},{5,8},{8,5},{9,4},{12,1},{13,0},{2,15},{3,14},... | collective-permute-start | bytes 24584 | tf_op jit(solution)/shard_map/ppermute | solution.py:518
  41.1 3.1 %collective-permute-start.18 = (f32[16,128]{1,0:T(8,128)S(1)}, f32[16,128]{1,0:T(8,128)S(1)}, u32[]{:S(2)}, u32[]{:S(2)}) collective-permute-start(f32[16,128]{1,0:T(8,128)S(1)} %add.32), channel_id=1, source_target_pairs={{0,5},{1,4},{4,1},{5,0},{8,13},{9,12},{12,9},{13,8},{2,7},{3,6},{6... | collective-permute-start | bytes 24584 | tf_op jit(solution)/shard_map/ppermute | solution.py:518

commit v7 on v6

--- a/solution.py
+++ b/solution.py
@@ -114,44 +114,46 @@
             out[b, c, below : below + 1, :] = after[c : c + 1]
 
 
+def three_passes(x, high, low, transposed):
+    rows = x.shape[0]
+    xh, xl = split(x)
+    contract = (((1,), (1 if transposed else 0,)), ((), ()))
+    both = lax.dot_general(jnp.concatenate([xh, xl], 0), high, contract, preferred_element_type=F32)
+    rest = lax.dot_general(xh, low, contract, preferred_element_type=F32)
+    return both[:rows] + both[rows:] + rest
+
+
 def fir(real, imag, high, low):
     rows = real.shape[0]
-    x = jnp.concatenate(
-        [real, pltpu.roll(real, rows - 1, 0), imag, pltpu.roll(imag, rows - 1, 0)], 1
-    )
-    xh, xl = split(x)
-    contract = (((1,), (1,)), ((), ()))
-    both = lax.dot_general(jnp.concatenate([xh, xl], 0), high, contract, preferred_element_type=F32)
-    rest = lax.dot_general(xh, low, contract, preferred_element_type=F32)
-    y = both[:rows] + both[rows:] + rest
-    return y[:, :LANES], y[:, LANES:]
+    x = [jnp.concatenate([part, pltpu.roll(part, rows - 1, 0)], 1) for part in (real, imag)]
+    y = three_passes(jnp.concatenate(x, 0), high, low, True)
+    first, second = y[:rows], y[rows:]
+    return first[:, :LANES] - second[:, LANES:], first[:, LANES:] + second[:, :LANES]
 
 
 def fir_adjoint(real, imag, high, low):
     rows = real.shape[0]
-    xh, xl = split(jnp.concatenate([real, imag], 1))
-    both = jnp.dot(jnp.concatenate([xh, xl], 0), high, preferred_element_type=F32)
-    rest = jnp.dot(xh, low, preferred_element_type=F32)
-    g = both[:rows] + both[rows:] + rest
-    out_real = g[:, :LANES] + pltpu.roll(g[:, LANES : 2 * LANES], 1, 0)
-    out_imag = g[:, 2 * LANES : 3 * LANES] + pltpu.roll(g[:, 3 * LANES :], 1, 0)
-    return out_real, out_imag
+    x = [jnp.concatenate([real, imag], 1), jnp.concatenate([imag, -real], 1)]
+    g = three_passes(jnp.concatenate(x, 0), high, low, False)
+    parts = (g[:rows], g[rows:])
+    return [part[:, :LANES] + pltpu.roll(part[:, LANES:], 1, 0) for part in parts]
 
 
 def scatter_delayed(values, delays, step, held, out):
-    bands = len(values)
-    rows = values[0].shape[0]
-    total = rows + REACH
+    bands = held.shape[0]
     base = REACH + 8
+    total = out.shape[0]
+    rows = total - REACH
     lane = lanes_of((total, LANES))
+    parts = []
+    for b, value in enumerate(values):
+        delay = at(delays, step, b)
+        parts.append((lax.shift_right_logical(delay, 7), delay & (LANES - 1)))
+        held[b, 0:base, :] = jnp.zeros((base, LANES), F32)
+        held[b, base : base + rows, :] = pltpu.roll(value, parts[b][1], 1)
+        held[b, base + rows :, :] = jnp.zeros((held.shape[1] - base - rows, LANES), F32)
     acc = None
-    for b in range(bands):
-        delay = at(delays, step, b)
-        q = lax.shift_right_logical(delay, 7)
-        s = delay & (LANES - 1)
-        held[b, 0:base, :] = jnp.zeros((base, LANES), F32)
-        held[b, base : base + rows, :] = pltpu.roll(values[b], s, 1)
-        held[b, base + rows :, :] = jnp.zeros((held.shape[1] - base - rows, LANES), F32)
+    for b, (q, s) in enumerate(parts):
         near = held[b, pl.ds(base - q, total), :]
         far = held[b, pl.ds(base - q - 1, total), :]
         part = jnp.where(lane >= s, near, far)
@@ -194,16 +196,21 @@
     return end_at_last(spread[...], rows)
 
 
-def read_spread(values, delay, held, b, rows):
-    total = values.shape[0]
-    q = lax.shift_right_logical(delay, 7)
-    s = delay & (LANES - 1)
-    held[b, 0:total, :] = pltpu.roll(values, (LANES - s) & (LANES - 1), 1)
-    held[b, total:, :] = jnp.zeros((held.shape[1] - total, LANES), F32)
+def read_spread(values, delays, step, held, rows):
+    bands, total = held.shape[0], values.shape[0]
     count = rows + 2 * PAD
-    near = held[b, pl.ds(q, count), :]
-    far = held[b, pl.ds(q + 1, count), :]
-    return jnp.where(lanes_of((count, LANES)) + s < LANES, near, far)
+    lane = lanes_of((count, LANES))
+    parts = []
+    for b in range(bands):
+        delay = at(delays, step, b)
+        parts.append((lax.shift_right_logical(delay, 7), delay & (LANES - 1)))
+    for b, (_, s) in enumerate(parts):
+        held[b, 0:total, :] = pltpu.roll(values, (LANES - s) & (LANES - 1), 1)
+        held[b, total:, :] = jnp.zeros((held.shape[1] - total, LANES), F32)
+    for b, (q, s) in enumerate(parts):
+        near = held[b, pl.ds(q, count), :]
+        far = held[b, pl.ds(q + 1, count), :]
+        yield jnp.where(lane + s < LANES, near, far)
 
 
 def k_begin(
@@ -272,16 +279,10 @@
                 row = jnp.broadcast_to(pack[tap : tap + 1, :], shape)
                 ring = pltpu.roll(row, 0, 1, stride=1, stride_axis=0)
                 near = jnp.where(diagonal, ring, 0.0)
-                for place, half in ((0, near), (1, ring - near)):
-                    for target, value in zip((high, low), split(half)):
-                        a = place * LANES
-                        d = (2 + place) * LANES
-                        if c == 0:
-                            target[b, 0:LANES, a : a + LANES] = value
-                            target[b, LANES:, d : d + LANES] = value
-                        else:
-                            target[b, LANES:, a : a + LANES] = value
-                            target[b, 0:LANES, d : d + LANES] = -value
+                rows_of = slice(c * LANES, (c + 1) * LANES)
+                for place, half in enumerate((near, ring - near)):
+                    lanes = slice(place * LANES, (place + 1) * LANES)
+                    high[b, rows_of, lanes], low[b, rows_of, lanes] = split(half)
 
 
 def k_cotangent(cots, sides, first, out):
@@ -335,14 +336,12 @@
 
 def k_second(
     delays, shifts, gains, linear0, own, high, low,
-    cosine0, sine0, field1, shifted, linear1, out, held, held_out,
+    cosine0, sine0, field1, shifted, linear1, out, moved, held, held_out,
 ):
     bands = linear1.shape[0]
     rows = linear1.shape[2] - 2 * PAD
     values = end_at_last(own[...], rows)
-    powers = []
-    for b in range(bands):
-        spread = read_spread(values, at(delays, 0, b), held, b, rows)
+    for b, spread in enumerate(read_spread(values, delays, 0, held, rows)):
         sine, cosine = sine_cosine(at(gains, 0, b) * spread)
         linear = of(linear0, b)
         lr, li = linear[0], linear[1]
@@ -353,16 +352,19 @@
         amount = LANES // 2 - at(shifts, 1, b)
         real = later(fr, amount)
         imag = later(fi, amount)
+        moved[b, 0] = real
+        moved[b, 1] = imag
         if b < shifted.shape[0]:
             cosine0[b] = cosine
             sine0[b] = sine
             shifted[b, 0] = real
             shifted[b, 1] = imag
-        lr, li = fir(real, imag, of(high, b)[...], of(low, b)[...])
+    for b in range(bands):
+        lr, li = fir(moved[b, 0], moved[b, 1], of(high, b)[...], of(low, b)[...])
         linear1[b, 0] = lr
         linear1[b, 1] = li
-        lr, li = lr[PAD : PAD + rows], li[PAD : PAD + rows]
-        powers.append(lr * lr + li * li)
+    inside = slice(PAD, PAD + rows)
+    powers = (linear1[b, 0, inside] ** 2 + linear1[b, 1, inside] ** 2 for b in range(bands))
     scatter_delayed(powers, delays, 1, held_out, out)
 
 
@@ -373,10 +375,9 @@
     rows = linear1.shape[2] - 2 * PAD
     values = gather_spread(own, even_in, odd_in, spread, rows)
     terms = []
-    for b in range(bands):
+    for b, spread_b in enumerate(read_spread(values, delays, 1, held, rows)):
         gain = at(gains, 1, b)
-        phase = gain * read_spread(values, at(delays, 1, b), held, b, rows)
-        sine, cosine = sine_cosine(phase)
+        sine, cosine = sine_cosine(gain * spread_b)
         gr, gi = cotangent[b, 0], cotangent[b, 1]
         er = gr * cosine + gi * sine
         ei = gi * cosine - gr * sine
@@ -389,23 +390,29 @@
 
 def k_fourth(
     delays, shifts, gains, turned1, linear1, own, even_in, odd_in, high, low, cosine0, sine0, field1,
-    grad1, turned0, out, spread, held, held_out,
+    grad1, turned0, out, spread, moved, held, held_out,
 ):
     bands = linear1.shape[0]
     rows = linear1.shape[2] - 2 * PAD
     values = gather_spread(own, even_in, odd_in, spread, rows)
-    terms = []
-    for b in range(bands):
-        twice = 2.0 * read_spread(values, at(delays, 1, b), held, b, rows)
+    for b, spread_b in enumerate(read_spread(values, delays, 1, held, rows)):
+        twice = 2.0 * spread_b
         gr = keep_inside(turned1[b, 0] + linear1[b, 0] * twice, rows)
         gi = keep_inside(turned1[b, 1] + linear1[b, 1] * twice, rows)
+        moved[b, 0] = gr
+        moved[b, 1] = gi
         if b < grad1.shape[0]:
             grad1[b, 0] = gr
             grad1[b, 1] = gi
-        gr, gi = fir_adjoint(gr, gi, of(high, b)[...], of(low, b)[...])
+    for b in range(bands):
+        gr, gi = fir_adjoint(moved[b, 0], moved[b, 1], of(high, b)[...], of(low, b)[...])
+        moved[b, 0] = gr
+        moved[b, 1] = gi
+    terms = []
+    for b in range(bands):
         amount = LANES // 2 - at(shifts, 1, b)
-        gr = earlier(gr, amount)
-        gi = earlier(gi, amount)
+        gr = earlier(moved[b, 0], amount)
+        gi = earlier(moved[b, 1], amount)
         if b < grad1.shape[0]:
             cosine, sine = cosine0[b], sine0[b]
             turned0[b, 0] = gr * cosine + gi * sine
@@ -465,8 +472,8 @@
     bands = turned0.shape[0]
     rows = turned0.shape[2] - 2 * PAD
     values = gather_spread(own, even_in, odd_in, spread, rows)
-    for b in range(bands):
-        twice = 2.0 * read_spread(values, at(delays, 0, b), held, b, rows)
+    for b, spread_b in enumerate(read_spread(values, delays, 0, held, rows)):
+        twice = 2.0 * spread_b
         gr = keep_inside(turned0[b, 0] + linear0[b, 0] * twice, rows)
         gi = keep_inside(turned0[b, 1] + linear0[b, 1] * twice, rows)
         grad0[b, 0] = gr
@@ -593,11 +600,13 @@
     angle = shape(own, held_rows, LANES)
     wide_part = shape(rows + REACH + 2 * PAD, LANES)
     part = shape(rows + REACH, LANES)
-    table = shape(own, 2 * LANES, 4 * LANES, dtype=BF16)
+    table = shape(own, 2 * LANES, 2 * LANES, dtype=BF16)
     ext_wide = (own, 2, rows + 2 * WIDE_PAD, LANES)
     held_wide = (own, rows + 2 * WIDE_PAD + 8, LANES)
     spread = (rows + REACH + 2 * PAD, LANES)
+    moved = (bands, 2, held_rows, LANES)
     held_in = (bands, rows + REACH + 3 * PAD, LANES)
+    held_own = (own, rows + REACH + 3 * PAD, LANES)
     held_out = (bands, rows + 3 * REACH, LANES)
 
     inputs = (signal, cotangent, taps, walk_off, tap_shift, gains)
@@ -617,13 +626,11 @@
         cost_estimate=pl.CostEstimate(flops=10**8, bytes_accessed=10**6, transcendentals=0),
     )(*(pltpu.with_memory_space_constraint(a, pltpu.HBM) for a in inputs))
 
-    packs, cots, first_cot = [pack_out], [cot_out], [WIDE]
+    packs = [pack_out]
     sides = [neighbours(even_out, odd_out, False)]
     if doubled:
         packs.append(swapped(pack_out, "band", evenly, False))
         sides.append((aslant(even_near, evenly), aslant(odd_near, oddly)))
-        cots.append(swapped(cot_out, "band", evenly, False))
-        first_cot.append(EDGE)
     tiny = [shape(steps, own, dtype=d) for d in (jnp.int32, jnp.int32, F32)]
     setup = functools.partial(k_setup, steps, rows)
     made = [call(setup, (p,), tiny + [table] * (2 * steps)) for p in packs]
@@ -634,7 +641,13 @@
         [own_field, own_field, wide_part], (ext_wide, held_wide),
     )
     sent, sides = lax.optimization_barrier((sent, sides))
-    spread0 = summed(over_cores(sent), "band")
+    sent = over_cores(sent)
+    cots, first_cot = [cot_out], [WIDE]
+    if doubled:
+        delays[1], cot_sent = lax.optimization_barrier((delays[1], cot_out))
+        cots.append(swapped(cot_sent, "band", evenly, False))
+        first_cot.append(EDGE)
+    spread0 = summed(sent, "band")
     linear0 = [linear]
     if doubled:
         linear0 += call(
@@ -646,7 +659,7 @@
     )
     cosine0, sine0, field1, shifted1, linear1, sent = call(
         k_second, (delays, shifts, gains, linear0, spread0, high1, low1),
-        [angle, angle, field, own_field, field, part], (held_in, held_out),
+        [angle, angle, field, own_field, field, part], (moved, held_in, held_out),
     )
     turned1, sent = call(
         k_third, (delays, gains, linear1, *exchanged(sent, doubled), cot_rows),
@@ -656,14 +669,14 @@
         k_fourth,
         (delays, shifts, gains, turned1, linear1, *exchanged(sent, doubled), high1, low1,
          cosine0, sine0, field1),
-        [own_field, own_field, part], (spread, held_in, held_out),
+        [own_field, own_field, part], (spread, moved, held_in, held_out),
     )
     (taps1,) = call(k_taps, (shifted1, grad1), [shape(2 * own, LANES)])
     scale = 1.0 / math.sqrt(2.0 * length * lax.axis_size("tm"))
     grad0, grad_taps = call(
         functools.partial(k_fifth, scale),
         (delays[:1], turned0, linear, *exchanged(sent, doubled), shifted0, taps1),
-        [own_field, shape(steps * 2 * own, LANES)], (spread, held_in),
+        [own_field, shape(steps * 2 * own, LANES)], (spread, held_own),
     )
     (grad_signal,) = call(
         k_last, (shifts[:1], grad0, high0[0], low0[0]), [shape(own, 1, 2, length)]

time: 44.9 us -> 45.3 us (level)
  Pallas kernels: 11 us -> 9.58 us
  waiting for transfers between devices: 10.4 us -> 11.8 us
    pallas_call x11, Pallas kernels: 9.86 us -> 8.4 us  [call(): pl.pallas_call(kernel, out_shape=shapes, in_specs=jax.tree.map(lambda _:...]
    ppermute x14, waiting for transfers between devices: 5.84 us -> 6.95 us  [swapped(): return lax.ppermute(x, (axis, 'pol'), pairs)]
    ppermute x14, starting transfers between devices: 17.1 us -> 17.8 us  [swapped(): return lax.ppermute(x, (axis, 'pol'), pairs)]
  transfers between devices with their start and end apart: 21 -> 21, of which waited for: 11 -> 10; matrix products, arithmetic and copies ran while one was open for 0% -> 0% of each run, Pallas kernels for 16% -> 13%
where the time goes in v7:
time: 45.3 us; the launch traced here: 45.2 us
  starting transfers between devices  22.4 us (49%)
  waiting for transfers between devices  11.8 us (26%)
  Pallas kernels  9.58 us (21%)
  between operations  0.77 us (2%)
  other arithmetic  0.63 us (1%)
    ppermute x14, starting transfers between devices, swapped(): return lax.ppermute(x, (axis, 'pol'), pairs)  17.8 us
    pallas_call x11, Pallas kernels, call(): pl.pallas_call(kernel, out_shape=shapes, in_specs=jax.tree.map(lambda _:...  8.4 us
    ppermute x14, waiting for transfers between devices, swapped(): return lax.ppermute(x, (axis, 'pol'), pairs)  6.95 us
    ppermute x5, waiting for transfers between devices, over_cores(): lax.ppermute(x, 'pol', [(p, cores - 1 - p) for p in range(cores)])  4.87 us
    ppermute x2, starting transfers between devices, aslant(): return lax.ppermute(x, ('tm', 'band', 'pol'), pairs)  3.12 us
    ppermute x5, starting transfers between devices, over_cores(): lax.ppermute(x, 'pol', [(p, cores - 1 - p) for p in range(cores)])  1.42 us
    pallas_call x1, Pallas kernels, on_device(): pl.pallas_call(k_begin, out_shape=[cut, cut, near, near, pack, shape(own,...  1.18 us
  transfers between devices with their start and end apart: 21, of which 10 were waited for; matrix products, arithmetic and copies ran while one was open for 0% of the time, Pallas kernels for 13%

profile of v7, /device:TPU:0, one launch (start us, length us, event | category | flops | bytes accessed | tf_op | source)
XLA Modules:
  0.0 45.2 jit_solution(10559089466099132512)
XLA Ops:
  0.6 1.2 %shard_map.77 = (f32[4,2,3072]{2,1,0:T(2,128)S(1)}, f32[4,2,3072]{2,1,0:T(2,128)S(1)}, f32[4,2,1024]{2,1,0:T(2,128)S(1)}, f32[4,2,1024]{2,1,0:T(2,128)S(1)}, f32...) custom-call(f32[4,1,2,4096]{3,2,1,0:T(2,128)} %signal.1, f32[4,1,2,4096]{3,2,1,0:T(2,128)} %cotangent.1, ...), custom_call_target="tpu_custom_call" | custom-call | flops 100000000 | bytes 1000000 | tf_op jit(solution)/shard_map/pallas_call | solution.py:618
  1.8 3.0 %collective-permute-start = (f32[280,128]{1,0:T(8,128)S(1)}, f32[280,128]{1,0:T(8,128)S(1)}, u32[]{:S(2)}, u32[]{:S(2)}) collective-permute-start(f32[280,128]{1,0:T(8,128)S(1)} %get-tuple-element.45.pack), channel_id=1, source_target_pairs={{0,2},{1,3},{2,0},{3,1},{4,6},{5,7},{6,4},{7,5},{8,10},{9,11},{10,... | collective-permute-start | bytes 430088 | tf_op jit(solution)/shard_map/ppermute | solution.py:525
  4.8 1.6 %collective-permute-start.1 = (f32[4,2,3072]{2,1,0:T(2,128)S(1)}, f32[4,2,3072]{2,1,0:T(2,128)S(1)}, u32[]{:S(2)}, u32[]{:S(2)}) collective-permute-start(f32[4,2,3072]{2,1,0:T(2,128)S(1)} %get-tuple-element.54), channel_id=1, source_target_pairs={{0,4},{1,5},{4,0},{5,1},{8,12},{9,13},{12,8},{13,9},{2,6},{3,7},{6... | collective-permute-start | bytes 294920 | tf_op jit(solution)/shard_map/ppermute | solution.py:525
  6.4 0.0 collective-permute-start.2
  6.4 3.1 %collective-permute-start.3 = (f32[4,2,1024]{2,1,0:T(2,128)S(1)}, f32[4,2,1024]{2,1,0:T(2,128)S(1)}, u32[]{:S(2)}, u32[]{:S(2)}) collective-permute-start(f32[4,2,1024]{2,1,0:T(2,128)S(1)} %get-tuple-element.60), channel_id=1, source_target_pairs={{0,6},{1,7},{2,4},{3,5},{4,2},{5,3},{6,0},{7,1},{8,14},{9,15},{10,... | collective-permute-start | bytes 98312 | tf_op jit(solution)/shard_map/ppermute | solution.py:570
  9.5 0.0 collective-permute-start.4
  9.5 0.4 shard_map.78
  10.0 0.0 collective-permute-done.pack
  10.0 0.4 shard_map.79
  10.5 1.6 %collective-permute-start.10 = (f32[4,2,32,128]{3,2,1,0:T(8,128)S(1)}, f32[4,2,32,128]{3,2,1,0:T(8,128)S(1)}, u32[]{:S(2)}, u32[]{:S(2)}) collective-permute-start(f32[4,2,32,128]{3,2,1,0:T(8,128)S(1)} %get-tuple-element.73.c_0_), channel_id=1, source_target_pairs={{0,2},{1,3},{2,0},{3,1},{4,6},{5,7},{6,4},{7,5},{8,10},{9,11},{10,... | collective-permute-start | bytes 393224 | tf_op jit(solution)/shard_map/ppermute | solution.py:525
  12.0 0.0 collective-permute-done.1.sides_0_.s_0__0_
  12.0 0.0 collective-permute-done.2.sides_1_.s_0__1_
  12.0 0.8 %shard_map.80 = (f32[4,2,48,128]{3,2,1,0:T(8,128)S(1)}, f32[4,2,48,128]{3,2,1,0:T(8,128)S(1)}, f32[64,128]{1,0:T(8,128)S(1)}) custom-call(s32[2,4]{1,0:T(2,128)S(1)} %get-tuple-element.47.delays_0_, s32[2,4]{1,0:T(2,128)S(1)} %get-tuple-element.46.shifts_0_, f32[280,128]{1,0:T(8,128)S(1)} %get-tuple-element.45.pack, ...), custom_call_target="tpu_custom_call" | custom-call | flops 200000000 | bytes 6000000 | tf_op jit(solution)/shard_map/pallas_call | solution.py:502
  12.8 0.0 collective-permute-done.3.sides_0_.s_1__0_
  12.8 0.0 collective-permute-done.4.sides_1_.s_1__1_
  12.8 0.3 collective-permute-start.5
  13.1 1.0 %collective-permute-done.5 = f32[64,128]{1,0:T(8,128)S(1)} collective-permute-done((f32[64,128]{1,0:T(8,128)S(1)}, f32[64,128]{1,0:T(8,128)S(1)}, u32[]{:S(2)}, u32[]{:S(2)}) %collective-permute-start.5) | collective-permute-done | bytes 32800 | tf_op jit(solution)/shard_map/ppermute | solution.py:541
  14.1 0.4 collective-permute-start.6
  14.5 0.6 %shard_map.81.linear0_1_ = f32[4,2,48,128]{3,2,1,0:T(8,128)S(1)} custom-call(s32[2,4]{1,0:T(2,128)S(1)} %get-tuple-element.51.shifts_0_.shifts_1_, f32[280,128]{1,0:T(8,128)S(1)} %collective-permute-done.pack, f32[4,2,1024]{2,1,0:T(2,128)S(1)} %collective-permute-done.3.sides_0_.s_1__0_, f32[4,2,1024]{2,1,0:T(2,128)S(1)} %collective-permute-done.4.sides_1_.s_1__1_, ...), custom_call_target="tpu_custom_call" | custom-call | flops 200000000 | bytes 6000000 | tf_op jit(solution)/shard_map/pallas_call | solution.py:502
  15.0 2.4 %collective-permute-done.6 = f32[64,128]{1,0:T(8,128)S(1)} collective-permute-done((f32[64,128]{1,0:T(8,128)S(1)}, f32[64,128]{1,0:T(8,128)S(1)}, u32[]{:S(2)}, u32[]{:S(2)}) %collective-permute-start.6) | collective-permute-done | bytes 32800 | tf_op jit(solution)/shard_map/ppermute | solution.py:525
  17.4 1.3 %shard_map.82 = (f32[4,48,128]{2,1,0:T(8,128)S(1)}, f32[4,48,128]{2,1,0:T(8,128)S(1)}, f32[8,2,48,128]{3,2,1,0:T(8,128)S(1)}, f32[4,2,48,128]{3,2,1,0:T(8,128)S(...) custom-call(s32[2,4]{1,0:T(2,128)S(1)} %get-tuple-element.47.delays_0_, ...), custom_call_target="tpu_custom_call" | custom-call | flops 200000000 | bytes 6000000 | tf_op jit(solution)/shard_map/pallas_call | solution.py:502
  18.7 0.3 collective-permute-start.7
  19.0 1.0 %collective-permute-done.7 = f32[48,128]{1,0:T(8,128)S(1)} collective-permute-done((f32[48,128]{1,0:T(8,128)S(1)}, f32[48,128]{1,0:T(8,128)S(1)}, u32[]{:S(2)}, u32[]{:S(2)}) %collective-permute-start.7) | collective-permute-done | bytes 24608 | tf_op jit(solution)/shard_map/ppermute | solution.py:541
  20.0 0.2 collective-permute-start.9
  20.2 2.0 %collective-permute-start.8 = (f32[48,128]{1,0:T(8,128)S(1)}, f32[48,128]{1,0:T(8,128)S(1)}, u32[]{:S(2)}, u32[]{:S(2)}) collective-permute-start(f32[48,128]{1,0:T(8,128)S(1)} %add.29.own), channel_id=1, source_target_pairs={{0,5},{1,4},{4,1},{5,0},{8,13},{9,12},{12,9},{13,8},{2,7},{3,6},{6... | collective-permute-start | bytes 73736 | tf_op jit(solution)/shard_map/ppermute | solution.py:525
  22.2 0.0 collective-permute-done.10.c_1_
  22.2 0.1 shard_map.83.cotangent
  22.3 0.0 collective-permute-done.9.odd_in
  22.3 1.4 %collective-permute-done.8.even_in = f32[48,128]{1,0:T(8,128)S(1)} collective-permute-done((f32[48,128]{1,0:T(8,128)S(1)}, f32[48,128]{1,0:T(8,128)S(1)}, u32[]{:S(2)}, u32[]{:S(2)}) %collective-permute-start.8) | collective-permute-done | bytes 24608 | tf_op jit(solution)/shard_map/ppermute | solution.py:525
  23.7 0.7 %shard_map.84 = (f32[8,2,48,128]{3,2,1,0:T(8,128)S(1)}, f32[48,128]{1,0:T(8,128)S(1)}) custom-call(s32[2,4]{1,0:T(2,128)S(1)} %get-tuple-element.47.delays_0_, s32[2,4]{1,0:T(2,128)S(1)} %get-tuple-element.50.delays_1_, f32[2,4]{1,0:T(2,128)S(1)} %get-tuple-element.52.gains_0_, f32[2,4]{1,0:T(2,128)S(1)} %get-tuple-element.53.gains_1_, ...), custom_call_target="tpu_custom_call" | custom-call | flops 200000000 | bytes 6000000 | tf_op jit(solution)/shard_map/pallas_call | solution.py:502
  24.4 0.2 collective-permute-start.11
  24.6 1.0 %collective-permute-done.11 = f32[48,128]{1,0:T(8,128)S(1)} collective-permute-done((f32[48,128]{1,0:T(8,128)S(1)}, f32[48,128]{1,0:T(8,128)S(1)}, u32[]{:S(2)}, u32[]{:S(2)}) %collective-permute-start.11) | collective-permute-done | bytes 24608 | tf_op jit(solution)/shard_map/ppermute | solution.py:541
  25.7 0.2 collective-permute-start.13
  25.9 2.7 %collective-permute-start.12 = (f32[48,128]{1,0:T(8,128)S(1)}, f32[48,128]{1,0:T(8,128)S(1)}, u32[]{:S(2)}, u32[]{:S(2)}) collective-permute-start(f32[48,128]{1,0:T(8,128)S(1)} %add.30.own), channel_id=1, source_target_pairs={{0,5},{1,4},{4,1},{5,0},{8,13},{9,12},{12,9},{13,8},{2,7},{3,6},{6... | collective-permute-start | bytes 73736 | tf_op jit(solution)/shard_map/ppermute | solution.py:525
  28.6 0.0 collective-permute-done.13.odd_in
  28.6 1.5 %collective-permute-done.12.even_in = f32[48,128]{1,0:T(8,128)S(1)} collective-permute-done((f32[48,128]{1,0:T(8,128)S(1)}, f32[48,128]{1,0:T(8,128)S(1)}, u32[]{:S(2)}, u32[]{:S(2)}) %collective-permute-start.12) | collective-permute-done | bytes 24608 | tf_op jit(solution)/shard_map/ppermute | solution.py:525
  30.1 1.0 %shard_map.85 = (f32[4,2,48,128]{3,2,1,0:T(8,128)S(1)}, f32[4,2,48,128]{3,2,1,0:T(8,128)S(1)}, f32[48,128]{1,0:T(8,128)S(1)}) custom-call(s32[2,4]{1,0:T(2,128)S(1)} %get-tuple-element.47.delays_0_, s32[2,4]{1,0:T(2,128)S(1)} %get-tuple-element.50.delays_1_, s32[2,4]{1,0:T(2,128)S(1)} %get-tuple-element.46.shifts_0_, ...), custom_call_target="tpu_custom_call" | custom-call | flops 200000000 | bytes 6000000 | tf_op jit(solution)/shard_map/pallas_call | solution.py:502
  31.1 0.4 collective-permute-start.14
  31.5 0.9 %collective-permute-done.14 = f32[48,128]{1,0:T(8,128)S(1)} collective-permute-done((f32[48,128]{1,0:T(8,128)S(1)}, f32[48,128]{1,0:T(8,128)S(1)}, u32[]{:S(2)}, u32[]{:S(2)}) %collective-permute-start.14) | collective-permute-done | bytes 24608 | tf_op jit(solution)/shard_map/ppermute | solution.py:541
  32.4 0.3 collective-permute-start.16
  32.7 2.0 %collective-permute-start.15 = (f32[48,128]{1,0:T(8,128)S(1)}, f32[48,128]{1,0:T(8,128)S(1)}, u32[]{:S(2)}, u32[]{:S(2)}) collective-permute-start(f32[48,128]{1,0:T(8,128)S(1)} %add.31.own), channel_id=1, source_target_pairs={{0,5},{1,4},{4,1},{5,0},{8,13},{9,12},{12,9},{13,8},{2,7},{3,6},{6... | collective-permute-start | bytes 73736 | tf_op jit(solution)/shard_map/ppermute | solution.py:525
  34.7 1.1 %shard_map.86.taps1 = f32[8,128]{1,0:T(8,128)S(1)} custom-call(f32[4,2,48,128]{3,2,1,0:T(8,128)S(1)} %get-tuple-element.84.shifted, f32[4,2,48,128]{3,2,1,0:T(8,128)S(1)} %get-tuple-element.85.grad), custom_call_target="tpu_custom_call" | custom-call | flops 200000000 | bytes 6000000 | tf_op jit(solution)/shard_map/pallas_call | solution.py:502
  35.7 0.0 collective-permute-done.16.odd_in
  35.8 0.4 collective-permute-done.15.even_in
  36.2 1.0 %shard_map.87 = (f32[4,2,48,128]{3,2,1,0:T(8,128)S(1)}, f32[16,128]{1,0:T(8,128)S(1)}) custom-call(s32[2,4]{1,0:T(2,128)S(1)} %get-tuple-element.47.delays_0_, f32[4,2,48,128]{3,2,1,0:T(8,128)S(1)} %get-tuple-element.81.turned0, f32[4,2,48,128]{3,2,1,0:T(8,128)S(1)} %get-tuple-element.58.linear0_0_.linear0, f32[48,128]{1,0:T(8,128)S(1)} %add.31.own, ...), custom_call_target="tpu_custom_call" | custom-call | flops 200000000 | bytes 6000000 | tf_op jit(solution)/shard_map/pallas_call | solution.py:502
  37.2 0.2 collective-permute-start.17
  37.4 1.0 %collective-permute-done.17 = f32[16,128]{1,0:T(8,128)S(1)} collective-permute-done((f32[16,128]{1,0:T(8,128)S(1)}, f32[16,128]{1,0:T(8,128)S(1)}, u32[]{:S(2)}, u32[]{:S(2)}) %collective-permute-start.17) | collective-permute-done | bytes 8224 | tf_op jit(solution)/shard_map/ppermute | solution.py:541
  38.4 2.1 %collective-permute-start.20 = (f32[16,128]{1,0:T(8,128)S(1)}, f32[16,128]{1,0:T(8,128)S(1)}, u32[]{:S(2)}, u32[]{:S(2)}) collective-permute-start(f32[16,128]{1,0:T(8,128)S(1)} %add.32), channel_id=1, source_target_pairs={{0,13},{1,12},{4,9},{5,8},{8,5},{9,4},{12,1},{13,0},{2,15},{3,14},... | collective-permute-start | bytes 24584 | tf_op jit(solution)/shard_map/ppermute | solution.py:525
  40.5 0.9 %collective-permute-start.19 = (f32[16,128]{1,0:T(8,128)S(1)}, f32[16,128]{1,0:T(8,128)S(1)}, u32[]{:S(2)}, u32[]{:S(2)}) collective-permute-start(f32[16,128]{1,0:T(8,128)S(1)} %add.32), channel_id=1, source_target_pairs={{0,9},{1,8},{4,13},{5,12},{8,1},{9,0},{12,5},{13,4},{2,11},{3,10},... | collective-permute-start | bytes 24584 | tf_op jit(solution)/shard_map/ppermute | solution.py:525
  41.4 0.9 %collective-permute-start.18 = (f32[16,128]{1,0:T(8,128)S(1)}, f32[16,128]{1,0:T(8,128)S(1)}, u32[]{:S(2)}, u32[]{:S(2)}) collective-permute-start(f32[16,128]{1,0:T(8,128)S(1)} %add.32), channel_id=1, source_target_pairs={{0,5},{1,4},{4,1},{5,0},{8,13},{9,12},{12,9},{13,8},{2,7},{3,6},{6... | collective-permute-start | bytes 24584 | tf_op jit(solution)/shard_map/ppermute | solution.py:525
  42.3 1.1 %shard_map.88 = f32[4,1,2,4096]{3,2,1,0:T(2,128)} custom-call(s32[2,4]{1,0:T(2,128)S(1)} %get-tuple-element.46.shifts_0_, f32[4,2,48,128]{3,2,1,0:T(8,128)S(1)} %get-tuple-element.86.grad0, bf16[4,256,256]{2,1,0:T(8,128)(2,1)S(1)} %get-tuple-element.56.high, bf16[4,256,256]{2,1,0:T(8,128)(2,1)S(1)} %get-tuple-element.57.low), custom_call_target="tpu_custom_call" | custom-call | flops 200000000 | bytes 6000000 | tf_op jit(solution)/shard_map/pallas_call | solution.py:502
  43.4 0.0 collective-permute-done.20
  43.4 1.1 %collective-permute-done.19 = f32[16,128]{1,0:T(8,128)S(1)} collective-permute-done((f32[16,128]{1,0:T(8,128)S(1)}, f32[16,128]{1,0:T(8,128)S(1)}, u32[]{:S(2)}, u32[]{:S(2)}) %collective-permute-start.19) | collective-permute-done | bytes 8224 | tf_op jit(solution)/shard_map/ppermute | solution.py:525
  44.6 0.0 collective-permute-done.18
  44.6 0.6 %add_add_fusion = f32[16,128]{1,0:T(8,128)} fusion(f32[16,128]{1,0:T(8,128)S(1)} %collective-permute-done.19, f32[16,128]{1,0:T(8,128)S(1)} %collective-permute-done.20, f32[16,128]{1,0:T(8,128)S(1)} %add.32, f32[16,128]{1,0:T(8,128)S(1)} %collective-permute-done.18), kind=kLoop, calls=%fused_computation | loop fusion | flops 6144 | bytes 40960 | tf_op jit(solution)/shard_map/add | solution.py:577
  (6 shorter events, 0.0 us)
Async XLA Ops:
  1.8 8.2 %collective-permute-start = (f32[280,128]{1,0:T(8,128)S(1)}, f32[280,128]{1,0:T(8,128)S(1)}, u32[]{:S(2)}, u32[]{:S(2)}) collective-permute-start(f32[280,128]{1,0:T(8,128)S(1)} %get-tuple-element.45.pack), channel_id=1, source_target_pairs={{0,2},{1,3},{2,0},{3,1},{4,6},{5,7},{6,4},{7,5},{8,10},{9,11},{10,... | collective-permute-start | bytes 430088 | tf_op jit(solution)/shard_map/ppermute | solution.py:525
  4.8 7.2 %collective-permute-start.1 = (f32[4,2,3072]{2,1,0:T(2,128)S(1)}, f32[4,2,3072]{2,1,0:T(2,128)S(1)}, u32[]{:S(2)}, u32[]{:S(2)}) collective-permute-start(f32[4,2,3072]{2,1,0:T(2,128)S(1)} %get-tuple-element.54), channel_id=1, source_target_pairs={{0,4},{1,5},{4,0},{5,1},{8,12},{9,13},{12,8},{13,9},{2,6},{3,7},{6... | collective-permute-start | bytes 294920 | tf_op jit(solution)/shard_map/ppermute | solution.py:525
  6.4 5.6 %collective-permute-start.2 = (f32[4,2,3072]{2,1,0:T(2,128)S(1)}, f32[4,2,3072]{2,1,0:T(2,128)S(1)}, u32[]{:S(2)}, u32[]{:S(2)}) collective-permute-start(f32[4,2,3072]{2,1,0:T(2,128)S(1)} %get-tuple-element.55), channel_id=1, source_target_pairs={{0,1},{1,0},{4,8},{5,9},{8,4},{9,5},{12,13},{13,12},{2,3},{3,2},{6... | collective-permute-start | bytes 294920 | tf_op jit(solution)/shard_map/ppermute | solution.py:525
  6.4 6.4 %collective-permute-start.3 = (f32[4,2,1024]{2,1,0:T(2,128)S(1)}, f32[4,2,1024]{2,1,0:T(2,128)S(1)}, u32[]{:S(2)}, u32[]{:S(2)}) collective-permute-start(f32[4,2,1024]{2,1,0:T(2,128)S(1)} %get-tuple-element.60), channel_id=1, source_target_pairs={{0,6},{1,7},{2,4},{3,5},{4,2},{5,3},{6,0},{7,1},{8,14},{9,15},{10,... | collective-permute-start | bytes 98312 | tf_op jit(solution)/shard_map/ppermute | solution.py:570
  9.5 3.3 %collective-permute-start.4 = (f32[4,2,1024]{2,1,0:T(2,128)S(1)}, f32[4,2,1024]{2,1,0:T(2,128)S(1)}, u32[]{:S(2)}, u32[]{:S(2)}) collective-permute-start(f32[4,2,1024]{2,1,0:T(2,128)S(1)} %get-tuple-element.61), channel_id=1, source_target_pairs={{0,1},{1,0},{2,3},{3,2},{4,10},{5,11},{6,8},{7,9},{8,6},{9,7},{10,... | collective-permute-start | bytes 98312 | tf_op jit(solution)/shard_map/ppermute | solution.py:570
  10.5 11.8 %collective-permute-start.10 = (f32[4,2,32,128]{3,2,1,0:T(8,128)S(1)}, f32[4,2,32,128]{3,2,1,0:T(8,128)S(1)}, u32[]{:S(2)}, u32[]{:S(2)}) collective-permute-start(f32[4,2,32,128]{3,2,1,0:T(8,128)S(1)} %get-tuple-element.73.c_0_), channel_id=1, source_target_pairs={{0,2},{1,3},{2,0},{3,1},{4,6},{5,7},{6,4},{7,5},{8,10},{9,11},{10,... | collective-permute-start | bytes 393224 | tf_op jit(solution)/shard_map/ppermute | solution.py:525
  12.8 1.3 %collective-permute-start.5 = (f32[64,128]{1,0:T(8,128)S(1)}, f32[64,128]{1,0:T(8,128)S(1)}, u32[]{:S(2)}, u32[]{:S(2)}) collective-permute-start(f32[64,128]{1,0:T(8,128)S(1)} %get-tuple-element.66), channel_id=1, source_target_pairs={{0,1},{1,0},{2,3},{3,2},{4,5},{5,4},{6,7},{7,6},{8,9},{9,8},{10,11... | collective-permute-start | bytes 98312 | tf_op jit(solution)/shard_map/ppermute | solution.py:541
  14.1 3.3 %collective-permute-start.6 = (f32[64,128]{1,0:T(8,128)S(1)}, f32[64,128]{1,0:T(8,128)S(1)}, u32[]{:S(2)}, u32[]{:S(2)}) collective-permute-start(f32[64,128]{1,0:T(8,128)S(1)} %add.27), channel_id=1, source_target_pairs={{0,3},{1,2},{2,1},{3,0},{4,7},{5,6},{6,5},{7,4},{8,11},{9,10},{10,... | collective-permute-start | bytes 98312 | tf_op jit(solution)/shard_map/ppermute | solution.py:525
  18.7 1.3 %collective-permute-start.7 = (f32[48,128]{1,0:T(8,128)S(1)}, f32[48,128]{1,0:T(8,128)S(1)}, u32[]{:S(2)}, u32[]{:S(2)}) collective-permute-start(f32[48,128]{1,0:T(8,128)S(1)} %get-tuple-element.72), channel_id=1, source_target_pairs={{0,1},{1,0},{2,3},{3,2},{4,5},{5,4},{6,7},{7,6},{8,9},{9,8},{10,11... | collective-permute-start | bytes 73736 | tf_op jit(solution)/shard_map/ppermute | solution.py:541
  20.0 2.3 %collective-permute-start.9 = (f32[48,128]{1,0:T(8,128)S(1)}, f32[48,128]{1,0:T(8,128)S(1)}, u32[]{:S(2)}, u32[]{:S(2)}) collective-permute-start(f32[48,128]{1,0:T(8,128)S(1)} %add.29.own), channel_id=1, source_target_pairs={{0,1},{1,0},{4,9},{5,8},{8,5},{9,4},{12,13},{13,12},{2,3},{3,2},{6... | collective-permute-start | bytes 73736 | tf_op jit(solution)/shard_map/ppermute | solution.py:525
  20.2 3.5 %collective-permute-start.8 = (f32[48,128]{1,0:T(8,128)S(1)}, f32[48,128]{1,0:T(8,128)S(1)}, u32[]{:S(2)}, u32[]{:S(2)}) collective-permute-start(f32[48,128]{1,0:T(8,128)S(1)} %add.29.own), channel_id=1, source_target_pairs={{0,5},{1,4},{4,1},{5,0},{8,13},{9,12},{12,9},{13,8},{2,7},{3,6},{6... | collective-permute-start | bytes 73736 | tf_op jit(solution)/shard_map/ppermute | solution.py:525
  24.4 1.3 %collective-permute-start.11 = (f32[48,128]{1,0:T(8,128)S(1)}, f32[48,128]{1,0:T(8,128)S(1)}, u32[]{:S(2)}, u32[]{:S(2)}) collective-permute-start(f32[48,128]{1,0:T(8,128)S(1)} %get-tuple-element.77), channel_id=1, source_target_pairs={{0,1},{1,0},{2,3},{3,2},{4,5},{5,4},{6,7},{7,6},{8,9},{9,8},{10,11... | collective-permute-start | bytes 73736 | tf_op jit(solution)/shard_map/ppermute | solution.py:541
  25.7 2.9 %collective-permute-start.13 = (f32[48,128]{1,0:T(8,128)S(1)}, f32[48,128]{1,0:T(8,128)S(1)}, u32[]{:S(2)}, u32[]{:S(2)}) collective-permute-start(f32[48,128]{1,0:T(8,128)S(1)} %add.30.own), channel_id=1, source_target_pairs={{0,1},{1,0},{4,9},{5,8},{8,5},{9,4},{12,13},{13,12},{2,3},{3,2},{6... | collective-permute-start | bytes 73736 | tf_op jit(solution)/shard_map/ppermute | solution.py:525
  25.9 4.3 %collective-permute-start.12 = (f32[48,128]{1,0:T(8,128)S(1)}, f32[48,128]{1,0:T(8,128)S(1)}, u32[]{:S(2)}, u32[]{:S(2)}) collective-permute-start(f32[48,128]{1,0:T(8,128)S(1)} %add.30.own), channel_id=1, source_target_pairs={{0,5},{1,4},{4,1},{5,0},{8,13},{9,12},{12,9},{13,8},{2,7},{3,6},{6... | collective-permute-start | bytes 73736 | tf_op jit(solution)/shard_map/ppermute | solution.py:525
  31.1 1.3 %collective-permute-start.14 = (f32[48,128]{1,0:T(8,128)S(1)}, f32[48,128]{1,0:T(8,128)S(1)}, u32[]{:S(2)}, u32[]{:S(2)}) collective-permute-start(f32[48,128]{1,0:T(8,128)S(1)} %get-tuple-element.82), channel_id=1, source_target_pairs={{0,1},{1,0},{2,3},{3,2},{4,5},{5,4},{6,7},{7,6},{8,9},{9,8},{10,11... | collective-permute-start | bytes 73736 | tf_op jit(solution)/shard_map/ppermute | solution.py:541
  32.4 3.4 %collective-permute-start.16 = (f32[48,128]{1,0:T(8,128)S(1)}, f32[48,128]{1,0:T(8,128)S(1)}, u32[]{:S(2)}, u32[]{:S(2)}) collective-permute-start(f32[48,128]{1,0:T(8,128)S(1)} %add.31.own), channel_id=1, source_target_pairs={{0,1},{1,0},{4,9},{5,8},{8,5},{9,4},{12,13},{13,12},{2,3},{3,2},{6... | collective-permute-start | bytes 73736 | tf_op jit(solution)/shard_map/ppermute | solution.py:525
  32.7 3.5 %collective-permute-start.15 = (f32[48,128]{1,0:T(8,128)S(1)}, f32[48,128]{1,0:T(8,128)S(1)}, u32[]{:S(2)}, u32[]{:S(2)}) collective-permute-start(f32[48,128]{1,0:T(8,128)S(1)} %add.31.own), channel_id=1, source_target_pairs={{0,5},{1,4},{4,1},{5,0},{8,13},{9,12},{12,9},{13,8},{2,7},{3,6},{6... | collective-permute-start | bytes 73736 | tf_op jit(solution)/shard_map/ppermute | solution.py:525
  37.2 1.2 %collective-permute-start.17 = (f32[16,128]{1,0:T(8,128)S(1)}, f32[16,128]{1,0:T(8,128)S(1)}, u32[]{:S(2)}, u32[]{:S(2)}) collective-permute-start(f32[16,128]{1,0:T(8,128)S(1)} %get-tuple-element.87), channel_id=1, source_target_pairs={{0,1},{1,0},{2,3},{3,2},{4,5},{5,4},{6,7},{7,6},{8,9},{9,8},{10,11... | collective-permute-start | bytes 24584 | tf_op jit(solution)/shard_map/ppermute | solution.py:541
  38.4 5.0 %collective-permute-start.20 = (f32[16,128]{1,0:T(8,128)S(1)}, f32[16,128]{1,0:T(8,128)S(1)}, u32[]{:S(2)}, u32[]{:S(2)}) collective-permute-start(f32[16,128]{1,0:T(8,128)S(1)} %add.32), channel_id=1, source_target_pairs={{0,13},{1,12},{4,9},{5,8},{8,5},{9,4},{12,1},{13,0},{2,15},{3,14},... | collective-permute-start | bytes 24584 | tf_op jit(solution)/shard_map/ppermute | solution.py:525
  40.5 4.1 %collective-permute-start.19 = (f32[16,128]{1,0:T(8,128)S(1)}, f32[16,128]{1,0:T(8,128)S(1)}, u32[]{:S(2)}, u32[]{:S(2)}) collective-permute-start(f32[16,128]{1,0:T(8,128)S(1)} %add.32), channel_id=1, source_target_pairs={{0,9},{1,8},{4,13},{5,12},{8,1},{9,0},{12,5},{13,4},{2,11},{3,10},... | collective-permute-start | bytes 24584 | tf_op jit(solution)/shard_map/ppermute | solution.py:525
  41.4 3.2 %collective-permute-start.18 = (f32[16,128]{1,0:T(8,128)S(1)}, f32[16,128]{1,0:T(8,128)S(1)}, u32[]{:S(2)}, u32[]{:S(2)}) collective-permute-start(f32[16,128]{1,0:T(8,128)S(1)} %add.32), channel_id=1, source_target_pairs={{0,5},{1,4},{4,1},{5,0},{8,13},{9,12},{12,9},{13,8},{2,7},{3,6},{6... | collective-permute-start | bytes 24584 | tf_op jit(solution)/shard_map/ppermute | solution.py:525

commit v8 on v7

--- a/solution.py
+++ b/solution.py
@@ -215,11 +215,11 @@
 
 def k_begin(
     signal, cotangent, taps, delays, shifts, gains,
-    even_out, odd_out, even_near, odd_near, sent, cot_rows,
+    even_out, odd_out, even_near, odd_near, sent,
     sig_held, cot_held, taps_held, delays_held, shifts_held, gains_held, done,
 ):
     steps, bands = taps.shape[:2]
-    rows = cot_rows.shape[2]
+    rows = signal.shape[3] // LANES
     pairs = (
         (signal, sig_held), (cotangent, cot_held), (taps, taps_held),
         (delays, delays_held), (shifts, shifts_held), (gains, gains_held),
@@ -249,14 +249,16 @@
             for c in range(2):
                 row = (2 * b + c) * rows + r
                 sent[row : row + 1, :] = pair[c : c + 1]
-                cot_rows[b, c, r : r + 1, :] = other[c : c + 1]
+                row = row + sent.shape[0] - 2 * bands * rows
+                sent[row : row + 1, :] = other[c : c + 1]
     first = 2 * bands * rows
     for step in range(steps):
         for b in range(bands):
             row = first + 2 * (step * bands + b)
             sent[row : row + 2, :] = taps_held[step, b]
     first = first + 2 * steps * bands
-    sent[first:, :] = jnp.zeros((sent.shape[0] - first, LANES), F32)
+    small = sent.shape[0] - 2 * bands * rows - first
+    sent[first : first + small, :] = jnp.zeros((small, LANES), F32)
     for k, held in enumerate((delays_held, shifts_held, gains_held)):
         row = first + k * steps
         sent[row : row + steps, 0:bands] = held[...].astype(F32)
@@ -285,14 +287,16 @@
                     high[b, rows_of, lanes], low[b, rows_of, lanes] = split(half)
 
 
-def k_cotangent(cots, sides, first, out):
-    own = cots[0].shape[0]
+def k_cotangent(packs, sides, first, out):
+    own = sides[0][0].shape[0]
     rows = out.shape[2] - 2 * PAD
+    base = packs[0].shape[0] - 2 * own * rows
     for b in range(out.shape[0]):
         k = b // own
         extend(out, b, *sides[k], first[k], EDGE)
         for c in range(2):
-            out[b, c, PAD : PAD + rows, :] = cots[k][b % own, c]
+            row = base + (2 * (b % own) + c) * rows
+            out[b, c, PAD : PAD + rows, :] = packs[k][row : row + rows, :]
 
 
 def widened(ext, pack, sides, edge, b):
@@ -614,48 +618,46 @@
     cut = shape(own, 2, (WIDE + EDGE) * LANES)
     near = shape(own, 2, 2 * EDGE * LANES)
     pack_rows = 2 * own * rows + 2 * steps * own + 3 * steps
-    pack = shape(pack_rows + -pack_rows % 8, LANES)
-    even_out, odd_out, even_near, odd_near, pack_out, cot_out = pl.pallas_call(
+    pack = shape(pack_rows + -pack_rows % 8 + 2 * own * rows, LANES)
+    even_out, odd_out, even_near, odd_near, pack_out = pl.pallas_call(
         k_begin,
-        out_shape=[cut, cut, near, near, pack, shape(own, 2, rows, LANES)],
+        out_shape=[cut, cut, near, near, pack],
         in_specs=[hbm] * len(inputs),
-        out_specs=[vmem] * 6,
+        out_specs=[vmem] * 5,
         scratch_shapes=[pltpu.VMEM(a.shape, a.dtype) for a in inputs]
         + [pltpu.SemaphoreType.DMA((len(inputs),))],
         compiler_params=pltpu.CompilerParams(vmem_limit_bytes=24 * 1024 * 1024),
         cost_estimate=pl.CostEstimate(flops=10**8, bytes_accessed=10**6, transcendentals=0),
     )(*(pltpu.with_memory_space_constraint(a, pltpu.HBM) for a in inputs))
 
-    packs = [pack_out]
     sides = [neighbours(even_out, odd_out, False)]
     if doubled:
-        packs.append(swapped(pack_out, "band", evenly, False))
+        pack_in = swapped(pack_out, "band", evenly, False)
         sides.append((aslant(even_near, evenly), aslant(odd_near, oddly)))
     tiny = [shape(steps, own, dtype=d) for d in (jnp.int32, jnp.int32, F32)]
     setup = functools.partial(k_setup, steps, rows)
-    made = [call(setup, (p,), tiny + [table] * (2 * steps)) for p in packs]
-    delays, shifts, gains, high0, low0, high1, low1 = (list(m) for m in zip(*made))
-
+    made = [call(setup, (pack_out,), tiny + [table] * (2 * steps))]
     shifted0, linear, sent = call(
-        k_first, (delays[:1], shifts[:1], pack_out, sides[0], high0[0], low0[0]),
+        k_first, (made[0][:1], made[0][1:2], pack_out, sides[0], *made[0][3:5]),
         [own_field, own_field, wide_part], (ext_wide, held_wide),
     )
     sent, sides = lax.optimization_barrier((sent, sides))
     sent = over_cores(sent)
-    cots, first_cot = [cot_out], [WIDE]
+    linear0, packs, first_cot = [linear], [pack_out], [WIDE]
     if doubled:
-        delays[1], cot_sent = lax.optimization_barrier((delays[1], cot_out))
-        cots.append(swapped(cot_sent, "band", evenly, False))
+        sent, pack_in = lax.optimization_barrier((sent, pack_in))
+        made.append(call(setup, (pack_in,), tiny + [table] * (2 * steps)))
+        (other,) = call(
+            k_beside, (made[1][1:2], pack_in, sides[1], *made[1][3:5]), [own_field],
+            ((own, 2, held_rows, LANES),),
+        )
+        linear0.append(other)
+        packs.append(pack_in)
         first_cot.append(EDGE)
     spread0 = summed(sent, "band")
-    linear0 = [linear]
-    if doubled:
-        linear0 += call(
-            k_beside, (shifts[1:], packs[1], sides[1], high0[1], low0[1]), [own_field],
-            ((own, 2, held_rows, LANES),),
-        )
+    delays, shifts, gains, high0, low0, high1, low1 = (list(m) for m in zip(*made))
     (cot_rows,) = call(
-        lambda c, s, out: k_cotangent(c, s, first_cot, out), (cots, sides), [field]
+        lambda c, s, out: k_cotangent(c, s, first_cot, out), (packs, sides), [field]
     )
     cosine0, sine0, field1, shifted1, linear1, sent = call(
         k_second, (delays, shifts, gains, linear0, spread0, high1, low1),

time: 45.3 us -> 45.4 us (level)
  starting transfers between devices: 22.4 us -> 22.9 us
    ppermute x14 -> x13, waiting for transfers between devices: 6.95 us -> 5.52 us  [swapped(): return lax.ppermute(x, (axis, 'pol'), pairs)]
    ppermute x14 -> x13, starting transfers between devices: 17.8 us -> 18.7 us  [swapped(): return lax.ppermute(x, (axis, 'pol'), pairs)]
    ppermute x2, waiting for transfers between devices: 0.01 us -> 0.7 us  [aslant(): return lax.ppermute(x, ('tm', 'band', 'pol'), pairs)]
  transfers between devices with their start and end apart: 21 -> 20, of which waited for: 10 -> 12; matrix products, arithmetic and copies ran while one was open for 0% -> 0% of each run, Pallas kernels for 13% -> 10%
where the time goes in v8:
time: 45.4 us; the launch traced here: 45.2 us
  starting transfers between devices  22.9 us (50%)
  waiting for transfers between devices  11.4 us (25%)
  Pallas kernels  9.57 us (21%)
  between operations  0.76 us (2%)
  other arithmetic  0.63 us (1%)
    ppermute x13, starting transfers between devices, swapped(): return lax.ppermute(x, (axis, 'pol'), pairs)  18.7 us
    pallas_call x11, Pallas kernels, call(): pl.pallas_call(kernel, out_shape=shapes, in_specs=jax.tree.map(lambda _:...  8.39 us
    ppermute x13, waiting for transfers between devices, swapped(): return lax.ppermute(x, (axis, 'pol'), pairs)  5.52 us
    ppermute x5, waiting for transfers between devices, over_cores(): lax.ppermute(x, 'pol', [(p, cores - 1 - p) for p in range(cores)])  5.15 us
    ppermute x2, starting transfers between devices, aslant(): return lax.ppermute(x, ('tm', 'band', 'pol'), pairs)  3.12 us
    pallas_call x1, Pallas kernels, on_device(): pl.pallas_call(k_begin, out_shape=[cut, cut, near, near, pack], in_specs=...  1.18 us
    ppermute x5, starting transfers between devices, over_cores(): lax.ppermute(x, 'pol', [(p, cores - 1 - p) for p in range(cores)])  1.07 us
  transfers between devices with their start and end apart: 20, of which 12 were waited for; matrix products, arithmetic and copies ran while one was open for 0% of the time, Pallas kernels for 10%

profile of v8, /device:TPU:0, one launch (start us, length us, event | category | flops | bytes accessed | tf_op | source)
XLA Modules:
  0.0 45.2 jit_solution(448875737310438105)
XLA Ops:
  0.6 1.2 %shard_map.77 = (f32[4,2,3072]{2,1,0:T(2,128)S(1)}, f32[4,2,3072]{2,1,0:T(2,128)S(1)}, f32[4,2,1024]{2,1,0:T(2,128)S(1)}, f32[4,2,1024]{2,1,0:T(2,128)S(1)}, f32[536,128]{1,0:T(8,128)S(1)}) custom-call(f32[4,1,2,4096]{3,2,1,0:T(2,128)} %signal.1, f32[4,1,2,4096]{3,2,1,0:T(2,128)} %cotangent.1, f32[2,4,2,128]{3,2,1,0:T(2,128)} %taps.1, s32[2,4]{1,0:T(2,128)} %delays.1, ...), custom_call_target="tpu_custom_call" | custom-call | flops 100000000 | bytes 1000000 | tf_op jit(solution)/shard_map/pallas_call | solution.py:622
  1.8 3.0 %collective-permute-start.5 = (f32[536,128]{1,0:T(8,128)S(1)}, f32[536,128]{1,0:T(8,128)S(1)}, u32[]{:S(2)}, u32[]{:S(2)}) collective-permute-start(f32[536,128]{1,0:T(8,128)S(1)} %get-tuple-element.44.pack.c_0_), channel_id=1, source_target_pairs={{0,2},{1,3},{2,0},{3,1},{4,6},{5,7},{6,4},{7,5},{8,10},{9,11},{10,... | collective-permute-start | bytes 823304 | tf_op jit(solution)/shard_map/ppermute | solution.py:529
  4.8 1.6 %collective-permute-start = (f32[4,2,3072]{2,1,0:T(2,128)S(1)}, f32[4,2,3072]{2,1,0:T(2,128)S(1)}, u32[]{:S(2)}, u32[]{:S(2)}) collective-permute-start(f32[4,2,3072]{2,1,0:T(2,128)S(1)} %get-tuple-element.47), channel_id=1, source_target_pairs={{0,4},{1,5},{4,0},{5,1},{8,12},{9,13},{12,8},{13,9},{2,6},{3,7},{6... | collective-permute-start | bytes 294920 | tf_op jit(solution)/shard_map/ppermute | solution.py:529
  6.4 0.0 collective-permute-start.1
  6.4 3.1 %collective-permute-start.2 = (f32[4,2,1024]{2,1,0:T(2,128)S(1)}, f32[4,2,1024]{2,1,0:T(2,128)S(1)}, u32[]{:S(2)}, u32[]{:S(2)}) collective-permute-start(f32[4,2,1024]{2,1,0:T(2,128)S(1)} %get-tuple-element.52), channel_id=1, source_target_pairs={{0,6},{1,7},{2,4},{3,5},{4,2},{5,3},{6,0},{7,1},{8,14},{9,15},{10,... | collective-permute-start | bytes 98312 | tf_op jit(solution)/shard_map/ppermute | solution.py:574
  9.5 0.0 collective-permute-start.3
  9.5 0.4 shard_map.78
  10.0 0.0 collective-permute-done.sides_0_.s_0__0_
  10.0 0.0 collective-permute-done.1.sides_1_.s_0__1_
  10.0 0.8 %shard_map.79 = (f32[4,2,48,128]{3,2,1,0:T(8,128)S(1)}, f32[4,2,48,128]{3,2,1,0:T(8,128)S(1)}, f32[64,128]{1,0:T(8,128)S(1)}) custom-call(s32[2,4]{1,0:T(2,128)S(1)} %get-tuple-element.46.delays_0_, s32[2,4]{1,0:T(2,128)S(1)} %get-tuple-element.45.shifts_0_, f32[536,128]{1,0:T(8,128)S(1)} %get-tuple-element.44.pack.c_0_, ...), custom_call_target="tpu_custom_call" | custom-call | flops 200000000 | bytes 6000000 | tf_op jit(solution)/shard_map/pallas_call | solution.py:506
  10.8 0.7 %collective-permute-done.2.sides_0_.s_1__0_ = f32[4,2,1024]{2,1,0:T(2,128)S(1)} collective-permute-done((f32[4,2,1024]{2,1,0:T(2,128)S(1)}, f32[4,2,1024]{2,1,0:T(2,128)S(1)}, u32[]{:S(2)}, u32[]{:S(2)}) %collective-permute-start.2) | collective-permute-done | bytes 32800 | tf_op jit(solution)/shard_map/ppermute | solution.py:574
  11.5 0.0 collective-permute-done.3.sides_1_.s_1__1_
  11.5 0.0 collective-permute-start.4
  11.5 1.2 %collective-permute-done.4 = f32[64,128]{1,0:T(8,128)S(1)} collective-permute-done((f32[64,128]{1,0:T(8,128)S(1)}, f32[64,128]{1,0:T(8,128)S(1)}, u32[]{:S(2)}, u32[]{:S(2)}) %collective-permute-start.4) | collective-permute-done | bytes 32800 | tf_op jit(solution)/shard_map/ppermute | solution.py:545
  12.7 0.0 collective-permute-done.5.pack.c_1_
  12.7 1.4 %collective-permute-start.6 = (f32[64,128]{1,0:T(8,128)S(1)}, f32[64,128]{1,0:T(8,128)S(1)}, u32[]{:S(2)}, u32[]{:S(2)}) collective-permute-start(f32[64,128]{1,0:T(8,128)S(1)} %add.27), channel_id=1, source_target_pairs={{0,3},{1,2},{2,1},{3,0},{4,7},{5,6},{6,5},{7,4},{8,11},{9,10},{10,... | collective-permute-start | bytes 98312 | tf_op jit(solution)/shard_map/ppermute | solution.py:529
  14.1 0.4 shard_map.80
  14.5 0.6 %shard_map.81.linear0_1_ = f32[4,2,48,128]{3,2,1,0:T(8,128)S(1)} custom-call(s32[2,4]{1,0:T(2,128)S(1)} %get-tuple-element.57.shifts_0_.shifts_1_, f32[536,128]{1,0:T(8,128)S(1)} %collective-permute-done.5.pack.c_1_, f32[4,2,1024]{2,1,0:T(2,128)S(1)} %collective-permute-done.2.sides_0_.s_1__0_, f32[4,2,1024]{2,1,0:T(2,128)S(1)} %collective-permute-done.3.sides_1_.s_1__1_, ...), custom_call_target="tpu_custom_call" | custom-call | flops 200000000 | bytes 6000000 | tf_op jit(solution)/shard_map/pallas_call | solution.py:506
  15.1 1.0 %collective-permute-done.6 = f32[64,128]{1,0:T(8,128)S(1)} collective-permute-done((f32[64,128]{1,0:T(8,128)S(1)}, f32[64,128]{1,0:T(8,128)S(1)}, u32[]{:S(2)}, u32[]{:S(2)}) %collective-permute-start.6) | collective-permute-done | bytes 32800 | tf_op jit(solution)/shard_map/ppermute | solution.py:529
  16.1 1.3 %shard_map.82 = (f32[4,48,128]{2,1,0:T(8,128)S(1)}, f32[4,48,128]{2,1,0:T(8,128)S(1)}, f32[8,2,48,128]{3,2,1,0:T(8,128)S(1)}, f32[4,2,48,128]{3,2,1,0:T(8,128)S(...) custom-call(s32[2,4]{1,0:T(2,128)S(1)} %get-tuple-element.46.delays_0_, ...), custom_call_target="tpu_custom_call" | custom-call | flops 200000000 | bytes 6000000 | tf_op jit(solution)/shard_map/pallas_call | solution.py:506
  17.4 0.2 collective-permute-start.7
  17.6 1.0 %collective-permute-done.7 = f32[48,128]{1,0:T(8,128)S(1)} collective-permute-done((f32[48,128]{1,0:T(8,128)S(1)}, f32[48,128]{1,0:T(8,128)S(1)}, u32[]{:S(2)}, u32[]{:S(2)}) %collective-permute-start.7) | collective-permute-done | bytes 24608 | tf_op jit(solution)/shard_map/ppermute | solution.py:545
  18.7 0.2 collective-permute-start.9
  18.8 3.5 %collective-permute-start.8 = (f32[48,128]{1,0:T(8,128)S(1)}, f32[48,128]{1,0:T(8,128)S(1)}, u32[]{:S(2)}, u32[]{:S(2)}) collective-permute-start(f32[48,128]{1,0:T(8,128)S(1)} %add.29.own), channel_id=1, source_target_pairs={{0,5},{1,4},{4,1},{5,0},{8,13},{9,12},{12,9},{13,8},{2,7},{3,6},{6... | collective-permute-start | bytes 73736 | tf_op jit(solution)/shard_map/ppermute | solution.py:529
  22.3 0.1 shard_map.83.cotangent
  22.4 0.0 collective-permute-done.9.odd_in
  22.4 1.4 %collective-permute-done.8.even_in = f32[48,128]{1,0:T(8,128)S(1)} collective-permute-done((f32[48,128]{1,0:T(8,128)S(1)}, f32[48,128]{1,0:T(8,128)S(1)}, u32[]{:S(2)}, u32[]{:S(2)}) %collective-permute-start.8) | collective-permute-done | bytes 24608 | tf_op jit(solution)/shard_map/ppermute | solution.py:529
  23.8 0.7 %shard_map.84 = (f32[8,2,48,128]{3,2,1,0:T(8,128)S(1)}, f32[48,128]{1,0:T(8,128)S(1)}) custom-call(s32[2,4]{1,0:T(2,128)S(1)} %get-tuple-element.46.delays_0_, s32[2,4]{1,0:T(2,128)S(1)} %get-tuple-element.56.delays_1_, f32[2,4]{1,0:T(2,128)S(1)} %get-tuple-element.58.gains_0_, f32[2,4]{1,0:T(2,128)S(1)} %get-tuple-element.59.gains_1_, ...), custom_call_target="tpu_custom_call" | custom-call | flops 200000000 | bytes 6000000 | tf_op jit(solution)/shard_map/pallas_call | solution.py:506
  24.5 0.2 collective-permute-start.10
  24.7 1.0 %collective-permute-done.10 = f32[48,128]{1,0:T(8,128)S(1)} collective-permute-done((f32[48,128]{1,0:T(8,128)S(1)}, f32[48,128]{1,0:T(8,128)S(1)}, u32[]{:S(2)}, u32[]{:S(2)}) %collective-permute-start.10) | collective-permute-done | bytes 24608 | tf_op jit(solution)/shard_map/ppermute | solution.py:545
  25.8 0.2 collective-permute-start.12
  25.9 2.7 %collective-permute-start.11 = (f32[48,128]{1,0:T(8,128)S(1)}, f32[48,128]{1,0:T(8,128)S(1)}, u32[]{:S(2)}, u32[]{:S(2)}) collective-permute-start(f32[48,128]{1,0:T(8,128)S(1)} %add.30.own), channel_id=1, source_target_pairs={{0,5},{1,4},{4,1},{5,0},{8,13},{9,12},{12,9},{13,8},{2,7},{3,6},{6... | collective-permute-start | bytes 73736 | tf_op jit(solution)/shard_map/ppermute | solution.py:529
  28.6 0.0 collective-permute-done.12.odd_in
  28.6 1.5 %collective-permute-done.11.even_in = f32[48,128]{1,0:T(8,128)S(1)} collective-permute-done((f32[48,128]{1,0:T(8,128)S(1)}, f32[48,128]{1,0:T(8,128)S(1)}, u32[]{:S(2)}, u32[]{:S(2)}) %collective-permute-start.11) | collective-permute-done | bytes 24608 | tf_op jit(solution)/shard_map/ppermute | solution.py:529
  30.2 1.0 %shard_map.85 = (f32[4,2,48,128]{3,2,1,0:T(8,128)S(1)}, f32[4,2,48,128]{3,2,1,0:T(8,128)S(1)}, f32[48,128]{1,0:T(8,128)S(1)}) custom-call(s32[2,4]{1,0:T(2,128)S(1)} %get-tuple-element.46.delays_0_, s32[2,4]{1,0:T(2,128)S(1)} %get-tuple-element.56.delays_1_, s32[2,4]{1,0:T(2,128)S(1)} %get-tuple-element.45.shifts_0_, ...), custom_call_target="tpu_custom_call" | custom-call | flops 200000000 | bytes 6000000 | tf_op jit(solution)/shard_map/pallas_call | solution.py:506
  31.1 0.4 collective-permute-start.13
  31.5 0.9 %collective-permute-done.13 = f32[48,128]{1,0:T(8,128)S(1)} collective-permute-done((f32[48,128]{1,0:T(8,128)S(1)}, f32[48,128]{1,0:T(8,128)S(1)}, u32[]{:S(2)}, u32[]{:S(2)}) %collective-permute-start.13) | collective-permute-done | bytes 24608 | tf_op jit(solution)/shard_map/ppermute | solution.py:545
  32.4 0.3 collective-permute-start.15
  32.7 2.0 %collective-permute-start.14 = (f32[48,128]{1,0:T(8,128)S(1)}, f32[48,128]{1,0:T(8,128)S(1)}, u32[]{:S(2)}, u32[]{:S(2)}) collective-permute-start(f32[48,128]{1,0:T(8,128)S(1)} %add.31.own), channel_id=1, source_target_pairs={{0,5},{1,4},{4,1},{5,0},{8,13},{9,12},{12,9},{13,8},{2,7},{3,6},{6... | collective-permute-start | bytes 73736 | tf_op jit(solution)/shard_map/ppermute | solution.py:529
  34.7 1.1 %shard_map.86.taps1 = f32[8,128]{1,0:T(8,128)S(1)} custom-call(f32[4,2,48,128]{3,2,1,0:T(8,128)S(1)} %get-tuple-element.82.shifted, f32[4,2,48,128]{3,2,1,0:T(8,128)S(1)} %get-tuple-element.83.grad), custom_call_target="tpu_custom_call" | custom-call | flops 200000000 | bytes 6000000 | tf_op jit(solution)/shard_map/pallas_call | solution.py:506
  35.8 0.0 collective-permute-done.15.odd_in
  35.8 0.4 collective-permute-done.14.even_in
  36.3 1.0 %shard_map.87 = (f32[4,2,48,128]{3,2,1,0:T(8,128)S(1)}, f32[16,128]{1,0:T(8,128)S(1)}) custom-call(s32[2,4]{1,0:T(2,128)S(1)} %get-tuple-element.46.delays_0_, f32[4,2,48,128]{3,2,1,0:T(8,128)S(1)} %get-tuple-element.79.turned0, f32[4,2,48,128]{3,2,1,0:T(8,128)S(1)} %get-tuple-element.60.linear0_0_.linear0, f32[48,128]{1,0:T(8,128)S(1)} %add.31.own, ...), custom_call_target="tpu_custom_call" | custom-call | flops 200000000 | bytes 6000000 | tf_op jit(solution)/shard_map/pallas_call | solution.py:506
  37.3 0.2 collective-permute-start.16
  37.5 1.0 %collective-permute-done.16 = f32[16,128]{1,0:T(8,128)S(1)} collective-permute-done((f32[16,128]{1,0:T(8,128)S(1)}, f32[16,128]{1,0:T(8,128)S(1)}, u32[]{:S(2)}, u32[]{:S(2)}) %collective-permute-start.16) | collective-permute-done | bytes 8224 | tf_op jit(solution)/shard_map/ppermute | solution.py:545
  38.5 2.0 %collective-permute-start.19 = (f32[16,128]{1,0:T(8,128)S(1)}, f32[16,128]{1,0:T(8,128)S(1)}, u32[]{:S(2)}, u32[]{:S(2)}) collective-permute-start(f32[16,128]{1,0:T(8,128)S(1)} %add.32), channel_id=1, source_target_pairs={{0,13},{1,12},{4,9},{5,8},{8,5},{9,4},{12,1},{13,0},{2,15},{3,14},... | collective-permute-start | bytes 24584 | tf_op jit(solution)/shard_map/ppermute | solution.py:529
  40.5 0.9 %collective-permute-start.18 = (f32[16,128]{1,0:T(8,128)S(1)}, f32[16,128]{1,0:T(8,128)S(1)}, u32[]{:S(2)}, u32[]{:S(2)}) collective-permute-start(f32[16,128]{1,0:T(8,128)S(1)} %add.32), channel_id=1, source_target_pairs={{0,9},{1,8},{4,13},{5,12},{8,1},{9,0},{12,5},{13,4},{2,11},{3,10},... | collective-permute-start | bytes 24584 | tf_op jit(solution)/shard_map/ppermute | solution.py:529
  41.5 0.9 %collective-permute-start.17 = (f32[16,128]{1,0:T(8,128)S(1)}, f32[16,128]{1,0:T(8,128)S(1)}, u32[]{:S(2)}, u32[]{:S(2)}) collective-permute-start(f32[16,128]{1,0:T(8,128)S(1)} %add.32), channel_id=1, source_target_pairs={{0,5},{1,4},{4,1},{5,0},{8,13},{9,12},{12,9},{13,8},{2,7},{3,6},{6... | collective-permute-start | bytes 24584 | tf_op jit(solution)/shard_map/ppermute | solution.py:529
  42.4 1.1 %shard_map.88 = f32[4,1,2,4096]{3,2,1,0:T(2,128)} custom-call(s32[2,4]{1,0:T(2,128)S(1)} %get-tuple-element.45.shifts_0_, f32[4,2,48,128]{3,2,1,0:T(8,128)S(1)} %get-tuple-element.84.grad0, bf16[4,256,256]{2,1,0:T(8,128)(2,1)S(1)} %get-tuple-element.49.high, bf16[4,256,256]{2,1,0:T(8,128)(2,1)S(1)} %get-tuple-element.50.low), custom_call_target="tpu_custom_call" | custom-call | flops 200000000 | bytes 6000000 | tf_op jit(solution)/shard_map/pallas_call | solution.py:506
  43.5 0.0 collective-permute-done.19
  43.5 1.0 %collective-permute-done.18 = f32[16,128]{1,0:T(8,128)S(1)} collective-permute-done((f32[16,128]{1,0:T(8,128)S(1)}, f32[16,128]{1,0:T(8,128)S(1)}, u32[]{:S(2)}, u32[]{:S(2)}) %collective-permute-start.18) | collective-permute-done | bytes 8224 | tf_op jit(solution)/shard_map/ppermute | solution.py:529
  44.5 0.1 collective-permute-done.17
  44.6 0.6 %add_add_fusion = f32[16,128]{1,0:T(8,128)} fusion(f32[16,128]{1,0:T(8,128)S(1)} %collective-permute-done.18, f32[16,128]{1,0:T(8,128)S(1)} %collective-permute-done.19, f32[16,128]{1,0:T(8,128)S(1)} %add.32, f32[16,128]{1,0:T(8,128)S(1)} %collective-permute-done.17), kind=kLoop, calls=%fused_computation | loop fusion | flops 6144 | bytes 40960 | tf_op jit(solution)/shard_map/add | solution.py:581
  (6 shorter events, 0.0 us)
Async XLA Ops:
  1.8 10.9 %collective-permute-start.5 = (f32[536,128]{1,0:T(8,128)S(1)}, f32[536,128]{1,0:T(8,128)S(1)}, u32[]{:S(2)}, u32[]{:S(2)}) collective-permute-start(f32[536,128]{1,0:T(8,128)S(1)} %get-tuple-element.44.pack.c_0_), channel_id=1, source_target_pairs={{0,2},{1,3},{2,0},{3,1},{4,6},{5,7},{6,4},{7,5},{8,10},{9,11},{10,... | collective-permute-start | bytes 823304 | tf_op jit(solution)/shard_map/ppermute | solution.py:529
  4.8 5.2 %collective-permute-start = (f32[4,2,3072]{2,1,0:T(2,128)S(1)}, f32[4,2,3072]{2,1,0:T(2,128)S(1)}, u32[]{:S(2)}, u32[]{:S(2)}) collective-permute-start(f32[4,2,3072]{2,1,0:T(2,128)S(1)} %get-tuple-element.47), channel_id=1, source_target_pairs={{0,4},{1,5},{4,0},{5,1},{8,12},{9,13},{12,8},{13,9},{2,6},{3,7},{6... | collective-permute-start | bytes 294920 | tf_op jit(solution)/shard_map/ppermute | solution.py:529
  6.4 3.6 %collective-permute-start.1 = (f32[4,2,3072]{2,1,0:T(2,128)S(1)}, f32[4,2,3072]{2,1,0:T(2,128)S(1)}, u32[]{:S(2)}, u32[]{:S(2)}) collective-permute-start(f32[4,2,3072]{2,1,0:T(2,128)S(1)} %get-tuple-element.48), channel_id=1, source_target_pairs={{0,1},{1,0},{4,8},{5,9},{8,4},{9,5},{12,13},{13,12},{2,3},{3,2},{6... | collective-permute-start | bytes 294920 | tf_op jit(solution)/shard_map/ppermute | solution.py:529
  6.4 5.1 %collective-permute-start.2 = (f32[4,2,1024]{2,1,0:T(2,128)S(1)}, f32[4,2,1024]{2,1,0:T(2,128)S(1)}, u32[]{:S(2)}, u32[]{:S(2)}) collective-permute-start(f32[4,2,1024]{2,1,0:T(2,128)S(1)} %get-tuple-element.52), channel_id=1, source_target_pairs={{0,6},{1,7},{2,4},{3,5},{4,2},{5,3},{6,0},{7,1},{8,14},{9,15},{10,... | collective-permute-start | bytes 98312 | tf_op jit(solution)/shard_map/ppermute | solution.py:574
  9.5 1.9 %collective-permute-start.3 = (f32[4,2,1024]{2,1,0:T(2,128)S(1)}, f32[4,2,1024]{2,1,0:T(2,128)S(1)}, u32[]{:S(2)}, u32[]{:S(2)}) collective-permute-start(f32[4,2,1024]{2,1,0:T(2,128)S(1)} %get-tuple-element.53), channel_id=1, source_target_pairs={{0,1},{1,0},{2,3},{3,2},{4,10},{5,11},{6,8},{7,9},{8,6},{9,7},{10,... | collective-permute-start | bytes 98312 | tf_op jit(solution)/shard_map/ppermute | solution.py:574
  11.5 1.2 %collective-permute-start.4 = (f32[64,128]{1,0:T(8,128)S(1)}, f32[64,128]{1,0:T(8,128)S(1)}, u32[]{:S(2)}, u32[]{:S(2)}) collective-permute-start(f32[64,128]{1,0:T(8,128)S(1)} %get-tuple-element.54), channel_id=1, source_target_pairs={{0,1},{1,0},{2,3},{3,2},{4,5},{5,4},{6,7},{7,6},{8,9},{9,8},{10,11... | collective-permute-start | bytes 98312 | tf_op jit(solution)/shard_map/ppermute | solution.py:545
  12.7 3.4 %collective-permute-start.6 = (f32[64,128]{1,0:T(8,128)S(1)}, f32[64,128]{1,0:T(8,128)S(1)}, u32[]{:S(2)}, u32[]{:S(2)}) collective-permute-start(f32[64,128]{1,0:T(8,128)S(1)} %add.27), channel_id=1, source_target_pairs={{0,3},{1,2},{2,1},{3,0},{4,7},{5,6},{6,5},{7,4},{8,11},{9,10},{10,... | collective-permute-start | bytes 98312 | tf_op jit(solution)/shard_map/ppermute | solution.py:529
  17.4 1.3 %collective-permute-start.7 = (f32[48,128]{1,0:T(8,128)S(1)}, f32[48,128]{1,0:T(8,128)S(1)}, u32[]{:S(2)}, u32[]{:S(2)}) collective-permute-start(f32[48,128]{1,0:T(8,128)S(1)} %get-tuple-element.71), channel_id=1, source_target_pairs={{0,1},{1,0},{2,3},{3,2},{4,5},{5,4},{6,7},{7,6},{8,9},{9,8},{10,11... | collective-permute-start | bytes 73736 | tf_op jit(solution)/shard_map/ppermute | solution.py:545
  18.7 3.7 %collective-permute-start.9 = (f32[48,128]{1,0:T(8,128)S(1)}, f32[48,128]{1,0:T(8,128)S(1)}, u32[]{:S(2)}, u32[]{:S(2)}) collective-permute-start(f32[48,128]{1,0:T(8,128)S(1)} %add.29.own), channel_id=1, source_target_pairs={{0,1},{1,0},{4,9},{5,8},{8,5},{9,4},{12,13},{13,12},{2,3},{3,2},{6... | collective-permute-start | bytes 73736 | tf_op jit(solution)/shard_map/ppermute | solution.py:529
  18.8 5.0 %collective-permute-start.8 = (f32[48,128]{1,0:T(8,128)S(1)}, f32[48,128]{1,0:T(8,128)S(1)}, u32[]{:S(2)}, u32[]{:S(2)}) collective-permute-start(f32[48,128]{1,0:T(8,128)S(1)} %add.29.own), channel_id=1, source_target_pairs={{0,5},{1,4},{4,1},{5,0},{8,13},{9,12},{12,9},{13,8},{2,7},{3,6},{6... | collective-permute-start | bytes 73736 | tf_op jit(solution)/shard_map/ppermute | solution.py:529
  24.5 1.3 %collective-permute-start.10 = (f32[48,128]{1,0:T(8,128)S(1)}, f32[48,128]{1,0:T(8,128)S(1)}, u32[]{:S(2)}, u32[]{:S(2)}) collective-permute-start(f32[48,128]{1,0:T(8,128)S(1)} %get-tuple-element.75), channel_id=1, source_target_pairs={{0,1},{1,0},{2,3},{3,2},{4,5},{5,4},{6,7},{7,6},{8,9},{9,8},{10,11... | collective-permute-start | bytes 73736 | tf_op jit(solution)/shard_map/ppermute | solution.py:545
  25.8 2.9 %collective-permute-start.12 = (f32[48,128]{1,0:T(8,128)S(1)}, f32[48,128]{1,0:T(8,128)S(1)}, u32[]{:S(2)}, u32[]{:S(2)}) collective-permute-start(f32[48,128]{1,0:T(8,128)S(1)} %add.30.own), channel_id=1, source_target_pairs={{0,1},{1,0},{4,9},{5,8},{8,5},{9,4},{12,13},{13,12},{2,3},{3,2},{6... | collective-permute-start | bytes 73736 | tf_op jit(solution)/shard_map/ppermute | solution.py:529
  25.9 4.2 %collective-permute-start.11 = (f32[48,128]{1,0:T(8,128)S(1)}, f32[48,128]{1,0:T(8,128)S(1)}, u32[]{:S(2)}, u32[]{:S(2)}) collective-permute-start(f32[48,128]{1,0:T(8,128)S(1)} %add.30.own), channel_id=1, source_target_pairs={{0,5},{1,4},{4,1},{5,0},{8,13},{9,12},{12,9},{13,8},{2,7},{3,6},{6... | collective-permute-start | bytes 73736 | tf_op jit(solution)/shard_map/ppermute | solution.py:529
  31.1 1.3 %collective-permute-start.13 = (f32[48,128]{1,0:T(8,128)S(1)}, f32[48,128]{1,0:T(8,128)S(1)}, u32[]{:S(2)}, u32[]{:S(2)}) collective-permute-start(f32[48,128]{1,0:T(8,128)S(1)} %get-tuple-element.80), channel_id=1, source_target_pairs={{0,1},{1,0},{2,3},{3,2},{4,5},{5,4},{6,7},{7,6},{8,9},{9,8},{10,11... | collective-permute-start | bytes 73736 | tf_op jit(solution)/shard_map/ppermute | solution.py:545
  32.4 3.4 %collective-permute-start.15 = (f32[48,128]{1,0:T(8,128)S(1)}, f32[48,128]{1,0:T(8,128)S(1)}, u32[]{:S(2)}, u32[]{:S(2)}) collective-permute-start(f32[48,128]{1,0:T(8,128)S(1)} %add.31.own), channel_id=1, source_target_pairs={{0,1},{1,0},{4,9},{5,8},{8,5},{9,4},{12,13},{13,12},{2,3},{3,2},{6... | collective-permute-start | bytes 73736 | tf_op jit(solution)/shard_map/ppermute | solution.py:529
  32.7 3.5 %collective-permute-start.14 = (f32[48,128]{1,0:T(8,128)S(1)}, f32[48,128]{1,0:T(8,128)S(1)}, u32[]{:S(2)}, u32[]{:S(2)}) collective-permute-start(f32[48,128]{1,0:T(8,128)S(1)} %add.31.own), channel_id=1, source_target_pairs={{0,5},{1,4},{4,1},{5,0},{8,13},{9,12},{12,9},{13,8},{2,7},{3,6},{6... | collective-permute-start | bytes 73736 | tf_op jit(solution)/shard_map/ppermute | solution.py:529
  37.3 1.2 %collective-permute-start.16 = (f32[16,128]{1,0:T(8,128)S(1)}, f32[16,128]{1,0:T(8,128)S(1)}, u32[]{:S(2)}, u32[]{:S(2)}) collective-permute-start(f32[16,128]{1,0:T(8,128)S(1)} %get-tuple-element.85), channel_id=1, source_target_pairs={{0,1},{1,0},{2,3},{3,2},{4,5},{5,4},{6,7},{7,6},{8,9},{9,8},{10,11... | collective-permute-start | bytes 24584 | tf_op jit(solution)/shard_map/ppermute | solution.py:545
  38.5 5.0 %collective-permute-start.19 = (f32[16,128]{1,0:T(8,128)S(1)}, f32[16,128]{1,0:T(8,128)S(1)}, u32[]{:S(2)}, u32[]{:S(2)}) collective-permute-start(f32[16,128]{1,0:T(8,128)S(1)} %add.32), channel_id=1, source_target_pairs={{0,13},{1,12},{4,9},{5,8},{8,5},{9,4},{12,1},{13,0},{2,15},{3,14},... | collective-permute-start | bytes 24584 | tf_op jit(solution)/shard_map/ppermute | solution.py:529
  40.5 4.0 %collective-permute-start.18 = (f32[16,128]{1,0:T(8,128)S(1)}, f32[16,128]{1,0:T(8,128)S(1)}, u32[]{:S(2)}, u32[]{:S(2)}) collective-permute-start(f32[16,128]{1,0:T(8,128)S(1)} %add.32), channel_id=1, source_target_pairs={{0,9},{1,8},{4,13},{5,12},{8,1},{9,0},{12,5},{13,4},{2,11},{3,10},... | collective-permute-start | bytes 24584 | tf_op jit(solution)/shard_map/ppermute | solution.py:529
  41.5 3.1 %collective-permute-start.17 = (f32[16,128]{1,0:T(8,128)S(1)}, f32[16,128]{1,0:T(8,128)S(1)}, u32[]{:S(2)}, u32[]{:S(2)}) collective-permute-start(f32[16,128]{1,0:T(8,128)S(1)} %add.32), channel_id=1, source_target_pairs={{0,5},{1,4},{4,1},{5,0},{8,13},{9,12},{12,9},{13,8},{2,7},{3,6},{6... | collective-permute-start | bytes 24584 | tf_op jit(solution)/shard_map/ppermute | solution.py:529

commit v9 on v7

--- a/solution.py
+++ b/solution.py
@@ -644,8 +644,7 @@
     sent = over_cores(sent)
     cots, first_cot = [cot_out], [WIDE]
     if doubled:
-        delays[1], cot_sent = lax.optimization_barrier((delays[1], cot_out))
-        cots.append(swapped(cot_sent, "band", evenly, False))
+        cots.append(swapped(cot_out, "band", evenly, False))
         first_cot.append(EDGE)
     spread0 = summed(sent, "band")
     linear0 = [linear]

time: 45.3 us -> 45.3 us (level)
  no operation moved by 1% of the time
where the time goes in v9:
time: 45.3 us; the launch traced here: 45.2 us
  starting transfers between devices  22.6 us (50%)
  waiting for transfers between devices  11.6 us (26%)
  Pallas kernels  9.58 us (21%)
  between operations  0.76 us (2%)
  other arithmetic  0.63 us (1%)
    ppermute x14, starting transfers between devices, swapped(): return lax.ppermute(x, (axis, 'pol'), pairs)  17.9 us
    pallas_call x11, Pallas kernels, call(): pl.pallas_call(kernel, out_shape=shapes, in_specs=jax.tree.map(lambda _:...  8.39 us
    ppermute x14, waiting for transfers between devices, swapped(): return lax.ppermute(x, (axis, 'pol'), pairs)  6.9 us
    ppermute x5, waiting for transfers between devices, over_cores(): lax.ppermute(x, 'pol', [(p, cores - 1 - p) for p in range(cores)])  4.68 us
    ppermute x2, starting transfers between devices, aslant(): return lax.ppermute(x, ('tm', 'band', 'pol'), pairs)  3.12 us
    ppermute x5, starting transfers between devices, over_cores(): lax.ppermute(x, 'pol', [(p, cores - 1 - p) for p in range(cores)])  1.61 us
    pallas_call x1, Pallas kernels, on_device(): pl.pallas_call(k_begin, out_shape=[cut, cut, near, near, pack, shape(own,...  1.18 us
  transfers between devices with their start and end apart: 21, of which 10 were waited for; matrix products, arithmetic and copies ran while one was open for 0% of the time, Pallas kernels for 13%

profile of v9, /device:TPU:0, one launch (start us, length us, event | category | flops | bytes accessed | tf_op | source)
XLA Modules:
  0.0 45.2 jit_solution(16047996058876537417)
XLA Ops:
  0.6 1.2 %shard_map.77 = (f32[4,2,3072]{2,1,0:T(2,128)S(1)}, f32[4,2,3072]{2,1,0:T(2,128)S(1)}, f32[4,2,1024]{2,1,0:T(2,128)S(1)}, f32[4,2,1024]{2,1,0:T(2,128)S(1)}, f32...) custom-call(f32[4,1,2,4096]{3,2,1,0:T(2,128)} %signal.1, f32[4,1,2,4096]{3,2,1,0:T(2,128)} %cotangent.1, ...), custom_call_target="tpu_custom_call" | custom-call | flops 100000000 | bytes 1000000 | tf_op jit(solution)/shard_map/pallas_call | solution.py:618
  1.8 3.1 %collective-permute-start.1 = (f32[4,2,3072]{2,1,0:T(2,128)S(1)}, f32[4,2,3072]{2,1,0:T(2,128)S(1)}, u32[]{:S(2)}, u32[]{:S(2)}) collective-permute-start(f32[4,2,3072]{2,1,0:T(2,128)S(1)} %get-tuple-element.50), channel_id=1, source_target_pairs={{0,4},{1,5},{4,0},{5,1},{8,12},{9,13},{12,8},{13,9},{2,6},{3,7},{6... | collective-permute-start | bytes 294920 | tf_op jit(solution)/shard_map/ppermute | solution.py:525
  4.9 0.0 collective-permute-start.2
  4.9 1.5 %collective-permute-start = (f32[280,128]{1,0:T(8,128)S(1)}, f32[280,128]{1,0:T(8,128)S(1)}, u32[]{:S(2)}, u32[]{:S(2)}) collective-permute-start(f32[280,128]{1,0:T(8,128)S(1)} %get-tuple-element.43.pack), channel_id=1, source_target_pairs={{0,2},{1,3},{2,0},{3,1},{4,6},{5,7},{6,4},{7,5},{8,10},{9,11},{10,... | collective-permute-start | bytes 430088 | tf_op jit(solution)/shard_map/ppermute | solution.py:525
  6.4 3.1 %collective-permute-start.3 = (f32[4,2,1024]{2,1,0:T(2,128)S(1)}, f32[4,2,1024]{2,1,0:T(2,128)S(1)}, u32[]{:S(2)}, u32[]{:S(2)}) collective-permute-start(f32[4,2,1024]{2,1,0:T(2,128)S(1)} %get-tuple-element.56), channel_id=1, source_target_pairs={{0,6},{1,7},{2,4},{3,5},{4,2},{5,3},{6,0},{7,1},{8,14},{9,15},{10,... | collective-permute-start | bytes 98312 | tf_op jit(solution)/shard_map/ppermute | solution.py:570
  9.5 0.0 collective-permute-start.4
  9.5 0.4 shard_map.78
  10.0 0.0 collective-permute-done.1.sides_0_.s_0__0_
  10.0 1.6 %collective-permute-start.10 = (f32[4,2,32,128]{3,2,1,0:T(8,128)S(1)}, f32[4,2,32,128]{3,2,1,0:T(8,128)S(1)}, u32[]{:S(2)}, u32[]{:S(2)}) collective-permute-start(f32[4,2,32,128]{3,2,1,0:T(8,128)S(1)} %get-tuple-element.69.c_0_), channel_id=1, source_target_pairs={{0,2},{1,3},{2,0},{3,1},{4,6},{5,7},{6,4},{7,5},{8,10},{9,11},{10,... | collective-permute-start | bytes 393224 | tf_op jit(solution)/shard_map/ppermute | solution.py:525
  11.6 0.0 collective-permute-done.2.sides_1_.s_0__1_
  11.6 0.8 %shard_map.80 = (f32[4,2,48,128]{3,2,1,0:T(8,128)S(1)}, f32[4,2,48,128]{3,2,1,0:T(8,128)S(1)}, f32[64,128]{1,0:T(8,128)S(1)}) custom-call(s32[2,4]{1,0:T(2,128)S(1)} %get-tuple-element.45.delays_0_, s32[2,4]{1,0:T(2,128)S(1)} %get-tuple-element.44.shifts_0_, f32[280,128]{1,0:T(8,128)S(1)} %get-tuple-element.43.pack, ...), custom_call_target="tpu_custom_call" | custom-call | flops 200000000 | bytes 6000000 | tf_op jit(solution)/shard_map/pallas_call | solution.py:502
  12.3 0.0 collective-permute-done.3.sides_0_.s_1__0_
  12.3 0.0 collective-permute-done.4.sides_1_.s_1__1_
  12.3 0.3 collective-permute-start.5
  12.6 1.0 %collective-permute-done.5 = f32[64,128]{1,0:T(8,128)S(1)} collective-permute-done((f32[64,128]{1,0:T(8,128)S(1)}, f32[64,128]{1,0:T(8,128)S(1)}, u32[]{:S(2)}, u32[]{:S(2)}) %collective-permute-start.5) | collective-permute-done | bytes 32800 | tf_op jit(solution)/shard_map/ppermute | solution.py:541
  13.6 0.4 collective-permute-start.6
  14.0 0.0 collective-permute-done.pack
  14.0 0.4 shard_map.79
  14.5 0.6 %shard_map.81.linear0_1_ = f32[4,2,48,128]{3,2,1,0:T(8,128)S(1)} custom-call(s32[2,4]{1,0:T(2,128)S(1)} %get-tuple-element.47.shifts_0_.shifts_1_, f32[280,128]{1,0:T(8,128)S(1)} %collective-permute-done.pack, f32[4,2,1024]{2,1,0:T(2,128)S(1)} %collective-permute-done.3.sides_0_.s_1__0_, f32[4,2,1024]{2,1,0:T(2,128)S(1)} %collective-permute-done.4.sides_1_.s_1__1_, ...), custom_call_target="tpu_custom_call" | custom-call | flops 200000000 | bytes 6000000 | tf_op jit(solution)/shard_map/pallas_call | solution.py:502
  15.0 1.9 %collective-permute-done.6 = f32[64,128]{1,0:T(8,128)S(1)} collective-permute-done((f32[64,128]{1,0:T(8,128)S(1)}, f32[64,128]{1,0:T(8,128)S(1)}, u32[]{:S(2)}, u32[]{:S(2)}) %collective-permute-start.6) | collective-permute-done | bytes 32800 | tf_op jit(solution)/shard_map/ppermute | solution.py:525
  17.0 1.3 %shard_map.82 = (f32[4,48,128]{2,1,0:T(8,128)S(1)}, f32[4,48,128]{2,1,0:T(8,128)S(1)}, f32[8,2,48,128]{3,2,1,0:T(8,128)S(1)}, f32[4,2,48,128]{3,2,1,0:T(8,128)S(...) custom-call(s32[2,4]{1,0:T(2,128)S(1)} %get-tuple-element.45.delays_0_, ...), custom_call_target="tpu_custom_call" | custom-call | flops 200000000 | bytes 6000000 | tf_op jit(solution)/shard_map/pallas_call | solution.py:502
  18.3 0.3 collective-permute-start.7
  18.5 1.0 %collective-permute-done.7 = f32[48,128]{1,0:T(8,128)S(1)} collective-permute-done((f32[48,128]{1,0:T(8,128)S(1)}, f32[48,128]{1,0:T(8,128)S(1)}, u32[]{:S(2)}, u32[]{:S(2)}) %collective-permute-start.7) | collective-permute-done | bytes 24608 | tf_op jit(solution)/shard_map/ppermute | solution.py:541
  19.5 0.2 collective-permute-start.9
  19.7 2.0 %collective-permute-start.8 = (f32[48,128]{1,0:T(8,128)S(1)}, f32[48,128]{1,0:T(8,128)S(1)}, u32[]{:S(2)}, u32[]{:S(2)}) collective-permute-start(f32[48,128]{1,0:T(8,128)S(1)} %add.29.own), channel_id=1, source_target_pairs={{0,5},{1,4},{4,1},{5,0},{8,13},{9,12},{12,9},{13,8},{2,7},{3,6},{6... | collective-permute-start | bytes 73736 | tf_op jit(solution)/shard_map/ppermute | solution.py:525
  21.8 0.0 collective-permute-done.10.c_1_
  21.8 0.1 shard_map.83.cotangent
  21.9 0.0 collective-permute-done.9.odd_in
  21.9 1.4 %collective-permute-done.8.even_in = f32[48,128]{1,0:T(8,128)S(1)} collective-permute-done((f32[48,128]{1,0:T(8,128)S(1)}, f32[48,128]{1,0:T(8,128)S(1)}, u32[]{:S(2)}, u32[]{:S(2)}) %collective-permute-start.8) | collective-permute-done | bytes 24608 | tf_op jit(solution)/shard_map/ppermute | solution.py:525
  23.3 0.7 %shard_map.84 = (f32[8,2,48,128]{3,2,1,0:T(8,128)S(1)}, f32[48,128]{1,0:T(8,128)S(1)}) custom-call(s32[2,4]{1,0:T(2,128)S(1)} %get-tuple-element.45.delays_0_, s32[2,4]{1,0:T(2,128)S(1)} %get-tuple-element.46.delays_1_, f32[2,4]{1,0:T(2,128)S(1)} %get-tuple-element.48.gains_0_, f32[2,4]{1,0:T(2,128)S(1)} %get-tuple-element.49.gains_1_, ...), custom_call_target="tpu_custom_call" | custom-call | flops 200000000 | bytes 6000000 | tf_op jit(solution)/shard_map/pallas_call | solution.py:502
  24.0 0.4 collective-permute-start.11
  24.4 0.9 %collective-permute-done.11 = f32[48,128]{1,0:T(8,128)S(1)} collective-permute-done((f32[48,128]{1,0:T(8,128)S(1)}, f32[48,128]{1,0:T(8,128)S(1)}, u32[]{:S(2)}, u32[]{:S(2)}) %collective-permute-start.11) | collective-permute-done | bytes 24608 | tf_op jit(solution)/shard_map/ppermute | solution.py:541
  25.3 0.3 collective-permute-start.13
  25.6 3.1 %collective-permute-start.12 = (f32[48,128]{1,0:T(8,128)S(1)}, f32[48,128]{1,0:T(8,128)S(1)}, u32[]{:S(2)}, u32[]{:S(2)}) collective-permute-start(f32[48,128]{1,0:T(8,128)S(1)} %add.30.own), channel_id=1, source_target_pairs={{0,5},{1,4},{4,1},{5,0},{8,13},{9,12},{12,9},{13,8},{2,7},{3,6},{6... | collective-permute-start | bytes 73736 | tf_op jit(solution)/shard_map/ppermute | solution.py:525
  28.7 0.0 collective-permute-done.13.odd_in
  28.7 1.5 %collective-permute-done.12.even_in = f32[48,128]{1,0:T(8,128)S(1)} collective-permute-done((f32[48,128]{1,0:T(8,128)S(1)}, f32[48,128]{1,0:T(8,128)S(1)}, u32[]{:S(2)}, u32[]{:S(2)}) %collective-permute-start.12) | collective-permute-done | bytes 24608 | tf_op jit(solution)/shard_map/ppermute | solution.py:525
  30.2 1.0 %shard_map.85 = (f32[4,2,48,128]{3,2,1,0:T(8,128)S(1)}, f32[4,2,48,128]{3,2,1,0:T(8,128)S(1)}, f32[48,128]{1,0:T(8,128)S(1)}) custom-call(s32[2,4]{1,0:T(2,128)S(1)} %get-tuple-element.45.delays_0_, s32[2,4]{1,0:T(2,128)S(1)} %get-tuple-element.46.delays_1_, s32[2,4]{1,0:T(2,128)S(1)} %get-tuple-element.44.shifts_0_, ...), custom_call_target="tpu_custom_call" | custom-call | flops 200000000 | bytes 6000000 | tf_op jit(solution)/shard_map/pallas_call | solution.py:502
  31.2 0.4 collective-permute-start.14
  31.6 0.9 %collective-permute-done.14 = f32[48,128]{1,0:T(8,128)S(1)} collective-permute-done((f32[48,128]{1,0:T(8,128)S(1)}, f32[48,128]{1,0:T(8,128)S(1)}, u32[]{:S(2)}, u32[]{:S(2)}) %collective-permute-start.14) | collective-permute-done | bytes 24608 | tf_op jit(solution)/shard_map/ppermute | solution.py:541
  32.4 0.3 collective-permute-start.16
  32.8 1.5 %collective-permute-start.15 = (f32[48,128]{1,0:T(8,128)S(1)}, f32[48,128]{1,0:T(8,128)S(1)}, u32[]{:S(2)}, u32[]{:S(2)}) collective-permute-start(f32[48,128]{1,0:T(8,128)S(1)} %add.31.own), channel_id=1, source_target_pairs={{0,5},{1,4},{4,1},{5,0},{8,13},{9,12},{12,9},{13,8},{2,7},{3,6},{6... | collective-permute-start | bytes 73736 | tf_op jit(solution)/shard_map/ppermute | solution.py:525
  34.2 1.1 %shard_map.86.taps1 = f32[8,128]{1,0:T(8,128)S(1)} custom-call(f32[4,2,48,128]{3,2,1,0:T(8,128)S(1)} %get-tuple-element.80.shifted, f32[4,2,48,128]{3,2,1,0:T(8,128)S(1)} %get-tuple-element.81.grad), custom_call_target="tpu_custom_call" | custom-call | flops 200000000 | bytes 6000000 | tf_op jit(solution)/shard_map/pallas_call | solution.py:502
  35.3 0.0 collective-permute-done.16.odd_in
  35.3 0.7 %collective-permute-done.15.even_in = f32[48,128]{1,0:T(8,128)S(1)} collective-permute-done((f32[48,128]{1,0:T(8,128)S(1)}, f32[48,128]{1,0:T(8,128)S(1)}, u32[]{:S(2)}, u32[]{:S(2)}) %collective-permute-start.15) | collective-permute-done | bytes 24608 | tf_op jit(solution)/shard_map/ppermute | solution.py:525
  36.0 1.0 %shard_map.87 = (f32[4,2,48,128]{3,2,1,0:T(8,128)S(1)}, f32[16,128]{1,0:T(8,128)S(1)}) custom-call(s32[2,4]{1,0:T(2,128)S(1)} %get-tuple-element.45.delays_0_, f32[4,2,48,128]{3,2,1,0:T(8,128)S(1)} %get-tuple-element.77.turned0, f32[4,2,48,128]{3,2,1,0:T(8,128)S(1)} %get-tuple-element.54.linear0_0_.linear0, f32[48,128]{1,0:T(8,128)S(1)} %add.31.own, ...), custom_call_target="tpu_custom_call" | custom-call | flops 200000000 | bytes 6000000 | tf_op jit(solution)/shard_map/pallas_call | solution.py:502
  37.0 0.2 collective-permute-start.17
  37.3 1.0 %collective-permute-done.17 = f32[16,128]{1,0:T(8,128)S(1)} collective-permute-done((f32[16,128]{1,0:T(8,128)S(1)}, f32[16,128]{1,0:T(8,128)S(1)}, u32[]{:S(2)}, u32[]{:S(2)}) %collective-permute-start.17) | collective-permute-done | bytes 8224 | tf_op jit(solution)/shard_map/ppermute | solution.py:541
  38.3 2.3 %collective-permute-start.20 = (f32[16,128]{1,0:T(8,128)S(1)}, f32[16,128]{1,0:T(8,128)S(1)}, u32[]{:S(2)}, u32[]{:S(2)}) collective-permute-start(f32[16,128]{1,0:T(8,128)S(1)} %add.32), channel_id=1, source_target_pairs={{0,13},{1,12},{4,9},{5,8},{8,5},{9,4},{12,1},{13,0},{2,15},{3,14},... | collective-permute-start | bytes 24584 | tf_op jit(solution)/shard_map/ppermute | solution.py:525
  40.6 0.6 %collective-permute-start.19 = (f32[16,128]{1,0:T(8,128)S(1)}, f32[16,128]{1,0:T(8,128)S(1)}, u32[]{:S(2)}, u32[]{:S(2)}) collective-permute-start(f32[16,128]{1,0:T(8,128)S(1)} %add.32), channel_id=1, source_target_pairs={{0,9},{1,8},{4,13},{5,12},{8,1},{9,0},{12,5},{13,4},{2,11},{3,10},... | collective-permute-start | bytes 24584 | tf_op jit(solution)/shard_map/ppermute | solution.py:525
  41.2 1.0 %collective-permute-start.18 = (f32[16,128]{1,0:T(8,128)S(1)}, f32[16,128]{1,0:T(8,128)S(1)}, u32[]{:S(2)}, u32[]{:S(2)}) collective-permute-start(f32[16,128]{1,0:T(8,128)S(1)} %add.32), channel_id=1, source_target_pairs={{0,5},{1,4},{4,1},{5,0},{8,13},{9,12},{12,9},{13,8},{2,7},{3,6},{6... | collective-permute-start | bytes 24584 | tf_op jit(solution)/shard_map/ppermute | solution.py:525
  42.2 1.1 %shard_map.88 = f32[4,1,2,4096]{3,2,1,0:T(2,128)} custom-call(s32[2,4]{1,0:T(2,128)S(1)} %get-tuple-element.44.shifts_0_, f32[4,2,48,128]{3,2,1,0:T(8,128)S(1)} %get-tuple-element.82.grad0, bf16[4,256,256]{2,1,0:T(8,128)(2,1)S(1)} %get-tuple-element.52.high, bf16[4,256,256]{2,1,0:T(8,128)(2,1)S(1)} %get-tuple-element.53.low), custom_call_target="tpu_custom_call" | custom-call | flops 200000000 | bytes 6000000 | tf_op jit(solution)/shard_map/pallas_call | solution.py:502
  43.3 0.0 collective-permute-done.20
  43.3 1.3 %collective-permute-done.19 = f32[16,128]{1,0:T(8,128)S(1)} collective-permute-done((f32[16,128]{1,0:T(8,128)S(1)}, f32[16,128]{1,0:T(8,128)S(1)}, u32[]{:S(2)}, u32[]{:S(2)}) %collective-permute-start.19) | collective-permute-done | bytes 8224 | tf_op jit(solution)/shard_map/ppermute | solution.py:525
  44.6 0.0 collective-permute-done.18
  44.6 0.6 %add_add_fusion = f32[16,128]{1,0:T(8,128)} fusion(f32[16,128]{1,0:T(8,128)S(1)} %collective-permute-done.19, f32[16,128]{1,0:T(8,128)S(1)} %collective-permute-done.20, f32[16,128]{1,0:T(8,128)S(1)} %add.32, f32[16,128]{1,0:T(8,128)S(1)} %collective-permute-done.18), kind=kLoop, calls=%fused_computation | loop fusion | flops 6144 | bytes 40960 | tf_op jit(solution)/shard_map/add | solution.py:577
  (6 shorter events, 0.0 us)
Async XLA Ops:
  1.8 8.2 %collective-permute-start.1 = (f32[4,2,3072]{2,1,0:T(2,128)S(1)}, f32[4,2,3072]{2,1,0:T(2,128)S(1)}, u32[]{:S(2)}, u32[]{:S(2)}) collective-permute-start(f32[4,2,3072]{2,1,0:T(2,128)S(1)} %get-tuple-element.50), channel_id=1, source_target_pairs={{0,4},{1,5},{4,0},{5,1},{8,12},{9,13},{12,8},{13,9},{2,6},{3,7},{6... | collective-permute-start | bytes 294920 | tf_op jit(solution)/shard_map/ppermute | solution.py:525
  4.9 6.6 %collective-permute-start.2 = (f32[4,2,3072]{2,1,0:T(2,128)S(1)}, f32[4,2,3072]{2,1,0:T(2,128)S(1)}, u32[]{:S(2)}, u32[]{:S(2)}) collective-permute-start(f32[4,2,3072]{2,1,0:T(2,128)S(1)} %get-tuple-element.51), channel_id=1, source_target_pairs={{0,1},{1,0},{4,8},{5,9},{8,4},{9,5},{12,13},{13,12},{2,3},{3,2},{6... | collective-permute-start | bytes 294920 | tf_op jit(solution)/shard_map/ppermute | solution.py:525
  4.9 9.1 %collective-permute-start = (f32[280,128]{1,0:T(8,128)S(1)}, f32[280,128]{1,0:T(8,128)S(1)}, u32[]{:S(2)}, u32[]{:S(2)}) collective-permute-start(f32[280,128]{1,0:T(8,128)S(1)} %get-tuple-element.43.pack), channel_id=1, source_target_pairs={{0,2},{1,3},{2,0},{3,1},{4,6},{5,7},{6,4},{7,5},{8,10},{9,11},{10,... | collective-permute-start | bytes 430088 | tf_op jit(solution)/shard_map/ppermute | solution.py:525
  6.4 5.9 %collective-permute-start.3 = (f32[4,2,1024]{2,1,0:T(2,128)S(1)}, f32[4,2,1024]{2,1,0:T(2,128)S(1)}, u32[]{:S(2)}, u32[]{:S(2)}) collective-permute-start(f32[4,2,1024]{2,1,0:T(2,128)S(1)} %get-tuple-element.56), channel_id=1, source_target_pairs={{0,6},{1,7},{2,4},{3,5},{4,2},{5,3},{6,0},{7,1},{8,14},{9,15},{10,... | collective-permute-start | bytes 98312 | tf_op jit(solution)/shard_map/ppermute | solution.py:570
  9.5 2.8 %collective-permute-start.4 = (f32[4,2,1024]{2,1,0:T(2,128)S(1)}, f32[4,2,1024]{2,1,0:T(2,128)S(1)}, u32[]{:S(2)}, u32[]{:S(2)}) collective-permute-start(f32[4,2,1024]{2,1,0:T(2,128)S(1)} %get-tuple-element.57), channel_id=1, source_target_pairs={{0,1},{1,0},{2,3},{3,2},{4,10},{5,11},{6,8},{7,9},{8,6},{9,7},{10,... | collective-permute-start | bytes 98312 | tf_op jit(solution)/shard_map/ppermute | solution.py:570
  10.0 11.8 %collective-permute-start.10 = (f32[4,2,32,128]{3,2,1,0:T(8,128)S(1)}, f32[4,2,32,128]{3,2,1,0:T(8,128)S(1)}, u32[]{:S(2)}, u32[]{:S(2)}) collective-permute-start(f32[4,2,32,128]{3,2,1,0:T(8,128)S(1)} %get-tuple-element.69.c_0_), channel_id=1, source_target_pairs={{0,2},{1,3},{2,0},{3,1},{4,6},{5,7},{6,4},{7,5},{8,10},{9,11},{10,... | collective-permute-start | bytes 393224 | tf_op jit(solution)/shard_map/ppermute | solution.py:525
  12.3 1.3 %collective-permute-start.5 = (f32[64,128]{1,0:T(8,128)S(1)}, f32[64,128]{1,0:T(8,128)S(1)}, u32[]{:S(2)}, u32[]{:S(2)}) collective-permute-start(f32[64,128]{1,0:T(8,128)S(1)} %get-tuple-element.62), channel_id=1, source_target_pairs={{0,1},{1,0},{2,3},{3,2},{4,5},{5,4},{6,7},{7,6},{8,9},{9,8},{10,11... | collective-permute-start | bytes 98312 | tf_op jit(solution)/shard_map/ppermute | solution.py:541
  13.6 3.3 %collective-permute-start.6 = (f32[64,128]{1,0:T(8,128)S(1)}, f32[64,128]{1,0:T(8,128)S(1)}, u32[]{:S(2)}, u32[]{:S(2)}) collective-permute-start(f32[64,128]{1,0:T(8,128)S(1)} %add.27), channel_id=1, source_target_pairs={{0,3},{1,2},{2,1},{3,0},{4,7},{5,6},{6,5},{7,4},{8,11},{9,10},{10,... | collective-permute-start | bytes 98312 | tf_op jit(solution)/shard_map/ppermute | solution.py:525
  18.3 1.3 %collective-permute-start.7 = (f32[48,128]{1,0:T(8,128)S(1)}, f32[48,128]{1,0:T(8,128)S(1)}, u32[]{:S(2)}, u32[]{:S(2)}) collective-permute-start(f32[48,128]{1,0:T(8,128)S(1)} %get-tuple-element.68), channel_id=1, source_target_pairs={{0,1},{1,0},{2,3},{3,2},{4,5},{5,4},{6,7},{7,6},{8,9},{9,8},{10,11... | collective-permute-start | bytes 73736 | tf_op jit(solution)/shard_map/ppermute | solution.py:541
  19.5 2.3 %collective-permute-start.9 = (f32[48,128]{1,0:T(8,128)S(1)}, f32[48,128]{1,0:T(8,128)S(1)}, u32[]{:S(2)}, u32[]{:S(2)}) collective-permute-start(f32[48,128]{1,0:T(8,128)S(1)} %add.29.own), channel_id=1, source_target_pairs={{0,1},{1,0},{4,9},{5,8},{8,5},{9,4},{12,13},{13,12},{2,3},{3,2},{6... | collective-permute-start | bytes 73736 | tf_op jit(solution)/shard_map/ppermute | solution.py:525
  19.7 3.6 %collective-permute-start.8 = (f32[48,128]{1,0:T(8,128)S(1)}, f32[48,128]{1,0:T(8,128)S(1)}, u32[]{:S(2)}, u32[]{:S(2)}) collective-permute-start(f32[48,128]{1,0:T(8,128)S(1)} %add.29.own), channel_id=1, source_target_pairs={{0,5},{1,4},{4,1},{5,0},{8,13},{9,12},{12,9},{13,8},{2,7},{3,6},{6... | collective-permute-start | bytes 73736 | tf_op jit(solution)/shard_map/ppermute | solution.py:525
  24.0 1.3 %collective-permute-start.11 = (f32[48,128]{1,0:T(8,128)S(1)}, f32[48,128]{1,0:T(8,128)S(1)}, u32[]{:S(2)}, u32[]{:S(2)}) collective-permute-start(f32[48,128]{1,0:T(8,128)S(1)} %get-tuple-element.73), channel_id=1, source_target_pairs={{0,1},{1,0},{2,3},{3,2},{4,5},{5,4},{6,7},{7,6},{8,9},{9,8},{10,11... | collective-permute-start | bytes 73736 | tf_op jit(solution)/shard_map/ppermute | solution.py:541
  25.3 3.4 %collective-permute-start.13 = (f32[48,128]{1,0:T(8,128)S(1)}, f32[48,128]{1,0:T(8,128)S(1)}, u32[]{:S(2)}, u32[]{:S(2)}) collective-permute-start(f32[48,128]{1,0:T(8,128)S(1)} %add.30.own), channel_id=1, source_target_pairs={{0,1},{1,0},{4,9},{5,8},{8,5},{9,4},{12,13},{13,12},{2,3},{3,2},{6... | collective-permute-start | bytes 73736 | tf_op jit(solution)/shard_map/ppermute | solution.py:525
  25.6 4.6 %collective-permute-start.12 = (f32[48,128]{1,0:T(8,128)S(1)}, f32[48,128]{1,0:T(8,128)S(1)}, u32[]{:S(2)}, u32[]{:S(2)}) collective-permute-start(f32[48,128]{1,0:T(8,128)S(1)} %add.30.own), channel_id=1, source_target_pairs={{0,5},{1,4},{4,1},{5,0},{8,13},{9,12},{12,9},{13,8},{2,7},{3,6},{6... | collective-permute-start | bytes 73736 | tf_op jit(solution)/shard_map/ppermute | solution.py:525
  31.2 1.3 %collective-permute-start.14 = (f32[48,128]{1,0:T(8,128)S(1)}, f32[48,128]{1,0:T(8,128)S(1)}, u32[]{:S(2)}, u32[]{:S(2)}) collective-permute-start(f32[48,128]{1,0:T(8,128)S(1)} %get-tuple-element.78), channel_id=1, source_target_pairs={{0,1},{1,0},{2,3},{3,2},{4,5},{5,4},{6,7},{7,6},{8,9},{9,8},{10,11... | collective-permute-start | bytes 73736 | tf_op jit(solution)/shard_map/ppermute | solution.py:541
  32.4 2.9 %collective-permute-start.16 = (f32[48,128]{1,0:T(8,128)S(1)}, f32[48,128]{1,0:T(8,128)S(1)}, u32[]{:S(2)}, u32[]{:S(2)}) collective-permute-start(f32[48,128]{1,0:T(8,128)S(1)} %add.31.own), channel_id=1, source_target_pairs={{0,1},{1,0},{4,9},{5,8},{8,5},{9,4},{12,13},{13,12},{2,3},{3,2},{6... | collective-permute-start | bytes 73736 | tf_op jit(solution)/shard_map/ppermute | solution.py:525
  32.8 3.3 %collective-permute-start.15 = (f32[48,128]{1,0:T(8,128)S(1)}, f32[48,128]{1,0:T(8,128)S(1)}, u32[]{:S(2)}, u32[]{:S(2)}) collective-permute-start(f32[48,128]{1,0:T(8,128)S(1)} %add.31.own), channel_id=1, source_target_pairs={{0,5},{1,4},{4,1},{5,0},{8,13},{9,12},{12,9},{13,8},{2,7},{3,6},{6... | collective-permute-start | bytes 73736 | tf_op jit(solution)/shard_map/ppermute | solution.py:525
  37.0 1.2 %collective-permute-start.17 = (f32[16,128]{1,0:T(8,128)S(1)}, f32[16,128]{1,0:T(8,128)S(1)}, u32[]{:S(2)}, u32[]{:S(2)}) collective-permute-start(f32[16,128]{1,0:T(8,128)S(1)} %get-tuple-element.83), channel_id=1, source_target_pairs={{0,1},{1,0},{2,3},{3,2},{4,5},{5,4},{6,7},{7,6},{8,9},{9,8},{10,11... | collective-permute-start | bytes 24584 | tf_op jit(solution)/shard_map/ppermute | solution.py:541
  38.3 5.0 %collective-permute-start.20 = (f32[16,128]{1,0:T(8,128)S(1)}, f32[16,128]{1,0:T(8,128)S(1)}, u32[]{:S(2)}, u32[]{:S(2)}) collective-permute-start(f32[16,128]{1,0:T(8,128)S(1)} %add.32), channel_id=1, source_target_pairs={{0,13},{1,12},{4,9},{5,8},{8,5},{9,4},{12,1},{13,0},{2,15},{3,14},... | collective-permute-start | bytes 24584 | tf_op jit(solution)/shard_map/ppermute | solution.py:525
  40.6 4.0 %collective-permute-start.19 = (f32[16,128]{1,0:T(8,128)S(1)}, f32[16,128]{1,0:T(8,128)S(1)}, u32[]{:S(2)}, u32[]{:S(2)}) collective-permute-start(f32[16,128]{1,0:T(8,128)S(1)} %add.32), channel_id=1, source_target_pairs={{0,9},{1,8},{4,13},{5,12},{8,1},{9,0},{12,5},{13,4},{2,11},{3,10},... | collective-permute-start | bytes 24584 | tf_op jit(solution)/shard_map/ppermute | solution.py:525
  41.2 3.4 %collective-permute-start.18 = (f32[16,128]{1,0:T(8,128)S(1)}, f32[16,128]{1,0:T(8,128)S(1)}, u32[]{:S(2)}, u32[]{:S(2)}) collective-permute-start(f32[16,128]{1,0:T(8,128)S(1)} %add.32), channel_id=1, source_target_pairs={{0,5},{1,4},{4,1},{5,0},{8,13},{9,12},{12,9},{13,8},{2,7},{3,6},{6... | collective-permute-start | bytes 24584 | tf_op jit(solution)/shard_map/ppermute | solution.py:525

commit v10 on v9

--- a/solution.py
+++ b/solution.py
@@ -369,7 +369,7 @@
 
 
 def k_third(
-    delays, gains, linear1, own, even_in, odd_in, cotangent, turned1, out, spread, held, held_out
+    delays, gains, linear1, own, odd_in, even_in, cotangent, turned1, out, spread, held, held_out
 ):
     bands = linear1.shape[0]
     rows = linear1.shape[2] - 2 * PAD
@@ -389,7 +389,7 @@
 
 
 def k_fourth(
-    delays, shifts, gains, turned1, linear1, own, even_in, odd_in, high, low, cosine0, sine0, field1,
+    delays, shifts, gains, turned1, linear1, own, odd_in, even_in, high, low, cosine0, sine0, field1,
     grad1, turned0, out, spread, moved, held, held_out,
 ):
     bands = linear1.shape[0]
@@ -466,7 +466,7 @@
 
 
 def k_fifth(
-    scale, delays, turned0, linear0, own, even_in, odd_in, shifted, taps1,
+    scale, delays, turned0, linear0, own, odd_in, even_in, shifted, taps1,
     grad0, out, spread, held,
 ):
     bands = turned0.shape[0]
@@ -580,7 +580,7 @@
 def exchanged(part, doubled):
     part = over_cores(part)
     part = part if doubled else summed(part, "band")
-    return (part,) + neighbours(part, part, True)
+    return (part,) + neighbours(part, part, True)[::-1]
 
 
 def on_device(signal, cotangent, taps, gains, walk_off, tap_shift):

time: 45.3 us -> 43.4 us (0.958)
  waiting for transfers between devices: 11.6 us -> 9.99 us
    ppermute x14, waiting for transfers between devices: 6.9 us -> 5.46 us  [swapped(): return lax.ppermute(x, (axis, 'pol'), pairs)]
    ppermute x14, starting transfers between devices: 17.9 us -> 17.4 us  [swapped(): return lax.ppermute(x, (axis, 'pol'), pairs)]
where the time goes in v10:
time: 43.4 us; the launch traced here: 43.2 us
  starting transfers between devices  22.3 us (51%)
  waiting for transfers between devices  9.99 us (23%)
  Pallas kernels  9.57 us (22%)
  between operations  0.75 us (2%)
  other arithmetic  0.63 us (1%)
    ppermute x14, starting transfers between devices, swapped(): return lax.ppermute(x, (axis, 'pol'), pairs)  17.4 us
    pallas_call x11, Pallas kernels, call(): pl.pallas_call(kernel, out_shape=shapes, in_specs=jax.tree.map(lambda _:...  8.39 us
    ppermute x14, waiting for transfers between devices, swapped(): return lax.ppermute(x, (axis, 'pol'), pairs)  5.46 us
    ppermute x5, waiting for transfers between devices, over_cores(): lax.ppermute(x, 'pol', [(p, cores - 1 - p) for p in range(cores)])  4.52 us
    ppermute x2, starting transfers between devices, aslant(): return lax.ppermute(x, ('tm', 'band', 'pol'), pairs)  3.12 us
    ppermute x5, starting transfers between devices, over_cores(): lax.ppermute(x, 'pol', [(p, cores - 1 - p) for p in range(cores)])  1.77 us
    pallas_call x1, Pallas kernels, on_device(): pl.pallas_call(k_begin, out_shape=[cut, cut, near, near, pack, shape(own,...  1.18 us
  transfers between devices with their start and end apart: 21, of which 10 were waited for; matrix products, arithmetic and copies ran while one was open for 0% of the time, Pallas kernels for 13%

profile of v10, /device:TPU:0, one launch (start us, length us, event | category | flops | bytes accessed | tf_op | source)
XLA Modules:
  0.0 43.2 jit_solution(16137714523348169421)
XLA Ops:
  0.6 1.2 %shard_map.77 = (f32[4,2,3072]{2,1,0:T(2,128)S(1)}, f32[4,2,3072]{2,1,0:T(2,128)S(1)}, f32[4,2,1024]{2,1,0:T(2,128)S(1)}, f32[4,2,1024]{2,1,0:T(2,128)S(1)}, f32...) custom-call(f32[4,1,2,4096]{3,2,1,0:T(2,128)} %signal.1, f32[4,1,2,4096]{3,2,1,0:T(2,128)} %cotangent.1, ...), custom_call_target="tpu_custom_call" | custom-call | flops 100000000 | bytes 1000000 | tf_op jit(solution)/shard_map/pallas_call | solution.py:618
  1.8 3.1 %collective-permute-start.1 = (f32[4,2,3072]{2,1,0:T(2,128)S(1)}, f32[4,2,3072]{2,1,0:T(2,128)S(1)}, u32[]{:S(2)}, u32[]{:S(2)}) collective-permute-start(f32[4,2,3072]{2,1,0:T(2,128)S(1)} %get-tuple-element.50), channel_id=1, source_target_pairs={{0,4},{1,5},{4,0},{5,1},{8,12},{9,13},{12,8},{13,9},{2,6},{3,7},{6... | collective-permute-start | bytes 294920 | tf_op jit(solution)/shard_map/ppermute | solution.py:525
  4.9 0.0 collective-permute-start.2
  4.9 1.5 %collective-permute-start = (f32[280,128]{1,0:T(8,128)S(1)}, f32[280,128]{1,0:T(8,128)S(1)}, u32[]{:S(2)}, u32[]{:S(2)}) collective-permute-start(f32[280,128]{1,0:T(8,128)S(1)} %get-tuple-element.43.pack), channel_id=1, source_target_pairs={{0,2},{1,3},{2,0},{3,1},{4,6},{5,7},{6,4},{7,5},{8,10},{9,11},{10,... | collective-permute-start | bytes 430088 | tf_op jit(solution)/shard_map/ppermute | solution.py:525
  6.4 3.1 %collective-permute-start.3 = (f32[4,2,1024]{2,1,0:T(2,128)S(1)}, f32[4,2,1024]{2,1,0:T(2,128)S(1)}, u32[]{:S(2)}, u32[]{:S(2)}) collective-permute-start(f32[4,2,1024]{2,1,0:T(2,128)S(1)} %get-tuple-element.56), channel_id=1, source_target_pairs={{0,6},{1,7},{2,4},{3,5},{4,2},{5,3},{6,0},{7,1},{8,14},{9,15},{10,... | collective-permute-start | bytes 98312 | tf_op jit(solution)/shard_map/ppermute | solution.py:570
  9.5 0.0 collective-permute-start.4
  9.5 0.4 %shard_map.78 = (s32[2,4]{1,0:T(2,128)S(1)}, s32[2,4]{1,0:T(2,128)S(1)}, f32[2,4]{1,0:T(2,128)S(1)}, bf16[4,256,256]{2,1,0:T(8,128)(2,1)S(1)}, bf16[4,256,256]{2...) custom-call(f32[280,128]{1,0:T(8,128)S(1)} %get-tuple-element.43.pack), custom_call_target="tpu_custom_call" | custom-call | flops 200000000 | bytes 6000000 | tf_op jit(solution)/shard_map/pallas_call | solution.py:502
  10.0 0.0 collective-permute-done.1.sides_0_.s_0__0_
  10.0 1.6 %collective-permute-start.10 = (f32[4,2,32,128]{3,2,1,0:T(8,128)S(1)}, f32[4,2,32,128]{3,2,1,0:T(8,128)S(1)}, u32[]{:S(2)}, u32[]{:S(2)}) collective-permute-start(f32[4,2,32,128]{3,2,1,0:T(8,128)S(1)} %get-tuple-element.69.c_0_), channel_id=1, source_target_pairs={{0,2},{1,3},{2,0},{3,1},{4,6},{5,7},{6,4},{7,5},{8,10},{9,11},{10,... | collective-permute-start | bytes 393224 | tf_op jit(solution)/shard_map/ppermute | solution.py:525
  11.6 0.0 collective-permute-done.2.sides_1_.s_0__1_
  11.6 0.8 %shard_map.80 = (f32[4,2,48,128]{3,2,1,0:T(8,128)S(1)}, f32[4,2,48,128]{3,2,1,0:T(8,128)S(1)}, f32[64,128]{1,0:T(8,128)S(1)}) custom-call(s32[2,4]{1,0:T(2,128)S(1)} %get-tuple-element.45.delays_0_, s32[2,4]{1,0:T(2,128)S(1)} %get-tuple-element.44.shifts_0_, f32[280,128]{1,0:T(8,128)S(1)} %get-tuple-element.43.pack, ...), custom_call_target="tpu_custom_call" | custom-call | flops 200000000 | bytes 6000000 | tf_op jit(solution)/shard_map/pallas_call | solution.py:502
  12.3 0.0 collective-permute-done.3.sides_0_.s_1__0_
  12.3 0.0 collective-permute-done.4.sides_1_.s_1__1_
  12.3 0.3 collective-permute-start.5
  12.6 1.0 %collective-permute-done.5 = f32[64,128]{1,0:T(8,128)S(1)} collective-permute-done((f32[64,128]{1,0:T(8,128)S(1)}, f32[64,128]{1,0:T(8,128)S(1)}, u32[]{:S(2)}, u32[]{:S(2)}) %collective-permute-start.5) | collective-permute-done | bytes 32800 | tf_op jit(solution)/shard_map/ppermute | solution.py:541
  13.6 0.4 collective-permute-start.6
  14.0 0.0 collective-permute-done.pack
  14.0 0.4 %shard_map.79 = (s32[2,4]{1,0:T(2,128)S(1)}, s32[2,4]{1,0:T(2,128)S(1)}, f32[2,4]{1,0:T(2,128)S(1)}, bf16[4,256,256]{2,1,0:T(8,128)(2,1)S(1)}, bf16[4,256,256]{2...) custom-call(f32[280,128]{1,0:T(8,128)S(1)} %collective-permute-done.pack), custom_call_target="tpu_custom_call" | custom-call | flops 200000000 | bytes 6000000 | tf_op jit(solution)/shard_map/pallas_call | solution.py:502
  14.5 0.6 %shard_map.81.linear0_1_ = f32[4,2,48,128]{3,2,1,0:T(8,128)S(1)} custom-call(s32[2,4]{1,0:T(2,128)S(1)} %get-tuple-element.47.shifts_0_.shifts_1_, f32[280,128]{1,0:T(8,128)S(1)} %collective-permute-done.pack, f32[4,2,1024]{2,1,0:T(2,128)S(1)} %collective-permute-done.3.sides_0_.s_1__0_, f32[4,2,1024]{2,1,0:T(2,128)S(1)} %collective-permute-done.4.sides_1_.s_1__1_, ...), custom_call_target="tpu_custom_call" | custom-call | flops 200000000 | bytes 6000000 | tf_op jit(solution)/shard_map/pallas_call | solution.py:502
  15.0 1.9 %collective-permute-done.6 = f32[64,128]{1,0:T(8,128)S(1)} collective-permute-done((f32[64,128]{1,0:T(8,128)S(1)}, f32[64,128]{1,0:T(8,128)S(1)}, u32[]{:S(2)}, u32[]{:S(2)}) %collective-permute-start.6) | collective-permute-done | bytes 32800 | tf_op jit(solution)/shard_map/ppermute | solution.py:525
  17.0 1.3 %shard_map.82 = (f32[4,48,128]{2,1,0:T(8,128)S(1)}, f32[4,48,128]{2,1,0:T(8,128)S(1)}, f32[8,2,48,128]{3,2,1,0:T(8,128)S(1)}, f32[4,2,48,128]{3,2,1,0:T(8,128)S(...) custom-call(s32[2,4]{1,0:T(2,128)S(1)} %get-tuple-element.45.delays_0_, ...), custom_call_target="tpu_custom_call" | custom-call | flops 200000000 | bytes 6000000 | tf_op jit(solution)/shard_map/pallas_call | solution.py:502
  18.3 0.3 collective-permute-start.7
  18.5 1.0 %collective-permute-done.7 = f32[48,128]{1,0:T(8,128)S(1)} collective-permute-done((f32[48,128]{1,0:T(8,128)S(1)}, f32[48,128]{1,0:T(8,128)S(1)}, u32[]{:S(2)}, u32[]{:S(2)}) %collective-permute-start.7) | collective-permute-done | bytes 24608 | tf_op jit(solution)/shard_map/ppermute | solution.py:541
  19.5 2.2 %collective-permute-start.9 = (f32[48,128]{1,0:T(8,128)S(1)}, f32[48,128]{1,0:T(8,128)S(1)}, u32[]{:S(2)}, u32[]{:S(2)}) collective-permute-start(f32[48,128]{1,0:T(8,128)S(1)} %add.29.own), channel_id=1, source_target_pairs={{0,5},{1,4},{4,1},{5,0},{8,13},{9,12},{12,9},{13,8},{2,7},{3,6},{6... | collective-permute-start | bytes 73736 | tf_op jit(solution)/shard_map/ppermute | solution.py:525
  21.7 0.3 collective-permute-start.8
  22.1 0.0 collective-permute-done.10.c_1_
  22.1 0.1 shard_map.83.cotangent
  22.1 1.1 %collective-permute-done.9.even_in = f32[48,128]{1,0:T(8,128)S(1)} collective-permute-done((f32[48,128]{1,0:T(8,128)S(1)}, f32[48,128]{1,0:T(8,128)S(1)}, u32[]{:S(2)}, u32[]{:S(2)}) %collective-permute-start.9) | collective-permute-done | bytes 24608 | tf_op jit(solution)/shard_map/ppermute | solution.py:525
  23.2 0.0 collective-permute-done.8.odd_in
  23.2 0.7 %shard_map.84 = (f32[8,2,48,128]{3,2,1,0:T(8,128)S(1)}, f32[48,128]{1,0:T(8,128)S(1)}) custom-call(s32[2,4]{1,0:T(2,128)S(1)} %get-tuple-element.45.delays_0_, s32[2,4]{1,0:T(2,128)S(1)} %get-tuple-element.46.delays_1_, f32[2,4]{1,0:T(2,128)S(1)} %get-tuple-element.48.gains_0_, f32[2,4]{1,0:T(2,128)S(1)} %get-tuple-element.49.gains_1_, ...), custom_call_target="tpu_custom_call" | custom-call | flops 200000000 | bytes 6000000 | tf_op jit(solution)/shard_map/pallas_call | solution.py:502
  23.9 0.4 collective-permute-start.11
  24.3 0.9 %collective-permute-done.11 = f32[48,128]{1,0:T(8,128)S(1)} collective-permute-done((f32[48,128]{1,0:T(8,128)S(1)}, f32[48,128]{1,0:T(8,128)S(1)}, u32[]{:S(2)}, u32[]{:S(2)}) %collective-permute-start.11) | collective-permute-done | bytes 24608 | tf_op jit(solution)/shard_map/ppermute | solution.py:541
  25.2 1.8 %collective-permute-start.13 = (f32[48,128]{1,0:T(8,128)S(1)}, f32[48,128]{1,0:T(8,128)S(1)}, u32[]{:S(2)}, u32[]{:S(2)}) collective-permute-start(f32[48,128]{1,0:T(8,128)S(1)} %add.30.own), channel_id=1, source_target_pairs={{0,5},{1,4},{4,1},{5,0},{8,13},{9,12},{12,9},{13,8},{2,7},{3,6},{6... | collective-permute-start | bytes 73736 | tf_op jit(solution)/shard_map/ppermute | solution.py:525
  27.0 0.3 collective-permute-start.12
  27.3 1.2 %collective-permute-done.13.even_in = f32[48,128]{1,0:T(8,128)S(1)} collective-permute-done((f32[48,128]{1,0:T(8,128)S(1)}, f32[48,128]{1,0:T(8,128)S(1)}, u32[]{:S(2)}, u32[]{:S(2)}) %collective-permute-start.13) | collective-permute-done | bytes 24608 | tf_op jit(solution)/shard_map/ppermute | solution.py:525
  28.5 0.0 collective-permute-done.12.odd_in
  28.5 1.0 %shard_map.85 = (f32[4,2,48,128]{3,2,1,0:T(8,128)S(1)}, f32[4,2,48,128]{3,2,1,0:T(8,128)S(1)}, f32[48,128]{1,0:T(8,128)S(1)}) custom-call(s32[2,4]{1,0:T(2,128)S(1)} %get-tuple-element.45.delays_0_, s32[2,4]{1,0:T(2,128)S(1)} %get-tuple-element.46.delays_1_, s32[2,4]{1,0:T(2,128)S(1)} %get-tuple-element.44.shifts_0_, ...), custom_call_target="tpu_custom_call" | custom-call | flops 200000000 | bytes 6000000 | tf_op jit(solution)/shard_map/pallas_call | solution.py:502
  29.5 0.4 collective-permute-start.14
  29.9 0.9 %collective-permute-done.14 = f32[48,128]{1,0:T(8,128)S(1)} collective-permute-done((f32[48,128]{1,0:T(8,128)S(1)}, f32[48,128]{1,0:T(8,128)S(1)}, u32[]{:S(2)}, u32[]{:S(2)}) %collective-permute-start.14) | collective-permute-done | bytes 24608 | tf_op jit(solution)/shard_map/ppermute | solution.py:541
  30.8 1.8 %collective-permute-start.16 = (f32[48,128]{1,0:T(8,128)S(1)}, f32[48,128]{1,0:T(8,128)S(1)}, u32[]{:S(2)}, u32[]{:S(2)}) collective-permute-start(f32[48,128]{1,0:T(8,128)S(1)} %add.31.own), channel_id=1, source_target_pairs={{0,5},{1,4},{4,1},{5,0},{8,13},{9,12},{12,9},{13,8},{2,7},{3,6},{6... | collective-permute-start | bytes 73736 | tf_op jit(solution)/shard_map/ppermute | solution.py:525
  32.6 0.3 collective-permute-start.15
  32.9 1.1 %shard_map.86.taps1 = f32[8,128]{1,0:T(8,128)S(1)} custom-call(f32[4,2,48,128]{3,2,1,0:T(8,128)S(1)} %get-tuple-element.80.shifted, f32[4,2,48,128]{3,2,1,0:T(8,128)S(1)} %get-tuple-element.81.grad), custom_call_target="tpu_custom_call" | custom-call | flops 200000000 | bytes 6000000 | tf_op jit(solution)/shard_map/pallas_call | solution.py:502
  34.0 0.1 collective-permute-done.16.even_in
  34.1 0.0 collective-permute-done.15.odd_in
  34.1 1.0 %shard_map.87 = (f32[4,2,48,128]{3,2,1,0:T(8,128)S(1)}, f32[16,128]{1,0:T(8,128)S(1)}) custom-call(s32[2,4]{1,0:T(2,128)S(1)} %get-tuple-element.45.delays_0_, f32[4,2,48,128]{3,2,1,0:T(8,128)S(1)} %get-tuple-element.77.turned0, f32[4,2,48,128]{3,2,1,0:T(8,128)S(1)} %get-tuple-element.54.linear0_0_.linear0, f32[48,128]{1,0:T(8,128)S(1)} %add.31.own, ...), custom_call_target="tpu_custom_call" | custom-call | flops 200000000 | bytes 6000000 | tf_op jit(solution)/shard_map/pallas_call | solution.py:502
  35.1 0.4 collective-permute-start.17
  35.5 0.8 %collective-permute-done.17 = f32[16,128]{1,0:T(8,128)S(1)} collective-permute-done((f32[16,128]{1,0:T(8,128)S(1)}, f32[16,128]{1,0:T(8,128)S(1)}, u32[]{:S(2)}, u32[]{:S(2)}) %collective-permute-start.17) | collective-permute-done | bytes 8224 | tf_op jit(solution)/shard_map/ppermute | solution.py:541
  36.3 0.9 %collective-permute-start.20 = (f32[16,128]{1,0:T(8,128)S(1)}, f32[16,128]{1,0:T(8,128)S(1)}, u32[]{:S(2)}, u32[]{:S(2)}) collective-permute-start(f32[16,128]{1,0:T(8,128)S(1)} %add.32), channel_id=1, source_target_pairs={{0,13},{1,12},{4,9},{5,8},{8,5},{9,4},{12,1},{13,0},{2,15},{3,14},... | collective-permute-start | bytes 24584 | tf_op jit(solution)/shard_map/ppermute | solution.py:525
  37.2 2.3 %collective-permute-start.19 = (f32[16,128]{1,0:T(8,128)S(1)}, f32[16,128]{1,0:T(8,128)S(1)}, u32[]{:S(2)}, u32[]{:S(2)}) collective-permute-start(f32[16,128]{1,0:T(8,128)S(1)} %add.32), channel_id=1, source_target_pairs={{0,9},{1,8},{4,13},{5,12},{8,1},{9,0},{12,5},{13,4},{2,11},{3,10},... | collective-permute-start | bytes 24584 | tf_op jit(solution)/shard_map/ppermute | solution.py:525
  39.5 0.8 %collective-permute-start.18 = (f32[16,128]{1,0:T(8,128)S(1)}, f32[16,128]{1,0:T(8,128)S(1)}, u32[]{:S(2)}, u32[]{:S(2)}) collective-permute-start(f32[16,128]{1,0:T(8,128)S(1)} %add.32), channel_id=1, source_target_pairs={{0,5},{1,4},{4,1},{5,0},{8,13},{9,12},{12,9},{13,8},{2,7},{3,6},{6... | collective-permute-start | bytes 24584 | tf_op jit(solution)/shard_map/ppermute | solution.py:525
  40.4 1.1 %shard_map.88 = f32[4,1,2,4096]{3,2,1,0:T(2,128)} custom-call(s32[2,4]{1,0:T(2,128)S(1)} %get-tuple-element.44.shifts_0_, f32[4,2,48,128]{3,2,1,0:T(8,128)S(1)} %get-tuple-element.82.grad0, bf16[4,256,256]{2,1,0:T(8,128)(2,1)S(1)} %get-tuple-element.52.high, bf16[4,256,256]{2,1,0:T(8,128)(2,1)S(1)} %get-tuple-element.53.low), custom_call_target="tpu_custom_call" | custom-call | flops 200000000 | bytes 6000000 | tf_op jit(solution)/shard_map/pallas_call | solution.py:502
  41.5 0.0 collective-permute-done.20
  41.5 0.0 collective-permute-done.19
  41.5 1.1 %collective-permute-done.18 = f32[16,128]{1,0:T(8,128)S(1)} collective-permute-done((f32[16,128]{1,0:T(8,128)S(1)}, f32[16,128]{1,0:T(8,128)S(1)}, u32[]{:S(2)}, u32[]{:S(2)}) %collective-permute-start.18) | collective-permute-done | bytes 8224 | tf_op jit(solution)/shard_map/ppermute | solution.py:525
  42.6 0.6 %add_add_fusion = f32[16,128]{1,0:T(8,128)} fusion(f32[16,128]{1,0:T(8,128)S(1)} %collective-permute-done.19, f32[16,128]{1,0:T(8,128)S(1)} %collective-permute-done.20, f32[16,128]{1,0:T(8,128)S(1)} %add.32, f32[16,128]{1,0:T(8,128)S(1)} %collective-permute-done.18), kind=kLoop, calls=%fused_computation | loop fusion | flops 6144 | bytes 40960 | tf_op jit(solution)/shard_map/add | solution.py:577
  (6 shorter events, 0.0 us)
Async XLA Ops:
  1.8 8.2 %collective-permute-start.1 = (f32[4,2,3072]{2,1,0:T(2,128)S(1)}, f32[4,2,3072]{2,1,0:T(2,128)S(1)}, u32[]{:S(2)}, u32[]{:S(2)}) collective-permute-start(f32[4,2,3072]{2,1,0:T(2,128)S(1)} %get-tuple-element.50), channel_id=1, source_target_pairs={{0,4},{1,5},{4,0},{5,1},{8,12},{9,13},{12,8},{13,9},{2,6},{3,7},{6... | collective-permute-start | bytes 294920 | tf_op jit(solution)/shard_map/ppermute | solution.py:525
  4.9 6.6 %collective-permute-start.2 = (f32[4,2,3072]{2,1,0:T(2,128)S(1)}, f32[4,2,3072]{2,1,0:T(2,128)S(1)}, u32[]{:S(2)}, u32[]{:S(2)}) collective-permute-start(f32[4,2,3072]{2,1,0:T(2,128)S(1)} %get-tuple-element.51), channel_id=1, source_target_pairs={{0,1},{1,0},{4,8},{5,9},{8,4},{9,5},{12,13},{13,12},{2,3},{3,2},{6... | collective-permute-start | bytes 294920 | tf_op jit(solution)/shard_map/ppermute | solution.py:525
  4.9 9.1 %collective-permute-start = (f32[280,128]{1,0:T(8,128)S(1)}, f32[280,128]{1,0:T(8,128)S(1)}, u32[]{:S(2)}, u32[]{:S(2)}) collective-permute-start(f32[280,128]{1,0:T(8,128)S(1)} %get-tuple-element.43.pack), channel_id=1, source_target_pairs={{0,2},{1,3},{2,0},{3,1},{4,6},{5,7},{6,4},{7,5},{8,10},{9,11},{10,... | collective-permute-start | bytes 430088 | tf_op jit(solution)/shard_map/ppermute | solution.py:525
  6.4 5.9 %collective-permute-start.3 = (f32[4,2,1024]{2,1,0:T(2,128)S(1)}, f32[4,2,1024]{2,1,0:T(2,128)S(1)}, u32[]{:S(2)}, u32[]{:S(2)}) collective-permute-start(f32[4,2,1024]{2,1,0:T(2,128)S(1)} %get-tuple-element.56), channel_id=1, source_target_pairs={{0,6},{1,7},{2,4},{3,5},{4,2},{5,3},{6,0},{7,1},{8,14},{9,15},{10,... | collective-permute-start | bytes 98312 | tf_op jit(solution)/shard_map/ppermute | solution.py:570
  9.5 2.8 %collective-permute-start.4 = (f32[4,2,1024]{2,1,0:T(2,128)S(1)}, f32[4,2,1024]{2,1,0:T(2,128)S(1)}, u32[]{:S(2)}, u32[]{:S(2)}) collective-permute-start(f32[4,2,1024]{2,1,0:T(2,128)S(1)} %get-tuple-element.57), channel_id=1, source_target_pairs={{0,1},{1,0},{2,3},{3,2},{4,10},{5,11},{6,8},{7,9},{8,6},{9,7},{10,... | collective-permute-start | bytes 98312 | tf_op jit(solution)/shard_map/ppermute | solution.py:570
  10.0 12.1 %collective-permute-start.10 = (f32[4,2,32,128]{3,2,1,0:T(8,128)S(1)}, f32[4,2,32,128]{3,2,1,0:T(8,128)S(1)}, u32[]{:S(2)}, u32[]{:S(2)}) collective-permute-start(f32[4,2,32,128]{3,2,1,0:T(8,128)S(1)} %get-tuple-element.69.c_0_), channel_id=1, source_target_pairs={{0,2},{1,3},{2,0},{3,1},{4,6},{5,7},{6,4},{7,5},{8,10},{9,11},{10,... | collective-permute-start | bytes 393224 | tf_op jit(solution)/shard_map/ppermute | solution.py:525
  12.3 1.3 %collective-permute-start.5 = (f32[64,128]{1,0:T(8,128)S(1)}, f32[64,128]{1,0:T(8,128)S(1)}, u32[]{:S(2)}, u32[]{:S(2)}) collective-permute-start(f32[64,128]{1,0:T(8,128)S(1)} %get-tuple-element.62), channel_id=1, source_target_pairs={{0,1},{1,0},{2,3},{3,2},{4,5},{5,4},{6,7},{7,6},{8,9},{9,8},{10,11... | collective-permute-start | bytes 98312 | tf_op jit(solution)/shard_map/ppermute | solution.py:541
  13.6 3.3 %collective-permute-start.6 = (f32[64,128]{1,0:T(8,128)S(1)}, f32[64,128]{1,0:T(8,128)S(1)}, u32[]{:S(2)}, u32[]{:S(2)}) collective-permute-start(f32[64,128]{1,0:T(8,128)S(1)} %add.27), channel_id=1, source_target_pairs={{0,3},{1,2},{2,1},{3,0},{4,7},{5,6},{6,5},{7,4},{8,11},{9,10},{10,... | collective-permute-start | bytes 98312 | tf_op jit(solution)/shard_map/ppermute | solution.py:525
  18.3 1.3 %collective-permute-start.7 = (f32[48,128]{1,0:T(8,128)S(1)}, f32[48,128]{1,0:T(8,128)S(1)}, u32[]{:S(2)}, u32[]{:S(2)}) collective-permute-start(f32[48,128]{1,0:T(8,128)S(1)} %get-tuple-element.68), channel_id=1, source_target_pairs={{0,1},{1,0},{2,3},{3,2},{4,5},{5,4},{6,7},{7,6},{8,9},{9,8},{10,11... | collective-permute-start | bytes 73736 | tf_op jit(solution)/shard_map/ppermute | solution.py:541
  19.5 3.7 %collective-permute-start.9 = (f32[48,128]{1,0:T(8,128)S(1)}, f32[48,128]{1,0:T(8,128)S(1)}, u32[]{:S(2)}, u32[]{:S(2)}) collective-permute-start(f32[48,128]{1,0:T(8,128)S(1)} %add.29.own), channel_id=1, source_target_pairs={{0,5},{1,4},{4,1},{5,0},{8,13},{9,12},{12,9},{13,8},{2,7},{3,6},{6... | collective-permute-start | bytes 73736 | tf_op jit(solution)/shard_map/ppermute | solution.py:525
  21.7 1.5 %collective-permute-start.8 = (f32[48,128]{1,0:T(8,128)S(1)}, f32[48,128]{1,0:T(8,128)S(1)}, u32[]{:S(2)}, u32[]{:S(2)}) collective-permute-start(f32[48,128]{1,0:T(8,128)S(1)} %add.29.own), channel_id=1, source_target_pairs={{0,1},{1,0},{4,9},{5,8},{8,5},{9,4},{12,13},{13,12},{2,3},{3,2},{6... | collective-permute-start | bytes 73736 | tf_op jit(solution)/shard_map/ppermute | solution.py:525
  23.9 1.3 %collective-permute-start.11 = (f32[48,128]{1,0:T(8,128)S(1)}, f32[48,128]{1,0:T(8,128)S(1)}, u32[]{:S(2)}, u32[]{:S(2)}) collective-permute-start(f32[48,128]{1,0:T(8,128)S(1)} %get-tuple-element.73), channel_id=1, source_target_pairs={{0,1},{1,0},{2,3},{3,2},{4,5},{5,4},{6,7},{7,6},{8,9},{9,8},{10,11... | collective-permute-start | bytes 73736 | tf_op jit(solution)/shard_map/ppermute | solution.py:541
  25.2 3.3 %collective-permute-start.13 = (f32[48,128]{1,0:T(8,128)S(1)}, f32[48,128]{1,0:T(8,128)S(1)}, u32[]{:S(2)}, u32[]{:S(2)}) collective-permute-start(f32[48,128]{1,0:T(8,128)S(1)} %add.30.own), channel_id=1, source_target_pairs={{0,5},{1,4},{4,1},{5,0},{8,13},{9,12},{12,9},{13,8},{2,7},{3,6},{6... | collective-permute-start | bytes 73736 | tf_op jit(solution)/shard_map/ppermute | solution.py:525
  27.0 1.5 %collective-permute-start.12 = (f32[48,128]{1,0:T(8,128)S(1)}, f32[48,128]{1,0:T(8,128)S(1)}, u32[]{:S(2)}, u32[]{:S(2)}) collective-permute-start(f32[48,128]{1,0:T(8,128)S(1)} %add.30.own), channel_id=1, source_target_pairs={{0,1},{1,0},{4,9},{5,8},{8,5},{9,4},{12,13},{13,12},{2,3},{3,2},{6... | collective-permute-start | bytes 73736 | tf_op jit(solution)/shard_map/ppermute | solution.py:525
  29.5 1.3 %collective-permute-start.14 = (f32[48,128]{1,0:T(8,128)S(1)}, f32[48,128]{1,0:T(8,128)S(1)}, u32[]{:S(2)}, u32[]{:S(2)}) collective-permute-start(f32[48,128]{1,0:T(8,128)S(1)} %get-tuple-element.78), channel_id=1, source_target_pairs={{0,1},{1,0},{2,3},{3,2},{4,5},{5,4},{6,7},{7,6},{8,9},{9,8},{10,11... | collective-permute-start | bytes 73736 | tf_op jit(solution)/shard_map/ppermute | solution.py:541
  30.8 3.3 %collective-permute-start.16 = (f32[48,128]{1,0:T(8,128)S(1)}, f32[48,128]{1,0:T(8,128)S(1)}, u32[]{:S(2)}, u32[]{:S(2)}) collective-permute-start(f32[48,128]{1,0:T(8,128)S(1)} %add.31.own), channel_id=1, source_target_pairs={{0,5},{1,4},{4,1},{5,0},{8,13},{9,12},{12,9},{13,8},{2,7},{3,6},{6... | collective-permute-start | bytes 73736 | tf_op jit(solution)/shard_map/ppermute | solution.py:525
  32.6 1.5 %collective-permute-start.15 = (f32[48,128]{1,0:T(8,128)S(1)}, f32[48,128]{1,0:T(8,128)S(1)}, u32[]{:S(2)}, u32[]{:S(2)}) collective-permute-start(f32[48,128]{1,0:T(8,128)S(1)} %add.31.own), channel_id=1, source_target_pairs={{0,1},{1,0},{4,9},{5,8},{8,5},{9,4},{12,13},{13,12},{2,3},{3,2},{6... | collective-permute-start | bytes 73736 | tf_op jit(solution)/shard_map/ppermute | solution.py:525
  35.1 1.2 %collective-permute-start.17 = (f32[16,128]{1,0:T(8,128)S(1)}, f32[16,128]{1,0:T(8,128)S(1)}, u32[]{:S(2)}, u32[]{:S(2)}) collective-permute-start(f32[16,128]{1,0:T(8,128)S(1)} %get-tuple-element.83), channel_id=1, source_target_pairs={{0,1},{1,0},{2,3},{3,2},{4,5},{5,4},{6,7},{7,6},{8,9},{9,8},{10,11... | collective-permute-start | bytes 24584 | tf_op jit(solution)/shard_map/ppermute | solution.py:541
  36.3 5.2 %collective-permute-start.20 = (f32[16,128]{1,0:T(8,128)S(1)}, f32[16,128]{1,0:T(8,128)S(1)}, u32[]{:S(2)}, u32[]{:S(2)}) collective-permute-start(f32[16,128]{1,0:T(8,128)S(1)} %add.32), channel_id=1, source_target_pairs={{0,13},{1,12},{4,9},{5,8},{8,5},{9,4},{12,1},{13,0},{2,15},{3,14},... | collective-permute-start | bytes 24584 | tf_op jit(solution)/shard_map/ppermute | solution.py:525
  37.2 4.3 %collective-permute-start.19 = (f32[16,128]{1,0:T(8,128)S(1)}, f32[16,128]{1,0:T(8,128)S(1)}, u32[]{:S(2)}, u32[]{:S(2)}) collective-permute-start(f32[16,128]{1,0:T(8,128)S(1)} %add.32), channel_id=1, source_target_pairs={{0,9},{1,8},{4,13},{5,12},{8,1},{9,0},{12,5},{13,4},{2,11},{3,10},... | collective-permute-start | bytes 24584 | tf_op jit(solution)/shard_map/ppermute | solution.py:525
  39.5 3.1 %collective-permute-start.18 = (f32[16,128]{1,0:T(8,128)S(1)}, f32[16,128]{1,0:T(8,128)S(1)}, u32[]{:S(2)}, u32[]{:S(2)}) collective-permute-start(f32[16,128]{1,0:T(8,128)S(1)} %add.32), channel_id=1, source_target_pairs={{0,5},{1,4},{4,1},{5,0},{8,13},{9,12},{12,9},{13,8},{2,7},{3,6},{6... | collective-permute-start | bytes 24584 | tf_op jit(solution)/shard_map/ppermute | solution.py:525

commit v11 on v10

--- a/solution.py
+++ b/solution.py
@@ -497,7 +497,15 @@
             result[b, 0, 1:2, r * LANES : (r + 1) * LANES] = gi[r : r + 1]
 
 
-def call(kernel, arrays, shapes, scratch=(), micros=2.0):
+COST = {
+    "k_setup": 0.01, "k_first": 0.75, "k_beside": 0.01, "k_cotangent": 0.1, "k_second": 6.0,
+    "k_third": 0.7, "k_fourth": 1.0, "k_taps": 1.1, "k_fifth": 1.0, "k_last": 1.1,
+}
+
+
+def call(kernel, arrays, shapes, scratch=()):
+    named = kernel.func if isinstance(kernel, functools.partial) else kernel
+    micros = COST.get(named.__name__, 0.1)
     vmem = pl.BlockSpec(memory_space=pltpu.VMEM)
     return pl.pallas_call(
         kernel,

time: 43.4 us -> 43.4 us (level)
  waiting for transfers between devices: 9.99 us -> 10.7 us
  starting transfers between devices: 22.3 us -> 21.6 us
    ppermute x14, waiting for transfers between devices: 5.46 us -> 4.58 us  [swapped(): return lax.ppermute(x, (axis, 'pol'), pairs)]
    ppermute x5, starting transfers between devices: 1.77 us -> 0.89 us  [over_cores(): lax.ppermute(x, 'pol', [(p, cores - 1 - p) for p in range(cores)])]
    ppermute x5, waiting for transfers between devices: 4.52 us -> 5.34 us  [over_cores(): lax.ppermute(x, 'pol', [(p, cores - 1 - p) for p in range(cores)])]
    ppermute x2, waiting for transfers between devices: 0.01 us -> 0.75 us  [aslant(): return lax.ppermute(x, ('tm', 'band', 'pol'), pairs)]
  transfers between devices with their start and end apart: 21 -> 21, of which waited for: 10 -> 12; matrix products, arithmetic and copies ran while one was open for 0% -> 0% of each run, Pallas kernels for 13% -> 13%
where the time goes in v11:
time: 43.4 us; the launch traced here: 43.3 us
  starting transfers between devices  21.6 us (50%)
  waiting for transfers between devices  10.7 us (25%)
  Pallas kernels  9.58 us (22%)
  between operations  0.74 us (2%)
  other arithmetic  0.63 us (1%)
    ppermute x14, starting transfers between devices, swapped(): return lax.ppermute(x, (axis, 'pol'), pairs)  17.6 us
    pallas_call x11, Pallas kernels, call(): pl.pallas_call(kernel, out_shape=shapes, in_specs=jax.tree.map(lambda _:...  8.4 us
    ppermute x5, waiting for transfers between devices, over_cores(): lax.ppermute(x, 'pol', [(p, cores - 1 - p) for p in range(cores)])  5.34 us
    ppermute x14, waiting for transfers between devices, swapped(): return lax.ppermute(x, (axis, 'pol'), pairs)  4.58 us
    ppermute x2, starting transfers between devices, aslant(): return lax.ppermute(x, ('tm', 'band', 'pol'), pairs)  3.12 us
    pallas_call x1, Pallas kernels, on_device(): pl.pallas_call(k_begin, out_shape=[cut, cut, near, near, pack, shape(own,...  1.18 us
    ppermute x5, starting transfers between devices, over_cores(): lax.ppermute(x, 'pol', [(p, cores - 1 - p) for p in range(cores)])  0.89 us
  transfers between devices with their start and end apart: 21, of which 12 were waited for; matrix products, arithmetic and copies ran while one was open for 0% of the time, Pallas kernels for 13%

profile of v11, /device:TPU:0, one launch (start us, length us, event | category | flops | bytes accessed | tf_op | source)
XLA Modules:
  0.0 43.3 jit_solution(9976961571308525138)
XLA Ops:
  0.6 1.2 %shard_map.77 = (f32[4,2,3072]{2,1,0:T(2,128)S(1)}, f32[4,2,3072]{2,1,0:T(2,128)S(1)}, f32[4,2,1024]{2,1,0:T(2,128)S(1)}, f32[4,2,1024]{2,1,0:T(2,128)S(1)}, f32...) custom-call(f32[4,1,2,4096]{3,2,1,0:T(2,128)} %signal.1, f32[4,1,2,4096]{3,2,1,0:T(2,128)} %cotangent.1, ...), custom_call_target="tpu_custom_call" | custom-call | flops 100000000 | bytes 1000000 | tf_op jit(solution)/shard_map/pallas_call | solution.py:626
  1.8 3.1 %collective-permute-start.1 = (f32[4,2,3072]{2,1,0:T(2,128)S(1)}, f32[4,2,3072]{2,1,0:T(2,128)S(1)}, u32[]{:S(2)}, u32[]{:S(2)}) collective-permute-start(f32[4,2,3072]{2,1,0:T(2,128)S(1)} %get-tuple-element.50), channel_id=1, source_target_pairs={{0,4},{1,5},{4,0},{5,1},{8,12},{9,13},{12,8},{13,9},{2,6},{3,7},{6... | collective-permute-start | bytes 294920 | tf_op jit(solution)/shard_map/ppermute | solution.py:533
  4.9 0.0 collective-permute-start.2
  4.9 1.5 %collective-permute-start = (f32[280,128]{1,0:T(8,128)S(1)}, f32[280,128]{1,0:T(8,128)S(1)}, u32[]{:S(2)}, u32[]{:S(2)}) collective-permute-start(f32[280,128]{1,0:T(8,128)S(1)} %get-tuple-element.43.pack), channel_id=1, source_target_pairs={{0,2},{1,3},{2,0},{3,1},{4,6},{5,7},{6,4},{7,5},{8,10},{9,11},{10,... | collective-permute-start | bytes 430088 | tf_op jit(solution)/shard_map/ppermute | solution.py:533
  6.4 3.1 %collective-permute-start.3 = (f32[4,2,1024]{2,1,0:T(2,128)S(1)}, f32[4,2,1024]{2,1,0:T(2,128)S(1)}, u32[]{:S(2)}, u32[]{:S(2)}) collective-permute-start(f32[4,2,1024]{2,1,0:T(2,128)S(1)} %get-tuple-element.56), channel_id=1, source_target_pairs={{0,6},{1,7},{2,4},{3,5},{4,2},{5,3},{6,0},{7,1},{8,14},{9,15},{10,... | collective-permute-start | bytes 98312 | tf_op jit(solution)/shard_map/ppermute | solution.py:578
  9.5 0.0 collective-permute-start.4
  9.5 0.4 %shard_map.78 = (s32[2,4]{1,0:T(2,128)S(1)}, s32[2,4]{1,0:T(2,128)S(1)}, f32[2,4]{1,0:T(2,128)S(1)}, bf16[4,256,256]{2,1,0:T(8,128)(2,1)S(1)}, bf16[4,256,256]{2...) custom-call(f32[280,128]{1,0:T(8,128)S(1)} %get-tuple-element.43.pack), custom_call_target="tpu_custom_call" | custom-call | flops 1000000 | bytes 30000 | tf_op jit(solution)/shard_map/pallas_call | solution.py:510
  10.0 0.0 collective-permute-done.1.sides_0_.s_0__0_
  10.0 0.0 collective-permute-done.2.sides_1_.s_0__1_
  10.0 0.8 %shard_map.80 = (f32[4,2,48,128]{3,2,1,0:T(8,128)S(1)}, f32[4,2,48,128]{3,2,1,0:T(8,128)S(1)}, f32[64,128]{1,0:T(8,128)S(1)}) custom-call(s32[2,4]{1,0:T(2,128)S(1)} %get-tuple-element.45.delays_0_, s32[2,4]{1,0:T(2,128)S(1)} %get-tuple-element.44.shifts_0_, f32[280,128]{1,0:T(8,128)S(1)} %get-tuple-element.43.pack, ...), custom_call_target="tpu_custom_call" | custom-call | flops 75000000 | bytes 2250000 | tf_op jit(solution)/shard_map/pallas_call | solution.py:510
  10.8 0.8 %collective-permute-done.3.sides_0_.s_1__0_ = f32[4,2,1024]{2,1,0:T(2,128)S(1)} collective-permute-done((f32[4,2,1024]{2,1,0:T(2,128)S(1)}, f32[4,2,1024]{2,1,0:T(2,128)S(1)}, u32[]{:S(2)}, u32[]{:S(2)}) %collective-permute-start.3) | collective-permute-done | bytes 32800 | tf_op jit(solution)/shard_map/ppermute | solution.py:578
  11.5 0.0 collective-permute-done.4.sides_1_.s_1__1_
  11.5 0.0 collective-permute-start.5
  11.5 1.2 %collective-permute-done.5 = f32[64,128]{1,0:T(8,128)S(1)} collective-permute-done((f32[64,128]{1,0:T(8,128)S(1)}, f32[64,128]{1,0:T(8,128)S(1)}, u32[]{:S(2)}, u32[]{:S(2)}) %collective-permute-start.5) | collective-permute-done | bytes 32800 | tf_op jit(solution)/shard_map/ppermute | solution.py:549
  12.7 1.3 %collective-permute-start.6 = (f32[64,128]{1,0:T(8,128)S(1)}, f32[64,128]{1,0:T(8,128)S(1)}, u32[]{:S(2)}, u32[]{:S(2)}) collective-permute-start(f32[64,128]{1,0:T(8,128)S(1)} %add.27), channel_id=1, source_target_pairs={{0,3},{1,2},{2,1},{3,0},{4,7},{5,6},{6,5},{7,4},{8,11},{9,10},{10,... | collective-permute-start | bytes 98312 | tf_op jit(solution)/shard_map/ppermute | solution.py:533
  14.0 0.5 %collective-permute-start.10 = (f32[4,2,32,128]{3,2,1,0:T(8,128)S(1)}, f32[4,2,32,128]{3,2,1,0:T(8,128)S(1)}, u32[]{:S(2)}, u32[]{:S(2)}) collective-permute-start(f32[4,2,32,128]{3,2,1,0:T(8,128)S(1)} %get-tuple-element.69.c_0_), channel_id=1, source_target_pairs={{0,2},{1,3},{2,0},{3,1},{4,6},{5,7},{6,4},{7,5},{8,10},{9,11},{10,... | collective-permute-start | bytes 393224 | tf_op jit(solution)/shard_map/ppermute | solution.py:533
  14.5 0.0 collective-permute-done.pack
  14.5 0.4 %shard_map.79 = (s32[2,4]{1,0:T(2,128)S(1)}, s32[2,4]{1,0:T(2,128)S(1)}, f32[2,4]{1,0:T(2,128)S(1)}, bf16[4,256,256]{2,1,0:T(8,128)(2,1)S(1)}, bf16[4,256,256]{2...) custom-call(f32[280,128]{1,0:T(8,128)S(1)} %collective-permute-done.pack), custom_call_target="tpu_custom_call" | custom-call | flops 1000000 | bytes 30000 | tf_op jit(solution)/shard_map/pallas_call | solution.py:510
  15.0 0.6 %shard_map.81.linear0_1_ = f32[4,2,48,128]{3,2,1,0:T(8,128)S(1)} custom-call(s32[2,4]{1,0:T(2,128)S(1)} %get-tuple-element.47.shifts_0_.shifts_1_, f32[280,128]{1,0:T(8,128)S(1)} %collective-permute-done.pack, f32[4,2,1024]{2,1,0:T(2,128)S(1)} %collective-permute-done.3.sides_0_.s_1__0_, f32[4,2,1024]{2,1,0:T(2,128)S(1)} %collective-permute-done.4.sides_1_.s_1__1_, ...), custom_call_target="tpu_custom_call" | custom-call | flops 1000000 | bytes 30000 | tf_op jit(solution)/shard_map/pallas_call | solution.py:510
  15.6 0.5 %collective-permute-done.6 = f32[64,128]{1,0:T(8,128)S(1)} collective-permute-done((f32[64,128]{1,0:T(8,128)S(1)}, f32[64,128]{1,0:T(8,128)S(1)}, u32[]{:S(2)}, u32[]{:S(2)}) %collective-permute-start.6) | collective-permute-done | bytes 32800 | tf_op jit(solution)/shard_map/ppermute | solution.py:533
  16.1 1.3 %shard_map.82 = (f32[4,48,128]{2,1,0:T(8,128)S(1)}, f32[4,48,128]{2,1,0:T(8,128)S(1)}, f32[8,2,48,128]{3,2,1,0:T(8,128)S(1)}, f32[4,2,48,128]{3,2,1,0:T(8,128)S(...) custom-call(s32[2,4]{1,0:T(2,128)S(1)} %get-tuple-element.45.delays_0_, ...), custom_call_target="tpu_custom_call" | custom-call | flops 600000000 | bytes 18000000 | tf_op jit(solution)/shard_map/pallas_call | solution.py:510
  17.4 0.2 collective-permute-start.7
  17.6 1.0 %collective-permute-done.7 = f32[48,128]{1,0:T(8,128)S(1)} collective-permute-done((f32[48,128]{1,0:T(8,128)S(1)}, f32[48,128]{1,0:T(8,128)S(1)}, u32[]{:S(2)}, u32[]{:S(2)}) %collective-permute-start.7) | collective-permute-done | bytes 24608 | tf_op jit(solution)/shard_map/ppermute | solution.py:549
  18.6 3.3 %collective-permute-start.9 = (f32[48,128]{1,0:T(8,128)S(1)}, f32[48,128]{1,0:T(8,128)S(1)}, u32[]{:S(2)}, u32[]{:S(2)}) collective-permute-start(f32[48,128]{1,0:T(8,128)S(1)} %add.29.own), channel_id=1, source_target_pairs={{0,5},{1,4},{4,1},{5,0},{8,13},{9,12},{12,9},{13,8},{2,7},{3,6},{6... | collective-permute-start | bytes 73736 | tf_op jit(solution)/shard_map/ppermute | solution.py:533
  21.9 0.2 collective-permute-start.8
  22.1 0.0 collective-permute-done.10.c_1_
  22.1 0.1 shard_map.83.cotangent
  22.2 1.3 %collective-permute-done.9.even_in = f32[48,128]{1,0:T(8,128)S(1)} collective-permute-done((f32[48,128]{1,0:T(8,128)S(1)}, f32[48,128]{1,0:T(8,128)S(1)}, u32[]{:S(2)}, u32[]{:S(2)}) %collective-permute-start.9) | collective-permute-done | bytes 24608 | tf_op jit(solution)/shard_map/ppermute | solution.py:533
  23.5 0.0 collective-permute-done.8.odd_in
  23.5 0.7 %shard_map.84 = (f32[8,2,48,128]{3,2,1,0:T(8,128)S(1)}, f32[48,128]{1,0:T(8,128)S(1)}) custom-call(s32[2,4]{1,0:T(2,128)S(1)} %get-tuple-element.45.delays_0_, s32[2,4]{1,0:T(2,128)S(1)} %get-tuple-element.46.delays_1_, f32[2,4]{1,0:T(2,128)S(1)} %get-tuple-element.48.gains_0_, f32[2,4]{1,0:T(2,128)S(1)} %get-tuple-element.49.gains_1_, ...), custom_call_target="tpu_custom_call" | custom-call | flops 70000000 | bytes 2100000 | tf_op jit(solution)/shard_map/pallas_call | solution.py:510
  24.2 0.2 collective-permute-start.11
  24.4 1.0 %collective-permute-done.11 = f32[48,128]{1,0:T(8,128)S(1)} collective-permute-done((f32[48,128]{1,0:T(8,128)S(1)}, f32[48,128]{1,0:T(8,128)S(1)}, u32[]{:S(2)}, u32[]{:S(2)}) %collective-permute-start.11) | collective-permute-done | bytes 24608 | tf_op jit(solution)/shard_map/ppermute | solution.py:549
  25.4 1.8 %collective-permute-start.13 = (f32[48,128]{1,0:T(8,128)S(1)}, f32[48,128]{1,0:T(8,128)S(1)}, u32[]{:S(2)}, u32[]{:S(2)}) collective-permute-start(f32[48,128]{1,0:T(8,128)S(1)} %add.30.own), channel_id=1, source_target_pairs={{0,5},{1,4},{4,1},{5,0},{8,13},{9,12},{12,9},{13,8},{2,7},{3,6},{6... | collective-permute-start | bytes 73736 | tf_op jit(solution)/shard_map/ppermute | solution.py:533
  27.2 0.2 collective-permute-start.12
  27.4 1.4 %collective-permute-done.13.even_in = f32[48,128]{1,0:T(8,128)S(1)} collective-permute-done((f32[48,128]{1,0:T(8,128)S(1)}, f32[48,128]{1,0:T(8,128)S(1)}, u32[]{:S(2)}, u32[]{:S(2)}) %collective-permute-start.13) | collective-permute-done | bytes 24608 | tf_op jit(solution)/shard_map/ppermute | solution.py:533
  28.7 0.0 collective-permute-done.12.odd_in
  28.7 1.0 %shard_map.85 = (f32[4,2,48,128]{3,2,1,0:T(8,128)S(1)}, f32[4,2,48,128]{3,2,1,0:T(8,128)S(1)}, f32[48,128]{1,0:T(8,128)S(1)}) custom-call(s32[2,4]{1,0:T(2,128)S(1)} %get-tuple-element.45.delays_0_, s32[2,4]{1,0:T(2,128)S(1)} %get-tuple-element.46.delays_1_, s32[2,4]{1,0:T(2,128)S(1)} %get-tuple-element.44.shifts_0_, ...), custom_call_target="tpu_custom_call" | custom-call | flops 100000000 | bytes 3000000 | tf_op jit(solution)/shard_map/pallas_call | solution.py:510
  29.7 0.2 collective-permute-start.14
  29.9 1.0 %collective-permute-done.14 = f32[48,128]{1,0:T(8,128)S(1)} collective-permute-done((f32[48,128]{1,0:T(8,128)S(1)}, f32[48,128]{1,0:T(8,128)S(1)}, u32[]{:S(2)}, u32[]{:S(2)}) %collective-permute-start.14) | collective-permute-done | bytes 24608 | tf_op jit(solution)/shard_map/ppermute | solution.py:549
  31.0 1.8 %collective-permute-start.16 = (f32[48,128]{1,0:T(8,128)S(1)}, f32[48,128]{1,0:T(8,128)S(1)}, u32[]{:S(2)}, u32[]{:S(2)}) collective-permute-start(f32[48,128]{1,0:T(8,128)S(1)} %add.31.own), channel_id=1, source_target_pairs={{0,5},{1,4},{4,1},{5,0},{8,13},{9,12},{12,9},{13,8},{2,7},{3,6},{6... | collective-permute-start | bytes 73736 | tf_op jit(solution)/shard_map/ppermute | solution.py:533
  32.8 0.2 collective-permute-start.15
  33.0 1.1 %shard_map.86.taps1 = f32[8,128]{1,0:T(8,128)S(1)} custom-call(f32[4,2,48,128]{3,2,1,0:T(8,128)S(1)} %get-tuple-element.80.shifted, f32[4,2,48,128]{3,2,1,0:T(8,128)S(1)} %get-tuple-element.81.grad), custom_call_target="tpu_custom_call" | custom-call | flops 110000000 | bytes 3300000 | tf_op jit(solution)/shard_map/pallas_call | solution.py:510
  34.0 0.3 collective-permute-done.16.even_in
  34.3 0.0 collective-permute-done.15.odd_in
  34.3 1.0 %shard_map.87 = (f32[4,2,48,128]{3,2,1,0:T(8,128)S(1)}, f32[16,128]{1,0:T(8,128)S(1)}) custom-call(s32[2,4]{1,0:T(2,128)S(1)} %get-tuple-element.45.delays_0_, f32[4,2,48,128]{3,2,1,0:T(8,128)S(1)} %get-tuple-element.77.turned0, f32[4,2,48,128]{3,2,1,0:T(8,128)S(1)} %get-tuple-element.54.linear0_0_.linear0, f32[48,128]{1,0:T(8,128)S(1)} %add.31.own, ...), custom_call_target="tpu_custom_call" | custom-call | flops 100000000 | bytes 3000000 | tf_op jit(solution)/shard_map/pallas_call | solution.py:510
  35.3 0.2 collective-permute-start.17
  35.5 1.0 %collective-permute-done.17 = f32[16,128]{1,0:T(8,128)S(1)} collective-permute-done((f32[16,128]{1,0:T(8,128)S(1)}, f32[16,128]{1,0:T(8,128)S(1)}, u32[]{:S(2)}, u32[]{:S(2)}) %collective-permute-start.17) | collective-permute-done | bytes 8224 | tf_op jit(solution)/shard_map/ppermute | solution.py:549
  36.6 0.9 %collective-permute-start.20 = (f32[16,128]{1,0:T(8,128)S(1)}, f32[16,128]{1,0:T(8,128)S(1)}, u32[]{:S(2)}, u32[]{:S(2)}) collective-permute-start(f32[16,128]{1,0:T(8,128)S(1)} %add.32), channel_id=1, source_target_pairs={{0,13},{1,12},{4,9},{5,8},{8,5},{9,4},{12,1},{13,0},{2,15},{3,14},... | collective-permute-start | bytes 24584 | tf_op jit(solution)/shard_map/ppermute | solution.py:533
  37.5 2.1 %collective-permute-start.19 = (f32[16,128]{1,0:T(8,128)S(1)}, f32[16,128]{1,0:T(8,128)S(1)}, u32[]{:S(2)}, u32[]{:S(2)}) collective-permute-start(f32[16,128]{1,0:T(8,128)S(1)} %add.32), channel_id=1, source_target_pairs={{0,9},{1,8},{4,13},{5,12},{8,1},{9,0},{12,5},{13,4},{2,11},{3,10},... | collective-permute-start | bytes 24584 | tf_op jit(solution)/shard_map/ppermute | solution.py:533
  39.6 0.8 %collective-permute-start.18 = (f32[16,128]{1,0:T(8,128)S(1)}, f32[16,128]{1,0:T(8,128)S(1)}, u32[]{:S(2)}, u32[]{:S(2)}) collective-permute-start(f32[16,128]{1,0:T(8,128)S(1)} %add.32), channel_id=1, source_target_pairs={{0,5},{1,4},{4,1},{5,0},{8,13},{9,12},{12,9},{13,8},{2,7},{3,6},{6... | collective-permute-start | bytes 24584 | tf_op jit(solution)/shard_map/ppermute | solution.py:533
  40.4 1.1 %shard_map.88 = f32[4,1,2,4096]{3,2,1,0:T(2,128)} custom-call(s32[2,4]{1,0:T(2,128)S(1)} %get-tuple-element.44.shifts_0_, f32[4,2,48,128]{3,2,1,0:T(8,128)S(1)} %get-tuple-element.82.grad0, bf16[4,256,256]{2,1,0:T(8,128)(2,1)S(1)} %get-tuple-element.52.high, bf16[4,256,256]{2,1,0:T(8,128)(2,1)S(1)} %get-tuple-element.53.low), custom_call_target="tpu_custom_call" | custom-call | flops 110000000 | bytes 3300000 | tf_op jit(solution)/shard_map/pallas_call | solution.py:510
  41.6 0.0 collective-permute-done.20
  41.6 0.1 collective-permute-done.19
  41.6 1.1 %collective-permute-done.18 = f32[16,128]{1,0:T(8,128)S(1)} collective-permute-done((f32[16,128]{1,0:T(8,128)S(1)}, f32[16,128]{1,0:T(8,128)S(1)}, u32[]{:S(2)}, u32[]{:S(2)}) %collective-permute-start.18) | collective-permute-done | bytes 8224 | tf_op jit(solution)/shard_map/ppermute | solution.py:533
  42.7 0.6 %add_add_fusion = f32[16,128]{1,0:T(8,128)} fusion(f32[16,128]{1,0:T(8,128)S(1)} %collective-permute-done.19, f32[16,128]{1,0:T(8,128)S(1)} %collective-permute-done.20, f32[16,128]{1,0:T(8,128)S(1)} %add.32, f32[16,128]{1,0:T(8,128)S(1)} %collective-permute-done.18), kind=kLoop, calls=%fused_computation | loop fusion | flops 6144 | bytes 40960 | tf_op jit(solution)/shard_map/add | solution.py:585
  (6 shorter events, 0.0 us)
Async XLA Ops:
  1.8 8.2 %collective-permute-start.1 = (f32[4,2,3072]{2,1,0:T(2,128)S(1)}, f32[4,2,3072]{2,1,0:T(2,128)S(1)}, u32[]{:S(2)}, u32[]{:S(2)}) collective-permute-start(f32[4,2,3072]{2,1,0:T(2,128)S(1)} %get-tuple-element.50), channel_id=1, source_target_pairs={{0,4},{1,5},{4,0},{5,1},{8,12},{9,13},{12,8},{13,9},{2,6},{3,7},{6... | collective-permute-start | bytes 294920 | tf_op jit(solution)/shard_map/ppermute | solution.py:533
  4.9 5.1 %collective-permute-start.2 = (f32[4,2,3072]{2,1,0:T(2,128)S(1)}, f32[4,2,3072]{2,1,0:T(2,128)S(1)}, u32[]{:S(2)}, u32[]{:S(2)}) collective-permute-start(f32[4,2,3072]{2,1,0:T(2,128)S(1)} %get-tuple-element.51), channel_id=1, source_target_pairs={{0,1},{1,0},{4,8},{5,9},{8,4},{9,5},{12,13},{13,12},{2,3},{3,2},{6... | collective-permute-start | bytes 294920 | tf_op jit(solution)/shard_map/ppermute | solution.py:533
  4.9 9.6 %collective-permute-start = (f32[280,128]{1,0:T(8,128)S(1)}, f32[280,128]{1,0:T(8,128)S(1)}, u32[]{:S(2)}, u32[]{:S(2)}) collective-permute-start(f32[280,128]{1,0:T(8,128)S(1)} %get-tuple-element.43.pack), channel_id=1, source_target_pairs={{0,2},{1,3},{2,0},{3,1},{4,6},{5,7},{6,4},{7,5},{8,10},{9,11},{10,... | collective-permute-start | bytes 430088 | tf_op jit(solution)/shard_map/ppermute | solution.py:533
  6.4 5.1 %collective-permute-start.3 = (f32[4,2,1024]{2,1,0:T(2,128)S(1)}, f32[4,2,1024]{2,1,0:T(2,128)S(1)}, u32[]{:S(2)}, u32[]{:S(2)}) collective-permute-start(f32[4,2,1024]{2,1,0:T(2,128)S(1)} %get-tuple-element.56), channel_id=1, source_target_pairs={{0,6},{1,7},{2,4},{3,5},{4,2},{5,3},{6,0},{7,1},{8,14},{9,15},{10,... | collective-permute-start | bytes 98312 | tf_op jit(solution)/shard_map/ppermute | solution.py:578
  9.5 2.0 %collective-permute-start.4 = (f32[4,2,1024]{2,1,0:T(2,128)S(1)}, f32[4,2,1024]{2,1,0:T(2,128)S(1)}, u32[]{:S(2)}, u32[]{:S(2)}) collective-permute-start(f32[4,2,1024]{2,1,0:T(2,128)S(1)} %get-tuple-element.57), channel_id=1, source_target_pairs={{0,1},{1,0},{2,3},{3,2},{4,10},{5,11},{6,8},{7,9},{8,6},{9,7},{10,... | collective-permute-start | bytes 98312 | tf_op jit(solution)/shard_map/ppermute | solution.py:578
  11.5 1.2 %collective-permute-start.5 = (f32[64,128]{1,0:T(8,128)S(1)}, f32[64,128]{1,0:T(8,128)S(1)}, u32[]{:S(2)}, u32[]{:S(2)}) collective-permute-start(f32[64,128]{1,0:T(8,128)S(1)} %get-tuple-element.62), channel_id=1, source_target_pairs={{0,1},{1,0},{2,3},{3,2},{4,5},{5,4},{6,7},{7,6},{8,9},{9,8},{10,11... | collective-permute-start | bytes 98312 | tf_op jit(solution)/shard_map/ppermute | solution.py:549
  12.7 3.3 %collective-permute-start.6 = (f32[64,128]{1,0:T(8,128)S(1)}, f32[64,128]{1,0:T(8,128)S(1)}, u32[]{:S(2)}, u32[]{:S(2)}) collective-permute-start(f32[64,128]{1,0:T(8,128)S(1)} %add.27), channel_id=1, source_target_pairs={{0,3},{1,2},{2,1},{3,0},{4,7},{5,6},{6,5},{7,4},{8,11},{9,10},{10,... | collective-permute-start | bytes 98312 | tf_op jit(solution)/shard_map/ppermute | solution.py:533
  14.0 8.1 %collective-permute-start.10 = (f32[4,2,32,128]{3,2,1,0:T(8,128)S(1)}, f32[4,2,32,128]{3,2,1,0:T(8,128)S(1)}, u32[]{:S(2)}, u32[]{:S(2)}) collective-permute-start(f32[4,2,32,128]{3,2,1,0:T(8,128)S(1)} %get-tuple-element.69.c_0_), channel_id=1, source_target_pairs={{0,2},{1,3},{2,0},{3,1},{4,6},{5,7},{6,4},{7,5},{8,10},{9,11},{10,... | collective-permute-start | bytes 393224 | tf_op jit(solution)/shard_map/ppermute | solution.py:533
  17.4 1.3 %collective-permute-start.7 = (f32[48,128]{1,0:T(8,128)S(1)}, f32[48,128]{1,0:T(8,128)S(1)}, u32[]{:S(2)}, u32[]{:S(2)}) collective-permute-start(f32[48,128]{1,0:T(8,128)S(1)} %get-tuple-element.68), channel_id=1, source_target_pairs={{0,1},{1,0},{2,3},{3,2},{4,5},{5,4},{6,7},{7,6},{8,9},{9,8},{10,11... | collective-permute-start | bytes 73736 | tf_op jit(solution)/shard_map/ppermute | solution.py:549
  18.6 4.8 %collective-permute-start.9 = (f32[48,128]{1,0:T(8,128)S(1)}, f32[48,128]{1,0:T(8,128)S(1)}, u32[]{:S(2)}, u32[]{:S(2)}) collective-permute-start(f32[48,128]{1,0:T(8,128)S(1)} %add.29.own), channel_id=1, source_target_pairs={{0,5},{1,4},{4,1},{5,0},{8,13},{9,12},{12,9},{13,8},{2,7},{3,6},{6... | collective-permute-start | bytes 73736 | tf_op jit(solution)/shard_map/ppermute | solution.py:533
  21.9 1.5 %collective-permute-start.8 = (f32[48,128]{1,0:T(8,128)S(1)}, f32[48,128]{1,0:T(8,128)S(1)}, u32[]{:S(2)}, u32[]{:S(2)}) collective-permute-start(f32[48,128]{1,0:T(8,128)S(1)} %add.29.own), channel_id=1, source_target_pairs={{0,1},{1,0},{4,9},{5,8},{8,5},{9,4},{12,13},{13,12},{2,3},{3,2},{6... | collective-permute-start | bytes 73736 | tf_op jit(solution)/shard_map/ppermute | solution.py:533
  24.2 1.3 %collective-permute-start.11 = (f32[48,128]{1,0:T(8,128)S(1)}, f32[48,128]{1,0:T(8,128)S(1)}, u32[]{:S(2)}, u32[]{:S(2)}) collective-permute-start(f32[48,128]{1,0:T(8,128)S(1)} %get-tuple-element.73), channel_id=1, source_target_pairs={{0,1},{1,0},{2,3},{3,2},{4,5},{5,4},{6,7},{7,6},{8,9},{9,8},{10,11... | collective-permute-start | bytes 73736 | tf_op jit(solution)/shard_map/ppermute | solution.py:549
  25.4 3.3 %collective-permute-start.13 = (f32[48,128]{1,0:T(8,128)S(1)}, f32[48,128]{1,0:T(8,128)S(1)}, u32[]{:S(2)}, u32[]{:S(2)}) collective-permute-start(f32[48,128]{1,0:T(8,128)S(1)} %add.30.own), channel_id=1, source_target_pairs={{0,5},{1,4},{4,1},{5,0},{8,13},{9,12},{12,9},{13,8},{2,7},{3,6},{6... | collective-permute-start | bytes 73736 | tf_op jit(solution)/shard_map/ppermute | solution.py:533
  27.2 1.5 %collective-permute-start.12 = (f32[48,128]{1,0:T(8,128)S(1)}, f32[48,128]{1,0:T(8,128)S(1)}, u32[]{:S(2)}, u32[]{:S(2)}) collective-permute-start(f32[48,128]{1,0:T(8,128)S(1)} %add.30.own), channel_id=1, source_target_pairs={{0,1},{1,0},{4,9},{5,8},{8,5},{9,4},{12,13},{13,12},{2,3},{3,2},{6... | collective-permute-start | bytes 73736 | tf_op jit(solution)/shard_map/ppermute | solution.py:533
  29.7 1.3 %collective-permute-start.14 = (f32[48,128]{1,0:T(8,128)S(1)}, f32[48,128]{1,0:T(8,128)S(1)}, u32[]{:S(2)}, u32[]{:S(2)}) collective-permute-start(f32[48,128]{1,0:T(8,128)S(1)} %get-tuple-element.78), channel_id=1, source_target_pairs={{0,1},{1,0},{2,3},{3,2},{4,5},{5,4},{6,7},{7,6},{8,9},{9,8},{10,11... | collective-permute-start | bytes 73736 | tf_op jit(solution)/shard_map/ppermute | solution.py:549
  31.0 3.3 %collective-permute-start.16 = (f32[48,128]{1,0:T(8,128)S(1)}, f32[48,128]{1,0:T(8,128)S(1)}, u32[]{:S(2)}, u32[]{:S(2)}) collective-permute-start(f32[48,128]{1,0:T(8,128)S(1)} %add.31.own), channel_id=1, source_target_pairs={{0,5},{1,4},{4,1},{5,0},{8,13},{9,12},{12,9},{13,8},{2,7},{3,6},{6... | collective-permute-start | bytes 73736 | tf_op jit(solution)/shard_map/ppermute | solution.py:533
  32.8 1.5 %collective-permute-start.15 = (f32[48,128]{1,0:T(8,128)S(1)}, f32[48,128]{1,0:T(8,128)S(1)}, u32[]{:S(2)}, u32[]{:S(2)}) collective-permute-start(f32[48,128]{1,0:T(8,128)S(1)} %add.31.own), channel_id=1, source_target_pairs={{0,1},{1,0},{4,9},{5,8},{8,5},{9,4},{12,13},{13,12},{2,3},{3,2},{6... | collective-permute-start | bytes 73736 | tf_op jit(solution)/shard_map/ppermute | solution.py:533
  35.3 1.2 %collective-permute-start.17 = (f32[16,128]{1,0:T(8,128)S(1)}, f32[16,128]{1,0:T(8,128)S(1)}, u32[]{:S(2)}, u32[]{:S(2)}) collective-permute-start(f32[16,128]{1,0:T(8,128)S(1)} %get-tuple-element.83), channel_id=1, source_target_pairs={{0,1},{1,0},{2,3},{3,2},{4,5},{5,4},{6,7},{7,6},{8,9},{9,8},{10,11... | collective-permute-start | bytes 24584 | tf_op jit(solution)/shard_map/ppermute | solution.py:549
  36.6 5.0 %collective-permute-start.20 = (f32[16,128]{1,0:T(8,128)S(1)}, f32[16,128]{1,0:T(8,128)S(1)}, u32[]{:S(2)}, u32[]{:S(2)}) collective-permute-start(f32[16,128]{1,0:T(8,128)S(1)} %add.32), channel_id=1, source_target_pairs={{0,13},{1,12},{4,9},{5,8},{8,5},{9,4},{12,1},{13,0},{2,15},{3,14},... | collective-permute-start | bytes 24584 | tf_op jit(solution)/shard_map/ppermute | solution.py:533
  37.5 4.1 %collective-permute-start.19 = (f32[16,128]{1,0:T(8,128)S(1)}, f32[16,128]{1,0:T(8,128)S(1)}, u32[]{:S(2)}, u32[]{:S(2)}) collective-permute-start(f32[16,128]{1,0:T(8,128)S(1)} %add.32), channel_id=1, source_target_pairs={{0,9},{1,8},{4,13},{5,12},{8,1},{9,0},{12,5},{13,4},{2,11},{3,10},... | collective-permute-start | bytes 24584 | tf_op jit(solution)/shard_map/ppermute | solution.py:533
  39.6 3.1 %collective-permute-start.18 = (f32[16,128]{1,0:T(8,128)S(1)}, f32[16,128]{1,0:T(8,128)S(1)}, u32[]{:S(2)}, u32[]{:S(2)}) collective-permute-start(f32[16,128]{1,0:T(8,128)S(1)} %add.32), channel_id=1, source_target_pairs={{0,5},{1,4},{4,1},{5,0},{8,13},{9,12},{12,9},{13,8},{2,7},{3,6},{6... | collective-permute-start | bytes 24584 | tf_op jit(solution)/shard_map/ppermute | solution.py:533

commit v12 on v10

--- a/solution.py
+++ b/solution.py
@@ -227,7 +227,7 @@
     copies = [pltpu.make_async_copy(a, b, done.at[n]) for n, (a, b) in enumerate(pairs)]
     for copy in copies:
         copy.start()
-    for copy in copies:
+    for copy in copies[:2]:
         copy.wait()
     even = is_even()
     length, wide, edge = rows * LANES, WIDE * LANES, EDGE * LANES
@@ -250,6 +250,8 @@
                 row = (2 * b + c) * rows + r
                 sent[row : row + 1, :] = pair[c : c + 1]
                 cot_rows[b, c, r : r + 1, :] = other[c : c + 1]
+    for copy in copies[2:]:
+        copy.wait()
     first = 2 * bands * rows
     for step in range(steps):
         for b in range(bands):

time: 43.4 us -> 43.4 us (level)
  no operation moved by 1% of the time
where the time goes in v12:
time: 43.4 us; the launch traced here: 43.2 us
  starting transfers between devices  22.3 us (51%)
  waiting for transfers between devices  9.99 us (23%)
  Pallas kernels  9.58 us (22%)
  between operations  0.75 us (2%)
  other arithmetic  0.63 us (1%)
    ppermute x14, starting transfers between devices, swapped(): return lax.ppermute(x, (axis, 'pol'), pairs)  17.4 us
    pallas_call x11, Pallas kernels, call(): pl.pallas_call(kernel, out_shape=shapes, in_specs=jax.tree.map(lambda _:...  8.39 us
    ppermute x14, waiting for transfers between devices, swapped(): return lax.ppermute(x, (axis, 'pol'), pairs)  5.46 us
    ppermute x5, waiting for transfers between devices, over_cores(): lax.ppermute(x, 'pol', [(p, cores - 1 - p) for p in range(cores)])  4.52 us
    ppermute x2, starting transfers between devices, aslant(): return lax.ppermute(x, ('tm', 'band', 'pol'), pairs)  3.12 us
    ppermute x5, starting transfers between devices, over_cores(): lax.ppermute(x, 'pol', [(p, cores - 1 - p) for p in range(cores)])  1.77 us
    pallas_call x1, Pallas kernels, on_device(): pl.pallas_call(k_begin, out_shape=[cut, cut, near, near, pack, shape(own,...  1.19 us
  transfers between devices with their start and end apart: 21, of which 10 were waited for; matrix products, arithmetic and copies ran while one was open for 0% of the time, Pallas kernels for 13%

profile of v12, /device:TPU:0, one launch (start us, length us, event | category | flops | bytes accessed | tf_op | source)
XLA Modules:
  0.0 43.2 jit_solution(4569916391437004355)
XLA Ops:
  0.6 1.2 %shard_map.77 = (f32[4,2,3072]{2,1,0:T(2,128)S(1)}, f32[4,2,3072]{2,1,0:T(2,128)S(1)}, f32[4,2,1024]{2,1,0:T(2,128)S(1)}, f32[4,2,1024]{2,1,0:T(2,128)S(1)}, f32...) custom-call(f32[4,1,2,4096]{3,2,1,0:T(2,128)} %signal.1, f32[4,1,2,4096]{3,2,1,0:T(2,128)} %cotangent.1, ...), custom_call_target="tpu_custom_call" | custom-call | flops 100000000 | bytes 1000000 | tf_op jit(solution)/shard_map/pallas_call | solution.py:620
  1.8 3.1 %collective-permute-start.1 = (f32[4,2,3072]{2,1,0:T(2,128)S(1)}, f32[4,2,3072]{2,1,0:T(2,128)S(1)}, u32[]{:S(2)}, u32[]{:S(2)}) collective-permute-start(f32[4,2,3072]{2,1,0:T(2,128)S(1)} %get-tuple-element.50), channel_id=1, source_target_pairs={{0,4},{1,5},{4,0},{5,1},{8,12},{9,13},{12,8},{13,9},{2,6},{3,7},{6... | collective-permute-start | bytes 294920 | tf_op jit(solution)/shard_map/ppermute | solution.py:527
  4.9 0.0 collective-permute-start.2
  4.9 1.5 %collective-permute-start = (f32[280,128]{1,0:T(8,128)S(1)}, f32[280,128]{1,0:T(8,128)S(1)}, u32[]{:S(2)}, u32[]{:S(2)}) collective-permute-start(f32[280,128]{1,0:T(8,128)S(1)} %get-tuple-element.43.pack), channel_id=1, source_target_pairs={{0,2},{1,3},{2,0},{3,1},{4,6},{5,7},{6,4},{7,5},{8,10},{9,11},{10,... | collective-permute-start | bytes 430088 | tf_op jit(solution)/shard_map/ppermute | solution.py:527
  6.4 3.1 %collective-permute-start.3 = (f32[4,2,1024]{2,1,0:T(2,128)S(1)}, f32[4,2,1024]{2,1,0:T(2,128)S(1)}, u32[]{:S(2)}, u32[]{:S(2)}) collective-permute-start(f32[4,2,1024]{2,1,0:T(2,128)S(1)} %get-tuple-element.56), channel_id=1, source_target_pairs={{0,6},{1,7},{2,4},{3,5},{4,2},{5,3},{6,0},{7,1},{8,14},{9,15},{10,... | collective-permute-start | bytes 98312 | tf_op jit(solution)/shard_map/ppermute | solution.py:572
  9.5 0.0 collective-permute-start.4
  9.5 0.4 %shard_map.78 = (s32[2,4]{1,0:T(2,128)S(1)}, s32[2,4]{1,0:T(2,128)S(1)}, f32[2,4]{1,0:T(2,128)S(1)}, bf16[4,256,256]{2,1,0:T(8,128)(2,1)S(1)}, bf16[4,256,256]{2...) custom-call(f32[280,128]{1,0:T(8,128)S(1)} %get-tuple-element.43.pack), custom_call_target="tpu_custom_call" | custom-call | flops 200000000 | bytes 6000000 | tf_op jit(solution)/shard_map/pallas_call | solution.py:504
  10.0 0.0 collective-permute-done.1.sides_0_.s_0__0_
  10.0 1.6 %collective-permute-start.10 = (f32[4,2,32,128]{3,2,1,0:T(8,128)S(1)}, f32[4,2,32,128]{3,2,1,0:T(8,128)S(1)}, u32[]{:S(2)}, u32[]{:S(2)}) collective-permute-start(f32[4,2,32,128]{3,2,1,0:T(8,128)S(1)} %get-tuple-element.69.c_0_), channel_id=1, source_target_pairs={{0,2},{1,3},{2,0},{3,1},{4,6},{5,7},{6,4},{7,5},{8,10},{9,11},{10,... | collective-permute-start | bytes 393224 | tf_op jit(solution)/shard_map/ppermute | solution.py:527
  11.6 0.0 collective-permute-done.2.sides_1_.s_0__1_
  11.6 0.8 %shard_map.80 = (f32[4,2,48,128]{3,2,1,0:T(8,128)S(1)}, f32[4,2,48,128]{3,2,1,0:T(8,128)S(1)}, f32[64,128]{1,0:T(8,128)S(1)}) custom-call(s32[2,4]{1,0:T(2,128)S(1)} %get-tuple-element.45.delays_0_, s32[2,4]{1,0:T(2,128)S(1)} %get-tuple-element.44.shifts_0_, f32[280,128]{1,0:T(8,128)S(1)} %get-tuple-element.43.pack, ...), custom_call_target="tpu_custom_call" | custom-call | flops 200000000 | bytes 6000000 | tf_op jit(solution)/shard_map/pallas_call | solution.py:504
  12.3 0.0 collective-permute-done.3.sides_0_.s_1__0_
  12.3 0.0 collective-permute-done.4.sides_1_.s_1__1_
  12.3 0.3 collective-permute-start.5
  12.6 1.0 %collective-permute-done.5 = f32[64,128]{1,0:T(8,128)S(1)} collective-permute-done((f32[64,128]{1,0:T(8,128)S(1)}, f32[64,128]{1,0:T(8,128)S(1)}, u32[]{:S(2)}, u32[]{:S(2)}) %collective-permute-start.5) | collective-permute-done | bytes 32800 | tf_op jit(solution)/shard_map/ppermute | solution.py:543
  13.6 0.4 collective-permute-start.6
  14.0 0.0 collective-permute-done.pack
  14.0 0.4 %shard_map.79 = (s32[2,4]{1,0:T(2,128)S(1)}, s32[2,4]{1,0:T(2,128)S(1)}, f32[2,4]{1,0:T(2,128)S(1)}, bf16[4,256,256]{2,1,0:T(8,128)(2,1)S(1)}, bf16[4,256,256]{2...) custom-call(f32[280,128]{1,0:T(8,128)S(1)} %collective-permute-done.pack), custom_call_target="tpu_custom_call" | custom-call | flops 200000000 | bytes 6000000 | tf_op jit(solution)/shard_map/pallas_call | solution.py:504
  14.5 0.6 %shard_map.81.linear0_1_ = f32[4,2,48,128]{3,2,1,0:T(8,128)S(1)} custom-call(s32[2,4]{1,0:T(2,128)S(1)} %get-tuple-element.47.shifts_0_.shifts_1_, f32[280,128]{1,0:T(8,128)S(1)} %collective-permute-done.pack, f32[4,2,1024]{2,1,0:T(2,128)S(1)} %collective-permute-done.3.sides_0_.s_1__0_, f32[4,2,1024]{2,1,0:T(2,128)S(1)} %collective-permute-done.4.sides_1_.s_1__1_, ...), custom_call_target="tpu_custom_call" | custom-call | flops 200000000 | bytes 6000000 | tf_op jit(solution)/shard_map/pallas_call | solution.py:504
  15.0 1.9 %collective-permute-done.6 = f32[64,128]{1,0:T(8,128)S(1)} collective-permute-done((f32[64,128]{1,0:T(8,128)S(1)}, f32[64,128]{1,0:T(8,128)S(1)}, u32[]{:S(2)}, u32[]{:S(2)}) %collective-permute-start.6) | collective-permute-done | bytes 32800 | tf_op jit(solution)/shard_map/ppermute | solution.py:527
  17.0 1.3 %shard_map.82 = (f32[4,48,128]{2,1,0:T(8,128)S(1)}, f32[4,48,128]{2,1,0:T(8,128)S(1)}, f32[8,2,48,128]{3,2,1,0:T(8,128)S(1)}, f32[4,2,48,128]{3,2,1,0:T(8,128)S(...) custom-call(s32[2,4]{1,0:T(2,128)S(1)} %get-tuple-element.45.delays_0_, ...), custom_call_target="tpu_custom_call" | custom-call | flops 200000000 | bytes 6000000 | tf_op jit(solution)/shard_map/pallas_call | solution.py:504
  18.3 0.3 collective-permute-start.7
  18.5 1.0 %collective-permute-done.7 = f32[48,128]{1,0:T(8,128)S(1)} collective-permute-done((f32[48,128]{1,0:T(8,128)S(1)}, f32[48,128]{1,0:T(8,128)S(1)}, u32[]{:S(2)}, u32[]{:S(2)}) %collective-permute-start.7) | collective-permute-done | bytes 24608 | tf_op jit(solution)/shard_map/ppermute | solution.py:543
  19.5 2.2 %collective-permute-start.9 = (f32[48,128]{1,0:T(8,128)S(1)}, f32[48,128]{1,0:T(8,128)S(1)}, u32[]{:S(2)}, u32[]{:S(2)}) collective-permute-start(f32[48,128]{1,0:T(8,128)S(1)} %add.29.own), channel_id=1, source_target_pairs={{0,5},{1,4},{4,1},{5,0},{8,13},{9,12},{12,9},{13,8},{2,7},{3,6},{6... | collective-permute-start | bytes 73736 | tf_op jit(solution)/shard_map/ppermute | solution.py:527
  21.7 0.3 collective-permute-start.8
  22.1 0.0 collective-permute-done.10.c_1_
  22.1 0.1 shard_map.83.cotangent
  22.1 1.1 %collective-permute-done.9.even_in = f32[48,128]{1,0:T(8,128)S(1)} collective-permute-done((f32[48,128]{1,0:T(8,128)S(1)}, f32[48,128]{1,0:T(8,128)S(1)}, u32[]{:S(2)}, u32[]{:S(2)}) %collective-permute-start.9) | collective-permute-done | bytes 24608 | tf_op jit(solution)/shard_map/ppermute | solution.py:527
  23.2 0.0 collective-permute-done.8.odd_in
  23.2 0.7 %shard_map.84 = (f32[8,2,48,128]{3,2,1,0:T(8,128)S(1)}, f32[48,128]{1,0:T(8,128)S(1)}) custom-call(s32[2,4]{1,0:T(2,128)S(1)} %get-tuple-element.45.delays_0_, s32[2,4]{1,0:T(2,128)S(1)} %get-tuple-element.46.delays_1_, f32[2,4]{1,0:T(2,128)S(1)} %get-tuple-element.48.gains_0_, f32[2,4]{1,0:T(2,128)S(1)} %get-tuple-element.49.gains_1_, ...), custom_call_target="tpu_custom_call" | custom-call | flops 200000000 | bytes 6000000 | tf_op jit(solution)/shard_map/pallas_call | solution.py:504
  23.9 0.4 collective-permute-start.11
  24.3 0.9 %collective-permute-done.11 = f32[48,128]{1,0:T(8,128)S(1)} collective-permute-done((f32[48,128]{1,0:T(8,128)S(1)}, f32[48,128]{1,0:T(8,128)S(1)}, u32[]{:S(2)}, u32[]{:S(2)}) %collective-permute-start.11) | collective-permute-done | bytes 24608 | tf_op jit(solution)/shard_map/ppermute | solution.py:543
  25.2 1.8 %collective-permute-start.13 = (f32[48,128]{1,0:T(8,128)S(1)}, f32[48,128]{1,0:T(8,128)S(1)}, u32[]{:S(2)}, u32[]{:S(2)}) collective-permute-start(f32[48,128]{1,0:T(8,128)S(1)} %add.30.own), channel_id=1, source_target_pairs={{0,5},{1,4},{4,1},{5,0},{8,13},{9,12},{12,9},{13,8},{2,7},{3,6},{6... | collective-permute-start | bytes 73736 | tf_op jit(solution)/shard_map/ppermute | solution.py:527
  27.0 0.3 collective-permute-start.12
  27.3 1.2 %collective-permute-done.13.even_in = f32[48,128]{1,0:T(8,128)S(1)} collective-permute-done((f32[48,128]{1,0:T(8,128)S(1)}, f32[48,128]{1,0:T(8,128)S(1)}, u32[]{:S(2)}, u32[]{:S(2)}) %collective-permute-start.13) | collective-permute-done | bytes 24608 | tf_op jit(solution)/shard_map/ppermute | solution.py:527
  28.5 0.0 collective-permute-done.12.odd_in
  28.5 1.0 %shard_map.85 = (f32[4,2,48,128]{3,2,1,0:T(8,128)S(1)}, f32[4,2,48,128]{3,2,1,0:T(8,128)S(1)}, f32[48,128]{1,0:T(8,128)S(1)}) custom-call(s32[2,4]{1,0:T(2,128)S(1)} %get-tuple-element.45.delays_0_, s32[2,4]{1,0:T(2,128)S(1)} %get-tuple-element.46.delays_1_, s32[2,4]{1,0:T(2,128)S(1)} %get-tuple-element.44.shifts_0_, ...), custom_call_target="tpu_custom_call" | custom-call | flops 200000000 | bytes 6000000 | tf_op jit(solution)/shard_map/pallas_call | solution.py:504
  29.5 0.4 collective-permute-start.14
  29.9 0.9 %collective-permute-done.14 = f32[48,128]{1,0:T(8,128)S(1)} collective-permute-done((f32[48,128]{1,0:T(8,128)S(1)}, f32[48,128]{1,0:T(8,128)S(1)}, u32[]{:S(2)}, u32[]{:S(2)}) %collective-permute-start.14) | collective-permute-done | bytes 24608 | tf_op jit(solution)/shard_map/ppermute | solution.py:543
  30.8 1.8 %collective-permute-start.16 = (f32[48,128]{1,0:T(8,128)S(1)}, f32[48,128]{1,0:T(8,128)S(1)}, u32[]{:S(2)}, u32[]{:S(2)}) collective-permute-start(f32[48,128]{1,0:T(8,128)S(1)} %add.31.own), channel_id=1, source_target_pairs={{0,5},{1,4},{4,1},{5,0},{8,13},{9,12},{12,9},{13,8},{2,7},{3,6},{6... | collective-permute-start | bytes 73736 | tf_op jit(solution)/shard_map/ppermute | solution.py:527
  32.6 0.3 collective-permute-start.15
  32.9 1.1 %shard_map.86.taps1 = f32[8,128]{1,0:T(8,128)S(1)} custom-call(f32[4,2,48,128]{3,2,1,0:T(8,128)S(1)} %get-tuple-element.80.shifted, f32[4,2,48,128]{3,2,1,0:T(8,128)S(1)} %get-tuple-element.81.grad), custom_call_target="tpu_custom_call" | custom-call | flops 200000000 | bytes 6000000 | tf_op jit(solution)/shard_map/pallas_call | solution.py:504
  34.0 0.1 collective-permute-done.16.even_in
  34.1 0.0 collective-permute-done.15.odd_in
  34.1 1.0 %shard_map.87 = (f32[4,2,48,128]{3,2,1,0:T(8,128)S(1)}, f32[16,128]{1,0:T(8,128)S(1)}) custom-call(s32[2,4]{1,0:T(2,128)S(1)} %get-tuple-element.45.delays_0_, f32[4,2,48,128]{3,2,1,0:T(8,128)S(1)} %get-tuple-element.77.turned0, f32[4,2,48,128]{3,2,1,0:T(8,128)S(1)} %get-tuple-element.54.linear0_0_.linear0, f32[48,128]{1,0:T(8,128)S(1)} %add.31.own, ...), custom_call_target="tpu_custom_call" | custom-call | flops 200000000 | bytes 6000000 | tf_op jit(solution)/shard_map/pallas_call | solution.py:504
  35.1 0.4 collective-permute-start.17
  35.5 0.8 %collective-permute-done.17 = f32[16,128]{1,0:T(8,128)S(1)} collective-permute-done((f32[16,128]{1,0:T(8,128)S(1)}, f32[16,128]{1,0:T(8,128)S(1)}, u32[]{:S(2)}, u32[]{:S(2)}) %collective-permute-start.17) | collective-permute-done | bytes 8224 | tf_op jit(solution)/shard_map/ppermute | solution.py:543
  36.3 0.9 %collective-permute-start.20 = (f32[16,128]{1,0:T(8,128)S(1)}, f32[16,128]{1,0:T(8,128)S(1)}, u32[]{:S(2)}, u32[]{:S(2)}) collective-permute-start(f32[16,128]{1,0:T(8,128)S(1)} %add.32), channel_id=1, source_target_pairs={{0,13},{1,12},{4,9},{5,8},{8,5},{9,4},{12,1},{13,0},{2,15},{3,14},... | collective-permute-start | bytes 24584 | tf_op jit(solution)/shard_map/ppermute | solution.py:527
  37.2 2.3 %collective-permute-start.19 = (f32[16,128]{1,0:T(8,128)S(1)}, f32[16,128]{1,0:T(8,128)S(1)}, u32[]{:S(2)}, u32[]{:S(2)}) collective-permute-start(f32[16,128]{1,0:T(8,128)S(1)} %add.32), channel_id=1, source_target_pairs={{0,9},{1,8},{4,13},{5,12},{8,1},{9,0},{12,5},{13,4},{2,11},{3,10},... | collective-permute-start | bytes 24584 | tf_op jit(solution)/shard_map/ppermute | solution.py:527
  39.5 0.8 %collective-permute-start.18 = (f32[16,128]{1,0:T(8,128)S(1)}, f32[16,128]{1,0:T(8,128)S(1)}, u32[]{:S(2)}, u32[]{:S(2)}) collective-permute-start(f32[16,128]{1,0:T(8,128)S(1)} %add.32), channel_id=1, source_target_pairs={{0,5},{1,4},{4,1},{5,0},{8,13},{9,12},{12,9},{13,8},{2,7},{3,6},{6... | collective-permute-start | bytes 24584 | tf_op jit(solution)/shard_map/ppermute | solution.py:527
  40.4 1.1 %shard_map.88 = f32[4,1,2,4096]{3,2,1,0:T(2,128)} custom-call(s32[2,4]{1,0:T(2,128)S(1)} %get-tuple-element.44.shifts_0_, f32[4,2,48,128]{3,2,1,0:T(8,128)S(1)} %get-tuple-element.82.grad0, bf16[4,256,256]{2,1,0:T(8,128)(2,1)S(1)} %get-tuple-element.52.high, bf16[4,256,256]{2,1,0:T(8,128)(2,1)S(1)} %get-tuple-element.53.low), custom_call_target="tpu_custom_call" | custom-call | flops 200000000 | bytes 6000000 | tf_op jit(solution)/shard_map/pallas_call | solution.py:504
  41.5 0.0 collective-permute-done.20
  41.5 0.0 collective-permute-done.19
  41.5 1.1 %collective-permute-done.18 = f32[16,128]{1,0:T(8,128)S(1)} collective-permute-done((f32[16,128]{1,0:T(8,128)S(1)}, f32[16,128]{1,0:T(8,128)S(1)}, u32[]{:S(2)}, u32[]{:S(2)}) %collective-permute-start.18) | collective-permute-done | bytes 8224 | tf_op jit(solution)/shard_map/ppermute | solution.py:527
  42.6 0.6 %add_add_fusion = f32[16,128]{1,0:T(8,128)} fusion(f32[16,128]{1,0:T(8,128)S(1)} %collective-permute-done.19, f32[16,128]{1,0:T(8,128)S(1)} %collective-permute-done.20, f32[16,128]{1,0:T(8,128)S(1)} %add.32, f32[16,128]{1,0:T(8,128)S(1)} %collective-permute-done.18), kind=kLoop, calls=%fused_computation | loop fusion | flops 6144 | bytes 40960 | tf_op jit(solution)/shard_map/add | solution.py:579
  (6 shorter events, 0.0 us)
Async XLA Ops:
  1.8 8.2 %collective-permute-start.1 = (f32[4,2,3072]{2,1,0:T(2,128)S(1)}, f32[4,2,3072]{2,1,0:T(2,128)S(1)}, u32[]{:S(2)}, u32[]{:S(2)}) collective-permute-start(f32[4,2,3072]{2,1,0:T(2,128)S(1)} %get-tuple-element.50), channel_id=1, source_target_pairs={{0,4},{1,5},{4,0},{5,1},{8,12},{9,13},{12,8},{13,9},{2,6},{3,7},{6... | collective-permute-start | bytes 294920 | tf_op jit(solution)/shard_map/ppermute | solution.py:527
  4.9 6.6 %collective-permute-start.2 = (f32[4,2,3072]{2,1,0:T(2,128)S(1)}, f32[4,2,3072]{2,1,0:T(2,128)S(1)}, u32[]{:S(2)}, u32[]{:S(2)}) collective-permute-start(f32[4,2,3072]{2,1,0:T(2,128)S(1)} %get-tuple-element.51), channel_id=1, source_target_pairs={{0,1},{1,0},{4,8},{5,9},{8,4},{9,5},{12,13},{13,12},{2,3},{3,2},{6... | collective-permute-start | bytes 294920 | tf_op jit(solution)/shard_map/ppermute | solution.py:527
  4.9 9.1 %collective-permute-start = (f32[280,128]{1,0:T(8,128)S(1)}, f32[280,128]{1,0:T(8,128)S(1)}, u32[]{:S(2)}, u32[]{:S(2)}) collective-permute-start(f32[280,128]{1,0:T(8,128)S(1)} %get-tuple-element.43.pack), channel_id=1, source_target_pairs={{0,2},{1,3},{2,0},{3,1},{4,6},{5,7},{6,4},{7,5},{8,10},{9,11},{10,... | collective-permute-start | bytes 430088 | tf_op jit(solution)/shard_map/ppermute | solution.py:527
  6.4 5.9 %collective-permute-start.3 = (f32[4,2,1024]{2,1,0:T(2,128)S(1)}, f32[4,2,1024]{2,1,0:T(2,128)S(1)}, u32[]{:S(2)}, u32[]{:S(2)}) collective-permute-start(f32[4,2,1024]{2,1,0:T(2,128)S(1)} %get-tuple-element.56), channel_id=1, source_target_pairs={{0,6},{1,7},{2,4},{3,5},{4,2},{5,3},{6,0},{7,1},{8,14},{9,15},{10,... | collective-permute-start | bytes 98312 | tf_op jit(solution)/shard_map/ppermute | solution.py:572
  9.5 2.8 %collective-permute-start.4 = (f32[4,2,1024]{2,1,0:T(2,128)S(1)}, f32[4,2,1024]{2,1,0:T(2,128)S(1)}, u32[]{:S(2)}, u32[]{:S(2)}) collective-permute-start(f32[4,2,1024]{2,1,0:T(2,128)S(1)} %get-tuple-element.57), channel_id=1, source_target_pairs={{0,1},{1,0},{2,3},{3,2},{4,10},{5,11},{6,8},{7,9},{8,6},{9,7},{10,... | collective-permute-start | bytes 98312 | tf_op jit(solution)/shard_map/ppermute | solution.py:572
  10.0 12.1 %collective-permute-start.10 = (f32[4,2,32,128]{3,2,1,0:T(8,128)S(1)}, f32[4,2,32,128]{3,2,1,0:T(8,128)S(1)}, u32[]{:S(2)}, u32[]{:S(2)}) collective-permute-start(f32[4,2,32,128]{3,2,1,0:T(8,128)S(1)} %get-tuple-element.69.c_0_), channel_id=1, source_target_pairs={{0,2},{1,3},{2,0},{3,1},{4,6},{5,7},{6,4},{7,5},{8,10},{9,11},{10,... | collective-permute-start | bytes 393224 | tf_op jit(solution)/shard_map/ppermute | solution.py:527
  12.3 1.3 %collective-permute-start.5 = (f32[64,128]{1,0:T(8,128)S(1)}, f32[64,128]{1,0:T(8,128)S(1)}, u32[]{:S(2)}, u32[]{:S(2)}) collective-permute-start(f32[64,128]{1,0:T(8,128)S(1)} %get-tuple-element.62), channel_id=1, source_target_pairs={{0,1},{1,0},{2,3},{3,2},{4,5},{5,4},{6,7},{7,6},{8,9},{9,8},{10,11... | collective-permute-start | bytes 98312 | tf_op jit(solution)/shard_map/ppermute | solution.py:543
  13.6 3.3 %collective-permute-start.6 = (f32[64,128]{1,0:T(8,128)S(1)}, f32[64,128]{1,0:T(8,128)S(1)}, u32[]{:S(2)}, u32[]{:S(2)}) collective-permute-start(f32[64,128]{1,0:T(8,128)S(1)} %add.27), channel_id=1, source_target_pairs={{0,3},{1,2},{2,1},{3,0},{4,7},{5,6},{6,5},{7,4},{8,11},{9,10},{10,... | collective-permute-start | bytes 98312 | tf_op jit(solution)/shard_map/ppermute | solution.py:527
  18.3 1.3 %collective-permute-start.7 = (f32[48,128]{1,0:T(8,128)S(1)}, f32[48,128]{1,0:T(8,128)S(1)}, u32[]{:S(2)}, u32[]{:S(2)}) collective-permute-start(f32[48,128]{1,0:T(8,128)S(1)} %get-tuple-element.68), channel_id=1, source_target_pairs={{0,1},{1,0},{2,3},{3,2},{4,5},{5,4},{6,7},{7,6},{8,9},{9,8},{10,11... | collective-permute-start | bytes 73736 | tf_op jit(solution)/shard_map/ppermute | solution.py:543
  19.5 3.7 %collective-permute-start.9 = (f32[48,128]{1,0:T(8,128)S(1)}, f32[48,128]{1,0:T(8,128)S(1)}, u32[]{:S(2)}, u32[]{:S(2)}) collective-permute-start(f32[48,128]{1,0:T(8,128)S(1)} %add.29.own), channel_id=1, source_target_pairs={{0,5},{1,4},{4,1},{5,0},{8,13},{9,12},{12,9},{13,8},{2,7},{3,6},{6... | collective-permute-start | bytes 73736 | tf_op jit(solution)/shard_map/ppermute | solution.py:527
  21.7 1.5 %collective-permute-start.8 = (f32[48,128]{1,0:T(8,128)S(1)}, f32[48,128]{1,0:T(8,128)S(1)}, u32[]{:S(2)}, u32[]{:S(2)}) collective-permute-start(f32[48,128]{1,0:T(8,128)S(1)} %add.29.own), channel_id=1, source_target_pairs={{0,1},{1,0},{4,9},{5,8},{8,5},{9,4},{12,13},{13,12},{2,3},{3,2},{6... | collective-permute-start | bytes 73736 | tf_op jit(solution)/shard_map/ppermute | solution.py:527
  23.9 1.3 %collective-permute-start.11 = (f32[48,128]{1,0:T(8,128)S(1)}, f32[48,128]{1,0:T(8,128)S(1)}, u32[]{:S(2)}, u32[]{:S(2)}) collective-permute-start(f32[48,128]{1,0:T(8,128)S(1)} %get-tuple-element.73), channel_id=1, source_target_pairs={{0,1},{1,0},{2,3},{3,2},{4,5},{5,4},{6,7},{7,6},{8,9},{9,8},{10,11... | collective-permute-start | bytes 73736 | tf_op jit(solution)/shard_map/ppermute | solution.py:543
  25.2 3.3 %collective-permute-start.13 = (f32[48,128]{1,0:T(8,128)S(1)}, f32[48,128]{1,0:T(8,128)S(1)}, u32[]{:S(2)}, u32[]{:S(2)}) collective-permute-start(f32[48,128]{1,0:T(8,128)S(1)} %add.30.own), channel_id=1, source_target_pairs={{0,5},{1,4},{4,1},{5,0},{8,13},{9,12},{12,9},{13,8},{2,7},{3,6},{6... | collective-permute-start | bytes 73736 | tf_op jit(solution)/shard_map/ppermute | solution.py:527
  27.0 1.5 %collective-permute-start.12 = (f32[48,128]{1,0:T(8,128)S(1)}, f32[48,128]{1,0:T(8,128)S(1)}, u32[]{:S(2)}, u32[]{:S(2)}) collective-permute-start(f32[48,128]{1,0:T(8,128)S(1)} %add.30.own), channel_id=1, source_target_pairs={{0,1},{1,0},{4,9},{5,8},{8,5},{9,4},{12,13},{13,12},{2,3},{3,2},{6... | collective-permute-start | bytes 73736 | tf_op jit(solution)/shard_map/ppermute | solution.py:527
  29.5 1.3 %collective-permute-start.14 = (f32[48,128]{1,0:T(8,128)S(1)}, f32[48,128]{1,0:T(8,128)S(1)}, u32[]{:S(2)}, u32[]{:S(2)}) collective-permute-start(f32[48,128]{1,0:T(8,128)S(1)} %get-tuple-element.78), channel_id=1, source_target_pairs={{0,1},{1,0},{2,3},{3,2},{4,5},{5,4},{6,7},{7,6},{8,9},{9,8},{10,11... | collective-permute-start | bytes 73736 | tf_op jit(solution)/shard_map/ppermute | solution.py:543
  30.8 3.3 %collective-permute-start.16 = (f32[48,128]{1,0:T(8,128)S(1)}, f32[48,128]{1,0:T(8,128)S(1)}, u32[]{:S(2)}, u32[]{:S(2)}) collective-permute-start(f32[48,128]{1,0:T(8,128)S(1)} %add.31.own), channel_id=1, source_target_pairs={{0,5},{1,4},{4,1},{5,0},{8,13},{9,12},{12,9},{13,8},{2,7},{3,6},{6... | collective-permute-start | bytes 73736 | tf_op jit(solution)/shard_map/ppermute | solution.py:527
  32.6 1.5 %collective-permute-start.15 = (f32[48,128]{1,0:T(8,128)S(1)}, f32[48,128]{1,0:T(8,128)S(1)}, u32[]{:S(2)}, u32[]{:S(2)}) collective-permute-start(f32[48,128]{1,0:T(8,128)S(1)} %add.31.own), channel_id=1, source_target_pairs={{0,1},{1,0},{4,9},{5,8},{8,5},{9,4},{12,13},{13,12},{2,3},{3,2},{6... | collective-permute-start | bytes 73736 | tf_op jit(solution)/shard_map/ppermute | solution.py:527
  35.1 1.2 %collective-permute-start.17 = (f32[16,128]{1,0:T(8,128)S(1)}, f32[16,128]{1,0:T(8,128)S(1)}, u32[]{:S(2)}, u32[]{:S(2)}) collective-permute-start(f32[16,128]{1,0:T(8,128)S(1)} %get-tuple-element.83), channel_id=1, source_target_pairs={{0,1},{1,0},{2,3},{3,2},{4,5},{5,4},{6,7},{7,6},{8,9},{9,8},{10,11... | collective-permute-start | bytes 24584 | tf_op jit(solution)/shard_map/ppermute | solution.py:543
  36.3 5.2 %collective-permute-start.20 = (f32[16,128]{1,0:T(8,128)S(1)}, f32[16,128]{1,0:T(8,128)S(1)}, u32[]{:S(2)}, u32[]{:S(2)}) collective-permute-start(f32[16,128]{1,0:T(8,128)S(1)} %add.32), channel_id=1, source_target_pairs={{0,13},{1,12},{4,9},{5,8},{8,5},{9,4},{12,1},{13,0},{2,15},{3,14},... | collective-permute-start | bytes 24584 | tf_op jit(solution)/shard_map/ppermute | solution.py:527
  37.2 4.3 %collective-permute-start.19 = (f32[16,128]{1,0:T(8,128)S(1)}, f32[16,128]{1,0:T(8,128)S(1)}, u32[]{:S(2)}, u32[]{:S(2)}) collective-permute-start(f32[16,128]{1,0:T(8,128)S(1)} %add.32), channel_id=1, source_target_pairs={{0,9},{1,8},{4,13},{5,12},{8,1},{9,0},{12,5},{13,4},{2,11},{3,10},... | collective-permute-start | bytes 24584 | tf_op jit(solution)/shard_map/ppermute | solution.py:527
  39.5 3.1 %collective-permute-start.18 = (f32[16,128]{1,0:T(8,128)S(1)}, f32[16,128]{1,0:T(8,128)S(1)}, u32[]{:S(2)}, u32[]{:S(2)}) collective-permute-start(f32[16,128]{1,0:T(8,128)S(1)} %add.32), channel_id=1, source_target_pairs={{0,5},{1,4},{4,1},{5,0},{8,13},{9,12},{12,9},{13,8},{2,7},{3,6},{6... | collective-permute-start | bytes 24584 | tf_op jit(solution)/shard_map/ppermute | solution.py:527
